TPU v7x, 32 devices: a whole 2x2x4 slice. The times are simulated.
32 devices in a mesh: comp: 2 (over core), gx: 2 (over y), gy: 8 (over z, x).
Axes of the slice: x: 2, y: 2, z: 4, core: 2. Of those that a mesh axis runs over, the one named last changes fastest.
Arguments:
- state_incr: float32 [2, 2, 128, 32, 1024], P('comp', None, None, 'gx', 'gy'), may hold values from -6 to 6
- winds: float32 [2, 2, 128, 32, 1024], P('comp', None, None, 'gx', 'gy'), may hold values from -0.4 to 0.4
- coupling: float32 [32, 1024], P('gx', 'gy'), may hold values from 0.1 to 0.6
- background: float32 [2, 2, 128], P('comp'), may hold values from 0.5 to 2
- obs_dest: int32 [16384, 1], P(('comp', 'gx', 'gy')), may hold values from 0 to 15; in each aligned block of 512 rows (0 to 511, 512 to 1023, ...) at most 64 rows name the same one
- obs_col: int32 [16384], P(('comp', 'gx', 'gy')), may hold values from 0 to 2047
- obs_op: float32 [16384, 256], P(('comp', 'gx', 'gy')), may hold values from -0.375 to 0.375
- obs_prec: float32 [16384], P(('comp', 'gx', 'gy')), may hold values from 0.5 to 4
Outputs:
- hess_vec: float32 [2, 2, 128, 32, 1024], P('comp', None, None, 'gx', 'gy')
Inputs may be any that keep to these rules, and one draw needn't show every extreme that they name: `obs_dest`: among the rows of one device at most 64 name the same owner, a bound that some block reaches of them; owners are tiles of the record's own component. `obs_col`: column m of a tile is its cell (m // 128, m % 128).
All inputs are finite; a program needn't handle non-finite values.
Results may differ from a plain program's by a relative error of at most 0.000057.
Values sent between devices are 32-bit elements; how exact they have to be, the bound alone decides.
No kernel may reach another device: no remote copies, remote signals or barrier semaphores. Data moves between devices by JAX's collectives and lax.ppermute only.
A program may use at most 128 MiB of HBM per device.

v0:
```python
import jax
import jax.numpy as jnp
from jax import lax
from jax.sharding import PartitionSpec as P

HORIZ_MIX = 0.1
VERT_MIX = 0.15


def from_partner(block, axis, distance):
    count = lax.axis_size(axis)
    route = []
    for low in range(count):
        high = low | 1 << distance
        if high != low and high < count:
            route += [(low, high), (high, low)]
    return lax.ppermute(block, axis, route)


def extended_2(cells, sides, width):
    for axis, dim in sides:
        count = lax.axis_size(axis)
        ends = count - 1
        head = lax.slice_in_dim(cells, 0, width, axis=dim)
        tail = lax.slice_in_dim(cells, cells.shape[dim] - width, cells.shape[dim], axis=dim)
        cells = jnp.concatenate(
            [
                lax.ppermute(tail, axis, [(i, (i + 1) % count) for i in range(ends)]),
                cells,
                lax.ppermute(head, axis, [((i + 1) % count, i) for i in range(ends)]),
            ],
            axis=dim,
        )
    return cells


def vertical(field):
    upper = jnp.concatenate([field[:, 1:], field[:, -1:]], axis=1)
    lower = jnp.concatenate([field[:, :1], field[:, :-1]], axis=1)
    return VERT_MIX * (upper + lower - 2.0 * field)


def forward_stencil(extended, wind_x, wind_y):
    inner = extended[:, :, 1:-1, 1:-1]
    result = inner * (1.0 - 4.0 * HORIZ_MIX) + vertical(inner)
    result = result + (HORIZ_MIX - 0.5 * wind_x) * extended[:, :, 2:, 1:-1]
    result = result + (HORIZ_MIX + 0.5 * wind_x) * extended[:, :, :-2, 1:-1]
    result = result + (HORIZ_MIX - 0.5 * wind_y) * extended[:, :, 1:-1, 2:]
    result = result + (HORIZ_MIX + 0.5 * wind_y) * extended[:, :, 1:-1, :-2]
    return result


def adjoint_stencil(extended, wind_x_ext, wind_y_ext):
    inner = extended[:, :, 1:-1, 1:-1]
    result = inner * (1.0 - 4.0 * HORIZ_MIX) + vertical(inner)
    result = result + (HORIZ_MIX - 0.5 * wind_x_ext[:, :-2, 1:-1]) * extended[:, :, :-2, 1:-1]
    result = result + (HORIZ_MIX + 0.5 * wind_x_ext[:, 2:, 1:-1]) * extended[:, :, 2:, 1:-1]
    result = result + (HORIZ_MIX - 0.5 * wind_y_ext[:, 1:-1, :-2]) * extended[:, :, 1:-1, :-2]
    result = result + (HORIZ_MIX + 0.5 * wind_y_ext[:, 1:-1, 2:]) * extended[:, :, 1:-1, 2:]
    return result


def couple(field, gamma, transposed):
    surface_slab = field[:, 0]
    partner = from_partner(surface_slab, "comp", 0)
    own_share = jnp.where(lax.axis_index("comp") == 0, 1.0, 0.5)
    peer_share = 1.5 - own_share
    if transposed:
        updated = surface_slab - own_share * gamma * surface_slab + peer_share * gamma * partner
    else:
        updated = surface_slab - own_share * gamma * (surface_slab - partner)
    return field.at[:, 0].set(updated)


def local(state_incr, winds, coupling, background, obs_dest, obs_col, obs_op, obs_prec):
    state = state_incr[0]
    levels = state.shape[1]
    rows_x = state.shape[2]
    rows_y = state.shape[3]
    static = jnp.concatenate([winds[0].reshape(2 * levels, rows_x, rows_y), coupling[None]], axis=0)
    rimmed = extended_2(static, (("gx", 1), ("gy", 2)), 1)
    wind_x_ext = rimmed[:levels]
    wind_y_ext = rimmed[levels : 2 * levels]
    wind_x = wind_x_ext[:, 1:-1, 1:-1]
    wind_y = wind_y_ext[:, 1:-1, 1:-1]
    gx_count = lax.axis_size("gx")
    gy_count = lax.axis_size("gy")
    tile_count = gx_count * gy_count
    row_count = obs_col.shape[0]
    capacity = 2 * row_count // tile_count
    owners = obs_dest[:, 0]
    owner_iota = lax.broadcasted_iota(jnp.int32, (row_count, tile_count), 1)
    hits = (owners[:, None] == owner_iota).astype(jnp.int32)
    slots = jnp.sum(jnp.cumsum(hits, axis=0) * hits, axis=1) - 1
    position = owners * capacity + slots
    weighted = obs_op * jnp.sqrt(obs_prec)[:, None]
    record_width = weighted.shape[1]
    send_op = (
        jnp.zeros((tile_count * capacity, record_width), jnp.float32).at[position].set(weighted)
    )
    send_col = jnp.zeros((tile_count * capacity,), jnp.int32).at[position].set(obs_col)
    recv_op, recv_col = (
        lax.all_to_all(
            send_op.reshape(tile_count, capacity, record_width),
            ("gx", "gy"),
            split_axis=0,
            concat_axis=0,
            tiled=True,
        ),
        lax.all_to_all(
            send_col.reshape(tile_count, capacity),
            ("gx", "gy"),
            split_axis=0,
            concat_axis=0,
            tiled=True,
        ),
    )
    recv_op = recv_op.reshape(-1, record_width)
    recv_col = recv_col.reshape(-1)
    current = state
    for sweep in range(2):
        extended = extended_2(current, (("gx", 2), ("gy", 3)), 1)
        current = couple(forward_stencil(extended, wind_x, wind_y), coupling, False)
    cell_count = rows_x * rows_y
    columns = current.reshape(2 * levels, cell_count)
    cell_iota = lax.broadcasted_iota(jnp.int32, (recv_col.shape[0], cell_count), 1)
    selector = (recv_col[:, None] == cell_iota).astype(jnp.float32)
    sampled = lax.dot_general(
        selector,
        columns,
        (((1,), (1,)), ((), ())),
        precision=lax.Precision.HIGHEST,
        preferred_element_type=jnp.float32,
    )
    innovation = jnp.sum(sampled * recv_op, axis=1)
    spread = recv_op * innovation[:, None]
    adjoint_cols = lax.dot_general(
        spread,
        selector,
        (((0,), (0,)), ((), ())),
        precision=lax.Precision.HIGHEST,
        preferred_element_type=jnp.float32,
    )
    adjoint = adjoint_cols.reshape(2, levels, rows_x, rows_y)
    for sweep in range(2):
        adjoint = couple(adjoint, coupling, True)
        extended = extended_2(adjoint, (("gx", 2), ("gy", 3)), 1)
        adjoint = adjoint_stencil(extended, wind_x_ext, wind_y_ext)
    result = background[0][:, :, None, None] * state + adjoint
    return result[None]


def solution(mesh):
    placed = (
        P("comp", None, None, "gx", "gy"),
        P("comp", None, None, "gx", "gy"),
        P("gx", "gy"),
        P("comp", None, None),
        P(("comp", "gx", "gy"), None),
        P(("comp", "gx", "gy")),
        P(("comp", "gx", "gy"), None),
        P(("comp", "gx", "gy")),
    )
    return jax.shard_map(
        local,
        mesh=mesh,
        in_specs=placed,
        out_specs=P("comp", None, None, "gx", "gy"),
        check_vma=False,
    )
```

profile of v0, /device:TPU:8, one launch (start us, length us, event | category | flops | bytes accessed | tf_op | source)
XLA Modules:
  0.0 223.4 jit_solution(725924514547365847)
XLA Ops:
  3.3 4.6 %collective-permute-start.1 = (f32[2,128,1,128]{1,3,2,0:T(8,128)S(1)}, f32[2,128,1,128]{1,3,2,0:T(8,128)S(1)}, u32[]{:S(2)}, u32[]{:S(2)}) collective-permute-start(f32[2,128,1,128]{1,3,2,0:T(8,128)S(1)} %get-tuple-element.89), channel_id=1, source_target_pairs={{0,8},{1,9},{2,10},{3,11},{4,12},{5,13},{6,14},{7,15},{16,24},{17,... | collective-permute-start | bytes 393224 | tf_op jit(solution)/shard_map/ppermute | solution.py:28
  12.7 6.3 %all-to-all-start.1 = ((s32[16,1,64]{2,1,0:T(1,128)}), s32[16,1,64]{2,1,0:T(1,128)S(1)}, u32[]{:S(2)}, u32[]{:S(2)}) async-start(s32[16,1,64]{2,1,0:T(1,128)} %all_to_all.10), calls=%async_computation.1 | async-start | bytes 16384 | tf_op jit(solution)/shard_map/all_to_all | solution.py:110
  19.0 2.7 %fusion.88 = (f32[2,1,16,128]{1,3,2,0:T(8,128)}, f32[2,1,16,128]{1,3,2,0:T(8,128)}) fusion(f32[2,128,16,128]{1,3,2,0:T(8,128)S(1)} %bitcast.66), kind=kLoop, calls=%fused_computation.178 | loop fusion | bytes 65536 | tf_op jit(solution)/shard_map/slice | solution.py:39
  21.8 2.7 %fusion.89 = (f32[2,127,16,128]{1,3,2,0:T(8,128)}, f32[2,127,16,128]{1,3,2,0:T(8,128)}) fusion(f32[2,128,16,128]{1,3,2,0:T(8,128)S(1)} %bitcast.67), kind=kLoop, calls=%fused_computation.179 | loop fusion | bytes 8323072 | tf_op jit(solution)/shard_map/slice | solution.py:39
  24.5 3.5 %collective-permute-start.2 = (f32[2,128,18,1]{1,3,2,0:T(1,128)S(1)}, f32[2,128,18,1]{1,3,2,0:T(1,128)S(1)}, u32[]{:S(2)}, u32[]{:S(2)}) collective-permute-start(f32[2,128,18,1]{1,3,2,0:T(1,128)S(1)} %get-tuple-element.67), channel_id=1, source_target_pairs={{1,0},{2,1},{3,2},{4,3},{5,4},{6,5},{7,6},{9,8},{10,9},{11,10},{12... | collective-permute-start | bytes 55304 | tf_op jit(solution)/shard_map/ppermute | solution.py:30
  34.3 2.9 %copy.172 = f32[128,16,128]{0,2,1:T(8,128)} copy(f32[128,16,128]{2,1,0:T(8,128)} %get-tuple-element.83) | data formatting | bytes 2097152 | tf_op jit(solution)/shard_map/add | solution.py:47
  42.3 5.9 %fusion.36 = f32[2,128,16,128]{1,3,2,0:T(8,128)S(1)} fusion(f32[2,128,18,1]{1,3,2,0:T(1,128)S(1)} %collective-permute-done.3, f32[2,128,1,128]{1,3,2,0:T(8,128)S(1)} %collective-permute-done, f32[2,128,16,128]{1,3,2,0:T(8,128)S(1)} %bitcast.69, f32[2,128,1,128]{1,3,2,0:T(8,128)S(1)} %collective-permute-done.1, ...), kind=kLoop, calls=%fused_computation.68 | loop fusion | flops 12582912 | bytes 12881920 | tf_op jit(solution)/shard_map/add | solution.py:49
  50.6 3.4 %scatter_custom_fusion = f32[1024,256]{1,0:T(8,128)} fusion(s32[512]{0:T(512)S(1)} %bitcast.78, f32[512,256]{1,0:T(8,128)S(1)} %copy-done.25, f32[]{:T(128)} %constant.112.clone.1, f32[512]{0:T(512)S(1)} %sqrt.3), kind=kCustom, calls=%fused_computation.127 | custom fusion | flops 131072 | bytes 1574916 | tf_op jit(solution)/shard_map/scatter | solution.py:99
  56.0 6.1 %scatter.36 = f32[2,128,16,128]{1,3,2,0:T(8,128)} dynamic-update-slice(f32[2,128,16,128]{1,3,2,0:T(8,128)} %copy-done, f32[2,1,16,128]{1,3,2,0:T(8,128)} %copy.175, s32[]{:T(128)} %constant.114.clone.1, s32[]{:T(128)} %constant.114.clone.1, s32[]{:T(128)} %constant.114.clone.1, s32[]{:T(128)} %constant.114.clone.1) | dynamic-update-slice | bytes 32772 | tf_op jit(solution)/shard_map/scatter | solution.py:72
  62.1 6.9 %all-to-all-start = ((f32[16,64,256]{2,1,0:T(8,128)}), f32[16,64,256]{2,1,0:T(8,128)}, u32[]{:S(2)}, u32[]{:S(2)}) async-start(f32[16,64,256]{2,1,0:T(8,128)} %bitcast.7), calls=%async_computation | async-start | bytes 2097152 | tf_op jit(solution)/shard_map/all_to_all | solution.py:103
  72.0 5.8 %collective-permute-start.6 = (f32[2,128,1,128]{1,3,2,0:T(8,128)}, f32[2,128,1,128]{1,3,2,0:T(8,128)}, u32[]{:S(2)}, u32[]{:S(2)}) collective-permute-start(f32[2,128,1,128]{1,3,2,0:T(8,128)} %get-tuple-element.79), channel_id=1, source_target_pairs={{0,8},{1,9},{2,10},{3,11},{4,12},{5,13},{6,14},{7,15},{16,24},{17,... | collective-permute-start | bytes 393224 | tf_op jit(solution)/shard_map/ppermute | solution.py:28
  77.9 2.9 %copy.183 = f32[256,16,128]{0,2,1:T(8,128)} copy(f32[256,16,128]{2,1,0:T(8,128)} %bitcast.70) | data formatting | bytes 4194304 | tf_op jit(solution)/shard_map/reshape;squeeze | solution.py:80
  86.5 3.4 %collective-permute-start.7 = (f32[2,128,18,1]{1,3,2,0:T(1,128)S(1)}, f32[2,128,18,1]{1,3,2,0:T(1,128)S(1)}, u32[]{:S(2)}, u32[]{:S(2)}) collective-permute-start(f32[2,128,18,1]{1,3,2,0:T(1,128)S(1)} %get-tuple-element.65), channel_id=1, source_target_pairs={{1,0},{2,1},{3,2},{4,3},{5,4},{6,5},{7,6},{9,8},{10,9},{11,10},{12... | collective-permute-start | bytes 55304 | tf_op jit(solution)/shard_map/ppermute | solution.py:30
  96.4 3.9 %fusion.28 = f32[2,128,16,128]{1,3,2,0:T(8,128)S(1)} fusion(f32[2,128,18,1]{1,3,2,0:T(1,128)S(1)} %collective-permute-done.8, f32[2,128,1,128]{1,3,2,0:T(8,128)} %collective-permute-done.5, f32[2,128,16,128]{1,3,2,0:T(8,128)S(1)} %copy-done.1, f32[2,128,1,128]{1,3,2,0:T(8,128)} %collective-permute-done.6, f32[2,128,18,1]{1,3,2,0:T(1,128)S(1)} %collective-permute-done.7, ...), kind=kLoop, calls=%fused_computation.51 | loop fusion | flops 12582912 | bytes 12881920 | tf_op jit(solution)/shard_map/add | solution.py:49
  111.3 6.1 %scatter.37 = f32[2,128,16,128]{1,3,2,0:T(8,128)} dynamic-update-slice(f32[2,128,16,128]{1,3,2,0:T(8,128)} %copy-done.9, f32[2,1,16,128]{1,3,2,0:T(8,128)} %copy.177, s32[]{:T(128)} %constant.114.clone.1, s32[]{:T(128)} %constant.114.clone.1, s32[]{:T(128)} %constant.114.clone.1, s32[]{:T(128)} %constant.114.clone.1) | dynamic-update-slice | bytes 32772 | tf_op jit(solution)/shard_map/scatter | solution.py:72
  117.4 3.1 %copy.178 = f32[2,128,16,128]{3,2,1,0:T(8,128)} copy(f32[2,128,16,128]{1,3,2,0:T(8,128)} %scatter.37) | data formatting | bytes 4194304 | tf_op jit(solution)/shard_map/scatter | solution.py:72
  123.0 6.4 %fusion.58 = f32[1024]{0:T(1024)S(1)} fusion(f32[1024,256]{0,1:T(8,128)} %copy.179, f32[32,8,16,128]{3,2,1,0:T(8,128)} %bitcast.71, s32[1024]{0:T(1024)} %eq.50), kind=kOutput, calls=%fused_computation.99 | convolution fusion | flops 6445071360 | bytes 3153920 | tf_op jit(solution)/shard_map/dot_general | solution.py:128
  134.3 5.1 %fusion.1 = f32[2,128,16,128]{1,3,2,0:T(8,128)S(1)} fusion(f32[2,128,1024,1]{2,1,3,0:T(8,128)} %bitcast.72, s32[16,128]{1,0:T(8,128)} %multiply_add_fusion, s32[1024]{0:T(1024)} %eq.50), kind=kOutput, calls=%fused_computation.4 | convolution fusion | flops 6444548096 | bytes 3158016 | tf_op jit(solution)/shard_map/dot_general | solution.py:137
  142.4 3.4 %collective-permute-start.15 = (f32[257,18,1]{0,2,1:T(1,128)}, f32[257,18,1]{0,2,1:T(1,128)}, u32[]{:S(2)}, u32[]{:S(2)}) collective-permute-start(f32[257,18,1]{0,2,1:T(1,128)} %get-tuple-element.55), channel_id=1, source_target_pairs={{0,1},{1,2},{2,3},{3,4},{4,5},{5,6},{6,7},{8,9},{9,10},{10,11},{11... | collective-permute-start | bytes 55520 | tf_op jit(solution)/shard_map/ppermute | solution.py:28
  145.9 3.3 %collective-permute-start.17 = (f32[257,18,1]{0,2,1:T(1,128)}, f32[257,18,1]{0,2,1:T(1,128)}, u32[]{:S(2)}, u32[]{:S(2)}) collective-permute-start(f32[257,18,1]{0,2,1:T(1,128)} %get-tuple-element.56), channel_id=1, source_target_pairs={{1,0},{2,1},{3,2},{4,3},{5,4},{6,5},{7,6},{9,8},{10,9},{11,10},{12... | collective-permute-start | bytes 55520 | tf_op jit(solution)/shard_map/ppermute | solution.py:30
  152.5 6.1 %scatter.38 = f32[2,128,16,128]{1,3,2,0:T(8,128)} dynamic-update-slice(f32[2,128,16,128]{1,3,2,0:T(8,128)} %copy-done.4, f32[2,1,16,128]{1,3,2,0:T(8,128)} %copy.181, s32[]{:T(128)} %constant.114.clone.1, s32[]{:T(128)} %constant.114.clone.1, s32[]{:T(128)} %constant.114.clone.1, s32[]{:T(128)} %constant.114.clone.1) | dynamic-update-slice | bytes 32772 | tf_op jit(solution)/shard_map/scatter | solution.py:72
  159.6 4.6 %collective-permute-start.12 = (f32[2,128,1,128]{1,3,2,0:T(8,128)S(1)}, f32[2,128,1,128]{1,3,2,0:T(8,128)S(1)}, u32[]{:S(2)}, u32[]{:S(2)}) collective-permute-start(f32[2,128,1,128]{1,3,2,0:T(8,128)S(1)} %get-tuple-element.75), channel_id=1, source_target_pairs={{0,8},{1,9},{2,10},{3,11},{4,12},{5,13},{6,14},{7,15},{16,24},{17,... | collective-permute-start | bytes 393224 | tf_op jit(solution)/shard_map/ppermute | solution.py:28
  165.6 2.8 %fusion.64 = (f32[128,16,128]{0,2,1:T(8,128)S(1)}, f32[128,16,128]{0,2,1:T(8,128)S(1)}, f32[128,16,128]{0,2,1:T(8,128)S(1)}, f32[128,16,128]{0,2,1:T(8,128)S(1)}) fusion(f32[257,18,1]{0,2,1:T(1,128)} %collective-permute-done.15, f32[257,1,128]{0,2,1:T(8,128)S(1)} %collective-permute-done.13, f32[257,1,128]{0,2,1:T(8,128)S(1)} %collective-permute-done.11, ...), kind=kLoop, calls=%fused_computation.108 | loop fusion | flops 5242880 | bytes 6599824 | tf_op jit(solution)/shard_map/sub | solution.py:58
  168.5 2.8 %collective-permute-done.14 = f32[2,128,1,128]{1,3,2,0:T(8,128)S(1)} collective-permute-done((f32[2,128,1,128]{1,3,2,0:T(8,128)S(1)}, f32[2,128,1,128]{1,3,2,0:T(8,128)S(1)}, u32[]{:S(2)}, u32[]{:S(2)}) %collective-permute-start.14) | collective-permute-done | bytes 131104 | tf_op jit(solution)/shard_map/ppermute | solution.py:30
  173.9 4.4 %collective-permute-start.18 = (f32[2,128,18,1]{1,3,2,0:T(1,128)S(1)}, f32[2,128,18,1]{1,3,2,0:T(1,128)S(1)}, u32[]{:S(2)}, u32[]{:S(2)}) collective-permute-start(f32[2,128,18,1]{1,3,2,0:T(1,128)S(1)} %get-tuple-element.64), channel_id=1, source_target_pairs={{1,0},{2,1},{3,2},{4,3},{5,4},{6,5},{7,6},{9,8},{10,9},{11,10},{12... | collective-permute-start | bytes 55304 | tf_op jit(solution)/shard_map/ppermute | solution.py:30
  180.6 3.0 %fusion.20 = f32[2,128,16,128]{1,3,2,0:T(8,128)S(1)} fusion(f32[2,128,18,1]{1,3,2,0:T(1,128)S(1)} %collective-permute-done.18, f32[2,128,1,128]{1,3,2,0:T(8,128)S(1)} %collective-permute-done.14, f32[2,128,16,128]{1,3,2,0:T(8,128)S(1)} %copy-done.5, f32[2,128,1,128]{1,3,2,0:T(8,128)S(1)} %collective-permute-done.12, ...), kind=kLoop, calls=%fused_computation.33 | loop fusion | flops 12582912 | bytes 12881920 | tf_op jit(solution)/shard_map/add | solution.py:59
  188.9 6.1 %scatter.39 = f32[2,128,16,128]{1,3,2,0:T(8,128)} dynamic-update-slice(f32[2,128,16,128]{1,3,2,0:T(8,128)} %copy-done.2, f32[2,1,16,128]{1,3,2,0:T(8,128)} %copy.185, s32[]{:T(128)} %constant.114.clone.1, s32[]{:T(128)} %constant.114.clone.1, s32[]{:T(128)} %constant.114.clone.1, s32[]{:T(128)} %constant.114.clone.1) | dynamic-update-slice | bytes 32772 | tf_op jit(solution)/shard_map/scatter | solution.py:72
  201.0 4.1 %collective-permute-done.21 = f32[2,128,1,128]{1,3,2,0:T(8,128)S(1)} collective-permute-done((f32[2,128,1,128]{1,3,2,0:T(8,128)S(1)}, f32[2,128,1,128]{1,3,2,0:T(8,128)S(1)}, u32[]{:S(2)}, u32[]{:S(2)}) %collective-permute-start.21) | collective-permute-done | bytes 131104 | tf_op jit(solution)/shard_map/ppermute | solution.py:30
  206.2 4.0 %collective-permute-start.22 = (f32[2,128,18,1]{1,3,2,0:T(1,128)S(1)}, f32[2,128,18,1]{1,3,2,0:T(1,128)S(1)}, u32[]{:S(2)}, u32[]{:S(2)}) collective-permute-start(f32[2,128,18,1]{1,3,2,0:T(1,128)S(1)} %get-tuple-element.61), channel_id=1, source_target_pairs={{0,1},{1,2},{2,3},{3,4},{4,5},{5,6},{6,7},{8,9},{9,10},{10,11},{11... | collective-permute-start | bytes 55304 | tf_op jit(solution)/shard_map/ppermute | solution.py:28
  210.2 2.7 %collective-permute-start.23 = (f32[2,128,18,1]{1,3,2,0:T(1,128)S(1)}, f32[2,128,18,1]{1,3,2,0:T(1,128)S(1)}, u32[]{:S(2)}, u32[]{:S(2)}) collective-permute-start(f32[2,128,18,1]{1,3,2,0:T(1,128)S(1)} %get-tuple-element.62), channel_id=1, source_target_pairs={{1,0},{2,1},{3,2},{4,3},{5,4},{6,5},{7,6},{9,8},{10,9},{11,10},{12... | collective-permute-start | bytes 55304 | tf_op jit(solution)/shard_map/ppermute | solution.py:30
  216.0 4.3 %fusion.12 = f32[1,2,128,16,128]{2,4,3,1,0:T(8,128)} fusion(f32[2,128,18,1]{1,3,2,0:T(1,128)S(1)} %collective-permute-done.23, f32[2,128,1,128]{1,3,2,0:T(8,128)S(1)} %collective-permute-done.21, f32[2,128,16,128]{1,3,2,0:T(8,128)S(1)} %copy-done.3, f32[2,128,1,128]{1,3,2,0:T(8,128)S(1)} %collective-permute-done.20, ...), kind=kLoop, calls=%fused_computation.16 | loop fusion | flops 13631488 | bytes 14980096 | tf_op jit(solution)/shard_map/broadcast_in_dim | solution.py:150
  220.4 3.0 %copy.187 = f32[1,2,128,16,128]{4,3,2,1,0:T(8,128)} copy(f32[1,2,128,16,128]{2,4,3,1,0:T(8,128)} %fusion.12) | data formatting | bytes 4194304 | tf_op jit(solution)/shard_map/broadcast_in_dim | solution.py:150
  (153 shorter events, 86.1 us)
Async XLA Ops:
  2.0 22.5 %collective-permute-start = (f32[2,128,1,128]{1,3,2,0:T(8,128)S(1)}, f32[2,128,1,128]{1,3,2,0:T(8,128)S(1)}, u32[]{:S(2)}, u32[]{:S(2)}) collective-permute-start(f32[2,128,1,128]{1,3,2,0:T(8,128)S(1)} %get-tuple-element.90), channel_id=1, source_target_pairs={{8,0},{9,1},{10,2},{11,3},{12,4},{13,5},{14,6},{15,7},{24,16},{25,... | collective-permute-start | bytes 393224 | tf_op jit(solution)/shard_map/ppermute | solution.py:30
  3.3 21.2 %collective-permute-start.1 = (f32[2,128,1,128]{1,3,2,0:T(8,128)S(1)}, f32[2,128,1,128]{1,3,2,0:T(8,128)S(1)}, u32[]{:S(2)}, u32[]{:S(2)}) collective-permute-start(f32[2,128,1,128]{1,3,2,0:T(8,128)S(1)} %get-tuple-element.89), channel_id=1, source_target_pairs={{0,8},{1,9},{2,10},{3,11},{4,12},{5,13},{6,14},{7,15},{16,24},{17,... | collective-permute-start | bytes 393224 | tf_op jit(solution)/shard_map/ppermute | solution.py:28
  12.7 49.4 %all-to-all-start.1 = ((s32[16,1,64]{2,1,0:T(1,128)}), s32[16,1,64]{2,1,0:T(1,128)S(1)}, u32[]{:S(2)}, u32[]{:S(2)}) async-start(s32[16,1,64]{2,1,0:T(1,128)} %all_to_all.10), calls=%async_computation.1 | async-start | bytes 16384 | tf_op jit(solution)/shard_map/all_to_all | solution.py:110
  24.5 17.8 %collective-permute-start.2 = (f32[2,128,18,1]{1,3,2,0:T(1,128)S(1)}, f32[2,128,18,1]{1,3,2,0:T(1,128)S(1)}, u32[]{:S(2)}, u32[]{:S(2)}) collective-permute-start(f32[2,128,18,1]{1,3,2,0:T(1,128)S(1)} %get-tuple-element.67), channel_id=1, source_target_pairs={{1,0},{2,1},{3,2},{4,3},{5,4},{6,5},{7,6},{9,8},{10,9},{11,10},{12... | collective-permute-start | bytes 55304 | tf_op jit(solution)/shard_map/ppermute | solution.py:30
  28.0 14.3 %collective-permute-start.3 = (f32[2,128,18,1]{1,3,2,0:T(1,128)S(1)}, f32[2,128,18,1]{1,3,2,0:T(1,128)S(1)}, u32[]{:S(2)}, u32[]{:S(2)}) collective-permute-start(f32[2,128,18,1]{1,3,2,0:T(1,128)S(1)} %get-tuple-element.68), channel_id=1, source_target_pairs={{0,1},{1,2},{2,3},{3,4},{4,5},{5,6},{6,7},{8,9},{9,10},{10,11},{11... | collective-permute-start | bytes 55304 | tf_op jit(solution)/shard_map/ppermute | solution.py:28
  50.2 3.8 %collective-permute-start.4 = (f32[2,16,128]{2,1,0:T(8,128)S(1)}, f32[2,16,128]{2,1,0:T(8,128)S(1)}, u32[]{:S(2)}, u32[]{:S(2)}) collective-permute-start(f32[2,16,128]{2,1,0:T(8,128)S(1)} %slice_reduce_fusion.3), channel_id=1, source_target_pairs={{0,16},{16,0},{1,17},{17,1},{2,18},{18,2},{3,19},{19,3},{4,20},{20... | collective-permute-start | bytes 49160 | tf_op jit(solution)/shard_map/ppermute | solution.py:17
  62.1 18.6 %copy-start.27 = (s32[16,1,64]{2,1,0:T(1,128)}, s32[16,1,64]{2,1,0:T(1,128)S(1)}, u32[]{:S(2)}) copy-start(s32[16,1,64]{2,1,0:T(1,128)S(1)} %all-to-all-done.1) | copy-start | bytes 12292
  62.1 58.3 %all-to-all-start = ((f32[16,64,256]{2,1,0:T(8,128)}), f32[16,64,256]{2,1,0:T(8,128)}, u32[]{:S(2)}, u32[]{:S(2)}) async-start(f32[16,64,256]{2,1,0:T(8,128)} %bitcast.7), calls=%async_computation | async-start | bytes 2097152 | tf_op jit(solution)/shard_map/all_to_all | solution.py:103
  70.7 14.9 %collective-permute-start.5 = (f32[2,128,1,128]{1,3,2,0:T(8,128)}, f32[2,128,1,128]{1,3,2,0:T(8,128)}, u32[]{:S(2)}, u32[]{:S(2)}) collective-permute-start(f32[2,128,1,128]{1,3,2,0:T(8,128)} %get-tuple-element.80), channel_id=1, source_target_pairs={{8,0},{9,1},{10,2},{11,3},{12,4},{13,5},{14,6},{15,7},{24,16},{25,... | collective-permute-start | bytes 393224 | tf_op jit(solution)/shard_map/ppermute | solution.py:30
  72.0 13.6 %collective-permute-start.6 = (f32[2,128,1,128]{1,3,2,0:T(8,128)}, f32[2,128,1,128]{1,3,2,0:T(8,128)}, u32[]{:S(2)}, u32[]{:S(2)}) collective-permute-start(f32[2,128,1,128]{1,3,2,0:T(8,128)} %get-tuple-element.79), channel_id=1, source_target_pairs={{0,8},{1,9},{2,10},{3,11},{4,12},{5,13},{6,14},{7,15},{16,24},{17,... | collective-permute-start | bytes 393224 | tf_op jit(solution)/shard_map/ppermute | solution.py:28
  83.1 57.6 %collective-permute-start.11 = (f32[257,1,128]{0,2,1:T(8,128)}, f32[257,1,128]{0,2,1:T(8,128)S(1)}, u32[]{:S(2)}, u32[]{:S(2)}) collective-permute-start(f32[257,1,128]{0,2,1:T(8,128)} %get-tuple-element.59), channel_id=1, source_target_pairs={{0,8},{1,9},{2,10},{3,11},{4,12},{5,13},{6,14},{7,15},{16,24},{17,... | collective-permute-start | bytes 394760 | tf_op jit(solution)/shard_map/ppermute | solution.py:28
  84.3 56.3 %collective-permute-start.13 = (f32[257,1,128]{0,2,1:T(8,128)}, f32[257,1,128]{0,2,1:T(8,128)S(1)}, u32[]{:S(2)}, u32[]{:S(2)}) collective-permute-start(f32[257,1,128]{0,2,1:T(8,128)} %get-tuple-element.60), channel_id=1, source_target_pairs={{8,0},{9,1},{10,2},{11,3},{12,4},{13,5},{14,6},{15,7},{24,16},{25,... | collective-permute-start | bytes 394760 | tf_op jit(solution)/shard_map/ppermute | solution.py:30
  86.5 7.5 %collective-permute-start.7 = (f32[2,128,18,1]{1,3,2,0:T(1,128)S(1)}, f32[2,128,18,1]{1,3,2,0:T(1,128)S(1)}, u32[]{:S(2)}, u32[]{:S(2)}) collective-permute-start(f32[2,128,18,1]{1,3,2,0:T(1,128)S(1)} %get-tuple-element.65), channel_id=1, source_target_pairs={{1,0},{2,1},{3,2},{4,3},{5,4},{6,5},{7,6},{9,8},{10,9},{11,10},{12... | collective-permute-start | bytes 55304 | tf_op jit(solution)/shard_map/ppermute | solution.py:30
  89.8 6.6 %collective-permute-start.8 = (f32[2,128,18,1]{1,3,2,0:T(1,128)S(1)}, f32[2,128,18,1]{1,3,2,0:T(1,128)S(1)}, u32[]{:S(2)}, u32[]{:S(2)}) collective-permute-start(f32[2,128,18,1]{1,3,2,0:T(1,128)S(1)} %get-tuple-element.66), channel_id=1, source_target_pairs={{0,1},{1,2},{2,3},{3,4},{4,5},{5,6},{6,7},{8,9},{9,10},{10,11},{11... | collective-permute-start | bytes 55304 | tf_op jit(solution)/shard_map/ppermute | solution.py:28
  102.9 4.3 %collective-permute-start.9 = (f32[2,16,128]{2,1,0:T(8,128)}, f32[2,16,128]{2,1,0:T(8,128)}, u32[]{:S(2)}, u32[]{:S(2)}) collective-permute-start(f32[2,16,128]{2,1,0:T(8,128)} %slice_reduce_fusion.2), channel_id=1, source_target_pairs={{0,16},{16,0},{1,17},{17,1},{2,18},{18,2},{3,19},{19,3},{4,20},{20... | collective-permute-start | bytes 49160 | tf_op jit(solution)/shard_map/ppermute | solution.py:17
  140.0 9.1 %collective-permute-start.10 = (f32[2,16,128]{2,1,0:T(8,128)S(1)}, f32[2,16,128]{2,1,0:T(8,128)S(1)}, u32[]{:S(2)}, u32[]{:S(2)}) collective-permute-start(f32[2,16,128]{2,1,0:T(8,128)S(1)} %slice_reduce_fusion.1), channel_id=1, source_target_pairs={{0,16},{16,0},{1,17},{17,1},{2,18},{18,2},{3,19},{19,3},{4,20},{20... | collective-permute-start | bytes 49160 | tf_op jit(solution)/shard_map/ppermute | solution.py:17
  142.4 23.2 %collective-permute-start.15 = (f32[257,18,1]{0,2,1:T(1,128)}, f32[257,18,1]{0,2,1:T(1,128)}, u32[]{:S(2)}, u32[]{:S(2)}) collective-permute-start(f32[257,18,1]{0,2,1:T(1,128)} %get-tuple-element.55), channel_id=1, source_target_pairs={{0,1},{1,2},{2,3},{3,4},{4,5},{5,6},{6,7},{8,9},{9,10},{10,11},{11... | collective-permute-start | bytes 55520 | tf_op jit(solution)/shard_map/ppermute | solution.py:28
  145.9 19.8 %collective-permute-start.17 = (f32[257,18,1]{0,2,1:T(1,128)}, f32[257,18,1]{0,2,1:T(1,128)}, u32[]{:S(2)}, u32[]{:S(2)}) collective-permute-start(f32[257,18,1]{0,2,1:T(1,128)} %get-tuple-element.56), channel_id=1, source_target_pairs={{1,0},{2,1},{3,2},{4,3},{5,4},{6,5},{7,6},{9,8},{10,9},{11,10},{12... | collective-permute-start | bytes 55520 | tf_op jit(solution)/shard_map/ppermute | solution.py:30
  159.6 8.9 %collective-permute-start.12 = (f32[2,128,1,128]{1,3,2,0:T(8,128)S(1)}, f32[2,128,1,128]{1,3,2,0:T(8,128)S(1)}, u32[]{:S(2)}, u32[]{:S(2)}) collective-permute-start(f32[2,128,1,128]{1,3,2,0:T(8,128)S(1)} %get-tuple-element.75), channel_id=1, source_target_pairs={{0,8},{1,9},{2,10},{3,11},{4,12},{5,13},{6,14},{7,15},{16,24},{17,... | collective-permute-start | bytes 393224 | tf_op jit(solution)/shard_map/ppermute | solution.py:28
  164.2 7.1 %collective-permute-start.14 = (f32[2,128,1,128]{1,3,2,0:T(8,128)S(1)}, f32[2,128,1,128]{1,3,2,0:T(8,128)S(1)}, u32[]{:S(2)}, u32[]{:S(2)}) collective-permute-start(f32[2,128,1,128]{1,3,2,0:T(8,128)S(1)} %get-tuple-element.76), channel_id=1, source_target_pairs={{8,0},{9,1},{10,2},{11,3},{12,4},{13,5},{14,6},{15,7},{24,16},{25,... | collective-permute-start | bytes 393224 | tf_op jit(solution)/shard_map/ppermute | solution.py:30
  168.5 11.3 %copy-start.16 = (f32[128,16,128]{0,2,1:T(8,128)}, f32[128,16,128]{0,2,1:T(8,128)S(1)}, u32[]{:S(2)}) copy-start(f32[128,16,128]{0,2,1:T(8,128)S(1)} %get-tuple-element.53) | copy-start | bytes 3145732
  168.5 11.3 %copy-start.18 = (f32[128,16,128]{0,2,1:T(8,128)}, f32[128,16,128]{0,2,1:T(8,128)S(1)}, u32[]{:S(2)}) copy-start(f32[128,16,128]{0,2,1:T(8,128)S(1)} %get-tuple-element.54) | copy-start | bytes 3145732
  168.5 11.3 %copy-start.20 = (f32[128,16,128]{0,2,1:T(8,128)}, f32[128,16,128]{0,2,1:T(8,128)S(1)}, u32[]{:S(2)}) copy-start(f32[128,16,128]{0,2,1:T(8,128)S(1)} %get-tuple-element.57) | copy-start | bytes 3145732
  168.5 11.3 %copy-start.22 = (f32[128,16,128]{0,2,1:T(8,128)}, f32[128,16,128]{0,2,1:T(8,128)S(1)}, u32[]{:S(2)}) copy-start(f32[128,16,128]{0,2,1:T(8,128)S(1)} %get-tuple-element.58) | copy-start | bytes 3145732
  171.3 8.4 %collective-permute-start.16 = (f32[2,128,18,1]{1,3,2,0:T(1,128)S(1)}, f32[2,128,18,1]{1,3,2,0:T(1,128)S(1)}, u32[]{:S(2)}, u32[]{:S(2)}) collective-permute-start(f32[2,128,18,1]{1,3,2,0:T(1,128)S(1)} %get-tuple-element.63), channel_id=1, source_target_pairs={{0,1},{1,2},{2,3},{3,4},{4,5},{5,6},{6,7},{8,9},{9,10},{10,11},{11... | collective-permute-start | bytes 55304 | tf_op jit(solution)/shard_map/ppermute | solution.py:28
  173.9 5.9 %collective-permute-start.18 = (f32[2,128,18,1]{1,3,2,0:T(1,128)S(1)}, f32[2,128,18,1]{1,3,2,0:T(1,128)S(1)}, u32[]{:S(2)}, u32[]{:S(2)}) collective-permute-start(f32[2,128,18,1]{1,3,2,0:T(1,128)S(1)} %get-tuple-element.64), channel_id=1, source_target_pairs={{1,0},{2,1},{3,2},{4,3},{5,4},{6,5},{7,6},{9,8},{10,9},{11,10},{12... | collective-permute-start | bytes 55304 | tf_op jit(solution)/shard_map/ppermute | solution.py:30
  185.6 1.2 collective-permute-start.19
  195.0 17.9 %copy-start.3 = (f32[2,128,16,128]{1,3,2,0:T(8,128)S(1)}, f32[2,128,16,128]{1,3,2,0:T(8,128)}, u32[]{:S(2)}) copy-start(f32[2,128,16,128]{1,3,2,0:T(8,128)} %scatter.39) | copy-start | bytes 6291460
  196.2 4.9 %collective-permute-start.20 = (f32[2,128,1,128]{1,3,2,0:T(8,128)S(1)}, f32[2,128,1,128]{1,3,2,0:T(8,128)S(1)}, u32[]{:S(2)}, u32[]{:S(2)}) collective-permute-start(f32[2,128,1,128]{1,3,2,0:T(8,128)S(1)} %get-tuple-element.71), channel_id=1, source_target_pairs={{0,8},{1,9},{2,10},{3,11},{4,12},{5,13},{6,14},{7,15},{16,24},{17,... | collective-permute-start | bytes 393224 | tf_op jit(solution)/shard_map/ppermute | solution.py:28
  198.0 7.2 %collective-permute-start.21 = (f32[2,128,1,128]{1,3,2,0:T(8,128)S(1)}, f32[2,128,1,128]{1,3,2,0:T(8,128)S(1)}, u32[]{:S(2)}, u32[]{:S(2)}) collective-permute-start(f32[2,128,1,128]{1,3,2,0:T(8,128)S(1)} %get-tuple-element.72), channel_id=1, source_target_pairs={{8,0},{9,1},{10,2},{11,3},{12,4},{13,5},{14,6},{15,7},{24,16},{25,... | collective-permute-start | bytes 393224 | tf_op jit(solution)/shard_map/ppermute | solution.py:30
  206.2 8.2 %collective-permute-start.22 = (f32[2,128,18,1]{1,3,2,0:T(1,128)S(1)}, f32[2,128,18,1]{1,3,2,0:T(1,128)S(1)}, u32[]{:S(2)}, u32[]{:S(2)}) collective-permute-start(f32[2,128,18,1]{1,3,2,0:T(1,128)S(1)} %get-tuple-element.61), channel_id=1, source_target_pairs={{0,1},{1,2},{2,3},{3,4},{4,5},{5,6},{6,7},{8,9},{9,10},{10,11},{11... | collective-permute-start | bytes 55304 | tf_op jit(solution)/shard_map/ppermute | solution.py:28
  210.2 5.7 %collective-permute-start.23 = (f32[2,128,18,1]{1,3,2,0:T(1,128)S(1)}, f32[2,128,18,1]{1,3,2,0:T(1,128)S(1)}, u32[]{:S(2)}, u32[]{:S(2)}) collective-permute-start(f32[2,128,18,1]{1,3,2,0:T(1,128)S(1)} %get-tuple-element.62), channel_id=1, source_target_pairs={{1,0},{2,1},{3,2},{4,3},{5,4},{6,5},{7,6},{9,8},{10,9},{11,10},{12... | collective-permute-start | bytes 55304 | tf_op jit(solution)/shard_map/ppermute | solution.py:30
  (25 other events, 79.0 us)
where the time goes:
time: 227 us; the launch traced here: 223 us
  local copies, waits for them, and re-layouts  88.2 us (39%)
  starting transfers between devices  71 us (31%)
  other arithmetic  38.1 us (17%)
  waiting for transfers between devices  14 us (6%)
  matrix products  11.5 us (5%)
    ppermute x10, starting transfers between devices, extended_2(): lax.ppermute(tail, axis, [(i, (i + 1) % count) for i in range(ends)])  33.1 us
    scatter x5, local copies, waits for them, and re-layouts, couple(): return field.at[:, 0].set(updated)  27.6 us
    ppermute x10, starting transfers between devices, extended_2(): lax.ppermute(head, axis, [((i + 1) % count, i) for i in range(ends)])  23.9 us
    slice x8, local copies, waits for them, and re-layouts, vertical(): lower = jnp.concatenate([field[:, :1], field[:, :-1]], axis=1)  14.4 us
    add x2, other arithmetic, forward_stencil(): result = result + (HORIZ_MIX + 0.5 * wind_y) * extended[:, :, 1:-1, :-2]  9.83 us
    ppermute x10, waiting for transfers between devices, extended_2(): lax.ppermute(head, axis, [((i + 1) % count, i) for i in range(ends)])  8.52 us
    unnamed x63, local copies, waits for them, and re-layouts  8.5 us
    all_to_all x1, starting transfers between devices, local(): lax.all_to_all(send_op.reshape(tile_count, capacity, record_width), ('gx'...  6.92 us
  transfers between devices with their start and end apart: 26, of which 7 were waited for; matrix products, arithmetic and copies ran while one was open for 48% of the time, Pallas kernels for 0%

commit v1 on v0

v1 whole, which is shorter than its diff:
```python
import functools

import jax
import jax.numpy as jnp
from jax import lax
from jax.experimental import pallas as pl
from jax.experimental.pallas import tpu as pltpu
from jax.sharding import PartitionSpec as P

HORIZ_MIX = 0.1
VERT_MIX = 0.15
LANES = 128
GROUP = 8
VMEM_LIMIT = 40 * 1024 * 1024


def call(body, out_shape, scratch=(), **kw):
    return pl.pallas_call(
        body,
        out_shape=out_shape,
        scratch_shapes=list(scratch),
        compiler_params=pltpu.CompilerParams(vmem_limit_bytes=VMEM_LIMIT),
        **kw,
    )


def f32(*shape):
    return jax.ShapeDtypeStruct(shape, jnp.float32)


def lane_iota():
    return lax.broadcasted_iota(jnp.int32, (GROUP, LANES), 1)


def sub_iota():
    return lax.broadcasted_iota(jnp.int32, (GROUP, LANES), 0)


def pair_swap(block, axis, start):
    count = lax.axis_size(axis)
    route = []
    for low in range(start, count - 1, 2):
        route += [(low, low + 1), (low + 1, low)]
    return lax.ppermute(block, axis, route)


def exchange(strips, packed):
    even = pair_swap(strips[0], "gx", 0)
    odd = pair_swap(strips[1], "gx", 1) if lax.axis_size("gx") > 2 else None
    y_even = pair_swap(packed, "gy", 0)
    y_odd = pair_swap(packed, "gy", 1)
    return even, odd, y_even, y_odd


def halo_args(halos):
    even, odd, y_even, y_odd = halos
    return [even, y_even, y_odd] + ([] if odd is None else [odd])


def read_sides(scal, refs):
    even = refs[0]
    odd = refs[3] if len(refs) > 3 else None
    at_even = scal[0] == 0

    def after(at):
        other = jnp.zeros_like(even[at]) if odd is None else odd[at]
        return jnp.where(at_even, even[at], other)

    def before(at):
        other = jnp.zeros_like(even[at]) if odd is None else odd[at]
        return jnp.where(at_even, other, even[at])

    return before, after


def merge_columns(scal, y_even, y_odd, sides):
    lane = lax.broadcasted_iota(jnp.int32, sides.shape, 1)
    take_even = (lane % 2) == (1 - scal[1])
    sides[...] = jnp.where(take_even, y_even[...], y_odd[...])


def slot_of(group):
    return group // 4, group % 4


def side_columns(sides, i, group):
    m, part = slot_of(group)
    shift = LANES - 1 - 2 * (4 * i + part)
    return pltpu.roll(sides[m * GROUP : (m + 1) * GROUP, :], shift, 1)


def pack_columns(packed, value, i, group):
    m, part = slot_of(group)
    slot = 4 * i + part
    rolled = pltpu.roll(value, 2 * slot + 1, 1)
    at = pl.ds(m * GROUP, GROUP)
    packed[at, :] = jnp.where(lane_iota() // 2 == slot, rolled, packed[at, :])


def levels_around(cells, i, base, group, groups):
    here = cells[i + 1, pl.ds(base + group * GROUP, GROUP), :]
    if group == groups - 1:
        upper = jnp.where(sub_iota() == GROUP - 1, here, pltpu.roll(here, GROUP - 1, 0))
    else:
        upper = cells[i + 1, pl.ds(base + group * GROUP + 1, GROUP), :]
    if group == 0:
        lower = jnp.where(sub_iota() == 0, here, pltpu.roll(here, 1, 0))
    else:
        lower = cells[i + 1, pl.ds(base + group * GROUP - 1, GROUP), :]
    return here, upper, lower


def forward_point(cells, winds, sides, i, f, group, levels, held, wind_levels):
    base = f * held
    here, upper, lower = levels_around(cells, i, base, group, levels // GROUP)
    at = pl.ds(base + group * GROUP, GROUP)
    after, before = cells[i + 2, at, :], cells[i, at, :]
    edge = side_columns(sides, i, f * (levels // GROUP) + group)
    lane = lane_iota()
    right = pltpu.roll(jnp.where(lane == 0, edge, here), LANES - 1, 1)
    left = pltpu.roll(jnp.where(lane == LANES - 1, edge, here), 1, 1)
    u = winds[i, pl.ds(group * GROUP, GROUP), :]
    w = winds[i, pl.ds(wind_levels + group * GROUP, GROUP), :]
    return (
        (1.0 - 4.0 * HORIZ_MIX - 2.0 * VERT_MIX) * here
        + VERT_MIX * (upper + lower)
        + HORIZ_MIX * ((after + before) + (right + left))
        - 0.5 * (u * (after - before) + w * (right - left))
    )


def products(x, wind):
    slope = 0.5 * (wind * x)
    return HORIZ_MIX * x - slope, HORIZ_MIX * x + slope


def adjoint_point(cells, winds, sides, i, f, group, levels, held, wind_levels, rows):
    base = f * held
    here, upper, lower = levels_around(cells, i, base, group, levels // GROUP)
    at = pl.ds(base + group * GROUP, GROUP)
    wind_at = pl.ds(group * GROUP, GROUP)
    after, before = cells[i + 2, at, :], cells[i, at, :]
    u_after = winds[jnp.minimum(i + 1, rows - 1), wind_at, :]
    u_before = winds[jnp.maximum(i - 1, 0), wind_at, :]
    w = winds[i, pl.ds(wind_levels + group * GROUP, GROUP), :]
    down, up = products(here, w)
    edge = side_columns(sides, i, f * (levels // GROUP) + group)
    lane = lane_iota()
    right = pltpu.roll(jnp.where(lane == 0, edge, up), LANES - 1, 1)
    left = pltpu.roll(jnp.where(lane == LANES - 1, edge, down), 1, 1)
    return (
        (1.0 - 4.0 * HORIZ_MIX - 2.0 * VERT_MIX) * here
        + VERT_MIX * (upper + lower)
        + HORIZ_MIX * (after + before)
        + 0.5 * (u_after * after - u_before * before)
        + (right + left)
    )


def couple_forward(value, other, shares, i):
    own = shares[0, pl.ds(i, 1), :]
    mixed = value - own * (value - other)
    return jnp.where(sub_iota() == 0, mixed, value)


def couple_adjoint(value, other, shares, i):
    own = shares[0, pl.ds(i, 1), :]
    peer = shares[1, pl.ds(i, 1), :]
    mixed = value - own * value + peer * other
    return jnp.where(sub_iota() == 0, mixed, value)


def put_strip(scal, strip_even, strip_odd, at, first, last):
    at_even = scal[0] == 0
    strip_even[at, :] = jnp.where(at_even, last, first)
    strip_odd[at, :] = jnp.where(at_even, first, last)


def to_rows_kernel(rows, levels, scal, state, winds, state_rows, wind_rows, s_even, s_odd, packed):
    packed[...] = jnp.zeros_like(packed)
    groups = levels // GROUP

    def row(i, _):
        for c in range(2 * groups):
            at = pl.ds(c * GROUP, GROUP)
            value = state[pl.ds(c * GROUP * rows + i, GROUP, stride=rows), :]
            state_rows[i, at, :] = value
            pack_columns(packed, value, i, c)
            wind_rows[i, at, :] = winds[pl.ds(c * GROUP * rows + i, GROUP, stride=rows), :]
        return 0

    lax.fori_loop(0, rows, row, 0)
    put_strip(scal, s_even, s_odd, slice(None), state_rows[0], state_rows[rows - 1])


def fill(cells, source, rows, before=None, after=None, fix=None):
    width = source.shape[1]

    def row(i, _):
        cells[i + 1] = source[i]
        if fix is not None:
            fix(i)
        return 0

    lax.fori_loop(0, rows, row, 0)
    everything = slice(None)
    cells[0] = jnp.zeros((width, LANES), jnp.float32) if before is None else before(everything)
    cells[rows + 1] = jnp.zeros((width, LANES), jnp.float32) if after is None else after(everything)


def forward_floor_kernel(rows, levels, held, scal, field, winds, *rest):
    *halos, floor, cells, sides = rest
    merge_columns(scal, halos[1], halos[2], sides)
    before, after = read_sides(scal, halos)

    def bottom(side):
        return lambda _: jnp.concatenate([side(pl.ds(f * levels, held)) for f in range(2)], axis=0)

    def copy(i, _):
        for f in range(2):
            cells[i + 1, pl.ds(f * held, held), :] = field[i, f]
        return 0

    lax.fori_loop(0, rows, copy, 0)
    cells[0] = bottom(before)(None)
    cells[rows + 1] = bottom(after)(None)

    def row(i, _):
        for f in range(2):
            value = forward_point(cells, winds, sides, i, f, 0, levels, held, GROUP)
            floor[pl.ds(f * rows + i, 1), :] = value[0:1]
        return 0

    lax.fori_loop(0, rows, row, 0)


def forward_kernel(rows, levels, strips, scal, shares, other, field, winds, *rest):
    if strips:
        *halos, out, s_even, s_odd, packed, cells, sides = rest
        packed[...] = jnp.zeros_like(packed)
    else:
        *halos, out, cells, sides = rest
    merge_columns(scal, halos[1], halos[2], sides)
    before, after = read_sides(scal, halos)
    fill(cells, field, rows, before, after)
    groups = levels // GROUP

    def row(i, _):
        for group in range(groups):
            for f in range(2):
                value = forward_point(cells, winds, sides, i, f, group, levels, levels, levels)
                if group == 0:
                    value = couple_forward(value, other[pl.ds(f * rows + i, 1), :], shares, i)
                out[i, pl.ds(f * levels + group * GROUP, GROUP), :] = value
                if strips:
                    pack_columns(packed, value, i, f * groups + group)
        return 0

    lax.fori_loop(0, rows, row, 0)
    if strips:
        put_strip(scal, s_even, s_odd, slice(None), out[0], out[rows - 1])


def put_products(scal, s_even, s_odd, cells_first, cells_last, winds, rows, levels):
    for f in range(2):
        at = pl.ds(f * levels, levels)
        _, first = products(cells_first(at), winds[0, pl.ds(0, levels), :])
        last, _ = products(cells_last(at), winds[rows - 1, pl.ds(0, levels), :])
        put_strip(scal, s_even, s_odd, at, first, last)


def pack_products(packed, value, winds, i, f, group, levels):
    w = winds[i, pl.ds(levels + group * GROUP, GROUP), :]
    down, up = products(value, w)
    both = jnp.where(lane_iota() == 0, up, down)
    pack_columns(packed, both, i, f * (levels // GROUP) + group)


def adjoint_pack_kernel(rows, levels, scal, shares, other, field, winds, s_even, s_odd, packed):
    packed[...] = jnp.zeros_like(packed)
    groups = levels // GROUP

    def value_at(i, f, group):
        value = field[i, pl.ds(f * levels + group * GROUP, GROUP), :]
        if group == 0:
            value = couple_adjoint(value, other[pl.ds(f * rows + i, 1), :], shares, i)
        return value

    def row(i, _):
        for group in range(groups):
            for f in range(2):
                pack_products(packed, value_at(i, f, group), winds, i, f, group, levels)
        return 0

    lax.fori_loop(0, rows, row, 0)
    for f in range(2):
        for group in range(groups):
            wind_at = pl.ds(group * GROUP, GROUP)
            _, first = products(value_at(0, f, group), winds[0, wind_at, :])
            last, _ = products(value_at(rows - 1, f, group), winds[rows - 1, wind_at, :])
            put_strip(scal, s_even, s_odd, pl.ds(f * levels + group * GROUP, GROUP), first, last)


def adjoint_floor_kernel(rows, levels, held, scal, shares, other, field, winds, *rest):
    *halos, floor, cells, sides = rest
    merge_columns(scal, halos[1], halos[2], sides)
    before, after = read_sides(scal, halos)

    def copy(i, _):
        for f in range(2):
            cells[i + 1, pl.ds(f * held, held), :] = field[i, f]
            at = pl.ds(f * held, GROUP)
            cells[i + 1, at, :] = couple_adjoint(
                field[i, f, pl.ds(0, GROUP), :], other[pl.ds(f * rows + i, 1), :], shares, i
            )
        return 0

    lax.fori_loop(0, rows, copy, 0)
    cells[0] = jnp.zeros_like(cells[0])
    cells[rows + 1] = jnp.zeros_like(cells[0])

    def row(i, _):
        for f in range(2):
            value = adjoint_point(cells, winds, sides, i, f, 0, levels, held, GROUP, rows)
            floor[pl.ds(f * rows + i, 1), :] = value[0:1]
        return 0

    lax.fori_loop(0, rows, row, 0)
    for f in range(2):
        at = pl.ds(f * levels, GROUP)
        floor[pl.ds(f * rows, 1), :] += before(at)[0:1]
        floor[pl.ds(f * rows + rows - 1, 1), :] += after(at)[0:1]


def adjoint_kernel(rows, levels, scal, shares, other, other_next, field, winds, *rest):
    *halos, out, s_even, s_odd, packed, cells, sides = rest
    packed[...] = jnp.zeros_like(packed)
    merge_columns(scal, halos[1], halos[2], sides)
    before, after = read_sides(scal, halos)
    groups = levels // GROUP

    def fix(i):
        for f in range(2):
            at = pl.ds(f * levels, GROUP)
            cells[i + 1, at, :] = couple_adjoint(
                field[i, at, :], other[pl.ds(f * rows + i, 1), :], shares, i
            )

    fill(cells, field, rows, fix=fix)

    def point(i, group, f, extra=None):
        at = pl.ds(f * levels + group * GROUP, GROUP)
        value = adjoint_point(cells, winds, sides, i, f, group, levels, levels, levels, rows)
        if extra is not None:
            value = value + extra(at)
        if group == 0:
            value = couple_adjoint(value, other_next[pl.ds(f * rows + i, 1), :], shares, i)
        out[i, at, :] = value
        pack_products(packed, value, winds, i, f, group, levels)

    def row(i, extra=None):
        for group in range(groups):
            for f in range(2):
                point(i, group, f, extra)
        return 0

    row(0, before)
    row(rows - 1, after)
    lax.fori_loop(1, rows - 1, lambda i, _: row(i), 0)
    put_products(scal, s_even, s_odd, lambda at: out[0, at, :], lambda at: out[rows - 1, at, :], winds, rows, levels)


def final_kernel(rows, levels, scal, scale, field, winds, state, *rest):
    *halos, out, cells, sides = rest
    merge_columns(scal, halos[1], halos[2], sides)
    before, after = read_sides(scal, halos)
    groups = levels // GROUP
    fill(cells, field, rows)

    def row(i, extra=None):
        for group in range(groups):
            for f in range(2):
                at = pl.ds(f * levels + group * GROUP, GROUP)
                value = adjoint_point(cells, winds, sides, i, f, group, levels, levels, levels, rows)
                if extra is not None:
                    value = value + extra(at)
                value = value + scale[at, :] * state[i, at, :]
                out[pl.ds((f * levels + group * GROUP) * rows + i, GROUP, stride=rows), :] = value
        return 0

    row(0, before)
    row(rows - 1, after)
    lax.fori_loop(1, rows - 1, lambda i, _: row(i), 0)


def split(value, terms):
    parts = []
    for _ in range(terms):
        part = value.astype(jnp.bfloat16)
        parts.append(part)
        value = value - part.astype(jnp.float32)
    return parts


def dot(a, b, contract):
    return lax.dot_general(a, b, ((contract[:1], contract[1:]), ((), ())), preferred_element_type=jnp.float32)


def route_kernel(tiles, cap, dest, col, prec, op, out):
    count = op.shape[0]
    width = op.shape[1]
    halves = width // LANES
    owner = lax.broadcasted_iota(jnp.int32, (tiles, count), 0)
    hits = owner == dest[...]
    ones = jnp.where(hits, 1.0, 0.0)
    earlier = lax.broadcasted_iota(jnp.int32, (count, count), 0) <= lax.broadcasted_iota(jnp.int32, (count, count), 1)
    running = dot(ones.astype(jnp.bfloat16), jnp.where(earlier, 1.0, 0.0).astype(jnp.bfloat16), (1, 0))
    slot = jnp.sum(running * ones, axis=0, keepdims=True) - 1.0
    slot = slot.astype(jnp.int32)
    place = dest[...] * cap + slot
    at_slot = lax.broadcasted_iota(jnp.int32, (LANES, count), 0) == slot
    at_slot = jnp.where(at_slot, 1.0, 0.0).astype(jnp.bfloat16)
    column = col[...].astype(jnp.float32)
    pieces = [ones * part.astype(jnp.float32) for part in split(column, 2) + split(prec[...], 3)]
    aux = dot(jnp.concatenate(pieces, axis=0).astype(jnp.bfloat16), at_slot, (1, 1))
    columns = aux[0:tiles] + aux[tiles : 2 * tiles]
    precs = (aux[2 * tiles : 3 * tiles] + aux[3 * tiles : 4 * tiles]) + aux[4 * tiles : 5 * tiles]
    sub = sub_iota()
    for owner_at in range(tiles):
        block = jnp.where(sub == 0, columns[owner_at : owner_at + 1], 0.0)
        block = jnp.where(sub == 1, precs[owner_at : owner_at + 1], block)
        out[owner_at, pl.ds(halves * cap, GROUP), :] = block
    rows_high, rows_low = split(op[...], 2)
    chunk = 256
    for first in range(0, tiles * cap, chunk):
        picks = lax.broadcasted_iota(jnp.int32, (chunk, count), 0) + first == place
        picks = jnp.where(picks, 1.0, 0.0).astype(jnp.bfloat16)
        moved = dot(picks, rows_high, (1, 0)) + dot(picks, rows_low, (1, 0))
        for part in range(chunk // cap):
            for half in range(halves):
                out[first // cap + part, pl.ds(half * cap, cap), :] = moved[
                    part * cap : (part + 1) * cap, half * LANES : (half + 1) * LANES
                ]


def observe_kernel(rows, width, tiles, cap, records, field, adjoint, floor, cols, sel, places, precs, spread):
    halves = width // LANES
    block = halves * cap + GROUP
    for i in range(rows):
        high, low = split(field[i], 2)
        cols[0:width, i * LANES : (i + 1) * LANES] = high
        cols[width:, i * LANES : (i + 1) * LANES] = low
    lane = lax.broadcasted_iota(jnp.int32, (cap, LANES), 1)
    own = lane == lax.broadcasted_iota(jnp.int32, (cap, LANES), 0)

    def source(s, _):
        aux = records[s, pl.ds(halves * cap, GROUP), :]
        at = pl.ds(pl.multiple_of(s * cap, cap), cap)
        for part, target in enumerate((places, precs)):
            value = jnp.sum(jnp.where(own, aux[part : part + 1], 0.0), axis=1, keepdims=True)
            target[at, :] = jnp.broadcast_to(value, (cap, LANES))
        return 0

    step = 64
    lane = lax.broadcasted_iota(jnp.int32, (step, LANES), 1).astype(jnp.float32)

    def select(block, _):
        at = pl.ds(pl.multiple_of(block * step, step), step)
        column = places[at, :] - lane
        for i in range(rows):
            sel[at, i * LANES : (i + 1) * LANES] = jnp.where(column == float(i * LANES), 1.0, 0.0).astype(jnp.bfloat16)
        return 0

    chunk = 256
    for first in range(0, tiles * cap, chunk):
        lax.fori_loop(first // cap, (first + chunk) // cap, source, 0)
        lax.fori_loop(first // step, (first + chunk) // step, select, 0)
        both = dot(sel[first : first + chunk, :], cols[...], (1, 1))
        sampled = both[:, :width] + both[:, width:]
        sources = range(first // cap, (first + chunk) // cap)
        ops = [
            jnp.concatenate([records[s, half * cap : (half + 1) * cap, :] for s in sources], axis=0)
            for half in range(halves)
        ]
        total = sum(sampled[:, half * LANES : (half + 1) * LANES] * ops[half] for half in range(halves))
        innovation = jnp.sum(total, axis=1, keepdims=True) * precs[first : first + chunk, :]
        for half in range(halves):
            high, low = split((ops[half] * innovation).T, 2)
            spread[half * LANES : (half + 1) * LANES, first : first + chunk] = high
            spread[width + half * LANES : width + (half + 1) * LANES, first : first + chunk] = low
    for i in range(0, rows, 2):
        both = dot(spread[...], sel[:, i * LANES : (i + 2) * LANES], (1, 0))
        sums = both[:width] + both[width:]
        adjoint[i] = sums[:, :LANES]
        adjoint[i + 1] = sums[:, LANES:]
    for f in range(2):
        for i in range(rows):
            floor[f * rows + i : f * rows + i + 1, :] = adjoint[i, f * (width // 2) : f * (width // 2) + 1, :]


def local(state_incr, winds, coupling, background, obs_dest, obs_col, obs_op, obs_prec):
    _, fields, levels, rows, lanes = state_incr.shape
    width = fields * levels
    groups = width // GROUP
    held = 2 * GROUP
    tiles = lax.axis_size("gx") * lax.axis_size("gy")
    count = obs_col.shape[0]
    cap = 2 * count // tiles
    halves = obs_op.shape[1] // LANES

    scal = jnp.stack([lax.axis_index("gx") % 2, lax.axis_index("gy") % 2]).astype(jnp.int32)
    own_share = jnp.where(lax.axis_index("comp") == 0, 1.0, 0.5)
    shares = jnp.stack([own_share * coupling, (1.5 - own_share) * coupling])

    smem = pl.BlockSpec(memory_space=pltpu.SMEM)
    vmem = pl.BlockSpec(memory_space=pltpu.VMEM)
    cells_shape = pltpu.VMEM((rows + 2, width, LANES), jnp.float32)
    packed_shape = f32(groups // 4 * GROUP, LANES)
    sides_shape = pltpu.VMEM(packed_shape.shape, jnp.float32)
    strip_shape = f32(width, LANES)
    field_shape = f32(rows, width, LANES)
    floor_shape = f32(fields * rows, LANES)

    def swap_floor(floor):
        return lax.ppermute(floor, "comp", [(0, 1), (1, 0)])

    send = call(functools.partial(route_kernel, tiles, cap), f32(tiles, halves * cap + GROUP, LANES))(
        obs_dest.reshape(1, count), obs_col.reshape(1, count), obs_prec.reshape(1, count), obs_op
    )
    records = lax.all_to_all(send, ("gx", "gy"), split_axis=0, concat_axis=0, tiled=True)

    field, wind_rows, s_even, s_odd, packed = call(
        functools.partial(to_rows_kernel, rows, levels),
        [field_shape, field_shape, strip_shape, strip_shape, packed_shape],
        in_specs=[smem, vmem, vmem],
    )(scal, state_incr.reshape(width * rows, lanes), winds.reshape(width * rows, lanes))
    state_rows = field

    floor_winds = wind_rows.reshape(rows, 2, levels, lanes)[:, :, :GROUP].reshape(rows, 2 * GROUP, lanes)

    for sweep in range(2):
        halos = halo_args(exchange((s_even, s_odd), packed))
        floor = call(
            functools.partial(forward_floor_kernel, rows, levels, held),
            floor_shape,
            [pltpu.VMEM((rows + 2, fields * held, LANES), jnp.float32), sides_shape],
            grid=(1,),
            in_specs=[smem, pl.BlockSpec((rows, fields, held, LANES), lambda _: (0, 0, 0, 0)), vmem]
            + [vmem] * len(halos),
        )(scal, field.reshape(rows, fields, levels, lanes), floor_winds, *halos)
        other = swap_floor(floor)
        more = sweep == 0
        result = call(
            functools.partial(forward_kernel, rows, levels, more),
            [field_shape] + ([strip_shape, strip_shape, packed_shape] if more else []),
            [cells_shape, sides_shape],
            in_specs=[smem] + [vmem] * (4 + len(halos)),
        )(scal, shares, other, field, wind_rows, *halos)
        if more:
            field, s_even, s_odd, packed = result
        else:
            (field,) = result

    adjoint, floor = call(
        functools.partial(observe_kernel, rows, width, tiles, cap),
        [field_shape, floor_shape],
        [
            pltpu.VMEM((2 * width, rows * LANES), jnp.bfloat16),
            pltpu.VMEM((tiles * cap, rows * LANES), jnp.bfloat16),
            pltpu.VMEM((tiles * cap, LANES), jnp.float32),
            pltpu.VMEM((tiles * cap, LANES), jnp.float32),
            pltpu.VMEM((2 * width, tiles * cap), jnp.bfloat16),
        ],
    )(records, field)

    other = swap_floor(floor)
    s_even, s_odd, packed = call(
        functools.partial(adjoint_pack_kernel, rows, levels),
        [strip_shape, strip_shape, packed_shape],
        in_specs=[smem] + [vmem] * 4,
    )(scal, shares, other, adjoint, wind_rows)
    halos = halo_args(exchange((s_even, s_odd), packed))
    floor = call(
        functools.partial(adjoint_floor_kernel, rows, levels, held),
        floor_shape,
        [pltpu.VMEM((rows + 2, fields * held, LANES), jnp.float32), sides_shape],
        grid=(1,),
        in_specs=[smem, vmem, vmem, pl.BlockSpec((rows, fields, held, LANES), lambda _: (0, 0, 0, 0)), vmem]
        + [vmem] * len(halos),
    )(scal, shares, other, adjoint.reshape(rows, fields, levels, lanes), floor_winds, *halos)
    other_next = swap_floor(floor)
    adjoint, s_even, s_odd, packed = call(
        functools.partial(adjoint_kernel, rows, levels),
        [field_shape, strip_shape, strip_shape, packed_shape],
        [cells_shape, sides_shape],
        in_specs=[smem] + [vmem] * (5 + len(halos)),
    )(scal, shares, other, other_next, adjoint, wind_rows, *halos)
    halos = halo_args(exchange((s_even, s_odd), packed))
    scale = jnp.broadcast_to(background.reshape(width, 1), (width, LANES))
    result = call(
        functools.partial(final_kernel, rows, levels),
        f32(width * rows, LANES),
        [cells_shape, sides_shape],
        in_specs=[smem] + [vmem] * (4 + len(halos)),
    )(scal, scale, adjoint, wind_rows, state_rows, *halos)
    return result.reshape(state_incr.shape)


def solution(mesh):
    placed = (
        P("comp", None, None, "gx", "gy"),
        P("comp", None, None, "gx", "gy"),
        P("gx", "gy"),
        P("comp", None, None),
        P(("comp", "gx", "gy"), None),
        P(("comp", "gx", "gy")),
        P(("comp", "gx", "gy"), None),
        P(("comp", "gx", "gy")),
    )
    return jax.shard_map(
        local,
        mesh=mesh,
        in_specs=placed,
        out_specs=P("comp", None, None, "gx", "gy"),
        check_vma=False,
    )
```

time: 227 us -> 124 us (0.55); the launches traced: 223 us -> 123 us
  local copies, waits for them, and re-layouts: 88.2 us -> 12.9 us
  Pallas kernels: 0 us -> 53.2 us
  starting transfers between devices: 71 us -> 32 us
  other arithmetic: 38.1 us -> 0.09 us
  matrix products: 11.5 us -> 0 us
  waiting for transfers between devices: 14 us -> 24.6 us
    pallas_call x0 -> x11, Pallas kernels: none -> 53.2 us  [the longest x1 10.7 us: local(): call(functools.partial(observe_kernel, rows, width, tiles, cap), [field_s...]
    ppermute x24 -> x16, starting transfers between devices: 57.8 us -> 24.8 us  [the longest x12 24.5 us: pair_swap(): return lax.ppermute(block, axis, route)]
    scatter x6 -> x0, local copies, waits for them, and re-layouts: 30.2 us -> none  [the longest x5 27.6 us: couple(): return field.at[:, 0].set(updated)]
    slice x19 -> x0, local copies, waits for them, and re-layouts: 23.1 us -> none  [the longest x8 14.4 us: vertical(): lower = jnp.concatenate([field[:, :1], field[:, :-1]], axis=1)]
    add x3 -> x0, other arithmetic: 12.9 us -> none  [the longest x2 9.83 us: forward_stencil(): result = result + (HORIZ_MIX + 0.5 * wind_y) * extended[:, :, 1:-1, :-2]]
    dot_general x2 -> x0, matrix products: 11.5 us -> none  [the longest x1 6.39 us: local(): lax.dot_general(selector, columns, (((1,), (1,)), ((), ())), precision=la...]
    ppermute x24 -> x16, waiting for transfers between devices: 14 us -> 24.6 us  [the longest x12 20.1 us: pair_swap(): return lax.ppermute(block, axis, route)]
    all_to_all x2 -> x1, starting transfers between devices: 13.2 us -> 7.22 us  [local(): lax.all_to_all(send, ('gx', 'gy'), split_axis=0, concat_axis=0, tiled=True)]
  transfers between devices with their start and end apart: 26 -> 17, of which waited for: 7 -> 9; matrix products, arithmetic and copies ran while one was open for 48% -> 0% of each run, Pallas kernels for 0% -> 17%
where the time goes in v1:
time: 124 us; the launch traced here: 123 us
  Pallas kernels  53.2 us (43%)
  starting transfers between devices  32 us (26%)
  waiting for transfers between devices  24.6 us (20%)
  local copies, waits for them, and re-layouts  12.9 us (10%)
    ppermute x12, starting transfers between devices, pair_swap(): return lax.ppermute(block, axis, route)  24.5 us
    ppermute x12, waiting for transfers between devices, pair_swap(): return lax.ppermute(block, axis, route)  20.1 us
    unnamed x32, local copies, waits for them, and re-layouts  12.8 us
    pallas_call x1, Pallas kernels, local(): call(functools.partial(observe_kernel, rows, width, tiles, cap), [field_s...  10.7 us
    pallas_call x2, Pallas kernels, local(): call(functools.partial(forward_kernel, rows, levels, more), [field_shape]...  10 us
    all_to_all x1, starting transfers between devices, local(): lax.all_to_all(send, ('gx', 'gy'), split_axis=0, concat_axis=0, tiled=True)  7.22 us
    pallas_call x1, Pallas kernels, local(): call(functools.partial(adjoint_kernel, rows, levels), [field_shape, strip...  7.08 us
    pallas_call x1, Pallas kernels, local(): call(functools.partial(final_kernel, rows, levels), f32(width * rows, LAN...  7.01 us
  transfers between devices with their start and end apart: 17, of which 9 were waited for; matrix products, arithmetic and copies ran while one was open for 0% of the time, Pallas kernels for 17%

profile of v1, /device:TPU:8, one launch (start us, length us, event | category | flops | bytes accessed | tf_op | source)
XLA Modules:
  0.0 123.0 jit_solution(12153009699688060269)
XLA Ops:
  3.1 2.0 %shard_map.82 = f32[16,136,128]{2,1,0:T(8,128)} custom-call(s32[1,512]{1,0:T(1,128)S(1)} %bitcast.25, s32[1,512]{1,0:T(1,128)S(1)} %bitcast.26, f32[1,512]{1,0:T(1,128)S(1)} %bitcast.27, f32[512,256]{1,0:T(8,128)S(1)} %copy-done.7), custom_call_target="tpu_custom_call" | custom-call | tf_op jit(solution)/shard_map/pallas_call | solution.py:527
  5.1 7.2 %all-to-all-start = ((f32[16,136,128]{2,1,0:T(8,128)}), f32[16,136,128]{2,1,0:T(8,128)S(1)}, u32[]{:S(2)}, u32[]{:S(2)}) async-start(f32[16,136,128]{2,1,0:T(8,128)} %shard_map.82), calls=%async_computation | async-start | bytes 2228224 | tf_op jit(solution)/shard_map/all_to_all | solution.py:530
  12.4 1.6 %copy-done.5 = f32[1,2,128,16,128]{4,3,2,1,0:T(8,128)S(1)} copy-done((f32[1,2,128,16,128]{4,3,2,1,0:T(8,128)S(1)}, f32[1,2,128,16,128]{4,3,2,1,0:T(8,128)}, u32[]{:S(2)}) %copy-start.5) | copy-done | bytes 2097176
  14.0 1.6 %copy-done.6 = f32[1,2,128,16,128]{4,3,2,1,0:T(8,128)S(1)} copy-done((f32[1,2,128,16,128]{4,3,2,1,0:T(8,128)S(1)}, f32[1,2,128,16,128]{4,3,2,1,0:T(8,128)}, u32[]{:S(2)}) %copy-start.6) | copy-done | bytes 2097176
  15.6 4.5 %shard_map.83 = (f32[16,256,128]{2,1,0:T(8,128)S(1)}, f32[16,256,128]{2,1,0:T(8,128)S(1)}, f32[256,128]{1,0:T(8,128)}, f32[256,128]{1,0:T(8,128)}, f32[64,128]{1,0:T(8,128)}) custom-call(s32[2]{0:T(128)S(1)} %pad_add_fusion.scal, f32[4096,128]{1,0:T(8,128)S(1)} %bitcast.23, f32[4096,128]{1,0:T(8,128)S(1)} %bitcast.24), custom_call_target="tpu_custom_call" | custom-call | tf_op jit(solution)/shard_map/pallas_call | solution.py:532
  21.5 1.5 %collective-permute-start.1 = (f32[64,128]{1,0:T(8,128)}, f32[64,128]{1,0:T(8,128)S(1)}, u32[]{:S(2)}, u32[]{:S(2)}) collective-permute-start(f32[64,128]{1,0:T(8,128)} %get-tuple-element.22), channel_id=1, source_target_pairs={{0,1},{1,0},{2,3},{3,2},{4,5},{5,4},{6,7},{7,6},{8,9},{9,8},{10,11... | collective-permute-start | bytes 98312 | tf_op jit(solution)/shard_map/ppermute | solution.py:44
  22.9 2.0 %collective-permute-start.2 = (f32[64,128]{1,0:T(8,128)}, f32[64,128]{1,0:T(8,128)S(1)}, u32[]{:S(2)}, u32[]{:S(2)}) collective-permute-start(f32[64,128]{1,0:T(8,128)} %get-tuple-element.22), channel_id=1, source_target_pairs={{1,2},{2,1},{3,4},{4,3},{5,6},{6,5},{9,10},{10,9},{11,12},{12,11},... | collective-permute-start | bytes 98312 | tf_op jit(solution)/shard_map/ppermute | solution.py:44
  24.9 2.0 %collective-permute-start = (f32[256,128]{1,0:T(8,128)}, f32[256,128]{1,0:T(8,128)S(1)}, u32[]{:S(2)}, u32[]{:S(2)}) collective-permute-start(f32[256,128]{1,0:T(8,128)} %get-tuple-element.21), channel_id=1, source_target_pairs={{0,8},{8,0},{1,9},{9,1},{2,10},{10,2},{3,11},{11,3},{4,12},{12,4},... | collective-permute-start | bytes 393224 | tf_op jit(solution)/shard_map/ppermute | solution.py:44
  27.0 5.8 %collective-permute-done.2.rest_2_ = f32[64,128]{1,0:T(8,128)S(1)} collective-permute-done((f32[64,128]{1,0:T(8,128)}, f32[64,128]{1,0:T(8,128)S(1)}, u32[]{:S(2)}, u32[]{:S(2)}) %collective-permute-start.2) | collective-permute-done | bytes 32800 | tf_op jit(solution)/shard_map/ppermute | solution.py:44
  32.7 1.6 %copy-done.1 = f32[16,256,128]{2,1,0:T(8,128)S(1)} copy-done((f32[16,256,128]{2,1,0:T(8,128)S(1)}, f32[16,256,128]{2,1,0:T(8,128)}, u32[]{:S(2)}) %copy-start.1) | copy-done | bytes 2097176
  34.3 3.0 %shard_map.84 = f32[32,128]{1,0:T(8,128)S(1)} custom-call(s32[2]{0:T(128)S(1)} %pad_add_fusion.scal, f32[16,2,128,128]{3,2,1,0:T(8,128)S(1)} %bitcast.20, f32[16,16,128]{2,1,0:T(8,128)S(1)} %slice_bitcast_fusion.winds, f32[256,128]{1,0:T(8,128)S(1)} %collective-permute-done.rest_0_, f32[64,128]{1,0:T(8,128)S(1)} %collective-permute-done.1.rest_1_, ...), custom_call_target="tpu_custom_call" | custom-call | tf_op jit(solution)/shard_map/pallas_call | solution.py:543
  39.1 5.8 %shard_map.85 = (f32[16,256,128]{2,1,0:T(8,128)S(1)}, f32[256,128]{1,0:T(8,128)S(1)}, f32[256,128]{1,0:T(8,128)}, f32[64,128]{1,0:T(8,128)S(1)}) custom-call(s32[2]{0:T(128)S(1)} %copy-done.9, f32[2,16,128]{2,1,0:T(8,128)S(1)} %pad_maximum_fusion.shares, f32[32,128]{1,0:T(8,128)S(1)} %collective-permute-done.3.other, f32[16,256,128]{2,1,0:T(8,128)S(1)} %copy-done.1, ...), custom_call_target="tpu_custom_call" | custom-call | tf_op jit(solution)/shard_map/pallas_call | solution.py:553
  44.9 1.5 %collective-permute-start.4 = (f32[256,128]{1,0:T(8,128)S(1)}, f32[256,128]{1,0:T(8,128)S(1)}, u32[]{:S(2)}, u32[]{:S(2)}) collective-permute-start(f32[256,128]{1,0:T(8,128)S(1)} %get-tuple-element.24), channel_id=1, source_target_pairs={{0,8},{8,0},{1,9},{9,1},{2,10},{10,2},{3,11},{11,3},{4,12},{12,4},... | collective-permute-start | bytes 393224 | tf_op jit(solution)/shard_map/ppermute | solution.py:44
  46.4 7.8 %collective-permute-start.5 = (f32[64,128]{1,0:T(8,128)S(1)}, f32[64,128]{1,0:T(8,128)S(1)}, u32[]{:S(2)}, u32[]{:S(2)}) collective-permute-start(f32[64,128]{1,0:T(8,128)S(1)} %get-tuple-element.25), channel_id=1, source_target_pairs={{0,1},{1,0},{2,3},{3,2},{4,5},{5,4},{6,7},{7,6},{8,9},{9,8},{10,11... | collective-permute-start | bytes 98312 | tf_op jit(solution)/shard_map/ppermute | solution.py:44
  54.2 1.9 %collective-permute-start.6 = (f32[64,128]{1,0:T(8,128)S(1)}, f32[64,128]{1,0:T(8,128)S(1)}, u32[]{:S(2)}, u32[]{:S(2)}) collective-permute-start(f32[64,128]{1,0:T(8,128)S(1)} %get-tuple-element.25), channel_id=1, source_target_pairs={{1,2},{2,1},{3,4},{4,3},{5,6},{6,5},{9,10},{10,9},{11,12},{12,11},... | collective-permute-start | bytes 98312 | tf_op jit(solution)/shard_map/ppermute | solution.py:44
  56.1 4.8 %collective-permute-done.6.rest_2_ = f32[64,128]{1,0:T(8,128)S(1)} collective-permute-done((f32[64,128]{1,0:T(8,128)S(1)}, f32[64,128]{1,0:T(8,128)S(1)}, u32[]{:S(2)}, u32[]{:S(2)}) %collective-permute-start.6) | collective-permute-done | bytes 32800 | tf_op jit(solution)/shard_map/ppermute | solution.py:44
  60.9 3.0 %shard_map.86 = f32[32,128]{1,0:T(8,128)S(1)} custom-call(s32[2]{0:T(128)S(1)} %copy-done.9, f32[16,2,128,128]{3,2,1,0:T(8,128)S(1)} %bitcast.22, f32[16,16,128]{2,1,0:T(8,128)S(1)} %slice_bitcast_fusion.winds, f32[256,128]{1,0:T(8,128)S(1)} %collective-permute-done.4.rest_0_, f32[64,128]{1,0:T(8,128)S(1)} %collective-permute-done.5.rest_1_, ...), custom_call_target="tpu_custom_call" | custom-call | tf_op jit(solution)/shard_map/pallas_call | solution.py:543
  65.0 4.2 %shard_map.87.field = f32[16,256,128]{2,1,0:T(8,128)S(1)} custom-call(s32[2]{0:T(128)S(1)} %copy-done.9, f32[2,16,128]{2,1,0:T(8,128)S(1)} %pad_maximum_fusion.shares, f32[32,128]{1,0:T(8,128)S(1)} %collective-permute-done.7.other, f32[16,256,128]{2,1,0:T(8,128)S(1)} %get-tuple-element.23.field, f32[16,256,128]{2,1,0:T(8,128)S(1)} %get-tuple-element.20.winds, ...), custom_call_target="tpu_custom_call" | custom-call | tf_op jit(solution)/shard_map/pallas_call | solution.py:553
  69.2 1.4 %copy-done.3 = f32[16,256,128]{2,1,0:T(8,128)} copy-done((f32[16,256,128]{2,1,0:T(8,128)}, f32[16,256,128]{2,1,0:T(8,128)S(1)}, u32[]{:S(2)}) %copy-start.3) | copy-done | bytes 2097176
  70.6 1.6 %copy-done.4 = f32[16,256,128]{2,1,0:T(8,128)S(1)} copy-done((f32[16,256,128]{2,1,0:T(8,128)S(1)}, f32[16,256,128]{2,1,0:T(8,128)}, u32[]{:S(2)}) %copy-start.4) | copy-done | bytes 2097176
  72.2 10.7 %shard_map.88 = (f32[16,256,128]{2,1,0:T(8,128)S(1)}, f32[32,128]{1,0:T(8,128)S(1)}) custom-call(f32[16,136,128]{2,1,0:T(8,128)S(1)} %all-to-all-done.records, f32[16,256,128]{2,1,0:T(8,128)S(1)} %copy-done.4), custom_call_target="tpu_custom_call" | custom-call | tf_op jit(solution)/shard_map/pallas_call | solution.py:564
  84.1 3.0 %shard_map.89 = (f32[256,128]{1,0:T(8,128)S(1)}, f32[256,128]{1,0:T(8,128)}, f32[64,128]{1,0:T(8,128)S(1)}) custom-call(s32[2]{0:T(128)S(1)} %copy-done.10, f32[2,16,128]{2,1,0:T(8,128)S(1)} %pad_maximum_fusion.shares, f32[32,128]{1,0:T(8,128)S(1)} %collective-permute-done.8.other, f32[16,256,128]{2,1,0:T(8,128)S(1)} %get-tuple-element.27.field, ...), custom_call_target="tpu_custom_call" | custom-call | tf_op jit(solution)/shard_map/pallas_call | solution.py:577
  87.6 1.9 %collective-permute-start.11 = (f32[64,128]{1,0:T(8,128)S(1)}, f32[64,128]{1,0:T(8,128)S(1)}, u32[]{:S(2)}, u32[]{:S(2)}) collective-permute-start(f32[64,128]{1,0:T(8,128)S(1)} %get-tuple-element.29), channel_id=1, source_target_pairs={{1,2},{2,1},{3,4},{4,3},{5,6},{6,5},{9,10},{10,9},{11,12},{12,11},... | collective-permute-start | bytes 98312 | tf_op jit(solution)/shard_map/ppermute | solution.py:44
  89.6 2.0 %collective-permute-done.10.rest_1_ = f32[64,128]{1,0:T(8,128)S(1)} collective-permute-done((f32[64,128]{1,0:T(8,128)S(1)}, f32[64,128]{1,0:T(8,128)S(1)}, u32[]{:S(2)}, u32[]{:S(2)}) %collective-permute-start.10) | collective-permute-done | bytes 32800 | tf_op jit(solution)/shard_map/ppermute | solution.py:44
  91.6 2.8 %collective-permute-done.11.rest_2_ = f32[64,128]{1,0:T(8,128)S(1)} collective-permute-done((f32[64,128]{1,0:T(8,128)S(1)}, f32[64,128]{1,0:T(8,128)S(1)}, u32[]{:S(2)}, u32[]{:S(2)}) %collective-permute-start.11) | collective-permute-done | bytes 32800 | tf_op jit(solution)/shard_map/ppermute | solution.py:44
  94.3 3.0 %shard_map.90 = f32[32,128]{1,0:T(8,128)S(1)} custom-call(s32[2]{0:T(128)S(1)} %copy-done.10, f32[2,16,128]{2,1,0:T(8,128)S(1)} %pad_maximum_fusion.shares, f32[32,128]{1,0:T(8,128)S(1)} %collective-permute-done.8.other, f32[16,2,128,128]{3,2,1,0:T(8,128)S(1)} %bitcast.21, f32[16,16,128]{2,1,0:T(8,128)S(1)} %slice_bitcast_fusion.winds, ...), custom_call_target="tpu_custom_call" | custom-call | tf_op jit(solution)/shard_map/pallas_call | solution.py:583
  98.6 7.1 %shard_map.91 = (f32[16,256,128]{2,1,0:T(8,128)S(1)}, f32[256,128]{1,0:T(8,128)S(1)}, f32[256,128]{1,0:T(8,128)}, f32[64,128]{1,0:T(8,128)S(1)}) custom-call(s32[2]{0:T(128)S(1)} %copy-done.10, f32[2,16,128]{2,1,0:T(8,128)S(1)} %pad_maximum_fusion.shares, f32[32,128]{1,0:T(8,128)S(1)} %collective-permute-done.8.other, ...), custom_call_target="tpu_custom_call" | custom-call | tf_op jit(solution)/shard_map/pallas_call | solution.py:592
  105.7 1.5 %collective-permute-start.13 = (f32[256,128]{1,0:T(8,128)S(1)}, f32[256,128]{1,0:T(8,128)S(1)}, u32[]{:S(2)}, u32[]{:S(2)}) collective-permute-start(f32[256,128]{1,0:T(8,128)S(1)} %get-tuple-element.31), channel_id=1, source_target_pairs={{0,8},{8,0},{1,9},{9,1},{2,10},{10,2},{3,11},{11,3},{4,12},{12,4},... | collective-permute-start | bytes 393224 | tf_op jit(solution)/shard_map/ppermute | solution.py:44
  107.2 2.0 %collective-permute-start.14 = (f32[64,128]{1,0:T(8,128)S(1)}, f32[64,128]{1,0:T(8,128)S(1)}, u32[]{:S(2)}, u32[]{:S(2)}) collective-permute-start(f32[64,128]{1,0:T(8,128)S(1)} %get-tuple-element.32), channel_id=1, source_target_pairs={{0,1},{1,0},{2,3},{3,2},{4,5},{5,4},{6,7},{7,6},{8,9},{9,8},{10,11... | collective-permute-start | bytes 98312 | tf_op jit(solution)/shard_map/ppermute | solution.py:44
  109.2 1.9 %collective-permute-start.15 = (f32[64,128]{1,0:T(8,128)S(1)}, f32[64,128]{1,0:T(8,128)S(1)}, u32[]{:S(2)}, u32[]{:S(2)}) collective-permute-start(f32[64,128]{1,0:T(8,128)S(1)} %get-tuple-element.32), channel_id=1, source_target_pairs={{1,2},{2,1},{3,4},{4,3},{5,6},{6,5},{9,10},{10,9},{11,12},{12,11},... | collective-permute-start | bytes 98312 | tf_op jit(solution)/shard_map/ppermute | solution.py:44
  111.1 4.8 %collective-permute-done.15.rest_2_ = f32[64,128]{1,0:T(8,128)S(1)} collective-permute-done((f32[64,128]{1,0:T(8,128)S(1)}, f32[64,128]{1,0:T(8,128)S(1)}, u32[]{:S(2)}, u32[]{:S(2)}) %collective-permute-start.15) | collective-permute-done | bytes 32800 | tf_op jit(solution)/shard_map/ppermute | solution.py:44
  116.0 7.0 %shard_map.92 = f32[4096,128]{1,0:T(8,128)} custom-call(s32[2]{0:T(128)S(1)} %copy-done.10, f32[256,128]{1,0:T(8,128)S(1)} %broadcast_in_dim.8.scale, f32[16,256,128]{2,1,0:T(8,128)S(1)} %get-tuple-element.30.field, f32[16,256,128]{2,1,0:T(8,128)S(1)} %get-tuple-element.20.winds, f32[16,256,128]{2,1,0:T(8,128)S(1)} %copy-done.2, ...), custom_call_target="tpu_custom_call" | custom-call | tf_op jit(solution)/shard_map/pallas_call | solution.py:600
  (50 shorter events, 10.7 us)
Async XLA Ops:
  0.0 1.0 copy-start.7
  1.0 0.7 copy-start.11
  1.7 0.7 copy-start.12
  2.4 0.7 copy-start.13
  5.1 65.5 %all-to-all-start = ((f32[16,136,128]{2,1,0:T(8,128)}), f32[16,136,128]{2,1,0:T(8,128)S(1)}, u32[]{:S(2)}, u32[]{:S(2)}) async-start(f32[16,136,128]{2,1,0:T(8,128)} %shard_map.82), calls=%async_computation | async-start | bytes 2228224 | tf_op jit(solution)/shard_map/all_to_all | solution.py:530
  12.4 20.3 %copy-start.8 = (s32[2]{0:T(128)}, s32[2]{0:T(128)S(1)}, u32[]{:S(2)}) copy-start(s32[2]{0:T(128)S(1)} %pad_add_fusion.scal) | copy-start | bytes 28
  12.4 1.6 %copy-start.5 = (f32[1,2,128,16,128]{4,3,2,1,0:T(8,128)S(1)}, f32[1,2,128,16,128]{4,3,2,1,0:T(8,128)}, u32[]{:S(2)}) copy-start(f32[1,2,128,16,128]{4,3,2,1,0:T(8,128)} %param.8) | copy-start | bytes 6291460
  14.0 1.6 %copy-start.6 = (f32[1,2,128,16,128]{4,3,2,1,0:T(8,128)S(1)}, f32[1,2,128,16,128]{4,3,2,1,0:T(8,128)}, u32[]{:S(2)}) copy-start(f32[1,2,128,16,128]{4,3,2,1,0:T(8,128)} %param.9) | copy-start | bytes 6291460
  15.6 11.4 %copy-start.14 = (f32[16,128]{1,0:T(8,128)S(1)}, f32[16,128]{1,0:T(8,128)}, u32[]{:S(2)}) copy-start(f32[16,128]{1,0:T(8,128)} %param.10) | copy-start | bytes 24580
  20.1 1.3 %copy-start = (f32[16,256,128]{2,1,0:T(8,128)}, f32[16,256,128]{2,1,0:T(8,128)S(1)}, u32[]{:S(2)}) copy-start(f32[16,256,128]{2,1,0:T(8,128)S(1)} %get-tuple-element.19.field.state) | copy-start | bytes 6291460
  21.5 5.5 %collective-permute-start.1 = (f32[64,128]{1,0:T(8,128)}, f32[64,128]{1,0:T(8,128)S(1)}, u32[]{:S(2)}, u32[]{:S(2)}) collective-permute-start(f32[64,128]{1,0:T(8,128)} %get-tuple-element.22), channel_id=1, source_target_pairs={{0,1},{1,0},{2,3},{3,2},{4,5},{5,4},{6,7},{7,6},{8,9},{9,8},{10,11... | collective-permute-start | bytes 98312 | tf_op jit(solution)/shard_map/ppermute | solution.py:44
  22.9 9.8 %collective-permute-start.2 = (f32[64,128]{1,0:T(8,128)}, f32[64,128]{1,0:T(8,128)S(1)}, u32[]{:S(2)}, u32[]{:S(2)}) collective-permute-start(f32[64,128]{1,0:T(8,128)} %get-tuple-element.22), channel_id=1, source_target_pairs={{1,2},{2,1},{3,4},{4,3},{5,6},{6,5},{9,10},{10,9},{11,12},{12,11},... | collective-permute-start | bytes 98312 | tf_op jit(solution)/shard_map/ppermute | solution.py:44
  24.9 7.8 %collective-permute-start = (f32[256,128]{1,0:T(8,128)}, f32[256,128]{1,0:T(8,128)S(1)}, u32[]{:S(2)}, u32[]{:S(2)}) collective-permute-start(f32[256,128]{1,0:T(8,128)} %get-tuple-element.21), channel_id=1, source_target_pairs={{0,8},{8,0},{1,9},{9,1},{2,10},{10,2},{3,11},{11,3},{4,12},{12,4},... | collective-permute-start | bytes 393224 | tf_op jit(solution)/shard_map/ppermute | solution.py:44
  32.7 1.6 %copy-start.1 = (f32[16,256,128]{2,1,0:T(8,128)S(1)}, f32[16,256,128]{2,1,0:T(8,128)}, u32[]{:S(2)}) copy-start(f32[16,256,128]{2,1,0:T(8,128)} %copy-done) | copy-start | bytes 6291460
  37.3 1.2 collective-permute-start.3
  44.9 15.9 %collective-permute-start.4 = (f32[256,128]{1,0:T(8,128)S(1)}, f32[256,128]{1,0:T(8,128)S(1)}, u32[]{:S(2)}, u32[]{:S(2)}) collective-permute-start(f32[256,128]{1,0:T(8,128)S(1)} %get-tuple-element.24), channel_id=1, source_target_pairs={{0,8},{8,0},{1,9},{9,1},{2,10},{10,2},{3,11},{11,3},{4,12},{12,4},... | collective-permute-start | bytes 393224 | tf_op jit(solution)/shard_map/ppermute | solution.py:44
  46.4 9.7 %collective-permute-start.5 = (f32[64,128]{1,0:T(8,128)S(1)}, f32[64,128]{1,0:T(8,128)S(1)}, u32[]{:S(2)}, u32[]{:S(2)}) collective-permute-start(f32[64,128]{1,0:T(8,128)S(1)} %get-tuple-element.25), channel_id=1, source_target_pairs={{0,1},{1,0},{2,3},{3,2},{4,5},{5,4},{6,7},{7,6},{8,9},{9,8},{10,11... | collective-permute-start | bytes 98312 | tf_op jit(solution)/shard_map/ppermute | solution.py:44
  54.2 6.7 %collective-permute-start.6 = (f32[64,128]{1,0:T(8,128)S(1)}, f32[64,128]{1,0:T(8,128)S(1)}, u32[]{:S(2)}, u32[]{:S(2)}) collective-permute-start(f32[64,128]{1,0:T(8,128)S(1)} %get-tuple-element.25), channel_id=1, source_target_pairs={{1,2},{2,1},{3,4},{4,3},{5,6},{6,5},{9,10},{10,9},{11,12},{12,11},... | collective-permute-start | bytes 98312 | tf_op jit(solution)/shard_map/ppermute | solution.py:44
  63.8 1.2 collective-permute-start.7
  69.2 1.4 %copy-start.3 = (f32[16,256,128]{2,1,0:T(8,128)}, f32[16,256,128]{2,1,0:T(8,128)S(1)}, u32[]{:S(2)}) copy-start(f32[16,256,128]{2,1,0:T(8,128)S(1)} %shard_map.87.field) | copy-start | bytes 6291460
  70.6 1.6 %copy-start.4 = (f32[16,256,128]{2,1,0:T(8,128)S(1)}, f32[16,256,128]{2,1,0:T(8,128)}, u32[]{:S(2)}) copy-start(f32[16,256,128]{2,1,0:T(8,128)} %copy-done.3) | copy-start | bytes 6291460
  72.2 11.9 %copy-start.10 = (s32[2]{0:T(128)S(1)}, s32[2]{0:T(128)}, u32[]{:S(2)}) copy-start(s32[2]{0:T(128)} %copy-done.8) | copy-start | bytes 28
  82.9 1.2 %collective-permute-start.8 = (f32[32,128]{1,0:T(8,128)S(1)}, f32[32,128]{1,0:T(8,128)S(1)}, u32[]{:S(2)}, u32[]{:S(2)}) collective-permute-start(f32[32,128]{1,0:T(8,128)S(1)} %get-tuple-element.26), channel_id=1, source_target_pairs={{0,16},{16,0},{1,17},{17,1},{2,18},{18,2},{3,19},{19,3},{4,20},{20... | collective-permute-start | bytes 49160 | tf_op jit(solution)/shard_map/ppermute | solution.py:525
  87.1 7.2 %collective-permute-start.9 = (f32[256,128]{1,0:T(8,128)S(1)}, f32[256,128]{1,0:T(8,128)S(1)}, u32[]{:S(2)}, u32[]{:S(2)}) collective-permute-start(f32[256,128]{1,0:T(8,128)S(1)} %get-tuple-element.28), channel_id=1, source_target_pairs={{0,8},{8,0},{1,9},{9,1},{2,10},{10,2},{3,11},{11,3},{4,12},{12,4},... | collective-permute-start | bytes 393224 | tf_op jit(solution)/shard_map/ppermute | solution.py:44
  87.6 3.9 %collective-permute-start.10 = (f32[64,128]{1,0:T(8,128)S(1)}, f32[64,128]{1,0:T(8,128)S(1)}, u32[]{:S(2)}, u32[]{:S(2)}) collective-permute-start(f32[64,128]{1,0:T(8,128)S(1)} %get-tuple-element.29), channel_id=1, source_target_pairs={{0,1},{1,0},{2,3},{3,2},{4,5},{5,4},{6,7},{7,6},{8,9},{9,8},{10,11... | collective-permute-start | bytes 98312 | tf_op jit(solution)/shard_map/ppermute | solution.py:44
  87.6 6.7 %collective-permute-start.11 = (f32[64,128]{1,0:T(8,128)S(1)}, f32[64,128]{1,0:T(8,128)S(1)}, u32[]{:S(2)}, u32[]{:S(2)}) collective-permute-start(f32[64,128]{1,0:T(8,128)S(1)} %get-tuple-element.29), channel_id=1, source_target_pairs={{1,2},{2,1},{3,4},{4,3},{5,6},{6,5},{9,10},{10,9},{11,12},{12,11},... | collective-permute-start | bytes 98312 | tf_op jit(solution)/shard_map/ppermute | solution.py:44
  97.3 18.6 %copy-start.15 = (f32[1,2,128]{2,1,0:T(2,128)S(1)}, f32[1,2,128]{2,1,0:T(2,128)}, u32[]{:S(2)}) copy-start(f32[1,2,128]{2,1,0:T(2,128)} %param.11) | copy-start | bytes 3076
  97.3 18.7 %copy-start.2 = (f32[16,256,128]{2,1,0:T(8,128)S(1)}, f32[16,256,128]{2,1,0:T(8,128)}, u32[]{:S(2)}) copy-start(f32[16,256,128]{2,1,0:T(8,128)} %copy-done) | copy-start | bytes 6291460
  97.3 1.2 %collective-permute-start.12 = (f32[32,128]{1,0:T(8,128)S(1)}, f32[32,128]{1,0:T(8,128)S(1)}, u32[]{:S(2)}, u32[]{:S(2)}) collective-permute-start(f32[32,128]{1,0:T(8,128)S(1)} %shard_map.90), channel_id=1, source_target_pairs={{0,16},{16,0},{1,17},{17,1},{2,18},{18,2},{3,19},{19,3},{4,20},{20... | collective-permute-start | bytes 49160 | tf_op jit(solution)/shard_map/ppermute | solution.py:525
  105.7 10.2 %collective-permute-start.13 = (f32[256,128]{1,0:T(8,128)S(1)}, f32[256,128]{1,0:T(8,128)S(1)}, u32[]{:S(2)}, u32[]{:S(2)}) collective-permute-start(f32[256,128]{1,0:T(8,128)S(1)} %get-tuple-element.31), channel_id=1, source_target_pairs={{0,8},{8,0},{1,9},{9,1},{2,10},{10,2},{3,11},{11,3},{4,12},{12,4},... | collective-permute-start | bytes 393224 | tf_op jit(solution)/shard_map/ppermute | solution.py:44
  107.2 3.9 %collective-permute-start.14 = (f32[64,128]{1,0:T(8,128)S(1)}, f32[64,128]{1,0:T(8,128)S(1)}, u32[]{:S(2)}, u32[]{:S(2)}) collective-permute-start(f32[64,128]{1,0:T(8,128)S(1)} %get-tuple-element.32), channel_id=1, source_target_pairs={{0,1},{1,0},{2,3},{3,2},{4,5},{5,4},{6,7},{7,6},{8,9},{9,8},{10,11... | collective-permute-start | bytes 98312 | tf_op jit(solution)/shard_map/ppermute | solution.py:44
  109.2 6.7 %collective-permute-start.15 = (f32[64,128]{1,0:T(8,128)S(1)}, f32[64,128]{1,0:T(8,128)S(1)}, u32[]{:S(2)}, u32[]{:S(2)}) collective-permute-start(f32[64,128]{1,0:T(8,128)S(1)} %get-tuple-element.32), channel_id=1, source_target_pairs={{1,2},{2,1},{3,4},{4,3},{5,6},{6,5},{9,10},{10,9},{11,12},{12,11},... | collective-permute-start | bytes 98312 | tf_op jit(solution)/shard_map/ppermute | solution.py:44
  (1 other events, 0.6 us)

commit v2 on v1

v2 whole, which is shorter than its diff:
```python
import functools

import jax
import jax.numpy as jnp
from jax import lax
from jax.experimental import pallas as pl
from jax.experimental.pallas import tpu as pltpu
from jax.sharding import PartitionSpec as P

HORIZ_MIX = 0.1
VERT_MIX = 0.15
LANES = 128
GROUP = 8
MIB = 1024 * 1024
SWEEP_VMEM = 14 * MIB
OBSERVE_VMEM = 20 * MIB


def call(body, out_shape, scratch=(), limit=SWEEP_VMEM, **kw):
    return pl.pallas_call(
        body,
        out_shape=out_shape,
        scratch_shapes=list(scratch),
        compiler_params=pltpu.CompilerParams(vmem_limit_bytes=limit),
        **kw,
    )


def f32(*shape):
    return jax.ShapeDtypeStruct(shape, jnp.float32)


def lane_iota(rows=GROUP):
    return lax.broadcasted_iota(jnp.int32, (rows, LANES), 1)


def sub_iota(rows=GROUP):
    return lax.broadcasted_iota(jnp.int32, (rows, LANES), 0)


def pair_swap(block, axis, start):
    count = lax.axis_size(axis)
    route = []
    for low in range(start, count - 1, 2):
        route += [(low, low + 1), (low + 1, low)]
    return lax.ppermute(block, axis, route)


def exchange(strips, packed):
    y_even = pair_swap(packed, "gy", 0)
    y_odd = pair_swap(packed, "gy", 1)
    halos = [pair_swap(strips[0], "gx", 0), y_even, y_odd]
    if lax.axis_size("gx") > 2:
        halos.append(pair_swap(strips[1], "gx", 1))
    return halos


def read_sides(scal, refs):
    even = refs[0]
    odd = refs[3] if len(refs) > 3 else None
    at_even = scal[0] == 0

    def after(at):
        other = jnp.zeros_like(even[at]) if odd is None else odd[at]
        return jnp.where(at_even, even[at], other)

    def before(at):
        other = jnp.zeros_like(even[at]) if odd is None else odd[at]
        return jnp.where(at_even, other, even[at])

    return before, after


PARTS = 4


def merged(scal, y_even, y_odd, at):
    a, b = y_even[at, :], y_odd[at, :]
    lane = lax.broadcasted_iota(jnp.int32, a.shape, 1)
    return jnp.where((lane % 2) == (1 - scal[1]), a, b)


def merge_columns(scal, y_even, y_odd, sides):
    sides[...] = merged(scal, y_even, y_odd, slice(None))


def slot_of(i, part, rows):
    return PARTS * (rows - 1 - i) + part


def side_columns(sides, i, group):
    m, part = group // PARTS, group % PARTS
    rows = LANES // (2 * PARTS)
    return pltpu.roll(sides[m * GROUP : (m + 1) * GROUP, :], LANES - 1 - 2 * slot_of(i, part, rows), 1)


def pack_into(total, value, slot):
    return jnp.where(lane_iota() // 2 == slot, pltpu.roll(value, 2 * slot + 1, 1), total)


def pack_block(packed, values, i, m):
    at = pl.ds(m * GROUP, GROUP)
    total = packed[at, :]
    for part, value in enumerate(values):
        total = pack_into(total, value, slot_of(i, part, LANES // (2 * PARTS)))
    packed[at, :] = total


CENTRE = 1.0 - 4.0 * HORIZ_MIX - 2.0 * VERT_MIX


def levels_around(cells, i, base, group, groups):
    here = cells[i + 1, pl.ds(base + group * GROUP, GROUP), :]
    if group == groups - 1:
        upper = jnp.where(sub_iota() == GROUP - 1, here, pltpu.roll(here, GROUP - 1, 0))
    else:
        upper = cells[i + 1, pl.ds(base + group * GROUP + 1, GROUP), :]
    if group == 0:
        lower = jnp.where(sub_iota() == 0, here, pltpu.roll(here, 1, 0))
    else:
        lower = cells[i + 1, pl.ds(base + group * GROUP - 1, GROUP), :]
    return here, upper, lower


def shifted(first, last, edge, rows=GROUP):
    lane = lane_iota(rows)
    right = pltpu.roll(jnp.where(lane == 0, edge, first), LANES - 1, 1)
    left = pltpu.roll(jnp.where(lane == LANES - 1, edge, last), 1, 1)
    return right, left


def forward_sum(here, vertical, after, before, right, left, u, w):
    return (
        CENTRE * here
        + VERT_MIX * vertical
        + HORIZ_MIX * ((after + before) + (right + left))
        - 0.5 * (u * (after - before) + w * (right - left))
    )


def forward_point(cells, winds, sides, i, f, group, levels):
    groups = levels // GROUP
    here, upper, lower = levels_around(cells, i, f * levels, group, groups)
    at = pl.ds(f * levels + group * GROUP, GROUP)
    right, left = shifted(here, here, side_columns(sides, i, f * groups + group))
    u = winds[i + 1, pl.ds(group * GROUP, GROUP), :]
    w = winds[i + 1, pl.ds(levels + group * GROUP, GROUP), :]
    return forward_sum(here, upper + lower, cells[i + 2, at, :], cells[i, at, :], right, left, u, w)


def products(x, wind):
    slope = 0.5 * (wind * x)
    return HORIZ_MIX * x - slope, HORIZ_MIX * x + slope


def adjoint_point(cells, winds, sides, i, f, group, levels):
    groups = levels // GROUP
    here, upper, lower = levels_around(cells, i, f * levels, group, groups)
    at = pl.ds(f * levels + group * GROUP, GROUP)
    wind_at = pl.ds(group * GROUP, GROUP)
    after, before = cells[i + 2, at, :], cells[i, at, :]
    u_after, u_before = winds[i + 2, wind_at, :], winds[i, wind_at, :]
    w = winds[i + 1, pl.ds(levels + group * GROUP, GROUP), :]
    down, up = products(here, w)
    right, left = shifted(up, down, side_columns(sides, i, f * groups + group))
    return (
        CENTRE * here
        + VERT_MIX * (upper + lower)
        + HORIZ_MIX * (after + before)
        + 0.5 * (u_after * after - u_before * before)
        + (right + left)
    )


def couple_forward(value, other, shares):
    return value - shares[0] * (value - other)


def couple_adjoint(value, other, shares):
    return value - shares[0] * value + shares[1] * other


def coupled(rule, value, other, shares, i, f, rows):
    here = [shares[part, pl.ds(i, 1), :] for part in range(2)]
    return jnp.where(sub_iota() == 0, rule(value, other[pl.ds(f * rows + i, 1), :], here), value)


def put_strip(scal, strip_even, strip_odd, at, first, last):
    at_even = scal[0] == 0
    strip_even[at, :] = jnp.where(at_even, last, first)
    strip_odd[at, :] = jnp.where(at_even, first, last)


def edges_kernel(rows, levels, scal, state, s_even, s_odd, packed):
    width = state.shape[0] // rows

    def block(m, _):
        total = jnp.zeros((GROUP, LANES), jnp.float32)
        for part in range(PARTS):
            for i in range(rows):
                start = (m * PARTS + part) * GROUP * rows + i
                total = pack_into(total, state[pl.ds(start, GROUP, stride=rows), :], slot_of(i, part, rows))
        packed[pl.ds(pl.multiple_of(m * GROUP, GROUP), GROUP), :] = total
        return 0

    lax.fori_loop(0, width // (PARTS * GROUP), block, 0)
    first = state[pl.ds(0, width, stride=rows), :]
    last = state[pl.ds(rows - 1, width, stride=rows), :]
    put_strip(scal, s_even, s_odd, slice(None), first, last)


def to_rows_kernel(rows, state, winds, state_rows, wind_rows):
    width = state_rows.shape[1]

    def row(i, _):
        for c in range(width // GROUP):
            at = pl.ds(c * GROUP, GROUP)
            start = pl.ds(c * GROUP * rows + i, GROUP, stride=rows)
            state_rows[i, at, :] = state[start, :]
            wind_rows[i + 1, at, :] = winds[start, :]
        return 0

    lax.fori_loop(0, rows, row, 0)
    wind_rows[0] = jnp.zeros((width, LANES), jnp.float32)
    wind_rows[rows + 1] = jnp.zeros((width, LANES), jnp.float32)


def floor_inputs(scal, field, winds, halos, f, rows, levels):
    width = 2 * levels
    low = field[pl.ds(f * levels, rows, stride=width), :]
    next_up = field[pl.ds(f * levels + 1, rows, stride=width), :]
    u = winds[pl.ds(width, rows, stride=width), :]
    w = winds[pl.ds(width + levels, rows, stride=width), :]
    m = f * (levels // GROUP) // PARTS
    sides = jnp.broadcast_to(merged(scal, halos[1], halos[2], pl.ds(m * GROUP, 1)), (rows, LANES))
    edge = pltpu.roll(sides, 2 * PARTS - 1, 1, stride=2 * PARTS, stride_axis=0)
    return low, next_up, u, w, edge


def neighbours(value, first, last, rows):
    after = jnp.where(sub_iota(rows) == rows - 1, last, pltpu.roll(value, rows - 1, 0))
    before = jnp.where(sub_iota(rows) == 0, first, pltpu.roll(value, 1, 0))
    return after, before


def forward_floor_kernel(rows, levels, scal, field, winds, *rest):
    *halos, floor = rest
    side_before, side_after = read_sides(scal, halos)
    for f in range(2):
        low, up, u, w, edge = floor_inputs(scal, field, winds, halos, f, rows, levels)
        at = pl.ds(f * levels, 1)
        after, before = neighbours(low, side_before(at), side_after(at), rows)
        right, left = shifted(low, low, edge, rows)
        floor[f * rows : (f + 1) * rows, :] = forward_sum(low, up + low, after, before, right, left, u, w)


def adjoint_floor_kernel(rows, levels, scal, shares, other, field, winds, *rest):
    *halos, floor = rest
    side_before, side_after = read_sides(scal, halos)
    for f in range(2):
        low, up, u, w, edge = floor_inputs(scal, field, winds, halos, f, rows, levels)
        low = couple_adjoint(low, other[f * rows : (f + 1) * rows, :], shares)
        at = pl.ds(f * levels, 1)
        x_down, x_up = products(low, u)
        after, _ = neighbours(x_up, side_before(at), side_after(at), rows)
        _, before = neighbours(x_down, side_before(at), side_after(at), rows)
        down, up_wind = products(low, w)
        right, left = shifted(up_wind, down, edge, rows)
        floor[f * rows : (f + 1) * rows, :] = (
            CENTRE * low + VERT_MIX * (up + low) + (after + before) + (right + left)
        )


def fill(cells, source, rows, before, after, fix=None):
    def row(i, _):
        cells[i + 1] = source[i]
        if fix is not None:
            fix(i)
        return 0

    lax.fori_loop(0, rows, row, 0)
    cells[0] = before
    cells[rows + 1] = after


def forward_kernel(rows, levels, last, scal, shares, other, field, winds, *rest):
    if last:
        *halos, cols, cells, sides = rest
    else:
        *halos, out, s_even, s_odd, packed, cells, sides = rest
        packed[...] = jnp.zeros_like(packed)
    merge_columns(scal, halos[1], halos[2], sides)
    before, after = read_sides(scal, halos)
    fill(cells, field, rows, before(slice(None)), after(slice(None)))
    groups = levels // GROUP
    width = 2 * levels

    def row(i, _):
        for m in range(2 * groups // PARTS):
            f, first = m * PARTS // groups, m * PARTS % groups
            values = []
            for group in range(first, first + PARTS):
                value = forward_point(cells, winds, sides, i, f, group, levels)
                if group == 0:
                    value = coupled(couple_forward, value, other, shares, i, f, rows)
                values.append(value)
            base = m * PARTS * GROUP
            if last:
                lanes = pl.ds(pl.multiple_of(i * LANES, LANES), LANES)
                high, low = split(jnp.concatenate(values, axis=0), 2)
                cols[pl.ds(base, PARTS * GROUP), lanes] = high
                cols[pl.ds(width + base, PARTS * GROUP), lanes] = low
            else:
                for part, value in enumerate(values):
                    out[i, pl.ds(base + part * GROUP, GROUP), :] = value
                pack_block(packed, values, i, m)
        return 0

    lax.fori_loop(0, rows, row, 0)
    if not last:
        put_strip(scal, s_even, s_odd, slice(None), out[0], out[rows - 1])


def put_products(scal, s_even, s_odd, first_row, last_row, winds, rows, levels):
    for f in range(2):
        at = pl.ds(f * levels, levels)
        _, first = products(first_row(at), winds[1, pl.ds(0, levels), :])
        last, _ = products(last_row(at), winds[rows, pl.ds(0, levels), :])
        put_strip(scal, s_even, s_odd, at, first, last)


def with_products(value, winds, i, group, levels):
    down, up = products(value, winds[i + 1, pl.ds(levels + group * GROUP, GROUP), :])
    return jnp.where(lane_iota() == 0, up, down)


def adjoint_pack_kernel(rows, levels, scal, shares, other, field, winds, out, s_even, s_odd, packed):
    packed[...] = jnp.zeros_like(packed)
    groups = levels // GROUP

    def row(i, _):
        for m in range(2 * groups // PARTS):
            f, first = m * PARTS // groups, m * PARTS % groups
            values = []
            for group in range(first, first + PARTS):
                at = pl.ds(f * levels + group * GROUP, GROUP)
                value = field[i, at, :]
                if group == 0:
                    value = coupled(couple_adjoint, value, other, shares, i, f, rows)
                    out[i, pl.ds(f * GROUP, GROUP), :] = value
                values.append(with_products(value, winds, i, group, levels))
            pack_block(packed, values, i, m)
        return 0

    lax.fori_loop(0, rows, row, 0)

    def coupled_row(i):
        def read(at):
            f = at.start // levels
            bottom = out[i, pl.ds(f * GROUP, GROUP), :]
            return jnp.concatenate([bottom, field[i, pl.ds(f * levels + GROUP, levels - GROUP), :]], axis=0)

        return read

    put_products(scal, s_even, s_odd, coupled_row(0), coupled_row(rows - 1), winds, rows, levels)


def adjoint_kernel(rows, levels, scal, shares, bottom, other_next, field, winds, *rest):
    *halos, out, s_even, s_odd, packed, cells, sides = rest
    packed[...] = jnp.zeros_like(packed)
    merge_columns(scal, halos[1], halos[2], sides)
    before, after = read_sides(scal, halos)
    groups = levels // GROUP

    def fix(i):
        for f in range(2):
            cells[i + 1, pl.ds(f * levels, GROUP), :] = bottom[i, pl.ds(f * GROUP, GROUP), :]

    everything = slice(None)
    fill(cells, field, rows, before(everything) / HORIZ_MIX, after(everything) / HORIZ_MIX, fix)

    def row(i, _):
        for m in range(2 * groups // PARTS):
            f, first = m * PARTS // groups, m * PARTS % groups
            values = []
            for group in range(first, first + PARTS):
                value = adjoint_point(cells, winds, sides, i, f, group, levels)
                if group == 0:
                    value = coupled(couple_adjoint, value, other_next, shares, i, f, rows)
                out[i, pl.ds(f * levels + group * GROUP, GROUP), :] = value
                values.append(with_products(value, winds, i, group, levels))
            pack_block(packed, values, i, m)
        return 0

    lax.fori_loop(0, rows, row, 0)
    put_products(scal, s_even, s_odd, lambda at: out[0, at, :], lambda at: out[rows - 1, at, :], winds, rows, levels)


def final_kernel(rows, levels, scal, scale, field, winds, state, *rest):
    *halos, out, cells, sides = rest
    merge_columns(scal, halos[1], halos[2], sides)
    before, after = read_sides(scal, halos)
    groups = levels // GROUP
    everything = slice(None)
    fill(cells, field, rows, before(everything) / HORIZ_MIX, after(everything) / HORIZ_MIX)

    def row(i, _):
        for group in range(groups):
            for f in range(2):
                at = pl.ds(f * levels + group * GROUP, GROUP)
                value = adjoint_point(cells, winds, sides, i, f, group, levels)
                value = value + scale[at, :] * state[i, at, :]
                out[pl.ds((f * levels + group * GROUP) * rows + i, GROUP, stride=rows), :] = value
        return 0

    lax.fori_loop(0, rows, row, 0)


def split(value, terms):
    parts = []
    for _ in range(terms):
        part = value.astype(jnp.bfloat16)
        parts.append(part)
        value = value - part.astype(jnp.float32)
    return parts


def dot(a, b, contract):
    return lax.dot_general(a, b, ((contract[:1], contract[1:]), ((), ())), preferred_element_type=jnp.float32)


def route_kernel(tiles, cap, dest, col, prec, op, out):
    count = op.shape[0]
    width = op.shape[1]
    halves = width // LANES
    owner = lax.broadcasted_iota(jnp.int32, (tiles, count), 0)
    hits = owner == dest[...]
    ones = jnp.where(hits, 1.0, 0.0)
    earlier = lax.broadcasted_iota(jnp.int32, (count, count), 0) <= lax.broadcasted_iota(jnp.int32, (count, count), 1)
    running = dot(ones.astype(jnp.bfloat16), jnp.where(earlier, 1.0, 0.0).astype(jnp.bfloat16), (1, 0))
    slot = jnp.sum(running * ones, axis=0, keepdims=True) - 1.0
    slot = slot.astype(jnp.int32)
    place = dest[...] * cap + slot
    at_slot = lax.broadcasted_iota(jnp.int32, (LANES, count), 0) == slot
    at_slot = jnp.where(at_slot, 1.0, 0.0).astype(jnp.bfloat16)
    column = col[...].astype(jnp.float32)
    pieces = [ones * part.astype(jnp.float32) for part in split(column, 2) + split(prec[...], 3)]
    aux = dot(jnp.concatenate(pieces, axis=0).astype(jnp.bfloat16), at_slot, (1, 1))
    columns = aux[0:tiles] + aux[tiles : 2 * tiles]
    precs = (aux[2 * tiles : 3 * tiles] + aux[3 * tiles : 4 * tiles]) + aux[4 * tiles : 5 * tiles]
    sub = sub_iota()
    for owner_at in range(tiles):
        block = jnp.where(sub == 0, columns[owner_at : owner_at + 1], 0.0)
        block = jnp.where(sub == 1, precs[owner_at : owner_at + 1], block)
        out[owner_at, pl.ds(halves * cap, GROUP), :] = block
    rows_high, rows_low = split(op[...], 2)
    chunk = 256
    for first in range(0, tiles * cap, chunk):
        picks = lax.broadcasted_iota(jnp.int32, (chunk, count), 0) + first == place
        picks = jnp.where(picks, 1.0, 0.0).astype(jnp.bfloat16)
        moved = dot(picks, rows_high, (1, 0)) + dot(picks, rows_low, (1, 0))
        for part in range(chunk // cap):
            for half in range(halves):
                out[first // cap + part, pl.ds(half * cap, cap), :] = moved[
                    part * cap : (part + 1) * cap, half * LANES : (half + 1) * LANES
                ]


def observe_kernel(rows, width, tiles, cap, records, cols, adjoint, floor, sel, precs, both, spread):
    halves = width // LANES
    count = tiles * cap
    aux = halves * cap
    own = lax.broadcasted_iota(jnp.int32, (cap, LANES), 1) == lax.broadcasted_iota(jnp.int32, (cap, LANES), 0)
    ones = jnp.ones((LANES, LANES), jnp.bfloat16)
    step = 256
    lane = lax.broadcasted_iota(jnp.int32, (step, LANES), 1).astype(jnp.float32)

    def select(block, _):
        sources = step // cap

        def spread_out(part):
            rows_of = [
                jnp.where(own, records[block * sources + s, pl.ds(aux + part, 1), :], 0.0) for s in range(sources)
            ]
            terms = split(jnp.concatenate(rows_of, axis=0), 2 + part)
            return sum(dot(term, ones, (1, 0)) for term in terms)

        at = pl.ds(pl.multiple_of(block * step, step), step)
        column = spread_out(0) - lane
        precs[at, :] = spread_out(1)
        for i in range(rows):
            sel[at, i * LANES : (i + 1) * LANES] = jnp.where(column == float(i * LANES), 1.0, 0.0).astype(jnp.bfloat16)
        return 0

    lax.fori_loop(0, count // step, select, 0)
    both[...] = dot(sel[...], cols[...], (1, 1))

    def weigh(block, _):
        at = pl.ds(pl.multiple_of(block * LANES, LANES), LANES)
        sources = LANES // cap
        ops = [
            jnp.concatenate(
                [records[block * sources + s, half * cap : (half + 1) * cap, :] for s in range(sources)], axis=0
            )
            for half in range(halves)
        ]
        total = sum(
            (both[at, half * LANES : (half + 1) * LANES] + both[at, width + half * LANES : width + (half + 1) * LANES])
            * ops[half]
            for half in range(halves)
        )
        innovation = jnp.sum(total, axis=1, keepdims=True) * precs[at, :]
        for half in range(halves):
            high, low = split((ops[half] * innovation).T, 2)
            spread[half * LANES : (half + 1) * LANES, at] = high
            spread[width + half * LANES : width + (half + 1) * LANES, at] = low
        return 0

    lax.fori_loop(0, count // LANES, weigh, 0)
    sums = dot(spread[...], sel[...], (1, 0))
    for i in range(rows):
        lanes = slice(i * LANES, (i + 1) * LANES)
        adjoint[i] = sums[:width, lanes] + sums[width:, lanes]
        for f in range(2):
            floor[f * rows + i : f * rows + i + 1, :] = adjoint[i, f * (width // 2) : f * (width // 2) + 1, :]


def local(state_incr, winds, coupling, background, obs_dest, obs_col, obs_op, obs_prec):
    _, fields, levels, rows, lanes = state_incr.shape
    width = fields * levels
    groups = width // GROUP
    tiles = lax.axis_size("gx") * lax.axis_size("gy")
    count = obs_col.shape[0]
    cap = 2 * count // tiles
    halves = obs_op.shape[1] // LANES

    scal = jnp.stack([lax.axis_index("gx") % 2, lax.axis_index("gy") % 2]).astype(jnp.int32)
    own_share = jnp.where(lax.axis_index("comp") == 0, 1.0, 0.5)
    shares = jnp.stack([own_share * coupling, (1.5 - own_share) * coupling])
    scale = jnp.broadcast_to(background.reshape(width, 1), (width, LANES))

    smem = pl.BlockSpec(memory_space=pltpu.SMEM)
    vmem = pl.BlockSpec(memory_space=pltpu.VMEM)
    cells_shape = pltpu.VMEM((rows + 2, width, LANES), jnp.float32)
    packed_shape = f32(groups // PARTS * GROUP, LANES)
    sides_shape = pltpu.VMEM(packed_shape.shape, jnp.float32)
    strip_shapes = [f32(width, LANES), f32(width, LANES), packed_shape]
    field_shape = f32(rows, width, LANES)
    floor_shape = f32(fields * rows, LANES)

    def run(body, out_shape, scratch, *args, **kw):
        return call(functools.partial(body, rows, levels), out_shape, scratch, **kw, in_specs=[smem] + [vmem] * len(args))(
            scal, *args
        )

    def flat(field):
        return field.reshape(field.shape[0] * width, lanes)

    def swap_floor(floor):
        return lax.ppermute(floor, "comp", [(0, 1), (1, 0)])

    state_flat = state_incr.reshape(width * rows, lanes)
    s_even, s_odd, packed = run(edges_kernel, strip_shapes, [], state_flat)
    halos = exchange((s_even, s_odd), packed)

    send = call(functools.partial(route_kernel, tiles, cap), f32(tiles, halves * cap + GROUP, LANES))(
        obs_dest.reshape(1, count), obs_col.reshape(1, count), obs_prec.reshape(1, count), obs_op
    )
    send, halos[2] = lax.optimization_barrier((send, halos[2]))
    records = lax.all_to_all(send, ("gx", "gy"), split_axis=0, concat_axis=0, tiled=True)

    field, wind_rows = call(
        functools.partial(to_rows_kernel, rows), [field_shape, f32(rows + 2, width, LANES)], in_specs=[vmem, vmem]
    )(state_flat, winds.reshape(width * rows, lanes))
    state_rows = field

    for sweep in range(2):
        if sweep > 0:
            halos = exchange((s_even, s_odd), packed)
        floor = run(forward_floor_kernel, floor_shape, [], flat(field), flat(wind_rows), *halos)
        other = swap_floor(floor)
        args = (shares, other, field, wind_rows, *halos)
        scratch = [cells_shape, sides_shape]
        if sweep == 0:
            field, s_even, s_odd, packed = run(
                lambda r, v, *refs: forward_kernel(r, v, False, *refs), [field_shape] + strip_shapes, scratch, *args
            )
        else:
            cols = run(
                lambda r, v, *refs: forward_kernel(r, v, True, *refs),
                jax.ShapeDtypeStruct((2 * width, rows * LANES), jnp.bfloat16),
                scratch,
                *args,
            )

    slots = tiles * cap
    adjoint, floor = call(
        functools.partial(observe_kernel, rows, width, tiles, cap),
        [field_shape, floor_shape],
        [
            pltpu.VMEM((slots, rows * LANES), jnp.bfloat16),
            pltpu.VMEM((slots, LANES), jnp.float32),
            pltpu.VMEM((slots, 2 * width), jnp.float32),
            pltpu.VMEM((2 * width, slots), jnp.bfloat16),
        ],
        limit=OBSERVE_VMEM,
    )(records, cols)

    other = swap_floor(floor)
    bottom, s_even, s_odd, packed = run(
        adjoint_pack_kernel, [f32(rows, fields * GROUP, LANES)] + strip_shapes, [], shares, other, adjoint, wind_rows
    )
    halos = exchange((s_even, s_odd), packed)
    floor = run(adjoint_floor_kernel, floor_shape, [], shares, other, flat(adjoint), flat(wind_rows), *halos)
    other_next = swap_floor(floor)
    adjoint, s_even, s_odd, packed = run(
        adjoint_kernel,
        [field_shape] + strip_shapes,
        [cells_shape, sides_shape],
        shares, bottom, other_next, adjoint, wind_rows, *halos,
    )
    halos = exchange((s_even, s_odd), packed)
    result = run(
        final_kernel, f32(width * rows, LANES), [cells_shape, sides_shape], scale, adjoint, wind_rows, state_rows, *halos
    )
    return result.reshape(state_incr.shape)


def solution(mesh):
    placed = (
        P("comp", None, None, "gx", "gy"),
        P("comp", None, None, "gx", "gy"),
        P("gx", "gy"),
        P("comp", None, None),
        P(("comp", "gx", "gy"), None),
        P(("comp", "gx", "gy")),
        P(("comp", "gx", "gy"), None),
        P(("comp", "gx", "gy")),
    )
    return jax.shard_map(
        local,
        mesh=mesh,
        in_specs=placed,
        out_specs=P("comp", None, None, "gx", "gy"),
        check_vma=False,
    )
```

time: 124 us -> 101 us (0.81)
  Pallas kernels: 53.2 us -> 42.5 us
  starting transfers between devices: 32 us -> 26.1 us
  local copies, waits for them, and re-layouts: 12.9 us -> 8.46 us
  waiting for transfers between devices: 24.6 us -> 23.1 us
    pallas_call x9 -> x10, Pallas kernels: 40.5 us -> 32.4 us  [the longest x9 30.2 us: run(): call(functools.partial(body, rows, levels), out_shape, scratch, **kw, in_...]
    ppermute x12, starting transfers between devices: 24.5 us -> 19.4 us  [pair_swap(): return lax.ppermute(block, axis, route)]
    unnamed x32, local copies, waits for them, and re-layouts: 12.8 us -> 8.38 us
    pallas_call x1, Pallas kernels: 10.7 us -> 8.09 us  [local(): call(functools.partial(observe_kernel, rows, width, tiles, cap), [field_s...]
    ppermute x12, waiting for transfers between devices: 20.1 us -> 18.6 us  [pair_swap(): return lax.ppermute(block, axis, route)]
  transfers between devices with their start and end apart: 17 -> 17, of which waited for: 9 -> 12; matrix products, arithmetic and copies ran while one was open for 0% -> 0% of each run, Pallas kernels for 17% -> 16%
where the time goes in v2:
time: 101 us
  Pallas kernels  42.5 us (42%)
  starting transfers between devices  26.1 us (26%)
  waiting for transfers between devices  23.1 us (23%)
  local copies, waits for them, and re-layouts  8.46 us (8%)
    pallas_call x9, Pallas kernels, run(): call(functools.partial(body, rows, levels), out_shape, scratch, **kw, in_...  30.2 us
    ppermute x12, starting transfers between devices, pair_swap(): return lax.ppermute(block, axis, route)  19.4 us
    ppermute x12, waiting for transfers between devices, pair_swap(): return lax.ppermute(block, axis, route)  18.6 us
    unnamed x32, local copies, waits for them, and re-layouts  8.38 us
    pallas_call x1, Pallas kernels, local(): call(functools.partial(observe_kernel, rows, width, tiles, cap), [field_s...  8.09 us
    all_to_all x1, starting transfers between devices, local(): lax.all_to_all(send, ('gx', 'gy'), split_axis=0, concat_axis=0, tiled=True)  6.3 us
    ppermute x4, waiting for transfers between devices, swap_floor(): return lax.ppermute(floor, 'comp', [(0, 1), (1, 0)])  4.52 us
    pallas_call x1, Pallas kernels, local(): call(functools.partial(to_rows_kernel, rows), [field_shape, f32(rows + 2,...  2.22 us
  transfers between devices with their start and end apart: 17, of which 12 were waited for; matrix products, arithmetic and copies ran while one was open for 0% of the time, Pallas kernels for 16%

profile of v2, /device:TPU:8, one launch (start us, length us, event | category | flops | bytes accessed | tf_op | source)
XLA Modules:
  0.0 100.5 jit_solution(17820335003842071777)
XLA Ops:
  0.1 1.6 %copy-done.2 = f32[1,2,128,16,128]{4,3,2,1,0:T(8,128)S(1)} copy-done((f32[1,2,128,16,128]{4,3,2,1,0:T(8,128)S(1)}, f32[1,2,128,16,128]{4,3,2,1,0:T(8,128)}, u32[]{:S(2)}) %copy-start.2) | copy-done | bytes 2097176
  1.7 2.5 %shard_map.83 = (f32[256,128]{1,0:T(8,128)}, f32[256,128]{1,0:T(8,128)}, f32[64,128]{1,0:T(8,128)}) custom-call(s32[2]{0:T(128)S(1)} %pad_add_fusion.scal.refs_0_, f32[4096,128]{1,0:T(8,128)S(1)} %bitcast.23), custom_call_target="tpu_custom_call" | custom-call | tf_op jit(solution)/shard_map/pallas_call | solution.py:552
  4.2 3.4 %collective-permute-start = (f32[64,128]{1,0:T(8,128)}, f32[64,128]{1,0:T(8,128)S(1)}, u32[]{:S(2)}, u32[]{:S(2)}) collective-permute-start(f32[64,128]{1,0:T(8,128)} %get-tuple-element.22), channel_id=1, source_target_pairs={{1,2},{2,1},{3,4},{4,3},{5,6},{6,5},{9,10},{10,9},{11,12},{12,11},... | collective-permute-start | bytes 98312 | tf_op jit(solution)/shard_map/ppermute | solution.py:46
  7.6 2.0 %shard_map.82 = f32[16,136,128]{2,1,0:T(8,128)} custom-call(s32[1,512]{1,0:T(1,128)S(1)} %bitcast.26, s32[1,512]{1,0:T(1,128)S(1)} %bitcast.27, f32[1,512]{1,0:T(1,128)S(1)} %bitcast.28, f32[512,256]{1,0:T(8,128)S(1)} %copy-done.7), custom_call_target="tpu_custom_call" | custom-call | tf_op jit(solution)/shard_map/pallas_call | solution.py:566
  9.6 1.6 %collective-permute-done.rest_2_.refs_7_ = f32[64,128]{1,0:T(8,128)S(1)} collective-permute-done((f32[64,128]{1,0:T(8,128)}, f32[64,128]{1,0:T(8,128)S(1)}, u32[]{:S(2)}, u32[]{:S(2)}) %collective-permute-start) | collective-permute-done | bytes 32800 | tf_op jit(solution)/shard_map/ppermute | solution.py:46
  11.2 6.3 %all-to-all-start = ((f32[16,136,128]{2,1,0:T(8,128)}), f32[16,136,128]{2,1,0:T(8,128)S(1)}, u32[]{:S(2)}, u32[]{:S(2)}) async-start(f32[16,136,128]{2,1,0:T(8,128)} %shard_map.82), calls=%async_computation | async-start | bytes 2228224 | tf_op jit(solution)/shard_map/all_to_all | solution.py:570
  17.5 1.5 %collective-permute-start.2 = (f32[64,128]{1,0:T(8,128)}, f32[64,128]{1,0:T(8,128)S(1)}, u32[]{:S(2)}, u32[]{:S(2)}) collective-permute-start(f32[64,128]{1,0:T(8,128)} %get-tuple-element.22), channel_id=1, source_target_pairs={{0,1},{1,0},{2,3},{3,2},{4,5},{5,4},{6,7},{7,6},{8,9},{9,8},{10,11... | collective-permute-start | bytes 98312 | tf_op jit(solution)/shard_map/ppermute | solution.py:46
  19.0 1.5 %collective-permute-start.1 = (f32[256,128]{1,0:T(8,128)}, f32[256,128]{1,0:T(8,128)}, u32[]{:S(2)}, u32[]{:S(2)}) collective-permute-start(f32[256,128]{1,0:T(8,128)} %get-tuple-element.26), channel_id=1, source_target_pairs={{0,8},{8,0},{1,9},{9,1},{2,10},{10,2},{3,11},{11,3},{4,12},{12,4},... | collective-permute-start | bytes 393224 | tf_op jit(solution)/shard_map/ppermute | solution.py:46
  20.5 1.6 %copy-done.3 = f32[1,2,128,16,128]{4,3,2,1,0:T(8,128)S(1)} copy-done((f32[1,2,128,16,128]{4,3,2,1,0:T(8,128)S(1)}, f32[1,2,128,16,128]{4,3,2,1,0:T(8,128)}, u32[]{:S(2)}) %copy-start.3) | copy-done | bytes 2097176
  22.0 1.6 %copy-done.6 = f32[1,2,128,16,128]{4,3,2,1,0:T(8,128)S(1)} copy-done((f32[1,2,128,16,128]{4,3,2,1,0:T(8,128)S(1)}, f32[1,2,128,16,128]{4,3,2,1,0:T(8,128)}, u32[]{:S(2)}) %copy-start.6) | copy-done | bytes 2097176
  23.6 2.2 %shard_map.84 = (f32[16,256,128]{2,1,0:T(8,128)S(1)}, f32[18,256,128]{2,1,0:T(8,128)S(1)}) custom-call(f32[4096,128]{1,0:T(8,128)S(1)} %bitcast.24, f32[4096,128]{1,0:T(8,128)S(1)} %bitcast.25), custom_call_target="tpu_custom_call" | custom-call | tf_op jit(solution)/shard_map/pallas_call | solution.py:572
  25.9 2.7 %collective-permute-done.1.rest_0_.refs_5_ = f32[256,128]{1,0:T(8,128)} collective-permute-done((f32[256,128]{1,0:T(8,128)}, f32[256,128]{1,0:T(8,128)}, u32[]{:S(2)}, u32[]{:S(2)}) %collective-permute-start.1) | collective-permute-done | bytes 131104 | tf_op jit(solution)/shard_map/ppermute | solution.py:46
  31.6 6.2 %shard_map.86 = (f32[16,256,128]{2,1,0:T(8,128)S(1)}, f32[256,128]{1,0:T(8,128)S(1)}, f32[256,128]{1,0:T(8,128)}, f32[64,128]{1,0:T(8,128)S(1)}) custom-call(s32[2]{0:T(128)S(1)} %copy-done.9, f32[2,16,128]{2,1,0:T(8,128)S(1)} %pad_maximum_fusion.refs_1_.shares, f32[32,128]{1,0:T(8,128)S(1)} %collective-permute-done.3.refs_2_, ...), custom_call_target="tpu_custom_call" | custom-call | tf_op jit(solution)/shard_map/pallas_call | solution.py:552
  37.8 2.1 %collective-permute-start.4 = (f32[256,128]{1,0:T(8,128)S(1)}, f32[256,128]{1,0:T(8,128)S(1)}, u32[]{:S(2)}, u32[]{:S(2)}) collective-permute-start(f32[256,128]{1,0:T(8,128)S(1)} %get-tuple-element.29), channel_id=1, source_target_pairs={{0,8},{8,0},{1,9},{9,1},{2,10},{10,2},{3,11},{11,3},{4,12},{12,4},... | collective-permute-start | bytes 393224 | tf_op jit(solution)/shard_map/ppermute | solution.py:46
  39.9 1.2 %collective-permute-start.5 = (f32[64,128]{1,0:T(8,128)S(1)}, f32[64,128]{1,0:T(8,128)S(1)}, u32[]{:S(2)}, u32[]{:S(2)}) collective-permute-start(f32[64,128]{1,0:T(8,128)S(1)} %get-tuple-element.30), channel_id=1, source_target_pairs={{0,1},{1,0},{2,3},{3,2},{4,5},{5,4},{6,7},{7,6},{8,9},{9,8},{10,11... | collective-permute-start | bytes 98312 | tf_op jit(solution)/shard_map/ppermute | solution.py:46
  41.1 1.9 %collective-permute-start.6 = (f32[64,128]{1,0:T(8,128)S(1)}, f32[64,128]{1,0:T(8,128)S(1)}, u32[]{:S(2)}, u32[]{:S(2)}) collective-permute-start(f32[64,128]{1,0:T(8,128)S(1)} %get-tuple-element.30), channel_id=1, source_target_pairs={{1,2},{2,1},{3,4},{4,3},{5,6},{6,5},{9,10},{10,9},{11,12},{12,11},... | collective-permute-start | bytes 98312 | tf_op jit(solution)/shard_map/ppermute | solution.py:46
  43.8 4.0 %collective-permute-done.6.rest_2_.refs_7_ = f32[64,128]{1,0:T(8,128)S(1)} collective-permute-done((f32[64,128]{1,0:T(8,128)S(1)}, f32[64,128]{1,0:T(8,128)S(1)}, u32[]{:S(2)}, u32[]{:S(2)}) %collective-permute-start.6) | collective-permute-done | bytes 32800 | tf_op jit(solution)/shard_map/ppermute | solution.py:46
  49.8 4.3 %shard_map.88.cols = bf16[512,2048]{1,0:T(8,128)(2,1)S(1)} custom-call(s32[2]{0:T(128)S(1)} %copy-done.9, f32[2,16,128]{2,1,0:T(8,128)S(1)} %pad_maximum_fusion.refs_1_.shares, f32[32,128]{1,0:T(8,128)S(1)} %collective-permute-done.7.refs_2_, f32[16,256,128]{2,1,0:T(8,128)S(1)} %get-tuple-element.28.refs_3_, ...), custom_call_target="tpu_custom_call" | custom-call | tf_op jit(solution)/shard_map/pallas_call | solution.py:552
  54.1 1.3 %copy-done.4 = bf16[512,2048]{1,0:T(8,128)(2,1)} copy-done((bf16[512,2048]{1,0:T(8,128)(2,1)}, bf16[512,2048]{1,0:T(8,128)(2,1)S(1)}, u32[]{:S(2)}) %copy-start.4) | copy-done | bytes 2097176
  55.4 1.6 %copy-done.5 = bf16[512,2048]{1,0:T(8,128)(2,1)S(1)} copy-done((bf16[512,2048]{1,0:T(8,128)(2,1)S(1)}, bf16[512,2048]{1,0:T(8,128)(2,1)}, u32[]{:S(2)}) %copy-start.5) | copy-done | bytes 2097176
  57.0 8.1 %shard_map.89 = (f32[16,256,128]{2,1,0:T(8,128)S(1)}, f32[32,128]{1,0:T(8,128)S(1)}) custom-call(f32[16,136,128]{2,1,0:T(8,128)S(1)} %all-to-all-done.records, bf16[512,2048]{1,0:T(8,128)(2,1)S(1)} %copy-done.5), custom_call_target="tpu_custom_call" | custom-call | tf_op jit(solution)/shard_map/pallas_call | solution.py:597
  66.3 3.0 %shard_map.90 = (f32[16,16,128]{2,1,0:T(8,128)S(1)}, f32[256,128]{1,0:T(8,128)S(1)}, f32[256,128]{1,0:T(8,128)}, f32[64,128]{1,0:T(8,128)S(1)}) custom-call(s32[2]{0:T(128)S(1)} %copy-done.10, f32[2,16,128]{2,1,0:T(8,128)S(1)} %pad_maximum_fusion.refs_1_.shares, f32[32,128]{1,0:T(8,128)S(1)} %collective-permute-done.8.other, ...), custom_call_target="tpu_custom_call" | custom-call | tf_op jit(solution)/shard_map/pallas_call | solution.py:552
  69.3 1.5 %collective-permute-start.9 = (f32[256,128]{1,0:T(8,128)S(1)}, f32[256,128]{1,0:T(8,128)S(1)}, u32[]{:S(2)}, u32[]{:S(2)}) collective-permute-start(f32[256,128]{1,0:T(8,128)S(1)} %get-tuple-element.34), channel_id=1, source_target_pairs={{0,8},{8,0},{1,9},{9,1},{2,10},{10,2},{3,11},{11,3},{4,12},{12,4},... | collective-permute-start | bytes 393224 | tf_op jit(solution)/shard_map/ppermute | solution.py:46
  70.8 1.9 %collective-permute-start.11 = (f32[64,128]{1,0:T(8,128)S(1)}, f32[64,128]{1,0:T(8,128)S(1)}, u32[]{:S(2)}, u32[]{:S(2)}) collective-permute-start(f32[64,128]{1,0:T(8,128)S(1)} %get-tuple-element.35), channel_id=1, source_target_pairs={{1,2},{2,1},{3,4},{4,3},{5,6},{6,5},{9,10},{10,9},{11,12},{12,11},... | collective-permute-start | bytes 98312 | tf_op jit(solution)/shard_map/ppermute | solution.py:46
  72.7 2.0 %collective-permute-done.10.rest_1_ = f32[64,128]{1,0:T(8,128)S(1)} collective-permute-done((f32[64,128]{1,0:T(8,128)S(1)}, f32[64,128]{1,0:T(8,128)S(1)}, u32[]{:S(2)}, u32[]{:S(2)}) %collective-permute-start.10) | collective-permute-done | bytes 32800 | tf_op jit(solution)/shard_map/ppermute | solution.py:46
  74.7 2.8 %collective-permute-done.11.rest_2_ = f32[64,128]{1,0:T(8,128)S(1)} collective-permute-done((f32[64,128]{1,0:T(8,128)S(1)}, f32[64,128]{1,0:T(8,128)S(1)}, u32[]{:S(2)}, u32[]{:S(2)}) %collective-permute-start.11) | collective-permute-done | bytes 32800 | tf_op jit(solution)/shard_map/ppermute | solution.py:46
  79.4 5.9 %shard_map.92 = (f32[16,256,128]{2,1,0:T(8,128)S(1)}, f32[256,128]{1,0:T(8,128)S(1)}, f32[256,128]{1,0:T(8,128)}, f32[64,128]{1,0:T(8,128)S(1)}) custom-call(s32[2]{0:T(128)S(1)} %copy-done.10, f32[2,16,128]{2,1,0:T(8,128)S(1)} %pad_maximum_fusion.refs_1_.shares, f32[16,16,128]{2,1,0:T(8,128)S(1)} %get-tuple-element.33.bottom, ...), custom_call_target="tpu_custom_call" | custom-call | tf_op jit(solution)/shard_map/pallas_call | solution.py:552
  85.3 1.4 %collective-permute-start.13 = (f32[256,128]{1,0:T(8,128)S(1)}, f32[256,128]{1,0:T(8,128)S(1)}, u32[]{:S(2)}, u32[]{:S(2)}) collective-permute-start(f32[256,128]{1,0:T(8,128)S(1)} %get-tuple-element.37), channel_id=1, source_target_pairs={{0,8},{8,0},{1,9},{9,1},{2,10},{10,2},{3,11},{11,3},{4,12},{12,4},... | collective-permute-start | bytes 393224 | tf_op jit(solution)/shard_map/ppermute | solution.py:46
  86.6 1.2 %collective-permute-start.14 = (f32[64,128]{1,0:T(8,128)S(1)}, f32[64,128]{1,0:T(8,128)S(1)}, u32[]{:S(2)}, u32[]{:S(2)}) collective-permute-start(f32[64,128]{1,0:T(8,128)S(1)} %get-tuple-element.38), channel_id=1, source_target_pairs={{0,1},{1,0},{2,3},{3,2},{4,5},{5,4},{6,7},{7,6},{8,9},{9,8},{10,11... | collective-permute-start | bytes 98312 | tf_op jit(solution)/shard_map/ppermute | solution.py:46
  87.9 1.9 %collective-permute-start.15 = (f32[64,128]{1,0:T(8,128)S(1)}, f32[64,128]{1,0:T(8,128)S(1)}, u32[]{:S(2)}, u32[]{:S(2)}) collective-permute-start(f32[64,128]{1,0:T(8,128)S(1)} %get-tuple-element.38), channel_id=1, source_target_pairs={{1,2},{2,1},{3,4},{4,3},{5,6},{6,5},{9,10},{10,9},{11,12},{12,11},... | collective-permute-start | bytes 98312 | tf_op jit(solution)/shard_map/ppermute | solution.py:46
  90.6 4.0 %collective-permute-done.15.rest_2_ = f32[64,128]{1,0:T(8,128)S(1)} collective-permute-done((f32[64,128]{1,0:T(8,128)S(1)}, f32[64,128]{1,0:T(8,128)S(1)}, u32[]{:S(2)}, u32[]{:S(2)}) %collective-permute-start.15) | collective-permute-done | bytes 32800 | tf_op jit(solution)/shard_map/ppermute | solution.py:46
  94.7 5.8 %shard_map.93 = f32[4096,128]{1,0:T(8,128)} custom-call(s32[2]{0:T(128)S(1)} %copy-done.10, f32[256,128]{1,0:T(8,128)S(1)} %broadcast_in_dim.8.scale, f32[16,256,128]{2,1,0:T(8,128)S(1)} %get-tuple-element.36.field, f32[18,256,128]{2,1,0:T(8,128)S(1)} %get-tuple-element.25.refs_4_.winds, f32[16,256,128]{2,1,0:T(8,128)S(1)} %copy-done.1, ...), custom_call_target="tpu_custom_call" | custom-call | tf_op jit(solution)/shard_map/pallas_call | solution.py:552
  (50 shorter events, 9.8 us)
Async XLA Ops:
  0.0 7.6 %copy-start.11 = (s32[512,1]{0,1:T(1,128)S(1)}, s32[512,1]{0,1:T(1,128)}, u32[]{:S(2)}) copy-start(s32[512,1]{0,1:T(1,128)} %param.12) | copy-start | bytes 6148
  0.0 7.6 %copy-start.12 = (s32[512]{0:T(512)S(1)}, s32[512]{0:T(512)}, u32[]{:S(2)}) copy-start(s32[512]{0:T(512)} %param.13) | copy-start | bytes 6148
  0.0 7.6 %copy-start.13 = (f32[512]{0:T(512)S(1)}, f32[512]{0:T(512)}, u32[]{:S(2)}) copy-start(f32[512]{0:T(512)} %param.15) | copy-start | bytes 6148
  0.1 28.5 %copy-start.8 = (s32[2]{0:T(128)}, s32[2]{0:T(128)S(1)}, u32[]{:S(2)}) copy-start(s32[2]{0:T(128)S(1)} %pad_add_fusion.scal.refs_0_) | copy-start | bytes 28
  0.1 1.6 %copy-start.2 = (f32[1,2,128,16,128]{4,3,2,1,0:T(8,128)S(1)}, f32[1,2,128,16,128]{4,3,2,1,0:T(8,128)}, u32[]{:S(2)}) copy-start(f32[1,2,128,16,128]{4,3,2,1,0:T(8,128)} %param.8) | copy-start | bytes 6291460
  1.7 5.9 %copy-start.7 = (f32[512,256]{1,0:T(8,128)S(1)}, f32[512,256]{1,0:T(8,128)}, u32[]{:S(2)}) copy-start(f32[512,256]{1,0:T(8,128)} %op.1) | copy-start | bytes 1572868
  4.2 16.3 %copy-start.14 = (f32[16,128]{1,0:T(8,128)S(1)}, f32[16,128]{1,0:T(8,128)}, u32[]{:S(2)}) copy-start(f32[16,128]{1,0:T(8,128)} %param.10) | copy-start | bytes 24580
  4.2 7.0 %collective-permute-start = (f32[64,128]{1,0:T(8,128)}, f32[64,128]{1,0:T(8,128)S(1)}, u32[]{:S(2)}, u32[]{:S(2)}) collective-permute-start(f32[64,128]{1,0:T(8,128)} %get-tuple-element.22), channel_id=1, source_target_pairs={{1,2},{2,1},{3,4},{4,3},{5,6},{6,5},{9,10},{10,9},{11,12},{12,11},... | collective-permute-start | bytes 98312 | tf_op jit(solution)/shard_map/ppermute | solution.py:46
  11.2 44.2 %all-to-all-start = ((f32[16,136,128]{2,1,0:T(8,128)}), f32[16,136,128]{2,1,0:T(8,128)S(1)}, u32[]{:S(2)}, u32[]{:S(2)}) async-start(f32[16,136,128]{2,1,0:T(8,128)} %shard_map.82), calls=%async_computation | async-start | bytes 2228224 | tf_op jit(solution)/shard_map/all_to_all | solution.py:570
  17.5 8.4 %collective-permute-start.2 = (f32[64,128]{1,0:T(8,128)}, f32[64,128]{1,0:T(8,128)S(1)}, u32[]{:S(2)}, u32[]{:S(2)}) collective-permute-start(f32[64,128]{1,0:T(8,128)} %get-tuple-element.22), channel_id=1, source_target_pairs={{0,1},{1,0},{2,3},{3,2},{4,5},{5,4},{6,7},{7,6},{8,9},{9,8},{10,11... | collective-permute-start | bytes 98312 | tf_op jit(solution)/shard_map/ppermute | solution.py:46
  19.0 9.6 %collective-permute-start.1 = (f32[256,128]{1,0:T(8,128)}, f32[256,128]{1,0:T(8,128)}, u32[]{:S(2)}, u32[]{:S(2)}) collective-permute-start(f32[256,128]{1,0:T(8,128)} %get-tuple-element.26), channel_id=1, source_target_pairs={{0,8},{8,0},{1,9},{9,1},{2,10},{10,2},{3,11},{11,3},{4,12},{12,4},... | collective-permute-start | bytes 393224 | tf_op jit(solution)/shard_map/ppermute | solution.py:46
  20.5 1.6 %copy-start.3 = (f32[1,2,128,16,128]{4,3,2,1,0:T(8,128)S(1)}, f32[1,2,128,16,128]{4,3,2,1,0:T(8,128)}, u32[]{:S(2)}) copy-start(f32[1,2,128,16,128]{4,3,2,1,0:T(8,128)} %param.8) | copy-start | bytes 6291460
  22.0 1.6 %copy-start.6 = (f32[1,2,128,16,128]{4,3,2,1,0:T(8,128)S(1)}, f32[1,2,128,16,128]{4,3,2,1,0:T(8,128)}, u32[]{:S(2)}) copy-start(f32[1,2,128,16,128]{4,3,2,1,0:T(8,128)} %param.9) | copy-start | bytes 6291460
  25.9 5.0 %copy-start = (f32[16,256,128]{2,1,0:T(8,128)}, f32[16,256,128]{2,1,0:T(8,128)S(1)}, u32[]{:S(2)}) copy-start(f32[16,256,128]{2,1,0:T(8,128)S(1)} %get-tuple-element.24.refs_3_.state) | copy-start | bytes 6291460
  29.7 1.2 %collective-permute-start.3 = (f32[32,128]{1,0:T(8,128)S(1)}, f32[32,128]{1,0:T(8,128)S(1)}, u32[]{:S(2)}, u32[]{:S(2)}) collective-permute-start(f32[32,128]{1,0:T(8,128)S(1)} %shard_map.85), channel_id=1, source_target_pairs={{0,16},{16,0},{1,17},{17,1},{2,18},{18,2},{3,19},{19,3},{4,20},{20... | collective-permute-start | bytes 49160 | tf_op jit(solution)/shard_map/ppermute | solution.py:560
  37.8 10.0 %collective-permute-start.4 = (f32[256,128]{1,0:T(8,128)S(1)}, f32[256,128]{1,0:T(8,128)S(1)}, u32[]{:S(2)}, u32[]{:S(2)}) collective-permute-start(f32[256,128]{1,0:T(8,128)S(1)} %get-tuple-element.29), channel_id=1, source_target_pairs={{0,8},{8,0},{1,9},{9,1},{2,10},{10,2},{3,11},{11,3},{4,12},{12,4},... | collective-permute-start | bytes 393224 | tf_op jit(solution)/shard_map/ppermute | solution.py:46
  39.9 3.9 %collective-permute-start.5 = (f32[64,128]{1,0:T(8,128)S(1)}, f32[64,128]{1,0:T(8,128)S(1)}, u32[]{:S(2)}, u32[]{:S(2)}) collective-permute-start(f32[64,128]{1,0:T(8,128)S(1)} %get-tuple-element.30), channel_id=1, source_target_pairs={{0,1},{1,0},{2,3},{3,2},{4,5},{5,4},{6,7},{7,6},{8,9},{9,8},{10,11... | collective-permute-start | bytes 98312 | tf_op jit(solution)/shard_map/ppermute | solution.py:46
  41.1 6.7 %collective-permute-start.6 = (f32[64,128]{1,0:T(8,128)S(1)}, f32[64,128]{1,0:T(8,128)S(1)}, u32[]{:S(2)}, u32[]{:S(2)}) collective-permute-start(f32[64,128]{1,0:T(8,128)S(1)} %get-tuple-element.30), channel_id=1, source_target_pairs={{1,2},{2,1},{3,4},{4,3},{5,6},{6,5},{9,10},{10,9},{11,12},{12,11},... | collective-permute-start | bytes 98312 | tf_op jit(solution)/shard_map/ppermute | solution.py:46
  48.5 1.2 %collective-permute-start.7 = (f32[32,128]{1,0:T(8,128)S(1)}, f32[32,128]{1,0:T(8,128)S(1)}, u32[]{:S(2)}, u32[]{:S(2)}) collective-permute-start(f32[32,128]{1,0:T(8,128)S(1)} %shard_map.87), channel_id=1, source_target_pairs={{0,16},{16,0},{1,17},{17,1},{2,18},{18,2},{3,19},{19,3},{4,20},{20... | collective-permute-start | bytes 49160 | tf_op jit(solution)/shard_map/ppermute | solution.py:560
  54.1 1.3 %copy-start.4 = (bf16[512,2048]{1,0:T(8,128)(2,1)}, bf16[512,2048]{1,0:T(8,128)(2,1)S(1)}, u32[]{:S(2)}) copy-start(bf16[512,2048]{1,0:T(8,128)(2,1)S(1)} %shard_map.88.cols) | copy-start | bytes 6291460
  55.4 1.6 %copy-start.5 = (bf16[512,2048]{1,0:T(8,128)(2,1)S(1)}, bf16[512,2048]{1,0:T(8,128)(2,1)}, u32[]{:S(2)}) copy-start(bf16[512,2048]{1,0:T(8,128)(2,1)} %copy-done.4) | copy-start | bytes 6291460
  57.0 9.3 %copy-start.10 = (s32[2]{0:T(128)S(1)}, s32[2]{0:T(128)}, u32[]{:S(2)}) copy-start(s32[2]{0:T(128)} %copy-done.8) | copy-start | bytes 28
  65.1 1.2 %collective-permute-start.8 = (f32[32,128]{1,0:T(8,128)S(1)}, f32[32,128]{1,0:T(8,128)S(1)}, u32[]{:S(2)}, u32[]{:S(2)}) collective-permute-start(f32[32,128]{1,0:T(8,128)S(1)} %get-tuple-element.31), channel_id=1, source_target_pairs={{0,16},{16,0},{1,17},{17,1},{2,18},{18,2},{3,19},{19,3},{4,20},{20... | collective-permute-start | bytes 49160 | tf_op jit(solution)/shard_map/ppermute | solution.py:560
  69.3 8.2 %collective-permute-start.9 = (f32[256,128]{1,0:T(8,128)S(1)}, f32[256,128]{1,0:T(8,128)S(1)}, u32[]{:S(2)}, u32[]{:S(2)}) collective-permute-start(f32[256,128]{1,0:T(8,128)S(1)} %get-tuple-element.34), channel_id=1, source_target_pairs={{0,8},{8,0},{1,9},{9,1},{2,10},{10,2},{3,11},{11,3},{4,12},{12,4},... | collective-permute-start | bytes 393224 | tf_op jit(solution)/shard_map/ppermute | solution.py:46
  70.8 3.9 %collective-permute-start.10 = (f32[64,128]{1,0:T(8,128)S(1)}, f32[64,128]{1,0:T(8,128)S(1)}, u32[]{:S(2)}, u32[]{:S(2)}) collective-permute-start(f32[64,128]{1,0:T(8,128)S(1)} %get-tuple-element.35), channel_id=1, source_target_pairs={{0,1},{1,0},{2,3},{3,2},{4,5},{5,4},{6,7},{7,6},{8,9},{9,8},{10,11... | collective-permute-start | bytes 98312 | tf_op jit(solution)/shard_map/ppermute | solution.py:46
  70.8 6.7 %collective-permute-start.11 = (f32[64,128]{1,0:T(8,128)S(1)}, f32[64,128]{1,0:T(8,128)S(1)}, u32[]{:S(2)}, u32[]{:S(2)}) collective-permute-start(f32[64,128]{1,0:T(8,128)S(1)} %get-tuple-element.35), channel_id=1, source_target_pairs={{1,2},{2,1},{3,4},{4,3},{5,6},{6,5},{9,10},{10,9},{11,12},{12,11},... | collective-permute-start | bytes 98312 | tf_op jit(solution)/shard_map/ppermute | solution.py:46
  78.2 1.2 %collective-permute-start.12 = (f32[32,128]{1,0:T(8,128)S(1)}, f32[32,128]{1,0:T(8,128)S(1)}, u32[]{:S(2)}, u32[]{:S(2)}) collective-permute-start(f32[32,128]{1,0:T(8,128)S(1)} %shard_map.91), channel_id=1, source_target_pairs={{0,16},{16,0},{1,17},{17,1},{2,18},{18,2},{3,19},{19,3},{4,20},{20... | collective-permute-start | bytes 49160 | tf_op jit(solution)/shard_map/ppermute | solution.py:560
  79.4 15.2 %copy-start.15 = (f32[1,2,128]{2,1,0:T(2,128)S(1)}, f32[1,2,128]{2,1,0:T(2,128)}, u32[]{:S(2)}) copy-start(f32[1,2,128]{2,1,0:T(2,128)} %param.11) | copy-start | bytes 3076
  79.4 15.3 %copy-start.1 = (f32[16,256,128]{2,1,0:T(8,128)S(1)}, f32[16,256,128]{2,1,0:T(8,128)}, u32[]{:S(2)}) copy-start(f32[16,256,128]{2,1,0:T(8,128)} %copy-done) | copy-start | bytes 6291460
  85.3 9.3 %collective-permute-start.13 = (f32[256,128]{1,0:T(8,128)S(1)}, f32[256,128]{1,0:T(8,128)S(1)}, u32[]{:S(2)}, u32[]{:S(2)}) collective-permute-start(f32[256,128]{1,0:T(8,128)S(1)} %get-tuple-element.37), channel_id=1, source_target_pairs={{0,8},{8,0},{1,9},{9,1},{2,10},{10,2},{3,11},{11,3},{4,12},{12,4},... | collective-permute-start | bytes 393224 | tf_op jit(solution)/shard_map/ppermute | solution.py:46
  86.6 3.9 %collective-permute-start.14 = (f32[64,128]{1,0:T(8,128)S(1)}, f32[64,128]{1,0:T(8,128)S(1)}, u32[]{:S(2)}, u32[]{:S(2)}) collective-permute-start(f32[64,128]{1,0:T(8,128)S(1)} %get-tuple-element.38), channel_id=1, source_target_pairs={{0,1},{1,0},{2,3},{3,2},{4,5},{5,4},{6,7},{7,6},{8,9},{9,8},{10,11... | collective-permute-start | bytes 98312 | tf_op jit(solution)/shard_map/ppermute | solution.py:46
  87.9 6.7 %collective-permute-start.15 = (f32[64,128]{1,0:T(8,128)S(1)}, f32[64,128]{1,0:T(8,128)S(1)}, u32[]{:S(2)}, u32[]{:S(2)}) collective-permute-start(f32[64,128]{1,0:T(8,128)S(1)} %get-tuple-element.38), channel_id=1, source_target_pairs={{1,2},{2,1},{3,4},{4,3},{5,6},{6,5},{9,10},{10,9},{11,12},{12,11},... | collective-permute-start | bytes 98312 | tf_op jit(solution)/shard_map/ppermute | solution.py:46
  (1 other events, 0.7 us)

commit v3 on v2

v3 whole, which is shorter than its diff:
```python
import functools

import jax
import jax.numpy as jnp
from jax import lax
from jax.experimental import pallas as pl
from jax.experimental.pallas import tpu as pltpu
from jax.sharding import PartitionSpec as P

HORIZ_MIX = 0.1
VERT_MIX = 0.15
LANES = 128
GROUP = 8
MIB = 1024 * 1024
SWEEP_VMEM = 18 * MIB
OBSERVE_VMEM = 20 * MIB


def call(body, out_shape, scratch=(), limit=SWEEP_VMEM, **kw):
    return pl.pallas_call(
        body,
        out_shape=out_shape,
        scratch_shapes=list(scratch),
        compiler_params=pltpu.CompilerParams(vmem_limit_bytes=limit),
        **kw,
    )


def f32(*shape):
    return jax.ShapeDtypeStruct(shape, jnp.float32)


def lane_iota(rows=GROUP):
    return lax.broadcasted_iota(jnp.int32, (rows, LANES), 1)


def sub_iota(rows=GROUP):
    return lax.broadcasted_iota(jnp.int32, (rows, LANES), 0)


def pair_swap(block, axis, start):
    count = lax.axis_size(axis)
    route = []
    for low in range(start, count - 1, 2):
        route += [(low, low + 1), (low + 1, low)]
    return lax.ppermute(block, axis, route)


def exchange(strips, packed):
    y_even = pair_swap(packed, "gy", 0)
    y_odd = pair_swap(packed, "gy", 1)
    halos = [pair_swap(strips[0], "gx", 0), y_even, y_odd]
    if lax.axis_size("gx") > 2:
        halos.append(pair_swap(strips[1], "gx", 1))
    return halos


def is_odd(axis):
    return lax.rem(lax.axis_index(axis), 2) == 1


def read_sides(refs):
    even = refs[0]
    odd = refs[3] if len(refs) > 3 else None
    at_odd = is_odd("gx")

    def side(at, turned):
        other = jnp.zeros_like(even[at]) if odd is None else odd[at]
        return jnp.where(turned, other, even[at])

    return lambda at: side(at, jnp.logical_not(at_odd)), lambda at: side(at, at_odd)


PARTS = 4


def merged(y_even, y_odd, at):
    a, b = y_even[at, :], y_odd[at, :]
    lane = lax.broadcasted_iota(jnp.int32, a.shape, 1)
    return jnp.where((lane % 2 == 1) == jnp.logical_not(is_odd("gy")), a, b)


def merge_columns(y_even, y_odd, sides):
    sides[...] = merged(y_even, y_odd, slice(None))


def slot_of(i, part, rows):
    return PARTS * (rows - 1 - i) + part


def side_columns(sides, i, group):
    m, part = group // PARTS, group % PARTS
    rows = LANES // (2 * PARTS)
    return pltpu.roll(sides[m * GROUP : (m + 1) * GROUP, :], LANES - 1 - 2 * slot_of(i, part, rows), 1)


def pack_into(total, value, slot):
    return jnp.where(lane_iota() // 2 == slot, pltpu.roll(value, 2 * slot + 1, 1), total)


def pack_block(packed, values, i, m):
    at = pl.ds(m * GROUP, GROUP)
    total = packed[at, :]
    for part, value in enumerate(values):
        total = pack_into(total, value, slot_of(i, part, LANES // (2 * PARTS)))
    packed[at, :] = total


CENTRE = 1.0 - 4.0 * HORIZ_MIX - 2.0 * VERT_MIX


def levels_around(cells, i, base, group, groups):
    here = cells[i + 1, pl.ds(base + group * GROUP, GROUP), :]
    if group == groups - 1:
        upper = jnp.where(sub_iota() == GROUP - 1, here, pltpu.roll(here, GROUP - 1, 0))
    else:
        upper = cells[i + 1, pl.ds(base + group * GROUP + 1, GROUP), :]
    if group == 0:
        lower = jnp.where(sub_iota() == 0, here, pltpu.roll(here, 1, 0))
    else:
        lower = cells[i + 1, pl.ds(base + group * GROUP - 1, GROUP), :]
    return here, upper, lower


def shifted(first, last, edge, rows=GROUP):
    lane = lane_iota(rows)
    right = pltpu.roll(jnp.where(lane == 0, edge, first), LANES - 1, 1)
    left = pltpu.roll(jnp.where(lane == LANES - 1, edge, last), 1, 1)
    return right, left


def forward_sum(here, vertical, after, before, right, left, u, w):
    return (
        CENTRE * here
        + VERT_MIX * vertical
        + HORIZ_MIX * ((after + before) + (right + left))
        - 0.5 * (u * (after - before) + w * (right - left))
    )


def forward_point(cells, winds, sides, i, f, group, levels):
    groups = levels // GROUP
    here, upper, lower = levels_around(cells, i, f * levels, group, groups)
    at = pl.ds(f * levels + group * GROUP, GROUP)
    right, left = shifted(here, here, side_columns(sides, i, f * groups + group))
    u = winds[i, pl.ds(group * GROUP, GROUP), :]
    w = winds[i, pl.ds(levels + group * GROUP, GROUP), :]
    return forward_sum(here, upper + lower, cells[i + 2, at, :], cells[i, at, :], right, left, u, w)


def products(x, wind):
    slope = 0.5 * (wind * x)
    return HORIZ_MIX * x - slope, HORIZ_MIX * x + slope


def adjoint_point(cells, winds, sides, i, f, group, levels):
    groups = levels // GROUP
    here, upper, lower = levels_around(cells, i, f * levels, group, groups)
    at = pl.ds(f * levels + group * GROUP, GROUP)
    wind_at = pl.ds(group * GROUP, GROUP)
    after, before = cells[i + 2, at, :], cells[i, at, :]
    u_after, u_before = winds[i + 2, wind_at, :], winds[i, wind_at, :]
    w = winds[i + 1, pl.ds(levels + group * GROUP, GROUP), :]
    down, up = products(here, w)
    right, left = shifted(up, down, side_columns(sides, i, f * groups + group))
    return (
        CENTRE * here
        + VERT_MIX * (upper + lower)
        + HORIZ_MIX * (after + before)
        + 0.5 * (u_after * after - u_before * before)
        + (right + left)
    )


def shares_of(coupling):
    own = jnp.where(lax.axis_index("comp") == 0, 1.0, 0.5)
    return own * coupling, (1.5 - own) * coupling


def couple_forward(value, other, coupling):
    own, _ = shares_of(coupling)
    return value - own * (value - other)


def couple_adjoint(value, other, coupling):
    own, peer = shares_of(coupling)
    return value - own * value + peer * other


def coupled(rule, value, other, coupling, i, f, rows):
    mixed = rule(value, other[pl.ds(f * rows + i, 1), :], coupling[pl.ds(i, 1), :])
    return jnp.where(sub_iota() == 0, mixed, value)


def put_strip(strip_even, strip_odd, at, first, last):
    at_odd = is_odd("gx")
    strip_even[at, :] = jnp.where(at_odd, first, last)
    strip_odd[at, :] = jnp.where(at_odd, last, first)


def put_low(low, value, i, f, rows):
    for level in range(2):
        low[level][pl.ds(f * rows + i, 1), :] = value[level : level + 1]


class Rows:
    def __init__(self, source, target, sems, rows, as_it_comes, offset):
        self.source, self.target, self.sems = source, target, sems
        self.rows, self.as_it_comes, self.offset = rows, as_it_comes, offset

    def copy(self, i):
        row = self.source.at[:, i] if self.as_it_comes else self.source.at[i]
        return pltpu.make_async_copy(row, self.target.at[i + self.offset], self.sems.at[i])

    def wait(self, i):
        self.copy(i).wait()


def start_rows(rows, *groups):
    for i in range(rows):
        for group in groups:
            group.copy(i).start()


def edges_kernel(rows, levels, state, s_even, s_odd, packed, low0, low1, cells, sems):
    incoming = Rows(state, cells, sems, rows, True, 0)
    start_rows(rows, incoming)
    packed[...] = jnp.zeros_like(packed)
    groups = levels // GROUP

    def row(i, _):
        incoming.wait(i)
        for m in range(2 * groups // PARTS):
            values = [cells[i, pl.ds((m * PARTS + part) * GROUP, GROUP), :] for part in range(PARTS)]
            if m * PARTS % groups == 0:
                put_low((low0, low1), values[0], i, m * PARTS // groups, rows)
            pack_block(packed, values, i, m)
        return 0

    lax.fori_loop(0, rows, row, 0)
    put_strip(s_even, s_odd, slice(None), cells[0], cells[rows - 1])


def floor_edge(halos, f, rows, levels):
    m = f * (levels // GROUP) // PARTS
    sides = jnp.broadcast_to(merged(halos[1], halos[2], pl.ds(m * GROUP, 1)), (rows, LANES))
    return pltpu.roll(sides, 2 * PARTS - 1, 1, stride=2 * PARTS, stride_axis=0)


def row_after(value, last, rows):
    return jnp.where(sub_iota(rows) == rows - 1, last, pltpu.roll(value, rows - 1, 0))


def row_before(value, first, rows):
    return jnp.where(sub_iota(rows) == 0, first, pltpu.roll(value, 1, 0))


def forward_floor_kernel(rows, levels, low0, low1, winds, *rest):
    *halos, floor = rest
    side_before, side_after = read_sides(halos)
    for f in range(2):
        here = pl.ds(f * rows, rows)
        at = pl.ds(f * levels, 1)
        low, up = low0[here, :], low1[here, :]
        after, before = row_after(low, side_after(at), rows), row_before(low, side_before(at), rows)
        right, left = shifted(low, low, floor_edge(halos, f, rows, levels), rows)
        floor[here, :] = forward_sum(low, up + low, after, before, right, left, winds[0], winds[1])


def adjoint_floor_kernel(rows, levels, coupling, other, low0, low1, winds, *rest):
    *halos, floor = rest
    side_before, side_after = read_sides(halos)
    for f in range(2):
        here = pl.ds(f * rows, rows)
        at = pl.ds(f * levels, 1)
        low, up = couple_adjoint(low0[here, :], other[here, :], coupling[...]), low1[here, :]
        x_down, x_up = products(low, winds[0])
        after, before = row_after(x_up, side_after(at), rows), row_before(x_down, side_before(at), rows)
        y_down, y_up = products(low, winds[1])
        right, left = shifted(y_up, y_down, floor_edge(halos, f, rows, levels), rows)
        floor[here, :] = CENTRE * low + VERT_MIX * (up + low) + (after + before) + (right + left)


def forward_kernel(first, last, rows, levels, coupling, other, field, winds, *rest):
    if last:
        *halos, cols, cells, wind_cells, sides, sems, col_cells, col_sems = rest
    else:
        *halos, out, s_even, s_odd, packed, low0, low1, cells, wind_cells, sides, sems = rest
    incoming = Rows(field, cells, sems.at[0], rows, first, 1)
    wind_in = Rows(winds, wind_cells, sems.at[1], rows, True, 0)
    start_rows(rows, incoming, wind_in)
    if not last:
        packed[...] = jnp.zeros_like(packed)
    merge_columns(halos[1], halos[2], sides)
    before, after = read_sides(halos)
    cells[0] = before(slice(None))
    cells[rows + 1] = after(slice(None))
    groups = levels // GROUP
    width = 2 * levels
    incoming.wait(0)

    def col_copy(i):
        lanes = pl.ds(pl.multiple_of(i * LANES, LANES), LANES)
        return pltpu.make_async_copy(col_cells.at[:, lanes], cols.at[:, lanes], col_sems.at[i])

    def row(i, _):
        @pl.when(i < rows - 1)
        def _():
            incoming.wait(i + 1)

        wind_in.wait(i)
        for m in range(2 * groups // PARTS):
            f, start = m * PARTS // groups, m * PARTS % groups
            values = []
            for group in range(start, start + PARTS):
                value = forward_point(cells, wind_cells, sides, i, f, group, levels)
                if group == 0:
                    value = coupled(couple_forward, value, other, coupling, i, f, rows)
                    if not last:
                        put_low((low0, low1), value, i, f, rows)
                values.append(value)
            base = m * PARTS * GROUP
            if last:
                lanes = pl.ds(pl.multiple_of(i * LANES, LANES), LANES)
                high, low = split(jnp.concatenate(values, axis=0), 2)
                col_cells[pl.ds(base, PARTS * GROUP), lanes] = high
                col_cells[pl.ds(width + base, PARTS * GROUP), lanes] = low
            else:
                for part, value in enumerate(values):
                    out[i, pl.ds(base + part * GROUP, GROUP), :] = value
                pack_block(packed, values, i, m)
        if last:
            col_copy(i).start()
        return 0

    lax.fori_loop(0, rows, row, 0)
    if last:
        for i in range(rows):
            col_copy(i).wait()
    else:
        put_strip(s_even, s_odd, slice(None), out[0], out[rows - 1])


def with_products(value, w):
    down, up = products(value, w)
    return jnp.where(lane_iota() == 0, up, down)


def adjoint_pack_kernel(rows, levels, coupling, other, field, winds, bottom, s_even, s_odd, packed, w_cells, u_cells, sems):
    def w_copy(i):
        return pltpu.make_async_copy(winds.at[pl.ds(levels, levels), i], w_cells.at[i], sems.at[i])

    u_copies = [
        pltpu.make_async_copy(winds.at[pl.ds(0, levels), i], u_cells.at[k], sems.at[rows + k])
        for k, i in enumerate((0, rows - 1))
    ]
    for i in range(rows):
        w_copy(i).start()
    for copy in u_copies:
        copy.start()
    packed[...] = jnp.zeros_like(packed)
    groups = levels // GROUP

    def row(i, _):
        w_copy(i).wait()
        for m in range(2 * groups // PARTS):
            f, start = m * PARTS // groups, m * PARTS % groups
            values = []
            for group in range(start, start + PARTS):
                value = field[i, pl.ds(f * levels + group * GROUP, GROUP), :]
                if group == 0:
                    value = coupled(couple_adjoint, value, other, coupling, i, f, rows)
                    bottom[i, pl.ds(f * GROUP, GROUP), :] = value
                values.append(with_products(value, w_cells[i, pl.ds(group * GROUP, GROUP), :]))
            pack_block(packed, values, i, m)
        return 0

    lax.fori_loop(0, rows, row, 0)
    for copy in u_copies:
        copy.wait()
    for f in range(2):
        ends = []
        for i in (0, rows - 1):
            low = bottom[i, pl.ds(f * GROUP, GROUP), :]
            ends.append(jnp.concatenate([low, field[i, pl.ds(f * levels + GROUP, levels - GROUP), :]], axis=0))
        put_strip(
            s_even, s_odd, pl.ds(f * levels, levels), products(ends[0], u_cells[0])[1], products(ends[1], u_cells[1])[0]
        )


def adjoint_kernel(rows, levels, coupling, bottom, other_next, field, winds, *rest):
    *halos, out, s_even, s_odd, packed, cells, wind_cells, sides, sems = rest
    incoming = Rows(field, cells, sems.at[0], rows, False, 1)
    wind_in = Rows(winds, wind_cells, sems.at[1], rows, True, 1)
    start_rows(rows, incoming, wind_in)
    packed[...] = jnp.zeros_like(packed)
    groups = levels // GROUP
    adjoint_outside(halos, cells, wind_cells, sides, rows)

    def take(i):
        incoming.wait(i)
        wind_in.wait(i)
        for f in range(2):
            cells[i + 1, pl.ds(f * levels, GROUP), :] = bottom[i, pl.ds(f * GROUP, GROUP), :]

    take(0)

    def row(i, _):
        @pl.when(i < rows - 1)
        def _():
            take(i + 1)

        for m in range(2 * groups // PARTS):
            f, start = m * PARTS // groups, m * PARTS % groups
            values = []
            for group in range(start, start + PARTS):
                value = adjoint_point(cells, wind_cells, sides, i, f, group, levels)
                if group == 0:
                    value = coupled(couple_adjoint, value, other_next, coupling, i, f, rows)
                out[i, pl.ds(f * levels + group * GROUP, GROUP), :] = value
                values.append(with_products(value, wind_cells[i + 1, pl.ds(levels + group * GROUP, GROUP), :]))
            pack_block(packed, values, i, m)
        return 0

    lax.fori_loop(0, rows, row, 0)
    for f in range(2):
        at = pl.ds(f * levels, levels)
        first = products(out[0, at, :], wind_cells[1, pl.ds(0, levels), :])[1]
        last = products(out[rows - 1, at, :], wind_cells[rows, pl.ds(0, levels), :])[0]
        put_strip(s_even, s_odd, at, first, last)


def adjoint_outside(halos, cells, wind_cells, sides, rows):
    merge_columns(halos[1], halos[2], sides)
    before, after = read_sides(halos)
    cells[0] = before(slice(None)) / HORIZ_MIX
    cells[rows + 1] = after(slice(None)) / HORIZ_MIX
    wind_cells[0] = jnp.zeros_like(wind_cells[0])
    wind_cells[rows + 1] = jnp.zeros_like(wind_cells[0])


def final_kernel(rows, levels, scale, field, winds, state, *rest):
    *halos, out, cells, wind_cells, state_cells, out_cells, sides, sems = rest
    incoming = Rows(field, cells, sems.at[0], rows, False, 1)
    wind_in = Rows(winds, wind_cells, sems.at[1], rows, True, 1)
    state_in = Rows(state, state_cells, sems.at[2], rows, True, 0)
    start_rows(rows, incoming, wind_in, state_in)
    groups = levels // GROUP
    adjoint_outside(halos, cells, wind_cells, sides, rows)
    incoming.wait(0)
    wind_in.wait(0)

    def out_copy(i):
        return pltpu.make_async_copy(out_cells.at[i], out.at[:, i], sems.at[3, i])

    def row(i, _):
        @pl.when(i < rows - 1)
        def _():
            incoming.wait(i + 1)
            wind_in.wait(i + 1)

        state_in.wait(i)
        for group in range(groups):
            for f in range(2):
                at = pl.ds(f * levels + group * GROUP, GROUP)
                value = adjoint_point(cells, wind_cells, sides, i, f, group, levels)
                out_cells[i, at, :] = value + scale[at, :] * state_cells[i, at, :]
        out_copy(i).start()
        return 0

    lax.fori_loop(0, rows, row, 0)
    for i in range(rows):
        out_copy(i).wait()


def split(value, terms):
    parts = []
    for _ in range(terms):
        part = value.astype(jnp.bfloat16)
        parts.append(part)
        value = value - part.astype(jnp.float32)
    return parts


def dot(a, b, contract):
    return lax.dot_general(a, b, ((contract[:1], contract[1:]), ((), ())), preferred_element_type=jnp.float32)


def route_kernel(tiles, cap, dest, col, prec, op, out):
    count = op.shape[0]
    width = op.shape[1]
    halves = width // LANES
    owner = lax.broadcasted_iota(jnp.int32, (tiles, count), 0)
    hits = owner == dest[...]
    ones = jnp.where(hits, 1.0, 0.0)
    earlier = lax.broadcasted_iota(jnp.int32, (count, count), 0) <= lax.broadcasted_iota(jnp.int32, (count, count), 1)
    running = dot(ones.astype(jnp.bfloat16), jnp.where(earlier, 1.0, 0.0).astype(jnp.bfloat16), (1, 0))
    slot = jnp.sum(running * ones, axis=0, keepdims=True) - 1.0
    slot = slot.astype(jnp.int32)
    place = dest[...] * cap + slot
    at_slot = lax.broadcasted_iota(jnp.int32, (LANES, count), 0) == slot
    at_slot = jnp.where(at_slot, 1.0, 0.0).astype(jnp.bfloat16)
    column = col[...].astype(jnp.float32)
    pieces = [ones * part.astype(jnp.float32) for part in split(column, 2) + split(prec[...], 3)]
    aux = dot(jnp.concatenate(pieces, axis=0).astype(jnp.bfloat16), at_slot, (1, 1))
    columns = aux[0:tiles] + aux[tiles : 2 * tiles]
    precs = (aux[2 * tiles : 3 * tiles] + aux[3 * tiles : 4 * tiles]) + aux[4 * tiles : 5 * tiles]
    sub = sub_iota()
    for owner_at in range(tiles):
        block = jnp.where(sub == 0, columns[owner_at : owner_at + 1], 0.0)
        block = jnp.where(sub == 1, precs[owner_at : owner_at + 1], block)
        out[owner_at, pl.ds(halves * cap, GROUP), :] = block
    rows_high, rows_low = split(op[...], 2)
    chunk = 256
    for first in range(0, tiles * cap, chunk):
        picks = lax.broadcasted_iota(jnp.int32, (chunk, count), 0) + first == place
        picks = jnp.where(picks, 1.0, 0.0).astype(jnp.bfloat16)
        moved = dot(picks, rows_high, (1, 0)) + dot(picks, rows_low, (1, 0))
        for part in range(chunk // cap):
            for half in range(halves):
                out[first // cap + part, pl.ds(half * cap, cap), :] = moved[
                    part * cap : (part + 1) * cap, half * LANES : (half + 1) * LANES
                ]


def observe_kernel(rows, width, tiles, cap, records, cols, adjoint, low0, low1, col_cells, sel, precs, both, spread, sems):
    part_rows = 2 * width // sems.shape[0]
    copies = []
    for part in range(sems.shape[0]):
        at = pl.ds(part * part_rows, part_rows)
        copies.append(pltpu.make_async_copy(cols.at[at], col_cells.at[at], sems.at[part]))
        copies[-1].start()
    halves = width // LANES
    count = tiles * cap
    aux = halves * cap
    own = lax.broadcasted_iota(jnp.int32, (cap, LANES), 1) == lax.broadcasted_iota(jnp.int32, (cap, LANES), 0)
    ones = jnp.ones((LANES, LANES), jnp.bfloat16)
    step = 256
    lane = lax.broadcasted_iota(jnp.int32, (step, LANES), 1).astype(jnp.float32)

    def select(block, _):
        sources = step // cap

        def spread_out(part):
            rows_of = [
                jnp.where(own, records[block * sources + s, pl.ds(aux + part, 1), :], 0.0) for s in range(sources)
            ]
            terms = split(jnp.concatenate(rows_of, axis=0), 2 + part)
            return sum(dot(term, ones, (1, 0)) for term in terms)

        at = pl.ds(pl.multiple_of(block * step, step), step)
        column = spread_out(0) - lane
        precs[at, :] = spread_out(1)
        for i in range(rows):
            sel[at, i * LANES : (i + 1) * LANES] = jnp.where(column == float(i * LANES), 1.0, 0.0).astype(jnp.bfloat16)
        return 0

    lax.fori_loop(0, count // step, select, 0)
    for copy in copies:
        copy.wait()
    both[...] = dot(sel[...], col_cells[...], (1, 1))

    def weigh(block, _):
        at = pl.ds(pl.multiple_of(block * LANES, LANES), LANES)
        sources = LANES // cap
        ops = [
            jnp.concatenate(
                [records[block * sources + s, half * cap : (half + 1) * cap, :] for s in range(sources)], axis=0
            )
            for half in range(halves)
        ]
        total = sum(
            (both[at, half * LANES : (half + 1) * LANES] + both[at, width + half * LANES : width + (half + 1) * LANES])
            * ops[half]
            for half in range(halves)
        )
        innovation = jnp.sum(total, axis=1, keepdims=True) * precs[at, :]
        for half in range(halves):
            high, low = split((ops[half] * innovation).T, 2)
            spread[half * LANES : (half + 1) * LANES, at] = high
            spread[width + half * LANES : width + (half + 1) * LANES, at] = low
        return 0

    lax.fori_loop(0, count // LANES, weigh, 0)
    sums = dot(spread[...], sel[...], (1, 0))
    for i in range(rows):
        lanes = slice(i * LANES, (i + 1) * LANES)
        adjoint[i] = sums[:width, lanes] + sums[width:, lanes]
        for f in range(2):
            put_low((low0, low1), adjoint[i, f * (width // 2) : f * (width // 2) + GROUP, :], i, f, rows)


def local(state_incr, winds, coupling, background, obs_dest, obs_col, obs_op, obs_prec):
    _, fields, levels, rows, lanes = state_incr.shape
    width = fields * levels
    groups = width // GROUP
    tiles = lax.axis_size("gx") * lax.axis_size("gy")
    count = obs_col.shape[0]
    cap = 2 * count // tiles
    halves = obs_op.shape[1] // LANES

    scale = jnp.broadcast_to(background.reshape(width, 1), (width, LANES))

    vmem = pl.BlockSpec(memory_space=pltpu.VMEM)
    anywhere = pl.BlockSpec(memory_space=pl.ANY)
    hbm = pl.BlockSpec(memory_space=pltpu.HBM)
    own = pltpu.VMEM((rows, width, LANES), jnp.float32)
    framed = pltpu.VMEM((rows + 2, width, LANES), jnp.float32)
    packed_shape = f32(groups // PARTS * GROUP, LANES)
    sides = pltpu.VMEM(packed_shape.shape, jnp.float32)
    strip_shapes = [f32(width, LANES), f32(width, LANES), packed_shape]
    field_shape = f32(rows, width, LANES)
    low_shape = f32(fields * rows, LANES)
    cols_shape = ((2 * width, rows * LANES), jnp.bfloat16)

    def sems(*shape):
        return pltpu.SemaphoreType.DMA(shape)

    def run(body, out_shape, scratch, args, far=(), **kw):
        specs = [anywhere if k in far else vmem for k in range(len(args))]
        return call(functools.partial(body, rows, levels), out_shape, scratch, in_specs=specs, **kw)(*args)

    def swap_floor(floor):
        return lax.ppermute(floor, "comp", [(0, 1), (1, 0)])

    state = state_incr.reshape(width, rows, lanes)
    wind = winds.reshape(width, rows, lanes)
    floor_winds = winds[0, :, 0]

    s_even, s_odd, packed, low0, low1 = run(
        edges_kernel, strip_shapes + [low_shape] * 2, [own, sems(rows)], (state,), far=(0,)
    )
    halos = exchange((s_even, s_odd), packed)

    send = call(functools.partial(route_kernel, tiles, cap), f32(tiles, halves * cap + GROUP, LANES))(
        obs_dest.reshape(1, count), obs_col.reshape(1, count), obs_prec.reshape(1, count), obs_op
    )
    send, halos = lax.optimization_barrier((send, halos))
    records = lax.all_to_all(send, ("gx", "gy"), split_axis=0, concat_axis=0, tiled=True)

    floor = run(forward_floor_kernel, low_shape, [], (low0, low1, floor_winds, *halos))
    field, s_even, s_odd, packed, low0, low1 = run(
        functools.partial(forward_kernel, True, False),
        [field_shape] + strip_shapes + [low_shape] * 2,
        [framed, own, sides, sems(2, rows)],
        (coupling, swap_floor(floor), state, wind, *halos),
        far=(2, 3),
    )
    halos = exchange((s_even, s_odd), packed)
    floor = run(forward_floor_kernel, low_shape, [], (low0, low1, floor_winds, *halos))
    cols = run(
        functools.partial(forward_kernel, False, True),
        jax.ShapeDtypeStruct(*cols_shape),
        [framed, own, sides, sems(2, rows), pltpu.VMEM(*cols_shape), sems(rows)],
        (coupling, swap_floor(floor), field, wind, *halos),
        far=(2, 3),
        out_specs=hbm,
    )

    slots = tiles * cap
    adjoint, low0, low1 = call(
        functools.partial(observe_kernel, rows, width, tiles, cap),
        [field_shape, low_shape, low_shape],
        [
            pltpu.VMEM(*cols_shape),
            pltpu.VMEM((slots, rows * LANES), jnp.bfloat16),
            pltpu.VMEM((slots, LANES), jnp.float32),
            pltpu.VMEM((slots, 2 * width), jnp.float32),
            pltpu.VMEM((2 * width, slots), jnp.bfloat16),
            sems(8),
        ],
        limit=OBSERVE_VMEM,
        in_specs=[vmem, hbm],
    )(records, cols)

    other = swap_floor(low0)
    bottom, s_even, s_odd, packed = run(
        adjoint_pack_kernel,
        [f32(rows, fields * GROUP, LANES)] + strip_shapes,
        [pltpu.VMEM((rows, levels, LANES), jnp.float32), pltpu.VMEM((2, levels, LANES), jnp.float32), sems(rows + 2)],
        (coupling, other, adjoint, wind),
        far=(3,),
    )
    halos = exchange((s_even, s_odd), packed)
    floor = run(adjoint_floor_kernel, low_shape, [], (coupling, other, low0, low1, floor_winds, *halos))
    adjoint, s_even, s_odd, packed = run(
        adjoint_kernel,
        [field_shape] + strip_shapes,
        [framed, framed, sides, sems(2, rows)],
        (coupling, bottom, swap_floor(floor), adjoint, wind, *halos),
        far=(3, 4),
    )
    halos = exchange((s_even, s_odd), packed)
    result = run(
        final_kernel,
        f32(width, rows, LANES),
        [framed, framed, own, own, sides, sems(4, rows)],
        (scale, adjoint, wind, state, *halos),
        far=(1, 2, 3),
        out_specs=hbm,
    )
    return result.reshape(state_incr.shape)


def solution(mesh):
    placed = (
        P("comp", None, None, "gx", "gy"),
        P("comp", None, None, "gx", "gy"),
        P("gx", "gy"),
        P("comp", None, None),
        P(("comp", "gx", "gy"), None),
        P(("comp", "gx", "gy")),
        P(("comp", "gx", "gy"), None),
        P(("comp", "gx", "gy")),
    )
    return jax.shard_map(
        local,
        mesh=mesh,
        in_specs=placed,
        out_specs=P("comp", None, None, "gx", "gy"),
        check_vma=False,
    )
```

time: 101 us -> 112 us (1.11)
  Pallas kernels: 42.5 us -> 55.6 us
  waiting for transfers between devices: 23.1 us -> 20.3 us
  starting transfers between devices: 26.1 us -> 28.4 us
  local copies, waits for them, and re-layouts: 8.46 us -> 6.21 us
    pallas_call x10 -> x9, Pallas kernels: 32.4 us -> 45.3 us  [run(): call(functools.partial(body, rows, levels), out_shape, scratch, in_specs=...]
    ppermute x12, starting transfers between devices: 19.4 us -> 22.6 us  [pair_swap(): return lax.ppermute(block, axis, route)]
    ppermute x12, waiting for transfers between devices: 18.6 us -> 15.7 us  [pair_swap(): return lax.ppermute(block, axis, route)]
    unnamed x32 -> x24, local copies, waits for them, and re-layouts: 8.38 us -> 6.12 us
  transfers between devices with their start and end apart: 17 -> 17, of which waited for: 12 -> 9; matrix products, arithmetic and copies ran while one was open for 0% -> 0% of each run, Pallas kernels for 16% -> 18%
where the time goes in v3:
time: 112 us; the launch traced here: 111 us
  Pallas kernels  55.6 us (50%)
  starting transfers between devices  28.4 us (25%)
  waiting for transfers between devices  20.3 us (18%)
  local copies, waits for them, and re-layouts  6.21 us (6%)
    pallas_call x9, Pallas kernels, run(): call(functools.partial(body, rows, levels), out_shape, scratch, in_specs=...  45.3 us
    ppermute x12, starting transfers between devices, pair_swap(): return lax.ppermute(block, axis, route)  22.6 us
    ppermute x12, waiting for transfers between devices, pair_swap(): return lax.ppermute(block, axis, route)  15.7 us
    pallas_call x1, Pallas kernels, local(): call(functools.partial(observe_kernel, rows, width, tiles, cap), [field_s...  8.31 us
    unnamed x24, local copies, waits for them, and re-layouts  6.12 us
    all_to_all x1, starting transfers between devices, local(): lax.all_to_all(send, ('gx', 'gy'), split_axis=0, concat_axis=0, tiled=True)  5.34 us
    ppermute x4, waiting for transfers between devices, swap_floor(): return lax.ppermute(floor, 'comp', [(0, 1), (1, 0)])  4.53 us
  transfers between devices with their start and end apart: 17, of which 9 were waited for; matrix products, arithmetic and copies ran while one was open for 0% of the time, Pallas kernels for 18%

profile of v3, /device:TPU:8, one launch (start us, length us, event | category | flops | bytes accessed | tf_op | source)
XLA Modules:
  0.0 110.9 jit_solution(5318556694990499251)
XLA Ops:
  0.0 1.6 %copy-done.1 = f32[1,2,128,16,128]{4,3,2,1,0:T(8,128)S(1)} copy-done((f32[1,2,128,16,128]{4,3,2,1,0:T(8,128)S(1)}, f32[1,2,128,16,128]{4,3,2,1,0:T(8,128)}, u32[]{:S(2)}) %copy-start.1) | copy-done | bytes 2097176
  1.6 3.9 %shard_map.83 = (f32[256,128]{1,0:T(8,128)S(1)}, f32[256,128]{1,0:T(8,128)}, f32[64,128]{1,0:T(8,128)S(1)}, f32[32,128]{1,0:T(8,128)S(1)}, f32[32,128]{1,0:T(8,128)S(1)}) custom-call(f32[256,16,128]{2,1,0:T(8,128)S(1)} %bitcast.16), custom_call_target="tpu_custom_call" | custom-call | tf_op jit(solution)/shard_map/pallas_call | solution.py:621
  5.6 1.6 %collective-permute-start = (f32[256,128]{1,0:T(8,128)S(1)}, f32[256,128]{1,0:T(8,128)S(1)}, u32[]{:S(2)}, u32[]{:S(2)}) collective-permute-start(f32[256,128]{1,0:T(8,128)S(1)} %get-tuple-element.27), channel_id=1, source_target_pairs={{0,8},{8,0},{1,9},{9,1},{2,10},{10,2},{3,11},{11,3},{4,12},{12,4},... | collective-permute-start | bytes 393224 | tf_op jit(solution)/shard_map/ppermute | solution.py:46
  7.1 1.5 %collective-permute-start.1 = (f32[64,128]{1,0:T(8,128)S(1)}, f32[64,128]{1,0:T(8,128)S(1)}, u32[]{:S(2)}, u32[]{:S(2)}) collective-permute-start(f32[64,128]{1,0:T(8,128)S(1)} %get-tuple-element.28), channel_id=1, source_target_pairs={{0,1},{1,0},{2,3},{3,2},{4,5},{5,4},{6,7},{7,6},{8,9},{9,8},{10,11... | collective-permute-start | bytes 98312 | tf_op jit(solution)/shard_map/ppermute | solution.py:46
  8.6 2.3 %collective-permute-start.2 = (f32[64,128]{1,0:T(8,128)S(1)}, f32[64,128]{1,0:T(8,128)S(1)}, u32[]{:S(2)}, u32[]{:S(2)}) collective-permute-start(f32[64,128]{1,0:T(8,128)S(1)} %get-tuple-element.28), channel_id=1, source_target_pairs={{1,2},{2,1},{3,4},{4,3},{5,6},{6,5},{9,10},{10,9},{11,12},{12,11},... | collective-permute-start | bytes 98312 | tf_op jit(solution)/shard_map/ppermute | solution.py:46
  11.0 2.0 %shard_map.82 = f32[16,136,128]{2,1,0:T(8,128)} custom-call(s32[1,512]{1,0:T(1,128)S(1)} %bitcast.19, s32[1,512]{1,0:T(1,128)S(1)} %bitcast.20, f32[1,512]{1,0:T(1,128)S(1)} %bitcast.21, f32[512,256]{1,0:T(8,128)S(1)} %copy-done.6), custom_call_target="tpu_custom_call" | custom-call | tf_op jit(solution)/shard_map/pallas_call | solution.py:635
  13.0 2.3 %collective-permute-done.2.rest_2_ = f32[64,128]{1,0:T(8,128)S(1)} collective-permute-done((f32[64,128]{1,0:T(8,128)S(1)}, f32[64,128]{1,0:T(8,128)S(1)}, u32[]{:S(2)}, u32[]{:S(2)}) %collective-permute-start.2) | collective-permute-done | bytes 32800 | tf_op jit(solution)/shard_map/ppermute | solution.py:46
  15.3 5.3 %all-to-all-start = ((f32[16,136,128]{2,1,0:T(8,128)}), f32[16,136,128]{2,1,0:T(8,128)S(1)}, u32[]{:S(2)}, u32[]{:S(2)}) async-start(f32[16,136,128]{2,1,0:T(8,128)} %shard_map.82), calls=%async_computation | async-start | bytes 2228224 | tf_op jit(solution)/shard_map/all_to_all | solution.py:639
  20.9 1.2 %collective-permute-done.3.other = f32[32,128]{1,0:T(8,128)S(1)} collective-permute-done((f32[32,128]{1,0:T(8,128)S(1)}, f32[32,128]{1,0:T(8,128)S(1)}, u32[]{:S(2)}, u32[]{:S(2)}) %collective-permute-start.3) | collective-permute-done | bytes 16416 | tf_op jit(solution)/shard_map/ppermute | solution.py:624
  22.1 1.6 %copy-done.2 = f32[1,2,128,16,128]{4,3,2,1,0:T(8,128)S(1)} copy-done((f32[1,2,128,16,128]{4,3,2,1,0:T(8,128)S(1)}, f32[1,2,128,16,128]{4,3,2,1,0:T(8,128)}, u32[]{:S(2)}) %copy-start.2) | copy-done | bytes 2097176
  23.7 8.5 %shard_map.85 = (f32[16,256,128]{2,1,0:T(8,128)S(1)}, f32[256,128]{1,0:T(8,128)S(1)}, f32[256,128]{1,0:T(8,128)}, f32[64,128]{1,0:T(8,128)S(1)}, f32[32,128]{1,0:T(8,128)S(1)}, /*index=5*/f32[32,128]{1,0:T(8,128)S(1)}) custom-call(f32[16,128]{1,0:T(8,128)S(1)} %copy-done.7, f32[32,128]{1,0:T(8,128)S(1)} %collective-permute-done.3.other, ...), custom_call_target="tpu_custom_call" | custom-call | tf_op jit(solution)/shard_map/pallas_call | solution.py:621
  32.3 1.5 %collective-permute-start.4 = (f32[256,128]{1,0:T(8,128)S(1)}, f32[256,128]{1,0:T(8,128)S(1)}, u32[]{:S(2)}, u32[]{:S(2)}) collective-permute-start(f32[256,128]{1,0:T(8,128)S(1)} %get-tuple-element.37), channel_id=1, source_target_pairs={{0,8},{8,0},{1,9},{9,1},{2,10},{10,2},{3,11},{11,3},{4,12},{12,4},... | collective-permute-start | bytes 393224 | tf_op jit(solution)/shard_map/ppermute | solution.py:46
  33.8 1.5 %collective-permute-start.5 = (f32[64,128]{1,0:T(8,128)S(1)}, f32[64,128]{1,0:T(8,128)S(1)}, u32[]{:S(2)}, u32[]{:S(2)}) collective-permute-start(f32[64,128]{1,0:T(8,128)S(1)} %get-tuple-element.38), channel_id=1, source_target_pairs={{0,1},{1,0},{2,3},{3,2},{4,5},{5,4},{6,7},{7,6},{8,9},{9,8},{10,11... | collective-permute-start | bytes 98312 | tf_op jit(solution)/shard_map/ppermute | solution.py:46
  35.3 2.6 %collective-permute-start.6 = (f32[64,128]{1,0:T(8,128)S(1)}, f32[64,128]{1,0:T(8,128)S(1)}, u32[]{:S(2)}, u32[]{:S(2)}) collective-permute-start(f32[64,128]{1,0:T(8,128)S(1)} %get-tuple-element.38), channel_id=1, source_target_pairs={{1,2},{2,1},{3,4},{4,3},{5,6},{6,5},{9,10},{10,9},{11,12},{12,11},... | collective-permute-start | bytes 98312 | tf_op jit(solution)/shard_map/ppermute | solution.py:46
  37.9 4.0 %collective-permute-done.6.rest_2_ = f32[64,128]{1,0:T(8,128)S(1)} collective-permute-done((f32[64,128]{1,0:T(8,128)S(1)}, f32[64,128]{1,0:T(8,128)S(1)}, u32[]{:S(2)}, u32[]{:S(2)}) %collective-permute-start.6) | collective-permute-done | bytes 32800 | tf_op jit(solution)/shard_map/ppermute | solution.py:46
  42.2 1.2 %collective-permute-done.7.other = f32[32,128]{1,0:T(8,128)S(1)} collective-permute-done((f32[32,128]{1,0:T(8,128)S(1)}, f32[32,128]{1,0:T(8,128)S(1)}, u32[]{:S(2)}, u32[]{:S(2)}) %collective-permute-start.7) | collective-permute-done | bytes 16416 | tf_op jit(solution)/shard_map/ppermute | solution.py:624
  43.4 8.9 %shard_map.87.cols = bf16[512,2048]{1,0:T(8,128)(2,1)S(1)} custom-call(f32[16,128]{1,0:T(8,128)S(1)} %copy-done.7, f32[32,128]{1,0:T(8,128)S(1)} %collective-permute-done.7.other, f32[16,256,128]{2,1,0:T(8,128)S(1)} %get-tuple-element.39.field, f32[256,16,128]{2,1,0:T(8,128)S(1)} %bitcast.12, f32[256,128]{1,0:T(8,128)S(1)} %collective-permute-done.4.rest_0_, ...), custom_call_target="tpu_custom_call" | custom-call | tf_op jit(solution)/shard_map/pallas_call | solution.py:621
  52.3 1.3 %copy-done.4 = bf16[512,2048]{1,0:T(8,128)(2,1)} copy-done((bf16[512,2048]{1,0:T(8,128)(2,1)}, bf16[512,2048]{1,0:T(8,128)(2,1)S(1)}, u32[]{:S(2)}) %copy-start.4) | copy-done | bytes 2097176
  53.6 1.6 %copy-done.5 = bf16[512,2048]{1,0:T(8,128)(2,1)S(1)} copy-done((bf16[512,2048]{1,0:T(8,128)(2,1)S(1)}, bf16[512,2048]{1,0:T(8,128)(2,1)}, u32[]{:S(2)}) %copy-start.5) | copy-done | bytes 2097176
  55.2 8.3 %shard_map.88 = (f32[16,256,128]{2,1,0:T(8,128)S(1)}, f32[32,128]{1,0:T(8,128)S(1)}, f32[32,128]{1,0:T(8,128)S(1)}) custom-call(f32[16,136,128]{2,1,0:T(8,128)S(1)} %all-to-all-done.records, bf16[512,2048]{1,0:T(8,128)(2,1)S(1)} %copy-done.5), custom_call_target="tpu_custom_call" | custom-call | tf_op jit(solution)/shard_map/pallas_call | solution.py:661
  63.7 1.0 collective-permute-done.8.other
  64.8 3.4 %shard_map.89 = (f32[16,16,128]{2,1,0:T(8,128)S(1)}, f32[256,128]{1,0:T(8,128)S(1)}, f32[256,128]{1,0:T(8,128)}, f32[64,128]{1,0:T(8,128)S(1)}) custom-call(f32[16,128]{1,0:T(8,128)S(1)} %copy-done.7, f32[32,128]{1,0:T(8,128)S(1)} %collective-permute-done.8.other, f32[16,256,128]{2,1,0:T(8,128)S(1)} %get-tuple-element.41.field, f32[256,16,128]{2,1,0:T(8,128)S(1)} %bitcast.13), custom_call_target="tpu_custom_call" | custom-call | tf_op jit(solution)/shard_map/pallas_call | solution.py:621
  68.2 0.8 collective-permute-start.9
  69.0 6.0 %collective-permute-start.10 = (f32[64,128]{1,0:T(8,128)S(1)}, f32[64,128]{1,0:T(8,128)S(1)}, u32[]{:S(2)}, u32[]{:S(2)}) collective-permute-start(f32[64,128]{1,0:T(8,128)S(1)} %get-tuple-element.45), channel_id=1, source_target_pairs={{0,1},{1,0},{2,3},{3,2},{4,5},{5,4},{6,7},{7,6},{8,9},{9,8},{10,11... | collective-permute-start | bytes 98312 | tf_op jit(solution)/shard_map/ppermute | solution.py:46
  75.0 1.9 %collective-permute-start.11 = (f32[64,128]{1,0:T(8,128)S(1)}, f32[64,128]{1,0:T(8,128)S(1)}, u32[]{:S(2)}, u32[]{:S(2)}) collective-permute-start(f32[64,128]{1,0:T(8,128)S(1)} %get-tuple-element.45), channel_id=1, source_target_pairs={{1,2},{2,1},{3,4},{4,3},{5,6},{6,5},{9,10},{10,9},{11,12},{12,11},... | collective-permute-start | bytes 98312 | tf_op jit(solution)/shard_map/ppermute | solution.py:46
  76.9 4.8 %collective-permute-done.11.rest_2_ = f32[64,128]{1,0:T(8,128)S(1)} collective-permute-done((f32[64,128]{1,0:T(8,128)S(1)}, f32[64,128]{1,0:T(8,128)S(1)}, u32[]{:S(2)}, u32[]{:S(2)}) %collective-permute-start.11) | collective-permute-done | bytes 32800 | tf_op jit(solution)/shard_map/ppermute | solution.py:46
  81.8 1.2 %collective-permute-done.12.other_next = f32[32,128]{1,0:T(8,128)S(1)} collective-permute-done((f32[32,128]{1,0:T(8,128)S(1)}, f32[32,128]{1,0:T(8,128)S(1)}, u32[]{:S(2)}, u32[]{:S(2)}) %collective-permute-start.12) | collective-permute-done | bytes 16416 | tf_op jit(solution)/shard_map/ppermute | solution.py:624
  83.0 9.7 %shard_map.91 = (f32[16,256,128]{2,1,0:T(8,128)S(1)}, f32[256,128]{1,0:T(8,128)S(1)}, f32[256,128]{1,0:T(8,128)}, f32[64,128]{1,0:T(8,128)S(1)}) custom-call(f32[16,128]{1,0:T(8,128)S(1)} %copy-done.7, f32[16,16,128]{2,1,0:T(8,128)S(1)} %get-tuple-element.42.bottom, f32[32,128]{1,0:T(8,128)S(1)} %collective-permute-done.12.other_next, ...), custom_call_target="tpu_custom_call" | custom-call | tf_op jit(solution)/shard_map/pallas_call | solution.py:621
  93.5 2.1 %collective-permute-start.15 = (f32[64,128]{1,0:T(8,128)S(1)}, f32[64,128]{1,0:T(8,128)S(1)}, u32[]{:S(2)}, u32[]{:S(2)}) collective-permute-start(f32[64,128]{1,0:T(8,128)S(1)} %get-tuple-element.48), channel_id=1, source_target_pairs={{1,2},{2,1},{3,4},{4,3},{5,6},{6,5},{9,10},{10,9},{11,12},{12,11},... | collective-permute-start | bytes 98312 | tf_op jit(solution)/shard_map/ppermute | solution.py:46
  95.7 1.8 %collective-permute-done.14.rest_1_ = f32[64,128]{1,0:T(8,128)S(1)} collective-permute-done((f32[64,128]{1,0:T(8,128)S(1)}, f32[64,128]{1,0:T(8,128)S(1)}, u32[]{:S(2)}, u32[]{:S(2)}) %collective-permute-start.14) | collective-permute-done | bytes 32800 | tf_op jit(solution)/shard_map/ppermute | solution.py:46
  97.4 2.8 %collective-permute-done.15.rest_2_ = f32[64,128]{1,0:T(8,128)S(1)} collective-permute-done((f32[64,128]{1,0:T(8,128)S(1)}, f32[64,128]{1,0:T(8,128)S(1)}, u32[]{:S(2)}, u32[]{:S(2)}) %collective-permute-start.15) | collective-permute-done | bytes 32800 | tf_op jit(solution)/shard_map/ppermute | solution.py:46
  100.3 10.4 %shard_map.92 = f32[256,16,128]{2,1,0:T(8,128)} custom-call(f32[256,128]{1,0:T(8,128)S(1)} %broadcast_in_dim.8.scale, f32[16,256,128]{2,1,0:T(8,128)S(1)} %get-tuple-element.46.field, f32[256,16,128]{2,1,0:T(8,128)S(1)} %bitcast.15, f32[256,16,128]{2,1,0:T(8,128)S(1)} %bitcast.18, f32[256,128]{1,0:T(8,128)S(1)} %collective-permute-done.13.rest_0_, ...), custom_call_target="tpu_custom_call" | custom-call | tf_op jit(solution)/shard_map/pallas_call | solution.py:621
  (39 shorter events, 1.8 us)
Async XLA Ops:
  0.0 1.6 %copy-start.1 = (f32[1,2,128,16,128]{4,3,2,1,0:T(8,128)S(1)}, f32[1,2,128,16,128]{4,3,2,1,0:T(8,128)}, u32[]{:S(2)}) copy-start(f32[1,2,128,16,128]{4,3,2,1,0:T(8,128)} %param.8) | copy-start | bytes 6291460
  1.6 9.4 %copy-start.6 = (f32[512,256]{1,0:T(8,128)S(1)}, f32[512,256]{1,0:T(8,128)}, u32[]{:S(2)}) copy-start(f32[512,256]{1,0:T(8,128)} %op.1) | copy-start | bytes 1572868
  1.6 9.4 %copy-start.8 = (s32[512,1]{0,1:T(1,128)S(1)}, s32[512,1]{0,1:T(1,128)}, u32[]{:S(2)}) copy-start(s32[512,1]{0,1:T(1,128)} %param.12) | copy-start | bytes 6148
  1.6 9.4 %copy-start.9 = (s32[512]{0:T(512)S(1)}, s32[512]{0:T(512)}, u32[]{:S(2)}) copy-start(s32[512]{0:T(512)} %param.13) | copy-start | bytes 6148
  1.6 9.4 %copy-start.10 = (f32[512]{0:T(512)S(1)}, f32[512]{0:T(512)}, u32[]{:S(2)}) copy-start(f32[512]{0:T(512)} %param.15) | copy-start | bytes 6148
  5.5 15.1 %copy-start = (f32[1,2,128,16,128]{4,3,2,1,0:T(8,128)S(1)}, f32[1,2,128,16,128]{4,3,2,1,0:T(8,128)}, u32[]{:S(2)}) copy-start(f32[1,2,128,16,128]{4,3,2,1,0:T(8,128)} %param.9) | copy-start | bytes 6291460
  5.5 16.6 %copy-start.7 = (f32[16,128]{1,0:T(8,128)S(1)}, f32[16,128]{1,0:T(8,128)}, u32[]{:S(2)}) copy-start(f32[16,128]{1,0:T(8,128)} %coupling.9) | copy-start | bytes 24580
  5.6 9.8 %collective-permute-start = (f32[256,128]{1,0:T(8,128)S(1)}, f32[256,128]{1,0:T(8,128)S(1)}, u32[]{:S(2)}, u32[]{:S(2)}) collective-permute-start(f32[256,128]{1,0:T(8,128)S(1)} %get-tuple-element.27), channel_id=1, source_target_pairs={{0,8},{8,0},{1,9},{9,1},{2,10},{10,2},{3,11},{11,3},{4,12},{12,4},... | collective-permute-start | bytes 393224 | tf_op jit(solution)/shard_map/ppermute | solution.py:46
  7.1 5.8 %collective-permute-start.1 = (f32[64,128]{1,0:T(8,128)S(1)}, f32[64,128]{1,0:T(8,128)S(1)}, u32[]{:S(2)}, u32[]{:S(2)}) collective-permute-start(f32[64,128]{1,0:T(8,128)S(1)} %get-tuple-element.28), channel_id=1, source_target_pairs={{0,1},{1,0},{2,3},{3,2},{4,5},{5,4},{6,7},{7,6},{8,9},{9,8},{10,11... | collective-permute-start | bytes 98312 | tf_op jit(solution)/shard_map/ppermute | solution.py:46
  8.6 6.7 %collective-permute-start.2 = (f32[64,128]{1,0:T(8,128)S(1)}, f32[64,128]{1,0:T(8,128)S(1)}, u32[]{:S(2)}, u32[]{:S(2)}) collective-permute-start(f32[64,128]{1,0:T(8,128)S(1)} %get-tuple-element.28), channel_id=1, source_target_pairs={{1,2},{2,1},{3,4},{4,3},{5,6},{6,5},{9,10},{10,9},{11,12},{12,11},... | collective-permute-start | bytes 98312 | tf_op jit(solution)/shard_map/ppermute | solution.py:46
  15.3 38.3 %all-to-all-start = ((f32[16,136,128]{2,1,0:T(8,128)}), f32[16,136,128]{2,1,0:T(8,128)S(1)}, u32[]{:S(2)}, u32[]{:S(2)}) async-start(f32[16,136,128]{2,1,0:T(8,128)} %shard_map.82), calls=%async_computation | async-start | bytes 2228224 | tf_op jit(solution)/shard_map/all_to_all | solution.py:639
  20.9 1.2 %collective-permute-start.3 = (f32[32,128]{1,0:T(8,128)S(1)}, f32[32,128]{1,0:T(8,128)S(1)}, u32[]{:S(2)}, u32[]{:S(2)}) collective-permute-start(f32[32,128]{1,0:T(8,128)S(1)} %shard_map.84), channel_id=1, source_target_pairs={{0,16},{16,0},{1,17},{17,1},{2,18},{18,2},{3,19},{19,3},{4,20},{20... | collective-permute-start | bytes 49160 | tf_op jit(solution)/shard_map/ppermute | solution.py:624
  22.1 1.6 %copy-start.2 = (f32[1,2,128,16,128]{4,3,2,1,0:T(8,128)S(1)}, f32[1,2,128,16,128]{4,3,2,1,0:T(8,128)}, u32[]{:S(2)}) copy-start(f32[1,2,128,16,128]{4,3,2,1,0:T(8,128)} %param.8) | copy-start | bytes 6291460
  32.3 9.7 %collective-permute-start.4 = (f32[256,128]{1,0:T(8,128)S(1)}, f32[256,128]{1,0:T(8,128)S(1)}, u32[]{:S(2)}, u32[]{:S(2)}) collective-permute-start(f32[256,128]{1,0:T(8,128)S(1)} %get-tuple-element.37), channel_id=1, source_target_pairs={{0,8},{8,0},{1,9},{9,1},{2,10},{10,2},{3,11},{11,3},{4,12},{12,4},... | collective-permute-start | bytes 393224 | tf_op jit(solution)/shard_map/ppermute | solution.py:46
  33.8 4.1 %collective-permute-start.5 = (f32[64,128]{1,0:T(8,128)S(1)}, f32[64,128]{1,0:T(8,128)S(1)}, u32[]{:S(2)}, u32[]{:S(2)}) collective-permute-start(f32[64,128]{1,0:T(8,128)S(1)} %get-tuple-element.38), channel_id=1, source_target_pairs={{0,1},{1,0},{2,3},{3,2},{4,5},{5,4},{6,7},{7,6},{8,9},{9,8},{10,11... | collective-permute-start | bytes 98312 | tf_op jit(solution)/shard_map/ppermute | solution.py:46
  35.3 6.7 %collective-permute-start.6 = (f32[64,128]{1,0:T(8,128)S(1)}, f32[64,128]{1,0:T(8,128)S(1)}, u32[]{:S(2)}, u32[]{:S(2)}) collective-permute-start(f32[64,128]{1,0:T(8,128)S(1)} %get-tuple-element.38), channel_id=1, source_target_pairs={{1,2},{2,1},{3,4},{4,3},{5,6},{6,5},{9,10},{10,9},{11,12},{12,11},... | collective-permute-start | bytes 98312 | tf_op jit(solution)/shard_map/ppermute | solution.py:46
  42.1 1.2 %collective-permute-start.7 = (f32[32,128]{1,0:T(8,128)S(1)}, f32[32,128]{1,0:T(8,128)S(1)}, u32[]{:S(2)}, u32[]{:S(2)}) collective-permute-start(f32[32,128]{1,0:T(8,128)S(1)} %shard_map.86), channel_id=1, source_target_pairs={{0,16},{16,0},{1,17},{17,1},{2,18},{18,2},{3,19},{19,3},{4,20},{20... | collective-permute-start | bytes 49160 | tf_op jit(solution)/shard_map/ppermute | solution.py:624
  52.3 1.3 %copy-start.4 = (bf16[512,2048]{1,0:T(8,128)(2,1)}, bf16[512,2048]{1,0:T(8,128)(2,1)S(1)}, u32[]{:S(2)}) copy-start(bf16[512,2048]{1,0:T(8,128)(2,1)S(1)} %shard_map.87.cols) | copy-start | bytes 6291460
  53.6 1.6 %copy-start.5 = (bf16[512,2048]{1,0:T(8,128)(2,1)S(1)}, bf16[512,2048]{1,0:T(8,128)(2,1)}, u32[]{:S(2)}) copy-start(bf16[512,2048]{1,0:T(8,128)(2,1)} %copy-done.4) | copy-start | bytes 6291460
  63.5 1.2 %collective-permute-start.8 = (f32[32,128]{1,0:T(8,128)S(1)}, f32[32,128]{1,0:T(8,128)S(1)}, u32[]{:S(2)}, u32[]{:S(2)}) collective-permute-start(f32[32,128]{1,0:T(8,128)S(1)} %get-tuple-element.40.low0), channel_id=1, source_target_pairs={{0,16},{16,0},{1,17},{17,1},{2,18},{18,2},{3,19},{19,3},{4,20},{20... | collective-permute-start | bytes 49160 | tf_op jit(solution)/shard_map/ppermute | solution.py:624
  68.2 13.5 %collective-permute-start.9 = (f32[256,128]{1,0:T(8,128)S(1)}, f32[256,128]{1,0:T(8,128)S(1)}, u32[]{:S(2)}, u32[]{:S(2)}) collective-permute-start(f32[256,128]{1,0:T(8,128)S(1)} %get-tuple-element.44), channel_id=1, source_target_pairs={{0,8},{8,0},{1,9},{9,1},{2,10},{10,2},{3,11},{11,3},{4,12},{12,4},... | collective-permute-start | bytes 393224 | tf_op jit(solution)/shard_map/ppermute | solution.py:46
  69.0 7.9 %collective-permute-start.10 = (f32[64,128]{1,0:T(8,128)S(1)}, f32[64,128]{1,0:T(8,128)S(1)}, u32[]{:S(2)}, u32[]{:S(2)}) collective-permute-start(f32[64,128]{1,0:T(8,128)S(1)} %get-tuple-element.45), channel_id=1, source_target_pairs={{0,1},{1,0},{2,3},{3,2},{4,5},{5,4},{6,7},{7,6},{8,9},{9,8},{10,11... | collective-permute-start | bytes 98312 | tf_op jit(solution)/shard_map/ppermute | solution.py:46
  75.0 6.7 %collective-permute-start.11 = (f32[64,128]{1,0:T(8,128)S(1)}, f32[64,128]{1,0:T(8,128)S(1)}, u32[]{:S(2)}, u32[]{:S(2)}) collective-permute-start(f32[64,128]{1,0:T(8,128)S(1)} %get-tuple-element.45), channel_id=1, source_target_pairs={{1,2},{2,1},{3,4},{4,3},{5,6},{6,5},{9,10},{10,9},{11,12},{12,11},... | collective-permute-start | bytes 98312 | tf_op jit(solution)/shard_map/ppermute | solution.py:46
  81.8 1.2 %collective-permute-start.12 = (f32[32,128]{1,0:T(8,128)S(1)}, f32[32,128]{1,0:T(8,128)S(1)}, u32[]{:S(2)}, u32[]{:S(2)}) collective-permute-start(f32[32,128]{1,0:T(8,128)S(1)} %shard_map.90), channel_id=1, source_target_pairs={{0,16},{16,0},{1,17},{17,1},{2,18},{18,2},{3,19},{19,3},{4,20},{20... | collective-permute-start | bytes 49160 | tf_op jit(solution)/shard_map/ppermute | solution.py:624
  83.0 17.2 %copy-start.11 = (f32[1,2,128]{2,1,0:T(2,128)S(1)}, f32[1,2,128]{2,1,0:T(2,128)}, u32[]{:S(2)}) copy-start(f32[1,2,128]{2,1,0:T(2,128)} %param.11) | copy-start | bytes 3076
  83.0 17.3 %copy-start.3 = (f32[1,2,128,16,128]{4,3,2,1,0:T(8,128)S(1)}, f32[1,2,128,16,128]{4,3,2,1,0:T(8,128)}, u32[]{:S(2)}) copy-start(f32[1,2,128,16,128]{4,3,2,1,0:T(8,128)} %param.8) | copy-start | bytes 6291460
  92.7 7.5 %collective-permute-start.13 = (f32[256,128]{1,0:T(8,128)S(1)}, f32[256,128]{1,0:T(8,128)S(1)}, u32[]{:S(2)}, u32[]{:S(2)}) collective-permute-start(f32[256,128]{1,0:T(8,128)S(1)} %get-tuple-element.47), channel_id=1, source_target_pairs={{0,8},{8,0},{1,9},{9,1},{2,10},{10,2},{3,11},{11,3},{4,12},{12,4},... | collective-permute-start | bytes 393224 | tf_op jit(solution)/shard_map/ppermute | solution.py:46
  93.5 3.9 %collective-permute-start.14 = (f32[64,128]{1,0:T(8,128)S(1)}, f32[64,128]{1,0:T(8,128)S(1)}, u32[]{:S(2)}, u32[]{:S(2)}) collective-permute-start(f32[64,128]{1,0:T(8,128)S(1)} %get-tuple-element.48), channel_id=1, source_target_pairs={{0,1},{1,0},{2,3},{3,2},{4,5},{5,4},{6,7},{7,6},{8,9},{9,8},{10,11... | collective-permute-start | bytes 98312 | tf_op jit(solution)/shard_map/ppermute | solution.py:46
  93.5 6.7 %collective-permute-start.15 = (f32[64,128]{1,0:T(8,128)S(1)}, f32[64,128]{1,0:T(8,128)S(1)}, u32[]{:S(2)}, u32[]{:S(2)}) collective-permute-start(f32[64,128]{1,0:T(8,128)S(1)} %get-tuple-element.48), channel_id=1, source_target_pairs={{1,2},{2,1},{3,4},{4,3},{5,6},{6,5},{9,10},{10,9},{11,12},{12,11},... | collective-permute-start | bytes 98312 | tf_op jit(solution)/shard_map/ppermute | solution.py:46

commit v4 on v3

--- a/solution.py
+++ b/solution.py
@@ -12,11 +12,10 @@
 LANES = 128
 GROUP = 8
 MIB = 1024 * 1024
-SWEEP_VMEM = 18 * MIB
-OBSERVE_VMEM = 20 * MIB
-
-
-def call(body, out_shape, scratch=(), limit=SWEEP_VMEM, **kw):
+VMEM_GRANT = 59 * MIB
+
+
+def call(body, out_shape, scratch=(), limit=VMEM_GRANT, **kw):
     return pl.pallas_call(
         body,
         out_shape=out_shape,
@@ -153,16 +152,14 @@
     return HORIZ_MIX * x - slope, HORIZ_MIX * x + slope
 
 
-def adjoint_point(cells, winds, sides, i, f, group, levels):
-    groups = levels // GROUP
-    here, upper, lower = levels_around(cells, i, f * levels, group, groups)
+def adjoint_point(cells, winds, i, f, group, levels):
+    here, upper, lower = levels_around(cells, i, f * levels, group, levels // GROUP)
     at = pl.ds(f * levels + group * GROUP, GROUP)
     wind_at = pl.ds(group * GROUP, GROUP)
     after, before = cells[i + 2, at, :], cells[i, at, :]
     u_after, u_before = winds[i + 2, wind_at, :], winds[i, wind_at, :]
-    w = winds[i + 1, pl.ds(levels + group * GROUP, GROUP), :]
-    down, up = products(here, w)
-    right, left = shifted(up, down, side_columns(sides, i, f * groups + group))
+    down, up = products(here, winds[i + 1, pl.ds(levels + group * GROUP, GROUP), :])
+    right, left = shifted(up, down, 0.0)
     return (
         CENTRE * here
         + VERT_MIX * (upper + lower)
@@ -267,30 +264,44 @@
         floor[here, :] = forward_sum(low, up + low, after, before, right, left, winds[0], winds[1])
 
 
-def adjoint_floor_kernel(rows, levels, coupling, other, low0, low1, winds, *rest):
-    *halos, floor = rest
-    side_before, side_after = read_sides(halos)
-    for f in range(2):
-        here = pl.ds(f * rows, rows)
-        at = pl.ds(f * levels, 1)
-        low, up = couple_adjoint(low0[here, :], other[here, :], coupling[...]), low1[here, :]
-        x_down, x_up = products(low, winds[0])
-        after, before = row_after(x_up, side_after(at), rows), row_before(x_down, side_before(at), rows)
-        y_down, y_up = products(low, winds[1])
-        right, left = shifted(y_up, y_down, floor_edge(halos, f, rows, levels), rows)
-        floor[here, :] = CENTRE * low + VERT_MIX * (up + low) + (after + before) + (right + left)
+class Out:
+    def __init__(self, source, target, sems, rows, as_it_goes):
+        self.source, self.target, self.sems, self.rows, self.as_it_goes = source, target, sems, rows, as_it_goes
+
+    def copy(self, i):
+        row = self.target.at[:, i] if self.as_it_goes else self.target.at[i]
+        return pltpu.make_async_copy(self.source.at[i], row, self.sems.at[i])
+
+    def start(self, i):
+        self.copy(i).start()
+
+    def finish(self):
+        for i in range(self.rows):
+            self.copy(i).wait()
+
+
+def dense_row(field, first, rows):
+    total = jnp.zeros((1, LANES), jnp.float32)
+    lane = lax.broadcasted_iota(jnp.int32, (1, LANES), 1)
+    for i in range(rows):
+        slot = slot_of(i, 0, rows)
+        total = jnp.where(lane // 2 == slot, pltpu.roll(field[first + i : first + i + 1, :], 2 * slot + 1, 1), total)
+    return total
 
 
 def forward_kernel(first, last, rows, levels, coupling, other, field, winds, *rest):
+    halo_count = len(rest) - (7 if last else 14)
+    halos, rest = rest[:halo_count], rest[halo_count:]
     if last:
-        *halos, cols, cells, wind_cells, sides, sems, col_cells, col_sems = rest
+        cols, cells, wind_cells, sides, sems, col_cells, col_sems = rest
     else:
-        *halos, out, s_even, s_odd, packed, low0, low1, cells, wind_cells, sides, sems = rest
+        out, s_even, s_odd, packed, low0, low1, wind_ends, wind_dense, dense_g, cells, wind_cells, out_cells, sides, sems = rest
+        leaving = Out(out_cells, out, sems.at[2], rows, False)
+        packed[...] = jnp.zeros_like(packed)
+        wind_dense[...] = jnp.zeros_like(wind_dense)
     incoming = Rows(field, cells, sems.at[0], rows, first, 1)
     wind_in = Rows(winds, wind_cells, sems.at[1], rows, True, 0)
     start_rows(rows, incoming, wind_in)
-    if not last:
-        packed[...] = jnp.zeros_like(packed)
     merge_columns(halos[1], halos[2], sides)
     before, after = read_sides(halos)
     cells[0] = before(slice(None))
@@ -327,150 +338,260 @@
                 col_cells[pl.ds(width + base, PARTS * GROUP), lanes] = low
             else:
                 for part, value in enumerate(values):
-                    out[i, pl.ds(base + part * GROUP, GROUP), :] = value
+                    out_cells[i, pl.ds(base + part * GROUP, GROUP), :] = value
                 pack_block(packed, values, i, m)
+                if f == 0:
+                    w = [wind_cells[i, pl.ds(levels + base + part * GROUP, GROUP), :] for part in range(PARTS)]
+                    pack_block(wind_dense, w, i, m)
         if last:
             col_copy(i).start()
+        else:
+            leaving.start(i)
         return 0
 
     lax.fori_loop(0, rows, row, 0)
     if last:
         for i in range(rows):
             col_copy(i).wait()
-    else:
-        put_strip(s_even, s_odd, slice(None), out[0], out[rows - 1])
-
-
-def with_products(value, w):
-    down, up = products(value, w)
-    return jnp.where(lane_iota() == 0, up, down)
-
-
-def adjoint_pack_kernel(rows, levels, coupling, other, field, winds, bottom, s_even, s_odd, packed, w_cells, u_cells, sems):
-    def w_copy(i):
-        return pltpu.make_async_copy(winds.at[pl.ds(levels, levels), i], w_cells.at[i], sems.at[i])
-
-    u_copies = [
-        pltpu.make_async_copy(winds.at[pl.ds(0, levels), i], u_cells.at[k], sems.at[rows + k])
-        for k, i in enumerate((0, rows - 1))
-    ]
-    for i in range(rows):
-        w_copy(i).start()
-    for copy in u_copies:
-        copy.start()
-    packed[...] = jnp.zeros_like(packed)
+        return
+    put_strip(s_even, s_odd, slice(None), out_cells[0], out_cells[rows - 1])
+    wind_ends[0] = wind_cells[0, pl.ds(0, levels), :]
+    wind_ends[1] = wind_cells[rows - 1, pl.ds(0, levels), :]
+    dense_g[...] = jnp.broadcast_to(dense_row(coupling, 0, rows), dense_g.shape)
+    leaving.finish()
+
+
+def dense_products(packed, value, wind_dense):
+    half = wind_dense.shape[0]
+    for f in range(2):
+        at = slice(f * half, (f + 1) * half)
+        down, up = products(value[at], wind_dense[...])
+        lane = lax.broadcasted_iota(jnp.int32, down.shape, 1)
+        packed[at, :] = jnp.where(lane % 2 == 1, up, down)
+
+
+def level0_row(value, new, f):
+    half = value.shape[0] // 2
+    sub = lax.broadcasted_iota(jnp.int32, value.shape, 0)
+    lane = lax.broadcasted_iota(jnp.int32, value.shape, 1)
+    return jnp.where((sub == f * half) & (lane % (2 * PARTS) < 2), new, value)
+
+
+def end_rows(ends, s_even, s_odd, wind_ends, levels):
+    for f in range(2):
+        at = slice(f * levels, (f + 1) * levels)
+        put_strip(
+            s_even, s_odd, at, products(ends[0][at], wind_ends[0])[1], products(ends[1][at], wind_ends[1])[0]
+        )
+
+
+def with_first(value, new):
+    return jnp.where(lax.broadcasted_iota(jnp.int32, value.shape, 0) == 0, new, value)
+
+
+def border_kernel(rows, levels, coupling, other, ends, columns, wind_ends, wind_dense, dense_g, s_even, s_odd, packed):
+    half = columns.shape[0] // 2
+    dense = columns[...]
+    full = [ends[0], ends[1]]
+    for f in range(2):
+        mixed = couple_adjoint(columns[f * half : f * half + 1, :], other[4 + f : 5 + f, :], dense_g[0:1, :])
+        dense = level0_row(dense, mixed, f)
+    for k, i in enumerate((0, rows - 1)):
+        parts = []
+        for f in range(2):
+            value = ends[k, f * levels : (f + 1) * levels, :]
+            at = 2 * k + f
+            parts.append(with_first(value, couple_adjoint(value[0:1], other[at : at + 1, :], coupling[i : i + 1, :])))
+        full[k] = jnp.concatenate(parts, axis=0)
+    dense_products(packed, dense, wind_dense)
+    end_rows(full, s_even, s_odd, wind_ends, levels)
+
+
+def outside_floor(halos, low, f, rows, levels):
+    before, after = read_sides(halos)
+    at = pl.ds(f * levels, 1)
+    sub, lane = sub_iota(rows), lane_iota(rows)
+    low = low + jnp.where(sub == 0, before(at), 0.0) + jnp.where(sub == rows - 1, after(at), 0.0)
+    edge = floor_edge(halos, f, rows, levels)
+    edge = jnp.where(lane == 0, pltpu.roll(edge, 1, 1), pltpu.roll(edge, LANES - 1, 1))
+    return low + jnp.where((lane == 0) | (lane == LANES - 1), edge, 0.0)
+
+
+def floor_kernel(rows, levels, low0, *rest):
+    *halos, floor = rest
+    for f in range(2):
+        here = pl.ds(f * rows, rows)
+        floor[here, :] = outside_floor(halos, low0[here, :], f, rows, levels)
+
+
+def swap_pairs(value):
+    lane = lax.broadcasted_iota(jnp.int32, value.shape, 1)
+    return jnp.where(lane % 2 == 1, pltpu.roll(value, 1, 1), pltpu.roll(value, LANES - 1, 1))
+
+
+def edge_lanes(sides, i, group):
+    m, part = group // PARTS, group % PARTS
+    rows = LANES // (2 * PARTS)
+    moved = pltpu.roll(sides[m * GROUP : (m + 1) * GROUP, :], LANES - 1 - 2 * slot_of(i, part, rows), 1)
+    lane = lane_iota()
+    return jnp.where((lane == 0) | (lane == LANES - 1), moved, 0.0)
+
+
+def border_again_kernel(rows, levels, coupling, floor, other, ends, columns, wind_ends, wind_dense, dense_g, *rest):
+    *halos, s_even, s_odd, packed, sides = rest
+    before, after = read_sides(halos)
+    sides[...] = swap_pairs(merged(halos[1], halos[2], slice(None)))
+    half = columns.shape[0] // 2
     groups = levels // GROUP
+    outer = [before(slice(None)), after(slice(None))]
+    full = []
+    for k, i in enumerate((0, rows - 1)):
+        edges = jnp.concatenate([edge_lanes(sides, i, group) for group in range(2 * groups)], axis=0)
+        value = ends[k] + outer[k] + edges
+        parts = []
+        for f in range(2):
+            part = value[f * levels : (f + 1) * levels]
+            at = f * rows + i
+            parts.append(with_first(part, couple_adjoint(part[0:1], other[at : at + 1, :], coupling[i : i + 1, :])))
+        full.append(jnp.concatenate(parts, axis=0))
+    end_rows(full, s_even, s_odd, wind_ends, levels)
+    dense = columns[...] + sides[...]
+    corners = []
+    for m in range(2 * groups // PARTS):
+        total = jnp.zeros((GROUP, LANES), jnp.float32)
+        for part in range(PARTS):
+            at = slice((m * PARTS + part) * GROUP, (m * PARTS + part + 1) * GROUP)
+            for k, i in enumerate((0, rows - 1)):
+                total = pack_into(total, outer[k][at], slot_of(i, part, rows))
+        corners.append(total)
+    dense = dense + jnp.concatenate(corners, axis=0)
+    for f in range(2):
+        mine = dense_row(floor, f * rows, rows)
+        mixed = couple_adjoint(mine, dense_row(other, f * rows, rows), dense_g[0:1, :])
+        dense = level0_row(dense, mixed, f)
+    dense_products(packed, dense, wind_dense)
+
+
+def adjoint_rows(rows, levels, cells, wind_cells, out_cells, leaving, take, each):
+    groups = levels // GROUP
+    cells[0] = jnp.zeros_like(cells[0])
+    cells[rows + 1] = jnp.zeros_like(cells[0])
+    wind_cells[0] = jnp.zeros_like(wind_cells[0])
+    wind_cells[rows + 1] = jnp.zeros_like(wind_cells[0])
+    take(0)
 
     def row(i, _):
-        w_copy(i).wait()
+        @pl.when(i < rows - 1)
+        def _():
+            take(i + 1)
+
         for m in range(2 * groups // PARTS):
             f, start = m * PARTS // groups, m * PARTS % groups
             values = []
             for group in range(start, start + PARTS):
-                value = field[i, pl.ds(f * levels + group * GROUP, GROUP), :]
-                if group == 0:
-                    value = coupled(couple_adjoint, value, other, coupling, i, f, rows)
-                    bottom[i, pl.ds(f * GROUP, GROUP), :] = value
-                values.append(with_products(value, w_cells[i, pl.ds(group * GROUP, GROUP), :]))
-            pack_block(packed, values, i, m)
+                value = adjoint_point(cells, wind_cells, i, f, group, levels)
+                out_cells[i, pl.ds(f * levels + group * GROUP, GROUP), :] = value
+                values.append(value)
+            each(i, m, f, start, values)
+        leaving.start(i)
         return 0
 
     lax.fori_loop(0, rows, row, 0)
-    for copy in u_copies:
-        copy.wait()
-    for f in range(2):
-        ends = []
-        for i in (0, rows - 1):
-            low = bottom[i, pl.ds(f * GROUP, GROUP), :]
-            ends.append(jnp.concatenate([low, field[i, pl.ds(f * levels + GROUP, levels - GROUP), :]], axis=0))
-        put_strip(
-            s_even, s_odd, pl.ds(f * levels, levels), products(ends[0], u_cells[0])[1], products(ends[1], u_cells[1])[0]
-        )
-
-
-def adjoint_kernel(rows, levels, coupling, bottom, other_next, field, winds, *rest):
-    *halos, out, s_even, s_odd, packed, cells, wind_cells, sides, sems = rest
+
+
+def first_adjoint_kernel(
+    rows, levels, coupling, other, field, winds, out, ends, columns, low0, cells, wind_cells, out_cells, sems
+):
     incoming = Rows(field, cells, sems.at[0], rows, False, 1)
     wind_in = Rows(winds, wind_cells, sems.at[1], rows, True, 1)
     start_rows(rows, incoming, wind_in)
-    packed[...] = jnp.zeros_like(packed)
-    groups = levels // GROUP
-    adjoint_outside(halos, cells, wind_cells, sides, rows)
+    leaving = Out(out_cells, out, sems.at[2], rows, False)
+    columns[...] = jnp.zeros_like(columns)
 
     def take(i):
         incoming.wait(i)
         wind_in.wait(i)
         for f in range(2):
-            cells[i + 1, pl.ds(f * levels, GROUP), :] = bottom[i, pl.ds(f * GROUP, GROUP), :]
-
-    take(0)
-
-    def row(i, _):
-        @pl.when(i < rows - 1)
-        def _():
-            take(i + 1)
-
-        for m in range(2 * groups // PARTS):
-            f, start = m * PARTS // groups, m * PARTS % groups
-            values = []
-            for group in range(start, start + PARTS):
-                value = adjoint_point(cells, wind_cells, sides, i, f, group, levels)
-                if group == 0:
-                    value = coupled(couple_adjoint, value, other_next, coupling, i, f, rows)
-                out[i, pl.ds(f * levels + group * GROUP, GROUP), :] = value
-                values.append(with_products(value, wind_cells[i + 1, pl.ds(levels + group * GROUP, GROUP), :]))
-            pack_block(packed, values, i, m)
-        return 0
-
-    lax.fori_loop(0, rows, row, 0)
-    for f in range(2):
-        at = pl.ds(f * levels, levels)
-        first = products(out[0, at, :], wind_cells[1, pl.ds(0, levels), :])[1]
-        last = products(out[rows - 1, at, :], wind_cells[rows, pl.ds(0, levels), :])[0]
-        put_strip(s_even, s_odd, at, first, last)
-
-
-def adjoint_outside(halos, cells, wind_cells, sides, rows):
-    merge_columns(halos[1], halos[2], sides)
-    before, after = read_sides(halos)
-    cells[0] = before(slice(None)) / HORIZ_MIX
-    cells[rows + 1] = after(slice(None)) / HORIZ_MIX
-    wind_cells[0] = jnp.zeros_like(wind_cells[0])
-    wind_cells[rows + 1] = jnp.zeros_like(wind_cells[0])
-
-
-def final_kernel(rows, levels, scale, field, winds, state, *rest):
-    *halos, out, cells, wind_cells, state_cells, out_cells, sides, sems = rest
+            at = pl.ds(f * levels, GROUP)
+            cells[i + 1, at, :] = coupled(couple_adjoint, cells[i + 1, at, :], other, coupling, i, f, rows)
+
+    def each(i, m, f, start, values):
+        if start == 0:
+            low0[pl.ds(f * rows + i, 1), :] = values[0][0:1]
+        pack_block(columns, values, i, m)
+
+    adjoint_rows(rows, levels, cells, wind_cells, out_cells, leaving, take, each)
+    ends[0] = out_cells[0]
+    ends[1] = out_cells[rows - 1]
+    leaving.finish()
+
+
+def second_adjoint_kernel(rows, levels, coupling, other, field, winds, *rest):
+    *halos, out, cells, wind_cells, out_cells, sides, sems = rest
     incoming = Rows(field, cells, sems.at[0], rows, False, 1)
     wind_in = Rows(winds, wind_cells, sems.at[1], rows, True, 1)
-    state_in = Rows(state, state_cells, sems.at[2], rows, True, 0)
-    start_rows(rows, incoming, wind_in, state_in)
+    start_rows(rows, incoming, wind_in)
+    leaving = Out(out_cells, out, sems.at[2], rows, False)
+    sides[...] = swap_pairs(merged(halos[1], halos[2], slice(None)))
+    before, after = read_sides(halos)
     groups = levels // GROUP
-    adjoint_outside(halos, cells, wind_cells, sides, rows)
-    incoming.wait(0)
-    wind_in.wait(0)
-
-    def out_copy(i):
-        return pltpu.make_async_copy(out_cells.at[i], out.at[:, i], sems.at[3, i])
-
-    def row(i, _):
-        @pl.when(i < rows - 1)
+
+    def take(i):
+        incoming.wait(i)
+        wind_in.wait(i)
+        for group in range(2 * groups):
+            at = pl.ds(group * GROUP, GROUP)
+            value = cells[i + 1, at, :] + edge_lanes(sides, i, group)
+            if group % groups == 0:
+                f = group // groups
+                value = value + jnp.where(i == 0, before(at), 0.0) + jnp.where(i == rows - 1, after(at), 0.0)
+                value = coupled(couple_adjoint, value, other, coupling, i, f, rows)
+            cells[i + 1, at, :] = value
+
+    def add_outer(i, side):
+        for f in range(2):
+            at = pl.ds(f * levels + GROUP, levels - GROUP)
+            cells[i + 1, at, :] = cells[i + 1, at, :] + side(at)
+
+    def take_all(i):
+        take(i)
+
+        @pl.when(i == 0)
         def _():
-            incoming.wait(i + 1)
-            wind_in.wait(i + 1)
-
+            add_outer(0, before)
+
+        @pl.when(i == rows - 1)
+        def _():
+            add_outer(rows - 1, after)
+
+    adjoint_rows(rows, levels, cells, wind_cells, out_cells, leaving, take_all, lambda *_: None)
+    leaving.finish()
+
+
+def final_kernel(rows, levels, scale, field, state, *rest):
+    *halos, out, cells, state_cells, sides, sems = rest
+    incoming = Rows(field, cells, sems.at[0], rows, False, 0)
+    state_in = Rows(state, state_cells, sems.at[1], rows, True, 0)
+    start_rows(rows, incoming, state_in)
+    leaving = Out(cells, out, sems.at[2], rows, True)
+    sides[...] = swap_pairs(merged(halos[1], halos[2], slice(None)))
+    before, after = read_sides(halos)
+    groups = levels // GROUP
+
+    def add(i, outer):
+        incoming.wait(i)
         state_in.wait(i)
-        for group in range(groups):
-            for f in range(2):
-                at = pl.ds(f * levels + group * GROUP, GROUP)
-                value = adjoint_point(cells, wind_cells, sides, i, f, group, levels)
-                out_cells[i, at, :] = value + scale[at, :] * state_cells[i, at, :]
-        out_copy(i).start()
+        for group in range(2 * groups):
+            at = pl.ds(group * GROUP, GROUP)
+            value = cells[i, at, :] + scale[at, :] * state_cells[i, at, :] + edge_lanes(sides, i, group)
+            cells[i, at, :] = value if outer is None else value + outer(at)
+        leaving.start(i)
         return 0
 
-    lax.fori_loop(0, rows, row, 0)
-    for i in range(rows):
-        out_copy(i).wait()
+    add(0, before)
+    lax.fori_loop(1, rows - 1, lambda i, _: add(i, None), 0)
+    add(rows - 1, after)
+    leaving.finish()
 
 
 def split(value, terms):
@@ -523,11 +644,12 @@
                 ]
 
 
-def observe_kernel(rows, width, tiles, cap, records, cols, adjoint, low0, low1, col_cells, sel, precs, both, spread, sems):
-    part_rows = 2 * width // sems.shape[0]
+def innovate_kernel(rows, width, tiles, cap, records, cols, spread, sel, ends, columns, floor, *scratch):
+    col_cells, sel_cells, border_sel, places, precs, both, spread_cells, sems = scratch
+    chunks = 8
     copies = []
-    for part in range(sems.shape[0]):
-        at = pl.ds(part * part_rows, part_rows)
+    for part in range(chunks):
+        at = pl.ds(part * (2 * width // chunks), 2 * width // chunks)
         copies.append(pltpu.make_async_copy(cols.at[at], col_cells.at[at], sems.at[part]))
         copies[-1].start()
     halves = width // LANES
@@ -536,7 +658,14 @@
     own = lax.broadcasted_iota(jnp.int32, (cap, LANES), 1) == lax.broadcasted_iota(jnp.int32, (cap, LANES), 0)
     ones = jnp.ones((LANES, LANES), jnp.bfloat16)
     step = 256
-    lane = lax.broadcasted_iota(jnp.int32, (step, LANES), 1).astype(jnp.float32)
+    lane = lax.broadcasted_iota(jnp.int32, (step, LANES), 1)
+    border = (rows - 1 - lane // (2 * PARTS)) * LANES + jnp.where(lane % 2 == 1, 0, LANES - 1)
+    border = jnp.where(lane % (2 * PARTS) < 2, border, -1).astype(jnp.float32)
+    lane = lane.astype(jnp.float32)
+
+    def sel_copy(block):
+        at = pl.ds(pl.multiple_of(block * step, step), step)
+        return pltpu.make_async_copy(sel_cells.at[at], sel.at[at], sems.at[chunks + block])
 
     def select(block, _):
         sources = step // cap
@@ -549,16 +678,21 @@
             return sum(dot(term, ones, (1, 0)) for term in terms)
 
         at = pl.ds(pl.multiple_of(block * step, step), step)
-        column = spread_out(0) - lane
+        place = spread_out(0)
+        column = place - lane
         precs[at, :] = spread_out(1)
         for i in range(rows):
-            sel[at, i * LANES : (i + 1) * LANES] = jnp.where(column == float(i * LANES), 1.0, 0.0).astype(jnp.bfloat16)
+            sel_cells[at, i * LANES : (i + 1) * LANES] = jnp.where(column == float(i * LANES), 1.0, 0.0).astype(
+                jnp.bfloat16
+            )
+        border_sel[at, :] = jnp.where(place == border, 1.0, 0.0).astype(jnp.bfloat16)
+        sel_copy(block).start()
         return 0
 
     lax.fori_loop(0, count // step, select, 0)
     for copy in copies:
         copy.wait()
-    both[...] = dot(sel[...], col_cells[...], (1, 1))
+    both[...] = dot(sel_cells[...], col_cells[...], (1, 1))
 
     def weigh(block, _):
         at = pl.ds(pl.multiple_of(block * LANES, LANES), LANES)
@@ -577,17 +711,58 @@
         innovation = jnp.sum(total, axis=1, keepdims=True) * precs[at, :]
         for half in range(halves):
             high, low = split((ops[half] * innovation).T, 2)
-            spread[half * LANES : (half + 1) * LANES, at] = high
-            spread[width + half * LANES : width + (half + 1) * LANES, at] = low
+            spread_cells[half * LANES : (half + 1) * LANES, at] = high
+            spread_cells[width + half * LANES : width + (half + 1) * LANES, at] = low
         return 0
 
     lax.fori_loop(0, count // LANES, weigh, 0)
-    sums = dot(spread[...], sel[...], (1, 0))
+    spread_copy = pltpu.make_async_copy(spread_cells, spread, sems.at[chunks + count // step])
+    spread_copy.start()
+
+    def cells_of(ones_at):
+        terms = dot(spread_cells[...], ones_at, (1, 0))
+        return terms[:width] + terms[width:]
+
+    ends[0] = cells_of(sel_cells[:, 0:LANES])
+    ends[1] = cells_of(sel_cells[:, (rows - 1) * LANES : rows * LANES])
+    thin = cells_of(border_sel[...])
+    for m in range(width // (GROUP * PARTS)):
+        total = thin[m * PARTS * GROUP : (m * PARTS + 1) * GROUP]
+        for part in range(1, PARTS):
+            at = (m * PARTS + part) * GROUP
+            total = total + pltpu.roll(thin[at : at + GROUP], 2 * part, 1)
+        columns[m * GROUP : (m + 1) * GROUP, :] = total
+    half = columns.shape[0] // 2
+    floor[...] = jnp.zeros_like(floor)
+    for f in range(2):
+        for k in range(2):
+            floor[2 * k + f : 2 * k + f + 1, :] = ends[k, f * (width // 2) : f * (width // 2) + 1, :]
+        floor[4 + f : 5 + f, :] = columns[f * half : f * half + 1, :]
+    for block in range(count // step):
+        sel_copy(block).wait()
+    spread_copy.wait()
+
+
+def scatter_kernel(rows, width, spread, sel, adjoint, low0, low1, spread_cells, sel_cells, out_cells, sems):
+    count = sel.shape[0]
+    chunks = 4
+    copies = [pltpu.make_async_copy(spread, spread_cells, sems.at[2 * rows])]
+    for part in range(chunks):
+        at = pl.ds(part * (count // chunks), count // chunks)
+        copies.append(pltpu.make_async_copy(sel.at[at], sel_cells.at[at], sems.at[rows + part]))
+    for copy in copies:
+        copy.start()
+    for copy in copies:
+        copy.wait()
+    leaving = Out(out_cells, adjoint, sems, rows, False)
+    sums = dot(spread_cells[...], sel_cells[...], (1, 0))
     for i in range(rows):
         lanes = slice(i * LANES, (i + 1) * LANES)
-        adjoint[i] = sums[:width, lanes] + sums[width:, lanes]
+        out_cells[i] = sums[:width, lanes] + sums[width:, lanes]
+        leaving.start(i)
         for f in range(2):
-            put_low((low0, low1), adjoint[i, f * (width // 2) : f * (width // 2) + GROUP, :], i, f, rows)
+            put_low((low0, low1), out_cells[i, f * (width // 2) : f * (width // 2) + GROUP, :], i, f, rows)
+    leaving.finish()
 
 
 def local(state_incr, winds, coupling, background, obs_dest, obs_col, obs_op, obs_prec):
@@ -603,7 +778,6 @@
 
     vmem = pl.BlockSpec(memory_space=pltpu.VMEM)
     anywhere = pl.BlockSpec(memory_space=pl.ANY)
-    hbm = pl.BlockSpec(memory_space=pltpu.HBM)
     own = pltpu.VMEM((rows, width, LANES), jnp.float32)
     framed = pltpu.VMEM((rows + 2, width, LANES), jnp.float32)
     packed_shape = f32(groups // PARTS * GROUP, LANES)
@@ -616,9 +790,13 @@
     def sems(*shape):
         return pltpu.SemaphoreType.DMA(shape)
 
-    def run(body, out_shape, scratch, args, far=(), **kw):
+    def run(body, out_shape, scratch, args, far=(), out_far=()):
         specs = [anywhere if k in far else vmem for k in range(len(args))]
-        return call(functools.partial(body, rows, levels), out_shape, scratch, in_specs=specs, **kw)(*args)
+        outs = [anywhere if k in out_far else vmem for k in range(len(out_shape))]
+        return call(body, out_shape, scratch, in_specs=specs, out_specs=outs)(*args)
+
+    def on_rows(body):
+        return functools.partial(body, rows, levels)
 
     def swap_floor(floor):
         return lax.ppermute(floor, "comp", [(0, 1), (1, 0)])
@@ -626,9 +804,11 @@
     state = state_incr.reshape(width, rows, lanes)
     wind = winds.reshape(width, rows, lanes)
     floor_winds = winds[0, :, 0]
+    slots = tiles * cap
+    thin_shape = f32(GROUP, LANES)
 
     s_even, s_odd, packed, low0, low1 = run(
-        edges_kernel, strip_shapes + [low_shape] * 2, [own, sems(rows)], (state,), far=(0,)
+        on_rows(edges_kernel), strip_shapes + [low_shape] * 2, [own, sems(rows)], (state,), far=(0,)
     )
     halos = exchange((s_even, s_odd), packed)
 
@@ -638,66 +818,92 @@
     send, halos = lax.optimization_barrier((send, halos))
     records = lax.all_to_all(send, ("gx", "gy"), split_axis=0, concat_axis=0, tiled=True)
 
-    floor = run(forward_floor_kernel, low_shape, [], (low0, low1, floor_winds, *halos))
-    field, s_even, s_odd, packed, low0, low1 = run(
-        functools.partial(forward_kernel, True, False),
-        [field_shape] + strip_shapes + [low_shape] * 2,
-        [framed, own, sides, sems(2, rows)],
+    (floor,) = run(on_rows(forward_floor_kernel), [low_shape], [], (low0, low1, floor_winds, *halos))
+    field, s_even, s_odd, packed, low0, low1, wind_ends, wind_dense, dense_g = run(
+        on_rows(functools.partial(forward_kernel, True, False)),
+        [field_shape] + strip_shapes + [low_shape] * 2 + [f32(2, levels, LANES), f32(groups // PARTS * GROUP // 2, LANES), thin_shape],
+        [framed, own, own, sides, sems(3, rows)],
         (coupling, swap_floor(floor), state, wind, *halos),
         far=(2, 3),
+        out_far=(0,),
     )
     halos = exchange((s_even, s_odd), packed)
-    floor = run(forward_floor_kernel, low_shape, [], (low0, low1, floor_winds, *halos))
-    cols = run(
-        functools.partial(forward_kernel, False, True),
-        jax.ShapeDtypeStruct(*cols_shape),
+    (floor,) = run(on_rows(forward_floor_kernel), [low_shape], [], (low0, low1, floor_winds, *halos))
+    (cols,) = run(
+        on_rows(functools.partial(forward_kernel, False, True)),
+        [jax.ShapeDtypeStruct(*cols_shape)],
         [framed, own, sides, sems(2, rows), pltpu.VMEM(*cols_shape), sems(rows)],
         (coupling, swap_floor(floor), field, wind, *halos),
         far=(2, 3),
-        out_specs=hbm,
-    )
-
-    slots = tiles * cap
-    adjoint, low0, low1 = call(
-        functools.partial(observe_kernel, rows, width, tiles, cap),
-        [field_shape, low_shape, low_shape],
+        out_far=(0,),
+    )
+
+    spread_shape = ((2 * width, slots), jnp.bfloat16)
+    sel_shape = ((slots, rows * LANES), jnp.bfloat16)
+    spread, sel, ends, columns, border_floor = run(
+        functools.partial(innovate_kernel, rows, width, tiles, cap),
+        [jax.ShapeDtypeStruct(*spread_shape), jax.ShapeDtypeStruct(*sel_shape), f32(2, width, LANES), packed_shape, thin_shape],
         [
             pltpu.VMEM(*cols_shape),
-            pltpu.VMEM((slots, rows * LANES), jnp.bfloat16),
+            pltpu.VMEM(*sel_shape),
+            pltpu.VMEM((slots, LANES), jnp.bfloat16),
+            pltpu.VMEM((slots, LANES), jnp.float32),
             pltpu.VMEM((slots, LANES), jnp.float32),
             pltpu.VMEM((slots, 2 * width), jnp.float32),
-            pltpu.VMEM((2 * width, slots), jnp.bfloat16),
-            sems(8),
+            pltpu.VMEM(*spread_shape),
+            sems(8 + slots // 256 + 1),
         ],
-        limit=OBSERVE_VMEM,
-        in_specs=[vmem, hbm],
-    )(records, cols)
-
-    other = swap_floor(low0)
-    bottom, s_even, s_odd, packed = run(
-        adjoint_pack_kernel,
-        [f32(rows, fields * GROUP, LANES)] + strip_shapes,
-        [pltpu.VMEM((rows, levels, LANES), jnp.float32), pltpu.VMEM((2, levels, LANES), jnp.float32), sems(rows + 2)],
-        (coupling, other, adjoint, wind),
-        far=(3,),
-    )
-    halos = exchange((s_even, s_odd), packed)
-    floor = run(adjoint_floor_kernel, low_shape, [], (coupling, other, low0, low1, floor_winds, *halos))
-    adjoint, s_even, s_odd, packed = run(
-        adjoint_kernel,
-        [field_shape] + strip_shapes,
-        [framed, framed, sides, sems(2, rows)],
-        (coupling, bottom, swap_floor(floor), adjoint, wind, *halos),
-        far=(3, 4),
-    )
-    halos = exchange((s_even, s_odd), packed)
-    result = run(
-        final_kernel,
-        f32(width, rows, LANES),
-        [framed, framed, own, own, sides, sems(4, rows)],
-        (scale, adjoint, wind, state, *halos),
-        far=(1, 2, 3),
-        out_specs=hbm,
+        (records, cols),
+        far=(1,),
+        out_far=(0, 1),
+    )
+    strips = run(
+        on_rows(border_kernel),
+        strip_shapes,
+        [],
+        (coupling, swap_floor(border_floor), ends, columns, wind_ends, wind_dense, dense_g),
+    )
+    halos = exchange(strips[:2], strips[2])
+    adjoint, low0, _ = run(
+        functools.partial(scatter_kernel, rows, width),
+        [field_shape, low_shape, low_shape],
+        [pltpu.VMEM(*spread_shape), pltpu.VMEM(*sel_shape), own, sems(2 * rows + 1)],
+        (spread, sel),
+        far=(0, 1),
+        out_far=(0,),
+    )
+    adjoint, ends, columns, low0 = run(
+        on_rows(first_adjoint_kernel),
+        [field_shape, f32(2, width, LANES), packed_shape, low_shape],
+        [framed, framed, own, sems(3, rows)],
+        (coupling, swap_floor(low0), adjoint, wind),
+        far=(2, 3),
+        out_far=(0,),
+    )
+    (floor,) = run(on_rows(floor_kernel), [low_shape], [], (low0, *halos))
+    other = swap_floor(floor)
+    strips = run(
+        on_rows(border_again_kernel),
+        strip_shapes,
+        [sides],
+        (coupling, floor, other, ends, columns, wind_ends, wind_dense, dense_g, *halos),
+    )
+    last_halos = exchange(strips[:2], strips[2])
+    (adjoint,) = run(
+        on_rows(second_adjoint_kernel),
+        [field_shape],
+        [framed, framed, own, sides, sems(3, rows)],
+        (coupling, other, adjoint, wind, *halos),
+        far=(2, 3),
+        out_far=(0,),
+    )
+    (result,) = run(
+        on_rows(final_kernel),
+        [f32(width, rows, LANES)],
+        [own, own, sides, sems(3, rows)],
+        (scale, adjoint, state, *last_halos),
+        far=(1, 2),
+        out_far=(0,),
     )
     return result.reshape(state_incr.shape)
 

time: 112 us -> 116 us (1.036)
  Pallas kernels: 55.6 us -> 65.8 us
  waiting for transfers between devices: 20.3 us -> 12.9 us
  local copies, waits for them, and re-layouts: 6.21 us -> 7.37 us
    ppermute x12, waiting for transfers between devices: 15.7 us -> 6.28 us  [pair_swap(): return lax.ppermute(block, axis, route)]
    pallas_call x10 -> x13, Pallas kernels: 53.6 us -> 62.7 us  [run(): return call(body, out_shape, scratch, in_specs=specs, out_specs=outs)(*args)]
    ppermute x4 -> x5, waiting for transfers between devices: 4.53 us -> 6.61 us  [swap_floor(): return lax.ppermute(floor, 'comp', [(0, 1), (1, 0)])]
    squeeze x1, local copies, waits for them, and re-layouts: 0.01 us -> 1.31 us  [local(): floor_winds = winds[0, :, 0]]
    unnamed x24 -> x38, local copies, waits for them, and re-layouts: 6.12 us -> 5.3 us
  transfers between devices with their start and end apart: 17 -> 18, of which waited for: 9 -> 8; matrix products, arithmetic and copies ran while one was open for 0% -> 1% of each run, Pallas kernels for 18% -> 37%
where the time goes in v4:
time: 116 us; the launch traced here: 115 us
  Pallas kernels  65.8 us (57%)
  starting transfers between devices  28.9 us (25%)
  waiting for transfers between devices  12.9 us (11%)
  local copies, waits for them, and re-layouts  7.37 us (6%)
    pallas_call x13, Pallas kernels, run(): return call(body, out_shape, scratch, in_specs=specs, out_specs=outs)(*args)  62.7 us
    ppermute x12, starting transfers between devices, pair_swap(): return lax.ppermute(block, axis, route)  23.1 us
    ppermute x5, waiting for transfers between devices, swap_floor(): return lax.ppermute(floor, 'comp', [(0, 1), (1, 0)])  6.61 us
    ppermute x12, waiting for transfers between devices, pair_swap(): return lax.ppermute(block, axis, route)  6.28 us
    all_to_all x1, starting transfers between devices, local(): lax.all_to_all(send, ('gx', 'gy'), split_axis=0, concat_axis=0, tiled=True)  5.35 us
    unnamed x38, local copies, waits for them, and re-layouts  5.3 us
    pallas_call x1, Pallas kernels, local(): call(functools.partial(route_kernel, tiles, cap), f32(tiles, halves * cap...  3.1 us
  transfers between devices with their start and end apart: 18, of which 8 were waited for; matrix products, arithmetic and copies ran while one was open for 1% of the time, Pallas kernels for 37%

profile of v4, /device:TPU:8, one launch (start us, length us, event | category | flops | bytes accessed | tf_op | source)
XLA Modules:
  0.0 115.2 jit_solution(5692063247996173799)
XLA Ops:
  0.0 3.4 %shard_map.83 = (f32[256,128]{1,0:T(8,128)}, f32[256,128]{1,0:T(8,128)}, f32[64,128]{1,0:T(8,128)}, f32[32,128]{1,0:T(8,128)}, f32[32,128]{1,0:T(8,128)}) custom-call(f32[256,16,128]{2,1,0:T(8,128)} %bitcast.15), custom_call_target="tpu_custom_call" | custom-call | tf_op jit(solution)/shard_map/pallas_call | solution.py:796
  3.4 1.6 %collective-permute-start = (f32[256,128]{1,0:T(8,128)}, f32[256,128]{1,0:T(8,128)S(1)}, u32[]{:S(2)}, u32[]{:S(2)}) collective-permute-start(f32[256,128]{1,0:T(8,128)} %get-tuple-element.36), channel_id=1, source_target_pairs={{0,8},{8,0},{1,9},{9,1},{2,10},{10,2},{3,11},{11,3},{4,12},{12,4},... | collective-permute-start | bytes 393224 | tf_op jit(solution)/shard_map/ppermute | solution.py:45
  5.0 1.5 %collective-permute-start.1 = (f32[64,128]{1,0:T(8,128)}, f32[64,128]{1,0:T(8,128)S(1)}, u32[]{:S(2)}, u32[]{:S(2)}) collective-permute-start(f32[64,128]{1,0:T(8,128)} %get-tuple-element.37), channel_id=1, source_target_pairs={{0,1},{1,0},{2,3},{3,2},{4,5},{5,4},{6,7},{7,6},{8,9},{9,8},{10,11... | collective-permute-start | bytes 98312 | tf_op jit(solution)/shard_map/ppermute | solution.py:45
  6.5 2.3 %collective-permute-start.2 = (f32[64,128]{1,0:T(8,128)}, f32[64,128]{1,0:T(8,128)S(1)}, u32[]{:S(2)}, u32[]{:S(2)}) collective-permute-start(f32[64,128]{1,0:T(8,128)} %get-tuple-element.37), channel_id=1, source_target_pairs={{1,2},{2,1},{3,4},{4,3},{5,6},{6,5},{9,10},{10,9},{11,12},{12,11},... | collective-permute-start | bytes 98312 | tf_op jit(solution)/shard_map/ppermute | solution.py:45
  8.8 3.1 %shard_map.82 = f32[16,136,128]{2,1,0:T(8,128)} custom-call(s32[1,512]{1,0:T(1,128)} %bitcast.18, s32[1,512]{1,0:T(1,128)} %bitcast.19, f32[1,512]{1,0:T(1,128)} %bitcast.20, f32[512,256]{1,0:T(8,128)} %op.1), custom_call_target="tpu_custom_call" | custom-call | tf_op jit(solution)/shard_map/pallas_call | solution.py:815
  11.9 1.5 %collective-permute-done.2.rest_2_ = f32[64,128]{1,0:T(8,128)S(1)} collective-permute-done((f32[64,128]{1,0:T(8,128)}, f32[64,128]{1,0:T(8,128)S(1)}, u32[]{:S(2)}, u32[]{:S(2)}) %collective-permute-start.2) | collective-permute-done | bytes 32800 | tf_op jit(solution)/shard_map/ppermute | solution.py:45
  13.4 5.3 %all-to-all-start = ((f32[16,136,128]{2,1,0:T(8,128)}), f32[16,136,128]{2,1,0:T(8,128)S(1)}, u32[]{:S(2)}, u32[]{:S(2)}) async-start(f32[16,136,128]{2,1,0:T(8,128)} %shard_map.82), calls=%async_computation | async-start | bytes 2228224 | tf_op jit(solution)/shard_map/all_to_all | solution.py:819
  18.8 1.3 %slice_bitcast_fusion.winds = f32[2,16,128]{2,1,0:T(8,128)} fusion(f32[1,2,128,16,128]{4,3,2,1,0:T(8,128)} %param.9), kind=kLoop, calls=%fused_computation | loop fusion | bytes 32768 | tf_op jit(solution)/shard_map/squeeze | solution.py:806
  20.1 1.7 %shard_map.84 = f32[32,128]{1,0:T(8,128)} custom-call(f32[32,128]{1,0:T(8,128)} %get-tuple-element.39.low0, f32[32,128]{1,0:T(8,128)} %get-tuple-element.40.low1, f32[2,16,128]{2,1,0:T(8,128)} %slice_bitcast_fusion.winds, f32[256,128]{1,0:T(8,128)} %copy-done.2, f32[64,128]{1,0:T(8,128)} %copy-done.6, f32[64,128]{1,0:T(8,128)} %copy-done.7), custom_call_target="tpu_custom_call" | custom-call | tf_op jit(solution)/shard_map/pallas_call | solution.py:796
  21.8 1.4 %collective-permute-done.3.other = f32[32,128]{1,0:T(8,128)S(1)} collective-permute-done((f32[32,128]{1,0:T(8,128)}, f32[32,128]{1,0:T(8,128)S(1)}, u32[]{:S(2)}, u32[]{:S(2)}) %collective-permute-start.3) | collective-permute-done | bytes 16416 | tf_op jit(solution)/shard_map/ppermute | solution.py:802
  23.8 8.4 %shard_map.85 = (f32[16,256,128]{2,1,0:T(8,128)}, f32[256,128]{1,0:T(8,128)}, f32[256,128]{1,0:T(8,128)}, f32[64,128]{1,0:T(8,128)}, f32[32,128]{1,0:T(8,128)}, ...) custom-call(f32[16,128]{1,0:T(8,128)} %coupling.11, f32[32,128]{1,0:T(8,128)} %copy-done.14, ...), custom_call_target="tpu_custom_call" | custom-call | tf_op jit(solution)/shard_map/pallas_call | solution.py:796
  32.2 1.5 %collective-permute-start.4 = (f32[256,128]{1,0:T(8,128)}, f32[256,128]{1,0:T(8,128)S(1)}, u32[]{:S(2)}, u32[]{:S(2)}) collective-permute-start(f32[256,128]{1,0:T(8,128)} %get-tuple-element.46), channel_id=1, source_target_pairs={{0,8},{8,0},{1,9},{9,1},{2,10},{10,2},{3,11},{11,3},{4,12},{12,4},... | collective-permute-start | bytes 393224 | tf_op jit(solution)/shard_map/ppermute | solution.py:45
  33.7 1.5 %collective-permute-start.5 = (f32[64,128]{1,0:T(8,128)}, f32[64,128]{1,0:T(8,128)S(1)}, u32[]{:S(2)}, u32[]{:S(2)}) collective-permute-start(f32[64,128]{1,0:T(8,128)} %get-tuple-element.47), channel_id=1, source_target_pairs={{0,1},{1,0},{2,3},{3,2},{4,5},{5,4},{6,7},{7,6},{8,9},{9,8},{10,11... | collective-permute-start | bytes 98312 | tf_op jit(solution)/shard_map/ppermute | solution.py:45
  35.2 2.5 %collective-permute-start.6 = (f32[64,128]{1,0:T(8,128)}, f32[64,128]{1,0:T(8,128)S(1)}, u32[]{:S(2)}, u32[]{:S(2)}) collective-permute-start(f32[64,128]{1,0:T(8,128)} %get-tuple-element.47), channel_id=1, source_target_pairs={{1,2},{2,1},{3,4},{4,3},{5,6},{6,5},{9,10},{10,9},{11,12},{12,11},... | collective-permute-start | bytes 98312 | tf_op jit(solution)/shard_map/ppermute | solution.py:45
  38.4 4.0 %collective-permute-done.6.rest_2_ = f32[64,128]{1,0:T(8,128)S(1)} collective-permute-done((f32[64,128]{1,0:T(8,128)}, f32[64,128]{1,0:T(8,128)S(1)}, u32[]{:S(2)}, u32[]{:S(2)}) %collective-permute-start.6) | collective-permute-done | bytes 32800 | tf_op jit(solution)/shard_map/ppermute | solution.py:45
  43.1 1.7 %shard_map.86 = f32[32,128]{1,0:T(8,128)} custom-call(f32[32,128]{1,0:T(8,128)} %get-tuple-element.44.low0, f32[32,128]{1,0:T(8,128)} %get-tuple-element.45.low1, f32[2,16,128]{2,1,0:T(8,128)} %slice_bitcast_fusion.winds, f32[256,128]{1,0:T(8,128)} %copy-done.3, f32[64,128]{1,0:T(8,128)} %copy-done.8, f32[64,128]{1,0:T(8,128)} %copy-done.9), custom_call_target="tpu_custom_call" | custom-call | tf_op jit(solution)/shard_map/pallas_call | solution.py:796
  44.8 1.4 %collective-permute-done.7.other = f32[32,128]{1,0:T(8,128)S(1)} collective-permute-done((f32[32,128]{1,0:T(8,128)}, f32[32,128]{1,0:T(8,128)S(1)}, u32[]{:S(2)}, u32[]{:S(2)}) %collective-permute-start.7) | collective-permute-done | bytes 16416 | tf_op jit(solution)/shard_map/ppermute | solution.py:802
  46.8 6.6 %shard_map.87.cols = bf16[512,2048]{1,0:T(8,128)(2,1)} custom-call(f32[16,128]{1,0:T(8,128)} %coupling.11, f32[32,128]{1,0:T(8,128)} %copy-done.16, f32[16,256,128]{2,1,0:T(8,128)} %get-tuple-element.48.field, f32[256,16,128]{2,1,0:T(8,128)} %bitcast.12, f32[256,128]{1,0:T(8,128)} %copy-done.3, f32[64,128]{1,0:T(8,128)} %copy-done.8, f32[64,128]{1,0:T(8,128)} %copy-done.9), custom_call_target="tpu_custom_call" | custom-call | tf_op jit(solution)/shard_map/pallas_call | solution.py:796
  54.4 9.6 %shard_map.88 = (bf16[512,1024]{1,0:T(8,128)(2,1)}, bf16[1024,2048]{1,0:T(8,128)(2,1)}, f32[2,256,128]{2,1,0:T(8,128)}, f32[64,128]{1,0:T(8,128)}, f32[8,128]{1,0:T(8,128)}) custom-call(f32[16,136,128]{2,1,0:T(8,128)} %copy-done, bf16[512,2048]{1,0:T(8,128)(2,1)} %shard_map.87.cols), custom_call_target="tpu_custom_call" | custom-call | tf_op jit(solution)/shard_map/pallas_call | solution.py:796
  64.2 1.2 %collective-permute-done.9.other = f32[8,128]{1,0:T(8,128)S(1)} collective-permute-done((f32[8,128]{1,0:T(8,128)}, f32[8,128]{1,0:T(8,128)S(1)}, u32[]{:S(2)}, u32[]{:S(2)}) %collective-permute-start.9) | collective-permute-done | bytes 4128 | tf_op jit(solution)/shard_map/ppermute | solution.py:802
  66.0 1.8 %shard_map.91 = (f32[256,128]{1,0:T(8,128)}, f32[256,128]{1,0:T(8,128)}, f32[64,128]{1,0:T(8,128)}) custom-call(f32[16,128]{1,0:T(8,128)} %coupling.11, f32[8,128]{1,0:T(8,128)} %copy-done.17, f32[2,256,128]{2,1,0:T(8,128)} %get-tuple-element.55.ends, f32[64,128]{1,0:T(8,128)} %get-tuple-element.56.columns, f32[2,128,128]{2,1,0:T(8,128)} %get-tuple-element.57.wind_ends, ...), custom_call_target="tpu_custom_call" | custom-call | tf_op jit(solution)/shard_map/pallas_call | solution.py:796
  68.0 4.6 %collective-permute-start.11 = (f32[64,128]{1,0:T(8,128)}, f32[64,128]{1,0:T(8,128)S(1)}, u32[]{:S(2)}, u32[]{:S(2)}) collective-permute-start(f32[64,128]{1,0:T(8,128)} %get-tuple-element.61), channel_id=1, source_target_pairs={{0,1},{1,0},{2,3},{3,2},{4,5},{5,4},{6,7},{7,6},{8,9},{9,8},{10,11... | collective-permute-start | bytes 98312 | tf_op jit(solution)/shard_map/ppermute | solution.py:45
  72.6 1.9 %collective-permute-start.12 = (f32[64,128]{1,0:T(8,128)}, f32[64,128]{1,0:T(8,128)S(1)}, u32[]{:S(2)}, u32[]{:S(2)}) collective-permute-start(f32[64,128]{1,0:T(8,128)} %get-tuple-element.61), channel_id=1, source_target_pairs={{1,2},{2,1},{3,4},{4,3},{5,6},{6,5},{9,10},{10,9},{11,12},{12,11},... | collective-permute-start | bytes 98312 | tf_op jit(solution)/shard_map/ppermute | solution.py:45
  74.5 6.6 %shard_map.89 = (f32[16,256,128]{2,1,0:T(8,128)}, f32[32,128]{1,0:T(8,128)}, f32[32,128]{1,0:T(8,128)}) custom-call(bf16[512,1024]{1,0:T(8,128)(2,1)} %get-tuple-element.49.spread, bf16[1024,2048]{1,0:T(8,128)(2,1)} %get-tuple-element.50.sel), custom_call_target="tpu_custom_call" | custom-call | tf_op jit(solution)/shard_map/pallas_call | solution.py:796
  81.2 1.4 %collective-permute-done.8.other = f32[32,128]{1,0:T(8,128)S(1)} collective-permute-done((f32[32,128]{1,0:T(8,128)}, f32[32,128]{1,0:T(8,128)S(1)}, u32[]{:S(2)}, u32[]{:S(2)}) %collective-permute-start.8) | collective-permute-done | bytes 16416 | tf_op jit(solution)/shard_map/ppermute | solution.py:802
  83.2 7.1 %shard_map.90 = (f32[16,256,128]{2,1,0:T(8,128)}, f32[2,256,128]{2,1,0:T(8,128)}, f32[64,128]{1,0:T(8,128)}, f32[32,128]{1,0:T(8,128)}) custom-call(f32[16,128]{1,0:T(8,128)} %coupling.11, f32[32,128]{1,0:T(8,128)} %copy-done.15, f32[16,256,128]{2,1,0:T(8,128)} %get-tuple-element.52.field, f32[256,16,128]{2,1,0:T(8,128)} %bitcast.13), custom_call_target="tpu_custom_call" | custom-call | tf_op jit(solution)/shard_map/pallas_call | solution.py:796
  91.0 1.7 %shard_map.92.floor = f32[32,128]{1,0:T(8,128)} custom-call(f32[32,128]{1,0:T(8,128)} %get-tuple-element.53.low0, f32[256,128]{1,0:T(8,128)} %copy-done.1, f32[64,128]{1,0:T(8,128)} %copy-done.4, f32[64,128]{1,0:T(8,128)} %copy-done.5), custom_call_target="tpu_custom_call" | custom-call | tf_op jit(solution)/shard_map/pallas_call | solution.py:796
  92.8 1.2 %collective-permute-done.13.other = f32[32,128]{1,0:T(8,128)S(1)} collective-permute-done((f32[32,128]{1,0:T(8,128)}, f32[32,128]{1,0:T(8,128)S(1)}, u32[]{:S(2)}, u32[]{:S(2)}) %collective-permute-start.13) | collective-permute-done | bytes 16416 | tf_op jit(solution)/shard_map/ppermute | solution.py:802
  94.6 2.1 %shard_map.94 = (f32[256,128]{1,0:T(8,128)}, f32[256,128]{1,0:T(8,128)}, f32[64,128]{1,0:T(8,128)}) custom-call(f32[16,128]{1,0:T(8,128)} %coupling.11, f32[32,128]{1,0:T(8,128)} %shard_map.92.floor, f32[32,128]{1,0:T(8,128)} %copy-done.11, f32[2,256,128]{2,1,0:T(8,128)} %get-tuple-element.63.ends, f32[64,128]{1,0:T(8,128)} %get-tuple-element.64.columns, ...), custom_call_target="tpu_custom_call" | custom-call | tf_op jit(solution)/shard_map/pallas_call | solution.py:796
  98.4 3.9 %collective-permute-start.16 = (f32[64,128]{1,0:T(8,128)}, f32[64,128]{1,0:T(8,128)S(1)}, u32[]{:S(2)}, u32[]{:S(2)}) collective-permute-start(f32[64,128]{1,0:T(8,128)} %get-tuple-element.66), channel_id=1, source_target_pairs={{1,2},{2,1},{3,4},{4,3},{5,6},{6,5},{9,10},{10,9},{11,12},{12,11},... | collective-permute-start | bytes 98312 | tf_op jit(solution)/shard_map/ppermute | solution.py:45
  102.3 7.0 %shard_map.93.field = f32[16,256,128]{2,1,0:T(8,128)} custom-call(f32[16,128]{1,0:T(8,128)} %coupling.11, f32[32,128]{1,0:T(8,128)} %copy-done.11, f32[16,256,128]{2,1,0:T(8,128)} %get-tuple-element.62.field, f32[256,16,128]{2,1,0:T(8,128)} %bitcast.14, f32[256,128]{1,0:T(8,128)} %copy-done.1, f32[64,128]{1,0:T(8,128)} %copy-done.4, f32[64,128]{1,0:T(8,128)} %copy-done.5), custom_call_target="tpu_custom_call" | custom-call | tf_op jit(solution)/shard_map/pallas_call | solution.py:796
  110.2 5.0 %shard_map.95 = f32[256,16,128]{2,1,0:T(8,128)} custom-call(f32[256,128]{1,0:T(8,128)} %broadcast_in_dim.8.scale, f32[16,256,128]{2,1,0:T(8,128)} %shard_map.93.field, f32[256,16,128]{2,1,0:T(8,128)} %bitcast.17, f32[256,128]{1,0:T(8,128)} %copy-done.10, f32[64,128]{1,0:T(8,128)} %copy-done.12, f32[64,128]{1,0:T(8,128)} %copy-done.13), custom_call_target="tpu_custom_call" | custom-call | tf_op jit(solution)/shard_map/pallas_call | solution.py:796
  (58 shorter events, 9.2 us)
Async XLA Ops:
  3.4 10.0 %collective-permute-start = (f32[256,128]{1,0:T(8,128)}, f32[256,128]{1,0:T(8,128)S(1)}, u32[]{:S(2)}, u32[]{:S(2)}) collective-permute-start(f32[256,128]{1,0:T(8,128)} %get-tuple-element.36), channel_id=1, source_target_pairs={{0,8},{8,0},{1,9},{9,1},{2,10},{10,2},{3,11},{11,3},{4,12},{12,4},... | collective-permute-start | bytes 393224 | tf_op jit(solution)/shard_map/ppermute | solution.py:45
  5.0 6.9 %collective-permute-start.1 = (f32[64,128]{1,0:T(8,128)}, f32[64,128]{1,0:T(8,128)S(1)}, u32[]{:S(2)}, u32[]{:S(2)}) collective-permute-start(f32[64,128]{1,0:T(8,128)} %get-tuple-element.37), channel_id=1, source_target_pairs={{0,1},{1,0},{2,3},{3,2},{4,5},{5,4},{6,7},{7,6},{8,9},{9,8},{10,11... | collective-permute-start | bytes 98312 | tf_op jit(solution)/shard_map/ppermute | solution.py:45
  6.5 6.9 %collective-permute-start.2 = (f32[64,128]{1,0:T(8,128)}, f32[64,128]{1,0:T(8,128)S(1)}, u32[]{:S(2)}, u32[]{:S(2)}) collective-permute-start(f32[64,128]{1,0:T(8,128)} %get-tuple-element.37), channel_id=1, source_target_pairs={{1,2},{2,1},{3,4},{4,3},{5,6},{6,5},{9,10},{10,9},{11,12},{12,11},... | collective-permute-start | bytes 98312 | tf_op jit(solution)/shard_map/ppermute | solution.py:45
  11.9 8.1 %copy-start.6 = (f32[64,128]{1,0:T(8,128)}, f32[64,128]{1,0:T(8,128)S(1)}, u32[]{:S(2)}) copy-start(f32[64,128]{1,0:T(8,128)S(1)} %collective-permute-done.1.rest_1_) | copy-start | bytes 98308
  13.4 6.7 %copy-start.7 = (f32[64,128]{1,0:T(8,128)}, f32[64,128]{1,0:T(8,128)S(1)}, u32[]{:S(2)}) copy-start(f32[64,128]{1,0:T(8,128)S(1)} %collective-permute-done.2.rest_2_) | copy-start | bytes 98308
  13.4 6.7 %copy-start.2 = (f32[256,128]{1,0:T(8,128)}, f32[256,128]{1,0:T(8,128)S(1)}, u32[]{:S(2)}) copy-start(f32[256,128]{1,0:T(8,128)S(1)} %collective-permute-done.rest_0_) | copy-start | bytes 393220
  13.4 40.0 %all-to-all-start = ((f32[16,136,128]{2,1,0:T(8,128)}), f32[16,136,128]{2,1,0:T(8,128)S(1)}, u32[]{:S(2)}, u32[]{:S(2)}) async-start(f32[16,136,128]{2,1,0:T(8,128)} %shard_map.82), calls=%async_computation | async-start | bytes 2228224 | tf_op jit(solution)/shard_map/all_to_all | solution.py:819
  21.8 1.4 %collective-permute-start.3 = (f32[32,128]{1,0:T(8,128)}, f32[32,128]{1,0:T(8,128)S(1)}, u32[]{:S(2)}, u32[]{:S(2)}) collective-permute-start(f32[32,128]{1,0:T(8,128)} %shard_map.84), channel_id=1, source_target_pairs={{0,16},{16,0},{1,17},{17,1},{2,18},{18,2},{3,19},{19,3},{4,20},{20... | collective-permute-start | bytes 49160 | tf_op jit(solution)/shard_map/ppermute | solution.py:802
  32.2 10.3 %collective-permute-start.4 = (f32[256,128]{1,0:T(8,128)}, f32[256,128]{1,0:T(8,128)S(1)}, u32[]{:S(2)}, u32[]{:S(2)}) collective-permute-start(f32[256,128]{1,0:T(8,128)} %get-tuple-element.46), channel_id=1, source_target_pairs={{0,8},{8,0},{1,9},{9,1},{2,10},{10,2},{3,11},{11,3},{4,12},{12,4},... | collective-permute-start | bytes 393224 | tf_op jit(solution)/shard_map/ppermute | solution.py:45
  33.7 4.7 %collective-permute-start.5 = (f32[64,128]{1,0:T(8,128)}, f32[64,128]{1,0:T(8,128)S(1)}, u32[]{:S(2)}, u32[]{:S(2)}) collective-permute-start(f32[64,128]{1,0:T(8,128)} %get-tuple-element.47), channel_id=1, source_target_pairs={{0,1},{1,0},{2,3},{3,2},{4,5},{5,4},{6,7},{7,6},{8,9},{9,8},{10,11... | collective-permute-start | bytes 98312 | tf_op jit(solution)/shard_map/ppermute | solution.py:45
  35.2 7.3 %collective-permute-start.6 = (f32[64,128]{1,0:T(8,128)}, f32[64,128]{1,0:T(8,128)S(1)}, u32[]{:S(2)}, u32[]{:S(2)}) collective-permute-start(f32[64,128]{1,0:T(8,128)} %get-tuple-element.47), channel_id=1, source_target_pairs={{1,2},{2,1},{3,4},{4,3},{5,6},{6,5},{9,10},{10,9},{11,12},{12,11},... | collective-permute-start | bytes 98312 | tf_op jit(solution)/shard_map/ppermute | solution.py:45
  38.4 4.0 %copy-start.8 = (f32[64,128]{1,0:T(8,128)}, f32[64,128]{1,0:T(8,128)S(1)}, u32[]{:S(2)}) copy-start(f32[64,128]{1,0:T(8,128)S(1)} %collective-permute-done.5.rest_1_) | copy-start | bytes 98308
  42.4 0.6 copy-start.9
  42.5 0.7 copy-start.3
  44.8 1.4 %collective-permute-start.7 = (f32[32,128]{1,0:T(8,128)}, f32[32,128]{1,0:T(8,128)S(1)}, u32[]{:S(2)}, u32[]{:S(2)}) collective-permute-start(f32[32,128]{1,0:T(8,128)} %shard_map.86), channel_id=1, source_target_pairs={{0,16},{16,0},{1,17},{17,1},{2,18},{18,2},{3,19},{19,3},{4,20},{20... | collective-permute-start | bytes 49160 | tf_op jit(solution)/shard_map/ppermute | solution.py:802
  53.4 1.0 copy-start
  64.0 1.4 %collective-permute-start.9 = (f32[8,128]{1,0:T(8,128)}, f32[8,128]{1,0:T(8,128)S(1)}, u32[]{:S(2)}, u32[]{:S(2)}) collective-permute-start(f32[8,128]{1,0:T(8,128)} %get-tuple-element.54), channel_id=1, source_target_pairs={{0,16},{16,0},{1,17},{17,1},{2,18},{18,2},{3,19},{19,3},{4,20},{20... | collective-permute-start | bytes 12296 | tf_op jit(solution)/shard_map/ppermute | solution.py:802
  67.8 22.5 %collective-permute-start.10 = (f32[256,128]{1,0:T(8,128)}, f32[256,128]{1,0:T(8,128)S(1)}, u32[]{:S(2)}, u32[]{:S(2)}) collective-permute-start(f32[256,128]{1,0:T(8,128)} %get-tuple-element.60), channel_id=1, source_target_pairs={{0,8},{8,0},{1,9},{9,1},{2,10},{10,2},{3,11},{11,3},{4,12},{12,4},... | collective-permute-start | bytes 393224 | tf_op jit(solution)/shard_map/ppermute | solution.py:45
  68.0 22.3 %collective-permute-start.11 = (f32[64,128]{1,0:T(8,128)}, f32[64,128]{1,0:T(8,128)S(1)}, u32[]{:S(2)}, u32[]{:S(2)}) collective-permute-start(f32[64,128]{1,0:T(8,128)} %get-tuple-element.61), channel_id=1, source_target_pairs={{0,1},{1,0},{2,3},{3,2},{4,5},{5,4},{6,7},{7,6},{8,9},{9,8},{10,11... | collective-permute-start | bytes 98312 | tf_op jit(solution)/shard_map/ppermute | solution.py:45
  72.6 17.7 %collective-permute-start.12 = (f32[64,128]{1,0:T(8,128)}, f32[64,128]{1,0:T(8,128)S(1)}, u32[]{:S(2)}, u32[]{:S(2)}) collective-permute-start(f32[64,128]{1,0:T(8,128)} %get-tuple-element.61), channel_id=1, source_target_pairs={{1,2},{2,1},{3,4},{4,3},{5,6},{6,5},{9,10},{10,9},{11,12},{12,11},... | collective-permute-start | bytes 98312 | tf_op jit(solution)/shard_map/ppermute | solution.py:45
  81.1 1.5 %collective-permute-start.8 = (f32[32,128]{1,0:T(8,128)}, f32[32,128]{1,0:T(8,128)S(1)}, u32[]{:S(2)}, u32[]{:S(2)}) collective-permute-start(f32[32,128]{1,0:T(8,128)} %get-tuple-element.51), channel_id=1, source_target_pairs={{0,16},{16,0},{1,17},{17,1},{2,18},{18,2},{3,19},{19,3},{4,20},{20... | collective-permute-start | bytes 49160 | tf_op jit(solution)/shard_map/ppermute | solution.py:802
  90.3 0.6 copy-start.4
  90.3 0.6 copy-start.5
  90.3 0.7 copy-start.1
  92.7 1.4 %collective-permute-start.13 = (f32[32,128]{1,0:T(8,128)}, f32[32,128]{1,0:T(8,128)S(1)}, u32[]{:S(2)}, u32[]{:S(2)}) collective-permute-start(f32[32,128]{1,0:T(8,128)} %shard_map.92.floor), channel_id=1, source_target_pairs={{0,16},{16,0},{1,17},{17,1},{2,18},{18,2},{3,19},{19,3},{4,20},{20... | collective-permute-start | bytes 49160 | tf_op jit(solution)/shard_map/ppermute | solution.py:802
  96.8 12.6 %collective-permute-start.14 = (f32[256,128]{1,0:T(8,128)}, f32[256,128]{1,0:T(8,128)S(1)}, u32[]{:S(2)}, u32[]{:S(2)}) collective-permute-start(f32[256,128]{1,0:T(8,128)} %get-tuple-element.65), channel_id=1, source_target_pairs={{0,8},{8,0},{1,9},{9,1},{2,10},{10,2},{3,11},{11,3},{4,12},{12,4},... | collective-permute-start | bytes 393224 | tf_op jit(solution)/shard_map/ppermute | solution.py:45
  97.5 11.9 %collective-permute-start.15 = (f32[64,128]{1,0:T(8,128)}, f32[64,128]{1,0:T(8,128)S(1)}, u32[]{:S(2)}, u32[]{:S(2)}) collective-permute-start(f32[64,128]{1,0:T(8,128)} %get-tuple-element.66), channel_id=1, source_target_pairs={{0,1},{1,0},{2,3},{3,2},{4,5},{5,4},{6,7},{7,6},{8,9},{9,8},{10,11... | collective-permute-start | bytes 98312 | tf_op jit(solution)/shard_map/ppermute | solution.py:45
  98.4 11.0 %collective-permute-start.16 = (f32[64,128]{1,0:T(8,128)}, f32[64,128]{1,0:T(8,128)S(1)}, u32[]{:S(2)}, u32[]{:S(2)}) collective-permute-start(f32[64,128]{1,0:T(8,128)} %get-tuple-element.66), channel_id=1, source_target_pairs={{1,2},{2,1},{3,4},{4,3},{5,6},{6,5},{9,10},{10,9},{11,12},{12,11},... | collective-permute-start | bytes 98312 | tf_op jit(solution)/shard_map/ppermute | solution.py:45
  102.3 7.1 %copy-start.18 = (f32[1,2,128]{2,1,0:T(2,128)S(1)}, f32[1,2,128]{2,1,0:T(2,128)}, u32[]{:S(2)}) copy-start(f32[1,2,128]{2,1,0:T(2,128)} %param.11) | copy-start | bytes 3076
  109.4 0.8 copy-start.12
  109.4 0.8 copy-start.13
  109.4 0.8 copy-start.10
  (5 other events, 3.0 us)

commit v5 on v4

--- a/solution.py
+++ b/solution.py
@@ -12,14 +12,17 @@
 LANES = 128
 GROUP = 8
 MIB = 1024 * 1024
-VMEM_GRANT = 59 * MIB
-
-
-def call(body, out_shape, scratch=(), limit=VMEM_GRANT, **kw):
+SWEEP_VMEM = 16 * MIB
+OBSERVE_VMEM = 22 * MIB
+
+
+def call(body, out_shape, scratch=(), limit=SWEEP_VMEM, traffic=0, **kw):
+    cost = pl.CostEstimate(flops=0, bytes_accessed=traffic, transcendentals=0) if traffic else None
     return pl.pallas_call(
         body,
         out_shape=out_shape,
         scratch_shapes=list(scratch),
+        cost_estimate=cost,
         compiler_params=pltpu.CompilerParams(vmem_limit_bytes=limit),
         **kw,
     )
@@ -141,7 +144,7 @@
     groups = levels // GROUP
     here, upper, lower = levels_around(cells, i, f * levels, group, groups)
     at = pl.ds(f * levels + group * GROUP, GROUP)
-    right, left = shifted(here, here, side_columns(sides, i, f * groups + group))
+    right, left = shifted(here, here, 0.0 if sides is None else side_columns(sides, i, f * groups + group))
     u = winds[i, pl.ds(group * GROUP, GROUP), :]
     w = winds[i, pl.ds(levels + group * GROUP, GROUP), :]
     return forward_sum(here, upper + lower, cells[i + 2, at, :], cells[i, at, :], right, left, u, w)
@@ -220,22 +223,37 @@
 
 
 def edges_kernel(rows, levels, state, s_even, s_odd, packed, low0, low1, cells, sems):
-    incoming = Rows(state, cells, sems, rows, True, 0)
-    start_rows(rows, incoming)
-    packed[...] = jnp.zeros_like(packed)
-    groups = levels // GROUP
-
-    def row(i, _):
-        incoming.wait(i)
-        for m in range(2 * groups // PARTS):
-            values = [cells[i, pl.ds((m * PARTS + part) * GROUP, GROUP), :] for part in range(PARTS)]
-            if m * PARTS % groups == 0:
-                put_low((low0, low1), values[0], i, m * PARTS // groups, rows)
-            pack_block(packed, values, i, m)
+    part_levels = PARTS * GROUP
+    blocks = 2 * levels // part_levels
+
+    def copy(m):
+        return pltpu.make_async_copy(
+            state.at[pl.ds(m * part_levels * rows, part_levels * rows)],
+            cells.at[pl.ds(m * part_levels * rows, part_levels * rows)],
+            sems.at[m],
+        )
+
+    for m in range(blocks):
+        copy(m).start()
+
+    def block(m, _):
+        copy(m).wait()
+        total = jnp.zeros((GROUP, LANES), jnp.float32)
+        for part in range(PARTS):
+            for i in range(rows):
+                start = (m * PARTS + part) * GROUP * rows + i
+                total = pack_into(total, cells[pl.ds(start, GROUP, stride=rows), :], slot_of(i, part, rows))
+        packed[pl.ds(pl.multiple_of(m * GROUP, GROUP), GROUP), :] = total
+        start = m * part_levels * rows
+        first = cells[pl.ds(start, part_levels, stride=rows), :]
+        last = cells[pl.ds(start + rows - 1, part_levels, stride=rows), :]
+        put_strip(s_even, s_odd, pl.ds(pl.multiple_of(m * part_levels, part_levels), part_levels), first, last)
         return 0
 
-    lax.fori_loop(0, rows, row, 0)
-    put_strip(s_even, s_odd, slice(None), cells[0], cells[rows - 1])
+    lax.fori_loop(0, blocks, block, 0)
+    for f in range(2):
+        for level, low in enumerate((low0, low1)):
+            low[f * rows : (f + 1) * rows, :] = cells[pl.ds((f * levels + level) * rows, rows), :]
 
 
 def floor_edge(halos, f, rows, levels):
@@ -289,30 +307,21 @@
     return total
 
 
-def forward_kernel(first, last, rows, levels, coupling, other, field, winds, *rest):
-    halo_count = len(rest) - (7 if last else 14)
-    halos, rest = rest[:halo_count], rest[halo_count:]
-    if last:
-        cols, cells, wind_cells, sides, sems, col_cells, col_sems = rest
-    else:
-        out, s_even, s_odd, packed, low0, low1, wind_ends, wind_dense, dense_g, cells, wind_cells, out_cells, sides, sems = rest
-        leaving = Out(out_cells, out, sems.at[2], rows, False)
-        packed[...] = jnp.zeros_like(packed)
-        wind_dense[...] = jnp.zeros_like(wind_dense)
-    incoming = Rows(field, cells, sems.at[0], rows, first, 1)
+def forward_kernel(rows, levels, coupling, other, field, winds, *rest):
+    *halos, out, s_even, s_odd, packed, low0, low1, wind_ends, wind_dense, dense_g = rest[:-5]
+    cells, wind_cells, out_cells, sides, sems = rest[-5:]
+    leaving = Out(out_cells, out, sems.at[2], rows, False)
+    incoming = Rows(field, cells, sems.at[0], rows, True, 1)
     wind_in = Rows(winds, wind_cells, sems.at[1], rows, True, 0)
     start_rows(rows, incoming, wind_in)
+    packed[...] = jnp.zeros_like(packed)
+    wind_dense[...] = jnp.zeros_like(wind_dense)
     merge_columns(halos[1], halos[2], sides)
     before, after = read_sides(halos)
     cells[0] = before(slice(None))
     cells[rows + 1] = after(slice(None))
     groups = levels // GROUP
-    width = 2 * levels
     incoming.wait(0)
-
-    def col_copy(i):
-        lanes = pl.ds(pl.multiple_of(i * LANES, LANES), LANES)
-        return pltpu.make_async_copy(col_cells.at[:, lanes], cols.at[:, lanes], col_sems.at[i])
 
     def row(i, _):
         @pl.when(i < rows - 1)
@@ -327,38 +336,89 @@
                 value = forward_point(cells, wind_cells, sides, i, f, group, levels)
                 if group == 0:
                     value = coupled(couple_forward, value, other, coupling, i, f, rows)
-                    if not last:
-                        put_low((low0, low1), value, i, f, rows)
+                    put_low((low0, low1), value, i, f, rows)
                 values.append(value)
             base = m * PARTS * GROUP
-            if last:
-                lanes = pl.ds(pl.multiple_of(i * LANES, LANES), LANES)
-                high, low = split(jnp.concatenate(values, axis=0), 2)
-                col_cells[pl.ds(base, PARTS * GROUP), lanes] = high
-                col_cells[pl.ds(width + base, PARTS * GROUP), lanes] = low
-            else:
-                for part, value in enumerate(values):
-                    out_cells[i, pl.ds(base + part * GROUP, GROUP), :] = value
-                pack_block(packed, values, i, m)
-                if f == 0:
-                    w = [wind_cells[i, pl.ds(levels + base + part * GROUP, GROUP), :] for part in range(PARTS)]
-                    pack_block(wind_dense, w, i, m)
-        if last:
-            col_copy(i).start()
-        else:
-            leaving.start(i)
+            for part, value in enumerate(values):
+                out_cells[i, pl.ds(base + part * GROUP, GROUP), :] = value
+            pack_block(packed, values, i, m)
+            if f == 0:
+                w = [wind_cells[i, pl.ds(levels + base + part * GROUP, GROUP), :] for part in range(PARTS)]
+                pack_block(wind_dense, w, i, m)
+        leaving.start(i)
         return 0
 
     lax.fori_loop(0, rows, row, 0)
-    if last:
-        for i in range(rows):
-            col_copy(i).wait()
-        return
     put_strip(s_even, s_odd, slice(None), out_cells[0], out_cells[rows - 1])
     wind_ends[0] = wind_cells[0, pl.ds(0, levels), :]
     wind_ends[1] = wind_cells[rows - 1, pl.ds(0, levels), :]
     dense_g[...] = jnp.broadcast_to(dense_row(coupling, 0, rows), dense_g.shape)
     leaving.finish()
+
+
+def forward_again_kernel(rows, levels, field, winds, cols, cells, wind_cells, sems, col_cells, col_sems):
+    incoming = Rows(field, cells, sems.at[0], rows, False, 1)
+    wind_in = Rows(winds, wind_cells, sems.at[1], rows, True, 0)
+    start_rows(rows, incoming, wind_in)
+    cells[0] = jnp.zeros_like(cells[0])
+    cells[rows + 1] = jnp.zeros_like(cells[0])
+    groups = levels // GROUP
+    width = 2 * levels
+    incoming.wait(0)
+
+    def col_copy(i):
+        lanes = pl.ds(pl.multiple_of(i * LANES, LANES), LANES)
+        return pltpu.make_async_copy(col_cells.at[:, lanes], cols.at[:, lanes], col_sems.at[i])
+
+    def row(i, _):
+        @pl.when(i < rows - 1)
+        def _():
+            incoming.wait(i + 1)
+
+        wind_in.wait(i)
+        lanes = pl.ds(pl.multiple_of(i * LANES, LANES), LANES)
+        for m in range(2 * groups // PARTS):
+            f, start = m * PARTS // groups, m * PARTS % groups
+            values = [
+                forward_point(cells, wind_cells, None, i, f, group, levels) for group in range(start, start + PARTS)
+            ]
+            high, low = split(jnp.concatenate(values, axis=0), 2)
+            col_cells[pl.ds(m * PARTS * GROUP, PARTS * GROUP), lanes] = high
+            col_cells[pl.ds(width + m * PARTS * GROUP, PARTS * GROUP), lanes] = low
+        col_copy(i).start()
+        return 0
+
+    lax.fori_loop(0, rows, row, 0)
+    for i in range(rows):
+        col_copy(i).wait()
+
+
+def outside_kernel(rows, levels, coupling, floor, other, wind_ends, wind_dense, *rest):
+    *halos, extra, bottom, dense = rest
+    width = 2 * levels
+    for f in range(2):
+        here = pl.ds(f * rows, rows)
+        bottom[here, :] = couple_forward(floor[here, :], other[here, :], coupling[...])
+    dense_products(dense, swap_pairs(merged(halos[1], halos[2], slice(None))), wind_dense)
+    before, after = read_sides(halos)
+    sub = lax.broadcasted_iota(jnp.int32, (levels, LANES), 0)
+
+    def put(value, f, lanes):
+        high, low = split(jnp.where(sub == 0, 0.0, value), 2)
+        extra[f * levels : (f + 1) * levels, lanes] = high
+        extra[width + f * levels : width + (f + 1) * levels, lanes] = low
+
+    lane = lane_iota()
+    for f in range(2):
+        at = pl.ds(f * levels, levels)
+        put(products(before(at), wind_ends[0])[1], f, slice(0, LANES))
+        put(products(after(at), wind_ends[1])[0], f, slice(LANES, 2 * LANES))
+        thin = []
+        for group in range(f * levels // GROUP, (f + 1) * levels // GROUP):
+            m, part = group // PARTS, group % PARTS
+            moved = pltpu.roll(dense[m * GROUP : (m + 1) * GROUP, :], (LANES - 2 * part) % LANES, 1)
+            thin.append(jnp.where(lane % (2 * PARTS) < 2, moved, 0.0))
+        put(jnp.concatenate(thin, axis=0), f, slice(2 * LANES, 3 * LANES))
 
 
 def dense_products(packed, value, wind_dense):
@@ -472,7 +532,7 @@
     dense_products(packed, dense, wind_dense)
 
 
-def adjoint_rows(rows, levels, cells, wind_cells, out_cells, leaving, take, each):
+def adjoint_rows(rows, levels, cells, wind_cells, take, each):
     groups = levels // GROUP
     cells[0] = jnp.zeros_like(cells[0])
     cells[rows + 1] = jnp.zeros_like(cells[0])
@@ -487,61 +547,54 @@
 
         for m in range(2 * groups // PARTS):
             f, start = m * PARTS // groups, m * PARTS % groups
-            values = []
-            for group in range(start, start + PARTS):
-                value = adjoint_point(cells, wind_cells, i, f, group, levels)
-                out_cells[i, pl.ds(f * levels + group * GROUP, GROUP), :] = value
-                values.append(value)
-            each(i, m, f, start, values)
-        leaving.start(i)
+            each(i, m, f, start, [
+                adjoint_point(cells, wind_cells, i, f, group, levels) for group in range(start, start + PARTS)
+            ])
         return 0
 
     lax.fori_loop(0, rows, row, 0)
 
 
 def first_adjoint_kernel(
-    rows, levels, coupling, other, field, winds, out, ends, columns, low0, cells, wind_cells, out_cells, sems
+    rows, levels, coupling, other, field, winds, out, ends, columns, low0, cells, wind_cells, sems
 ):
-    incoming = Rows(field, cells, sems.at[0], rows, False, 1)
-    wind_in = Rows(winds, wind_cells, sems.at[1], rows, True, 1)
-    start_rows(rows, incoming, wind_in)
-    leaving = Out(out_cells, out, sems.at[2], rows, False)
+    wind_in = Rows(winds, wind_cells, sems, rows, True, 1)
+    start_rows(rows, wind_in)
     columns[...] = jnp.zeros_like(columns)
 
     def take(i):
-        incoming.wait(i)
         wind_in.wait(i)
+        cells[i + 1] = field[i]
         for f in range(2):
             at = pl.ds(f * levels, GROUP)
-            cells[i + 1, at, :] = coupled(couple_adjoint, cells[i + 1, at, :], other, coupling, i, f, rows)
+            cells[i + 1, at, :] = coupled(couple_adjoint, field[i, at, :], other, coupling, i, f, rows)
 
     def each(i, m, f, start, values):
+        for part, value in enumerate(values):
+            out[i, pl.ds((m * PARTS + part) * GROUP, GROUP), :] = value
         if start == 0:
             low0[pl.ds(f * rows + i, 1), :] = values[0][0:1]
         pack_block(columns, values, i, m)
 
-    adjoint_rows(rows, levels, cells, wind_cells, out_cells, leaving, take, each)
-    ends[0] = out_cells[0]
-    ends[1] = out_cells[rows - 1]
-    leaving.finish()
-
-
-def second_adjoint_kernel(rows, levels, coupling, other, field, winds, *rest):
-    *halos, out, cells, wind_cells, out_cells, sides, sems = rest
-    incoming = Rows(field, cells, sems.at[0], rows, False, 1)
-    wind_in = Rows(winds, wind_cells, sems.at[1], rows, True, 1)
-    start_rows(rows, incoming, wind_in)
-    leaving = Out(out_cells, out, sems.at[2], rows, False)
+    adjoint_rows(rows, levels, cells, wind_cells, take, each)
+    ends[0] = out[0]
+    ends[1] = out[rows - 1]
+
+
+def second_adjoint_kernel(rows, levels, coupling, other, field, winds, scale, state, *rest):
+    *halos, out, cells, wind_cells, state_cells, sides, sems = rest
+    wind_in = Rows(winds, wind_cells, sems.at[0], rows, True, 1)
+    state_in = Rows(state, state_cells, sems.at[1], rows, True, 0)
+    start_rows(rows, wind_in, state_in)
     sides[...] = swap_pairs(merged(halos[1], halos[2], slice(None)))
     before, after = read_sides(halos)
     groups = levels // GROUP
 
     def take(i):
-        incoming.wait(i)
         wind_in.wait(i)
         for group in range(2 * groups):
             at = pl.ds(group * GROUP, GROUP)
-            value = cells[i + 1, at, :] + edge_lanes(sides, i, group)
+            value = field[i, at, :] + edge_lanes(sides, i, group)
             if group % groups == 0:
                 f = group // groups
                 value = value + jnp.where(i == 0, before(at), 0.0) + jnp.where(i == rows - 1, after(at), 0.0)
@@ -564,32 +617,33 @@
         def _():
             add_outer(rows - 1, after)
 
-    adjoint_rows(rows, levels, cells, wind_cells, out_cells, leaving, take_all, lambda *_: None)
-    leaving.finish()
-
-
-def final_kernel(rows, levels, scale, field, state, *rest):
-    *halos, out, cells, state_cells, sides, sems = rest
-    incoming = Rows(field, cells, sems.at[0], rows, False, 0)
-    state_in = Rows(state, state_cells, sems.at[1], rows, True, 0)
-    start_rows(rows, incoming, state_in)
-    leaving = Out(cells, out, sems.at[2], rows, True)
+    def each(i, m, f, start, values):
+        if m == 0:
+            state_in.wait(i)
+        for part, value in enumerate(values):
+            at = pl.ds((m * PARTS + part) * GROUP, GROUP)
+            out[i, at, :] = value + scale[at, :] * state_cells[i, at, :]
+
+    adjoint_rows(rows, levels, cells, wind_cells, take_all, each)
+
+
+def final_kernel(rows, levels, field, *rest):
+    *halos, out, cells, sides, sems = rest
+    leaving = Out(cells, out, sems, rows, True)
     sides[...] = swap_pairs(merged(halos[1], halos[2], slice(None)))
     before, after = read_sides(halos)
     groups = levels // GROUP
 
     def add(i, outer):
-        incoming.wait(i)
-        state_in.wait(i)
         for group in range(2 * groups):
             at = pl.ds(group * GROUP, GROUP)
-            value = cells[i, at, :] + scale[at, :] * state_cells[i, at, :] + edge_lanes(sides, i, group)
+            value = field[i, at, :] + edge_lanes(sides, i, group)
             cells[i, at, :] = value if outer is None else value + outer(at)
         leaving.start(i)
         return 0
 
+    lax.fori_loop(1, rows - 1, lambda i, _: add(i, None), 0)
     add(0, before)
-    lax.fori_loop(1, rows - 1, lambda i, _: add(i, None), 0)
     add(rows - 1, after)
     leaving.finish()
 
@@ -644,8 +698,8 @@
                 ]
 
 
-def innovate_kernel(rows, width, tiles, cap, records, cols, spread, sel, ends, columns, floor, *scratch):
-    col_cells, sel_cells, border_sel, places, precs, both, spread_cells, sems = scratch
+def innovate_kernel(rows, width, tiles, cap, records, cols, extra, bottom, spread, sel, ends, columns, floor, *scratch):
+    col_cells, border_sel, precs, both, sems = scratch
     chunks = 8
     copies = []
     for part in range(chunks):
@@ -663,10 +717,6 @@
     border = jnp.where(lane % (2 * PARTS) < 2, border, -1).astype(jnp.float32)
     lane = lane.astype(jnp.float32)
 
-    def sel_copy(block):
-        at = pl.ds(pl.multiple_of(block * step, step), step)
-        return pltpu.make_async_copy(sel_cells.at[at], sel.at[at], sems.at[chunks + block])
-
     def select(block, _):
         sources = step // cap
 
@@ -682,17 +732,28 @@
         column = place - lane
         precs[at, :] = spread_out(1)
         for i in range(rows):
-            sel_cells[at, i * LANES : (i + 1) * LANES] = jnp.where(column == float(i * LANES), 1.0, 0.0).astype(
+            sel[at, i * LANES : (i + 1) * LANES] = jnp.where(column == float(i * LANES), 1.0, 0.0).astype(
                 jnp.bfloat16
             )
         border_sel[at, :] = jnp.where(place == border, 1.0, 0.0).astype(jnp.bfloat16)
-        sel_copy(block).start()
         return 0
 
     lax.fori_loop(0, count // step, select, 0)
     for copy in copies:
         copy.wait()
-    both[...] = dot(sel_cells[...], col_cells[...], (1, 1))
+    pair = 2 * GROUP
+    first = lax.broadcasted_iota(jnp.int32, (pair, LANES), 0) == 0
+    for f in range(2):
+        for i in range(rows):
+            lanes = slice(i * LANES, (i + 1) * LANES)
+            for term, value in enumerate(split(bottom[f * rows + i : f * rows + i + 1, :], 2)):
+                at = pl.ds(term * width + f * (width // 2), pair)
+                old = col_cells[at, lanes].astype(jnp.float32)
+                new = jnp.where(first, value.astype(jnp.float32), old)
+                col_cells[at, lanes] = new.astype(jnp.bfloat16)
+    both[...] = dot(sel[...], col_cells[...], (1, 1))
+    border_cells = jnp.concatenate([sel[:, 0:LANES], sel[:, (rows - 1) * LANES : rows * LANES], border_sel[...]], axis=1)
+    both[...] += dot(border_cells, extra[...], (1, 1))
 
     def weigh(block, _):
         at = pl.ds(pl.multiple_of(block * LANES, LANES), LANES)
@@ -711,21 +772,17 @@
         innovation = jnp.sum(total, axis=1, keepdims=True) * precs[at, :]
         for half in range(halves):
             high, low = split((ops[half] * innovation).T, 2)
-            spread_cells[half * LANES : (half + 1) * LANES, at] = high
-            spread_cells[width + half * LANES : width + (half + 1) * LANES, at] = low
+            spread[half * LANES : (half + 1) * LANES, at] = high
+            spread[width + half * LANES : width + (half + 1) * LANES, at] = low
         return 0
 
-    lax.fori_loop(0, count // LANES, weigh, 0)
-    spread_copy = pltpu.make_async_copy(spread_cells, spread, sems.at[chunks + count // step])
-    spread_copy.start()
-
-    def cells_of(ones_at):
-        terms = dot(spread_cells[...], ones_at, (1, 0))
-        return terms[:width] + terms[width:]
-
-    ends[0] = cells_of(sel_cells[:, 0:LANES])
-    ends[1] = cells_of(sel_cells[:, (rows - 1) * LANES : rows * LANES])
-    thin = cells_of(border_sel[...])
+    lax.fori_loop(0, count // LANES, weigh, 0, unroll=4)
+
+    terms = dot(spread[...], border_cells, (1, 0))
+    border_sums = terms[:width] + terms[width:]
+    ends[0] = border_sums[:, 0:LANES]
+    ends[1] = border_sums[:, LANES : 2 * LANES]
+    thin = border_sums[:, 2 * LANES :]
     for m in range(width // (GROUP * PARTS)):
         total = thin[m * PARTS * GROUP : (m * PARTS + 1) * GROUP]
         for part in range(1, PARTS):
@@ -738,31 +795,15 @@
         for k in range(2):
             floor[2 * k + f : 2 * k + f + 1, :] = ends[k, f * (width // 2) : f * (width // 2) + 1, :]
         floor[4 + f : 5 + f, :] = columns[f * half : f * half + 1, :]
-    for block in range(count // step):
-        sel_copy(block).wait()
-    spread_copy.wait()
-
-
-def scatter_kernel(rows, width, spread, sel, adjoint, low0, low1, spread_cells, sel_cells, out_cells, sems):
-    count = sel.shape[0]
-    chunks = 4
-    copies = [pltpu.make_async_copy(spread, spread_cells, sems.at[2 * rows])]
-    for part in range(chunks):
-        at = pl.ds(part * (count // chunks), count // chunks)
-        copies.append(pltpu.make_async_copy(sel.at[at], sel_cells.at[at], sems.at[rows + part]))
-    for copy in copies:
-        copy.start()
-    for copy in copies:
-        copy.wait()
-    leaving = Out(out_cells, adjoint, sems, rows, False)
-    sums = dot(spread_cells[...], sel_cells[...], (1, 0))
+
+
+def scatter_kernel(rows, width, spread, sel, adjoint, low0):
+    sums = dot(spread[...], sel[...], (1, 0))
     for i in range(rows):
         lanes = slice(i * LANES, (i + 1) * LANES)
-        out_cells[i] = sums[:width, lanes] + sums[width:, lanes]
-        leaving.start(i)
+        adjoint[i] = sums[:width, lanes] + sums[width:, lanes]
         for f in range(2):
-            put_low((low0, low1), out_cells[i, f * (width // 2) : f * (width // 2) + GROUP, :], i, f, rows)
-    leaving.finish()
+            low0[f * rows + i : f * rows + i + 1, :] = adjoint[i, f * (width // 2) : f * (width // 2) + 1, :]
 
 
 def local(state_incr, winds, coupling, background, obs_dest, obs_col, obs_op, obs_prec):
@@ -790,10 +831,12 @@
     def sems(*shape):
         return pltpu.SemaphoreType.DMA(shape)
 
-    def run(body, out_shape, scratch, args, far=(), out_far=()):
+    def run(body, out_shape, scratch, args, far=(), out_far=(), **kw):
+        args = [pltpu.with_memory_space_constraint(x, pltpu.HBM) if k in far else x for k, x in enumerate(args)]
         specs = [anywhere if k in far else vmem for k in range(len(args))]
         outs = [anywhere if k in out_far else vmem for k in range(len(out_shape))]
-        return call(body, out_shape, scratch, in_specs=specs, out_specs=outs)(*args)
+        out_shape = [pltpu.HBM(x.shape, x.dtype) if k in out_far else x for k, x in enumerate(out_shape)]
+        return call(body, out_shape, scratch, in_specs=specs, out_specs=outs, **kw)(*args)
 
     def on_rows(body):
         return functools.partial(body, rows, levels)
@@ -808,34 +851,49 @@
     thin_shape = f32(GROUP, LANES)
 
     s_even, s_odd, packed, low0, low1 = run(
-        on_rows(edges_kernel), strip_shapes + [low_shape] * 2, [own, sems(rows)], (state,), far=(0,)
+        on_rows(edges_kernel),
+        strip_shapes + [low_shape] * 2,
+        [pltpu.VMEM((width * rows, LANES), jnp.float32), sems(groups // PARTS)],
+        (state_incr.reshape(width * rows, lanes),),
+        far=(0,),
     )
     halos = exchange((s_even, s_odd), packed)
 
     send = call(functools.partial(route_kernel, tiles, cap), f32(tiles, halves * cap + GROUP, LANES))(
         obs_dest.reshape(1, count), obs_col.reshape(1, count), obs_prec.reshape(1, count), obs_op
     )
-    send, halos = lax.optimization_barrier((send, halos))
+    send, halos[0], halos[2] = lax.optimization_barrier((send, halos[0], halos[2]))
     records = lax.all_to_all(send, ("gx", "gy"), split_axis=0, concat_axis=0, tiled=True)
 
     (floor,) = run(on_rows(forward_floor_kernel), [low_shape], [], (low0, low1, floor_winds, *halos))
     field, s_even, s_odd, packed, low0, low1, wind_ends, wind_dense, dense_g = run(
-        on_rows(functools.partial(forward_kernel, True, False)),
-        [field_shape] + strip_shapes + [low_shape] * 2 + [f32(2, levels, LANES), f32(groups // PARTS * GROUP // 2, LANES), thin_shape],
+        on_rows(forward_kernel),
+        [field_shape]
+        + strip_shapes
+        + [low_shape] * 2
+        + [f32(2, levels, LANES), f32(groups // PARTS * GROUP // 2, LANES), thin_shape],
         [framed, own, own, sides, sems(3, rows)],
         (coupling, swap_floor(floor), state, wind, *halos),
         far=(2, 3),
         out_far=(0,),
     )
     halos = exchange((s_even, s_odd), packed)
+    (cols,) = run(
+        on_rows(forward_again_kernel),
+        [jax.ShapeDtypeStruct(*cols_shape)],
+        [framed, own, sems(2, rows), pltpu.VMEM(*cols_shape), sems(rows)],
+        (field, wind),
+        far=(0, 1),
+        out_far=(0,),
+        traffic=20 * MIB,
+    )
+    cols, halos = lax.optimization_barrier((cols, halos))
     (floor,) = run(on_rows(forward_floor_kernel), [low_shape], [], (low0, low1, floor_winds, *halos))
-    (cols,) = run(
-        on_rows(functools.partial(forward_kernel, False, True)),
-        [jax.ShapeDtypeStruct(*cols_shape)],
-        [framed, own, sides, sems(2, rows), pltpu.VMEM(*cols_shape), sems(rows)],
-        (coupling, swap_floor(floor), field, wind, *halos),
-        far=(2, 3),
-        out_far=(0,),
+    extra, bottom = run(
+        on_rows(outside_kernel),
+        [jax.ShapeDtypeStruct((2 * width, 3 * LANES), jnp.bfloat16), low_shape],
+        [sides],
+        (coupling, floor, swap_floor(floor), wind_ends, wind_dense, *halos),
     )
 
     spread_shape = ((2 * width, slots), jnp.bfloat16)
@@ -845,17 +903,14 @@
         [jax.ShapeDtypeStruct(*spread_shape), jax.ShapeDtypeStruct(*sel_shape), f32(2, width, LANES), packed_shape, thin_shape],
         [
             pltpu.VMEM(*cols_shape),
-            pltpu.VMEM(*sel_shape),
             pltpu.VMEM((slots, LANES), jnp.bfloat16),
             pltpu.VMEM((slots, LANES), jnp.float32),
-            pltpu.VMEM((slots, LANES), jnp.float32),
             pltpu.VMEM((slots, 2 * width), jnp.float32),
-            pltpu.VMEM(*spread_shape),
-            sems(8 + slots // 256 + 1),
+            sems(8),
         ],
-        (records, cols),
+        (records, cols, extra, bottom),
         far=(1,),
-        out_far=(0, 1),
+        limit=OBSERVE_VMEM,
     )
     strips = run(
         on_rows(border_kernel),
@@ -864,21 +919,15 @@
         (coupling, swap_floor(border_floor), ends, columns, wind_ends, wind_dense, dense_g),
     )
     halos = exchange(strips[:2], strips[2])
-    adjoint, low0, _ = run(
-        functools.partial(scatter_kernel, rows, width),
-        [field_shape, low_shape, low_shape],
-        [pltpu.VMEM(*spread_shape), pltpu.VMEM(*sel_shape), own, sems(2 * rows + 1)],
-        (spread, sel),
-        far=(0, 1),
-        out_far=(0,),
+    adjoint, low0 = run(
+        functools.partial(scatter_kernel, rows, width), [field_shape, low_shape], [], (spread, sel), limit=OBSERVE_VMEM
     )
     adjoint, ends, columns, low0 = run(
         on_rows(first_adjoint_kernel),
         [field_shape, f32(2, width, LANES), packed_shape, low_shape],
-        [framed, framed, own, sems(3, rows)],
+        [framed, framed, sems(rows)],
         (coupling, swap_floor(low0), adjoint, wind),
-        far=(2, 3),
-        out_far=(0,),
+        far=(3,),
     )
     (floor,) = run(on_rows(floor_kernel), [low_shape], [], (low0, *halos))
     other = swap_floor(floor)
@@ -892,17 +941,15 @@
     (adjoint,) = run(
         on_rows(second_adjoint_kernel),
         [field_shape],
-        [framed, framed, own, sides, sems(3, rows)],
-        (coupling, other, adjoint, wind, *halos),
-        far=(2, 3),
-        out_far=(0,),
+        [framed, framed, own, sides, sems(2, rows)],
+        (coupling, other, adjoint, wind, scale, state, *halos),
+        far=(3, 5),
     )
     (result,) = run(
         on_rows(final_kernel),
         [f32(width, rows, LANES)],
-        [own, own, sides, sems(3, rows)],
-        (scale, adjoint, state, *last_halos),
-        far=(1, 2),
+        [own, sides, sems(rows)],
+        (adjoint, *last_halos),
         out_far=(0,),
     )
     return result.reshape(state_incr.shape)

time: 116 us -> 83 us (0.72)
  Pallas kernels: 65.8 us -> 41.5 us
  local copies, waits for them, and re-layouts: 7.37 us -> 0.83 us
  waiting for transfers between devices: 12.9 us -> 9.89 us
    pallas_call x13 -> x14, Pallas kernels: 62.7 us -> 39.5 us  [run(): call(body, out_shape, scratch, in_specs=specs, out_specs=outs, **kw)(*args)]
    unnamed x38 -> x12, local copies, waits for them, and re-layouts: 5.3 us -> 0.03 us
    ppermute x12, waiting for transfers between devices: 6.28 us -> 4.36 us  [pair_swap(): return lax.ppermute(block, axis, route)]
  transfers between devices with their start and end apart: 18 -> 18, of which waited for: 8 -> 7; matrix products, arithmetic and copies ran while one was open for 1% -> 1% of each run, Pallas kernels for 37% -> 34%
where the time goes in v5:
time: 83 us; the launch traced here: 82 us
  Pallas kernels  41.5 us (50%)
  starting transfers between devices  29.4 us (35%)
  waiting for transfers between devices  9.89 us (12%)
    pallas_call x14, Pallas kernels, run(): call(body, out_shape, scratch, in_specs=specs, out_specs=outs, **kw)(*args)  39.5 us
    ppermute x12, starting transfers between devices, pair_swap(): return lax.ppermute(block, axis, route)  23.4 us
    ppermute x5, waiting for transfers between devices, swap_floor(): return lax.ppermute(floor, 'comp', [(0, 1), (1, 0)])  5.53 us
    all_to_all x1, starting transfers between devices, local(): lax.all_to_all(send, ('gx', 'gy'), split_axis=0, concat_axis=0, tiled=True)  5.34 us
    ppermute x12, waiting for transfers between devices, pair_swap(): return lax.ppermute(block, axis, route)  4.36 us
    pallas_call x1, Pallas kernels, local(): call(functools.partial(route_kernel, tiles, cap), f32(tiles, halves * cap...  2 us
  transfers between devices with their start and end apart: 18, of which 7 were waited for; matrix products, arithmetic and copies ran while one was open for 1% of the time, Pallas kernels for 34%

profile of v5, /device:TPU:8, one launch (start us, length us, event | category | flops | bytes accessed | tf_op | source)
XLA Modules:
  0.0 82.0 jit_solution(6482268035020039115)
XLA Ops:
  0.0 2.9 %shard_map.83 = (f32[256,128]{1,0:T(8,128)S(1)}, f32[256,128]{1,0:T(8,128)}, f32[64,128]{1,0:T(8,128)S(1)}, f32[32,128]{1,0:T(8,128)S(1)}, f32[32,128]{1,0:T(8,128)S(1)}) custom-call(f32[4096,128]{1,0:T(8,128)} %bitcast.19), custom_call_target="tpu_custom_call" | custom-call | tf_op jit(solution)/shard_map/pallas_call | solution.py:839
  2.9 1.6 %collective-permute-start = (f32[256,128]{1,0:T(8,128)S(1)}, f32[256,128]{1,0:T(8,128)S(1)}, u32[]{:S(2)}, u32[]{:S(2)}) collective-permute-start(f32[256,128]{1,0:T(8,128)S(1)} %get-tuple-element.41), channel_id=1, source_target_pairs={{0,8},{8,0},{1,9},{9,1},{2,10},{10,2},{3,11},{11,3},{4,12},{12,4},... | collective-permute-start | bytes 393224 | tf_op jit(solution)/shard_map/ppermute | solution.py:48
  4.5 3.3 %collective-permute-start.1 = (f32[64,128]{1,0:T(8,128)S(1)}, f32[64,128]{1,0:T(8,128)S(1)}, u32[]{:S(2)}, u32[]{:S(2)}) collective-permute-start(f32[64,128]{1,0:T(8,128)S(1)} %get-tuple-element.42), channel_id=1, source_target_pairs={{1,2},{2,1},{3,4},{4,3},{5,6},{6,5},{9,10},{10,9},{11,12},{12,11},... | collective-permute-start | bytes 98312 | tf_op jit(solution)/shard_map/ppermute | solution.py:48
  7.8 2.0 %shard_map.82 = f32[16,136,128]{2,1,0:T(8,128)} custom-call(s32[1,512]{1,0:T(1,128)S(1)} %bitcast.12, s32[1,512]{1,0:T(1,128)S(1)} %bitcast.13, f32[1,512]{1,0:T(1,128)S(1)} %bitcast.14, f32[512,256]{1,0:T(8,128)S(1)} %copy-done), custom_call_target="tpu_custom_call" | custom-call | tf_op jit(solution)/shard_map/pallas_call | solution.py:862
  9.8 1.4 %collective-permute-done.1.rest_2_ = f32[64,128]{1,0:T(8,128)S(1)} collective-permute-done((f32[64,128]{1,0:T(8,128)S(1)}, f32[64,128]{1,0:T(8,128)S(1)}, u32[]{:S(2)}, u32[]{:S(2)}) %collective-permute-start.1) | collective-permute-done | bytes 32800 | tf_op jit(solution)/shard_map/ppermute | solution.py:48
  11.2 5.3 %all-to-all-start = ((f32[16,136,128]{2,1,0:T(8,128)}), f32[16,136,128]{2,1,0:T(8,128)S(1)}, u32[]{:S(2)}, u32[]{:S(2)}) async-start(f32[16,136,128]{2,1,0:T(8,128)} %shard_map.82), calls=%async_computation | async-start | bytes 2228224 | tf_op jit(solution)/shard_map/all_to_all | solution.py:866
  16.5 1.5 %collective-permute-start.2 = (f32[64,128]{1,0:T(8,128)S(1)}, f32[64,128]{1,0:T(8,128)S(1)}, u32[]{:S(2)}, u32[]{:S(2)}) collective-permute-start(f32[64,128]{1,0:T(8,128)S(1)} %get-tuple-element.42), channel_id=1, source_target_pairs={{0,1},{1,0},{2,3},{3,2},{4,5},{5,4},{6,7},{7,6},{8,9},{9,8},{10,11... | collective-permute-start | bytes 98312 | tf_op jit(solution)/shard_map/ppermute | solution.py:48
  18.0 0.7 slice_bitcast_fusion.winds
  18.7 3.0 %collective-permute-done.2.rest_1_ = f32[64,128]{1,0:T(8,128)S(1)} collective-permute-done((f32[64,128]{1,0:T(8,128)S(1)}, f32[64,128]{1,0:T(8,128)S(1)}, u32[]{:S(2)}, u32[]{:S(2)}) %collective-permute-start.2) | collective-permute-done | bytes 32800 | tf_op jit(solution)/shard_map/ppermute | solution.py:48
  21.9 1.2 %collective-permute-done.3.other = f32[32,128]{1,0:T(8,128)S(1)} collective-permute-done((f32[32,128]{1,0:T(8,128)S(1)}, f32[32,128]{1,0:T(8,128)S(1)}, u32[]{:S(2)}, u32[]{:S(2)}) %collective-permute-start.3) | collective-permute-done | bytes 16416 | tf_op jit(solution)/shard_map/ppermute | solution.py:845
  23.1 7.4 %shard_map.85 = (f32[16,256,128]{2,1,0:T(8,128)}, f32[256,128]{1,0:T(8,128)S(1)}, f32[256,128]{1,0:T(8,128)}, f32[64,128]{1,0:T(8,128)S(1)}, f32[32,128]{1,0:T(8...) custom-call(f32[16,128]{1,0:T(8,128)S(1)} %copy-done.1, ...), custom_call_target="tpu_custom_call" | custom-call | tf_op jit(solution)/shard_map/pallas_call | solution.py:839
  30.5 1.5 %collective-permute-start.4 = (f32[256,128]{1,0:T(8,128)S(1)}, f32[256,128]{1,0:T(8,128)S(1)}, u32[]{:S(2)}, u32[]{:S(2)}) collective-permute-start(f32[256,128]{1,0:T(8,128)S(1)} %get-tuple-element.49), channel_id=1, source_target_pairs={{0,8},{8,0},{1,9},{9,1},{2,10},{10,2},{3,11},{11,3},{4,12},{12,4},... | collective-permute-start | bytes 393224 | tf_op jit(solution)/shard_map/ppermute | solution.py:48
  32.0 0.6 collective-permute-start.5
  32.6 4.8 %collective-permute-start.6 = (f32[64,128]{1,0:T(8,128)S(1)}, f32[64,128]{1,0:T(8,128)S(1)}, u32[]{:S(2)}, u32[]{:S(2)}) collective-permute-start(f32[64,128]{1,0:T(8,128)S(1)} %get-tuple-element.50), channel_id=1, source_target_pairs={{1,2},{2,1},{3,4},{4,3},{5,6},{6,5},{9,10},{10,9},{11,12},{12,11},... | collective-permute-start | bytes 98312 | tf_op jit(solution)/shard_map/ppermute | solution.py:48
  37.4 4.6 %shard_map.86.cols = bf16[512,2048]{1,0:T(8,128)(2,1)} custom-call(f32[16,256,128]{2,1,0:T(8,128)} %get-tuple-element.48.field, f32[256,16,128]{2,1,0:T(8,128)} %bitcast.16), custom_call_target="tpu_custom_call" | custom-call | bytes 20971520 | tf_op jit(solution)/shard_map/pallas_call | solution.py:839
  42.4 1.2 %collective-permute-done.7.other = f32[32,128]{1,0:T(8,128)S(1)} collective-permute-done((f32[32,128]{1,0:T(8,128)S(1)}, f32[32,128]{1,0:T(8,128)S(1)}, u32[]{:S(2)}, u32[]{:S(2)}) %collective-permute-start.7) | collective-permute-done | bytes 16416 | tf_op jit(solution)/shard_map/ppermute | solution.py:845
  43.8 6.3 %shard_map.89 = (bf16[512,1024]{1,0:T(8,128)(2,1)S(1)}, bf16[1024,2048]{1,0:T(8,128)(2,1)S(1)}, f32[2,256,128]{2,1,0:T(8,128)S(1)}, f32[64,128]{1,0:T(8,128)S(1)}, f32[8,128]{1,0:T(8,128)S(1)}) custom-call(f32[16,136,128]{2,1,0:T(8,128)S(1)} %all-to-all-done.records, bf16[512,2048]{1,0:T(8,128)(2,1)} %shard_map.86.cols, ...), custom_call_target="tpu_custom_call" | custom-call | tf_op jit(solution)/shard_map/pallas_call | solution.py:839
  50.3 1.0 %collective-permute-done.9.other = f32[8,128]{1,0:T(8,128)S(1)} collective-permute-done((f32[8,128]{1,0:T(8,128)S(1)}, f32[8,128]{1,0:T(8,128)S(1)}, u32[]{:S(2)}, u32[]{:S(2)}) %collective-permute-start.9) | collective-permute-done | bytes 4128 | tf_op jit(solution)/shard_map/ppermute | solution.py:845
  51.3 0.7 shard_map.92
  52.0 0.6 collective-permute-start.10
  52.6 2.2 %collective-permute-start.11 = (f32[64,128]{1,0:T(8,128)S(1)}, f32[64,128]{1,0:T(8,128)S(1)}, u32[]{:S(2)}, u32[]{:S(2)}) collective-permute-start(f32[64,128]{1,0:T(8,128)S(1)} %get-tuple-element.71), channel_id=1, source_target_pairs={{0,1},{1,0},{2,3},{3,2},{4,5},{5,4},{6,7},{7,6},{8,9},{9,8},{10,11... | collective-permute-start | bytes 98312 | tf_op jit(solution)/shard_map/ppermute | solution.py:48
  54.8 1.9 %collective-permute-start.12 = (f32[64,128]{1,0:T(8,128)S(1)}, f32[64,128]{1,0:T(8,128)S(1)}, u32[]{:S(2)}, u32[]{:S(2)}) collective-permute-start(f32[64,128]{1,0:T(8,128)S(1)} %get-tuple-element.71), channel_id=1, source_target_pairs={{1,2},{2,1},{3,4},{4,3},{5,6},{6,5},{9,10},{10,9},{11,12},{12,11},... | collective-permute-start | bytes 98312 | tf_op jit(solution)/shard_map/ppermute | solution.py:48
  56.7 2.4 %shard_map.90 = (f32[16,256,128]{2,1,0:T(8,128)S(1)}, f32[32,128]{1,0:T(8,128)S(1)}) custom-call(bf16[512,1024]{1,0:T(8,128)(2,1)S(1)} %get-tuple-element.61.spread, bf16[1024,2048]{1,0:T(8,128)(2,1)S(1)} %get-tuple-element.62.sel), custom_call_target="tpu_custom_call" | custom-call | tf_op jit(solution)/shard_map/pallas_call | solution.py:839
  59.1 1.2 %collective-permute-done.8.other = f32[32,128]{1,0:T(8,128)S(1)} collective-permute-done((f32[32,128]{1,0:T(8,128)S(1)}, f32[32,128]{1,0:T(8,128)S(1)}, u32[]{:S(2)}, u32[]{:S(2)}) %collective-permute-start.8) | collective-permute-done | bytes 16416 | tf_op jit(solution)/shard_map/ppermute | solution.py:845
  60.3 4.8 %shard_map.91 = (f32[16,256,128]{2,1,0:T(8,128)S(1)}, f32[2,256,128]{2,1,0:T(8,128)S(1)}, f32[64,128]{1,0:T(8,128)S(1)}, f32[32,128]{1,0:T(8,128)S(1)}) custom-call(f32[16,128]{1,0:T(8,128)S(1)} %copy-done.1, f32[32,128]{1,0:T(8,128)S(1)} %collective-permute-done.8.other, f32[16,256,128]{2,1,0:T(8,128)S(1)} %get-tuple-element.64.field, f32[256,16,128]{2,1,0:T(8,128)} %bitcast.17), custom_call_target="tpu_custom_call" | custom-call | tf_op jit(solution)/shard_map/pallas_call | solution.py:839
  65.5 1.0 %collective-permute-done.13.other = f32[32,128]{1,0:T(8,128)S(1)} collective-permute-done((f32[32,128]{1,0:T(8,128)S(1)}, f32[32,128]{1,0:T(8,128)S(1)}, u32[]{:S(2)}, u32[]{:S(2)}) %collective-permute-start.13) | collective-permute-done | bytes 16416 | tf_op jit(solution)/shard_map/ppermute | solution.py:845
  66.5 0.9 %shard_map.95 = (f32[256,128]{1,0:T(8,128)S(1)}, f32[256,128]{1,0:T(8,128)}, f32[64,128]{1,0:T(8,128)S(1)}) custom-call(f32[16,128]{1,0:T(8,128)S(1)} %copy-done.1, f32[32,128]{1,0:T(8,128)S(1)} %shard_map.93.floor, f32[32,128]{1,0:T(8,128)S(1)} %collective-permute-done.13.other, f32[2,256,128]{2,1,0:T(8,128)S(1)} %get-tuple-element.73.ends, ...), custom_call_target="tpu_custom_call" | custom-call | tf_op jit(solution)/shard_map/pallas_call | solution.py:839
  67.4 0.7 collective-permute-start.14
  68.1 2.0 %collective-permute-start.15 = (f32[64,128]{1,0:T(8,128)S(1)}, f32[64,128]{1,0:T(8,128)S(1)}, u32[]{:S(2)}, u32[]{:S(2)}) collective-permute-start(f32[64,128]{1,0:T(8,128)S(1)} %get-tuple-element.76), channel_id=1, source_target_pairs={{0,1},{1,0},{2,3},{3,2},{4,5},{5,4},{6,7},{7,6},{8,9},{9,8},{10,11... | collective-permute-start | bytes 98312 | tf_op jit(solution)/shard_map/ppermute | solution.py:48
  70.1 2.8 %collective-permute-start.16 = (f32[64,128]{1,0:T(8,128)S(1)}, f32[64,128]{1,0:T(8,128)S(1)}, u32[]{:S(2)}, u32[]{:S(2)}) collective-permute-start(f32[64,128]{1,0:T(8,128)S(1)} %get-tuple-element.76), channel_id=1, source_target_pairs={{1,2},{2,1},{3,4},{4,3},{5,6},{6,5},{9,10},{10,9},{11,12},{12,11},... | collective-permute-start | bytes 98312 | tf_op jit(solution)/shard_map/ppermute | solution.py:48
  73.0 6.4 %shard_map.94.field = f32[16,256,128]{2,1,0:T(8,128)S(1)} custom-call(f32[16,128]{1,0:T(8,128)S(1)} %copy-done.1, f32[32,128]{1,0:T(8,128)S(1)} %collective-permute-done.13.other, f32[16,256,128]{2,1,0:T(8,128)S(1)} %get-tuple-element.72.field, f32[256,16,128]{2,1,0:T(8,128)} %bitcast.18, f32[256,128]{1,0:T(8,128)S(1)} %broadcast_in_dim.8.scale, ...), custom_call_target="tpu_custom_call" | custom-call | tf_op jit(solution)/shard_map/pallas_call | solution.py:839
  79.5 2.5 %shard_map.96 = f32[256,16,128]{2,1,0:T(8,128)} custom-call(f32[16,256,128]{2,1,0:T(8,128)S(1)} %shard_map.94.field, f32[256,128]{1,0:T(8,128)S(1)} %collective-permute-done.14.rest_0_, f32[64,128]{1,0:T(8,128)S(1)} %collective-permute-done.15.rest_1_, f32[64,128]{1,0:T(8,128)S(1)} %collective-permute-done.16.rest_2_), custom_call_target="tpu_custom_call" | custom-call | tf_op jit(solution)/shard_map/pallas_call | solution.py:839
  (33 shorter events, 1.5 us)
Async XLA Ops:
  0.0 7.8 %copy-start.2 = (s32[512,1]{0,1:T(1,128)S(1)}, s32[512,1]{0,1:T(1,128)}, u32[]{:S(2)}) copy-start(s32[512,1]{0,1:T(1,128)} %param.12) | copy-start | bytes 6148
  0.0 7.8 %copy-start.3 = (s32[512]{0:T(512)S(1)}, s32[512]{0:T(512)}, u32[]{:S(2)}) copy-start(s32[512]{0:T(512)} %param.13) | copy-start | bytes 6148
  0.0 7.8 %copy-start.4 = (f32[512]{0:T(512)S(1)}, f32[512]{0:T(512)}, u32[]{:S(2)}) copy-start(f32[512]{0:T(512)} %param.15) | copy-start | bytes 6148
  0.0 7.8 %copy-start = (f32[512,256]{1,0:T(8,128)S(1)}, f32[512,256]{1,0:T(8,128)}, u32[]{:S(2)}) copy-start(f32[512,256]{1,0:T(8,128)} %op.1) | copy-start | bytes 1572868
  2.9 20.2 %copy-start.1 = (f32[16,128]{1,0:T(8,128)S(1)}, f32[16,128]{1,0:T(8,128)}, u32[]{:S(2)}) copy-start(f32[16,128]{1,0:T(8,128)} %coupling.11) | copy-start | bytes 24580
  2.9 8.3 %collective-permute-start = (f32[256,128]{1,0:T(8,128)S(1)}, f32[256,128]{1,0:T(8,128)S(1)}, u32[]{:S(2)}, u32[]{:S(2)}) collective-permute-start(f32[256,128]{1,0:T(8,128)S(1)} %get-tuple-element.41), channel_id=1, source_target_pairs={{0,8},{8,0},{1,9},{9,1},{2,10},{10,2},{3,11},{11,3},{4,12},{12,4},... | collective-permute-start | bytes 393224 | tf_op jit(solution)/shard_map/ppermute | solution.py:48
  4.5 6.7 %collective-permute-start.1 = (f32[64,128]{1,0:T(8,128)S(1)}, f32[64,128]{1,0:T(8,128)S(1)}, u32[]{:S(2)}, u32[]{:S(2)}) collective-permute-start(f32[64,128]{1,0:T(8,128)S(1)} %get-tuple-element.42), channel_id=1, source_target_pairs={{1,2},{2,1},{3,4},{4,3},{5,6},{6,5},{9,10},{10,9},{11,12},{12,11},... | collective-permute-start | bytes 98312 | tf_op jit(solution)/shard_map/ppermute | solution.py:48
  11.2 32.5 %all-to-all-start = ((f32[16,136,128]{2,1,0:T(8,128)}), f32[16,136,128]{2,1,0:T(8,128)S(1)}, u32[]{:S(2)}, u32[]{:S(2)}) async-start(f32[16,136,128]{2,1,0:T(8,128)} %shard_map.82), calls=%async_computation | async-start | bytes 2228224 | tf_op jit(solution)/shard_map/all_to_all | solution.py:866
  16.5 5.1 %collective-permute-start.2 = (f32[64,128]{1,0:T(8,128)S(1)}, f32[64,128]{1,0:T(8,128)S(1)}, u32[]{:S(2)}, u32[]{:S(2)}) collective-permute-start(f32[64,128]{1,0:T(8,128)S(1)} %get-tuple-element.42), channel_id=1, source_target_pairs={{0,1},{1,0},{2,3},{3,2},{4,5},{5,4},{6,7},{7,6},{8,9},{9,8},{10,11... | collective-permute-start | bytes 98312 | tf_op jit(solution)/shard_map/ppermute | solution.py:48
  21.9 1.2 %collective-permute-start.3 = (f32[32,128]{1,0:T(8,128)S(1)}, f32[32,128]{1,0:T(8,128)S(1)}, u32[]{:S(2)}, u32[]{:S(2)}) collective-permute-start(f32[32,128]{1,0:T(8,128)S(1)} %shard_map.84), channel_id=1, source_target_pairs={{0,16},{16,0},{1,17},{17,1},{2,18},{18,2},{3,19},{19,3},{4,20},{20... | collective-permute-start | bytes 49160 | tf_op jit(solution)/shard_map/ppermute | solution.py:845
  30.5 11.6 %collective-permute-start.4 = (f32[256,128]{1,0:T(8,128)S(1)}, f32[256,128]{1,0:T(8,128)S(1)}, u32[]{:S(2)}, u32[]{:S(2)}) collective-permute-start(f32[256,128]{1,0:T(8,128)S(1)} %get-tuple-element.49), channel_id=1, source_target_pairs={{0,8},{8,0},{1,9},{9,1},{2,10},{10,2},{3,11},{11,3},{4,12},{12,4},... | collective-permute-start | bytes 393224 | tf_op jit(solution)/shard_map/ppermute | solution.py:48
  32.0 10.1 %collective-permute-start.5 = (f32[64,128]{1,0:T(8,128)S(1)}, f32[64,128]{1,0:T(8,128)S(1)}, u32[]{:S(2)}, u32[]{:S(2)}) collective-permute-start(f32[64,128]{1,0:T(8,128)S(1)} %get-tuple-element.50), channel_id=1, source_target_pairs={{0,1},{1,0},{2,3},{3,2},{4,5},{5,4},{6,7},{7,6},{8,9},{9,8},{10,11... | collective-permute-start | bytes 98312 | tf_op jit(solution)/shard_map/ppermute | solution.py:48
  32.6 9.5 %collective-permute-start.6 = (f32[64,128]{1,0:T(8,128)S(1)}, f32[64,128]{1,0:T(8,128)S(1)}, u32[]{:S(2)}, u32[]{:S(2)}) collective-permute-start(f32[64,128]{1,0:T(8,128)S(1)} %get-tuple-element.50), channel_id=1, source_target_pairs={{1,2},{2,1},{3,4},{4,3},{5,6},{6,5},{9,10},{10,9},{11,12},{12,11},... | collective-permute-start | bytes 98312 | tf_op jit(solution)/shard_map/ppermute | solution.py:48
  42.3 1.2 %collective-permute-start.7 = (f32[32,128]{1,0:T(8,128)S(1)}, f32[32,128]{1,0:T(8,128)S(1)}, u32[]{:S(2)}, u32[]{:S(2)}) collective-permute-start(f32[32,128]{1,0:T(8,128)S(1)} %shard_map.87.floor), channel_id=1, source_target_pairs={{0,16},{16,0},{1,17},{17,1},{2,18},{18,2},{3,19},{19,3},{4,20},{20... | collective-permute-start | bytes 49160 | tf_op jit(solution)/shard_map/ppermute | solution.py:845
  50.1 1.2 %collective-permute-start.9 = (f32[8,128]{1,0:T(8,128)S(1)}, f32[8,128]{1,0:T(8,128)S(1)}, u32[]{:S(2)}, u32[]{:S(2)}) collective-permute-start(f32[8,128]{1,0:T(8,128)S(1)} %get-tuple-element.66), channel_id=1, source_target_pairs={{0,16},{16,0},{1,17},{17,1},{2,18},{18,2},{3,19},{19,3},{4,20},{20... | collective-permute-start | bytes 12296 | tf_op jit(solution)/shard_map/ppermute | solution.py:845
  52.0 13.0 %collective-permute-start.10 = (f32[256,128]{1,0:T(8,128)S(1)}, f32[256,128]{1,0:T(8,128)S(1)}, u32[]{:S(2)}, u32[]{:S(2)}) collective-permute-start(f32[256,128]{1,0:T(8,128)S(1)} %get-tuple-element.70), channel_id=1, source_target_pairs={{0,8},{8,0},{1,9},{9,1},{2,10},{10,2},{3,11},{11,3},{4,12},{12,4},... | collective-permute-start | bytes 393224 | tf_op jit(solution)/shard_map/ppermute | solution.py:48
  52.6 12.5 %collective-permute-start.11 = (f32[64,128]{1,0:T(8,128)S(1)}, f32[64,128]{1,0:T(8,128)S(1)}, u32[]{:S(2)}, u32[]{:S(2)}) collective-permute-start(f32[64,128]{1,0:T(8,128)S(1)} %get-tuple-element.71), channel_id=1, source_target_pairs={{0,1},{1,0},{2,3},{3,2},{4,5},{5,4},{6,7},{7,6},{8,9},{9,8},{10,11... | collective-permute-start | bytes 98312 | tf_op jit(solution)/shard_map/ppermute | solution.py:48
  54.8 10.3 %collective-permute-start.12 = (f32[64,128]{1,0:T(8,128)S(1)}, f32[64,128]{1,0:T(8,128)S(1)}, u32[]{:S(2)}, u32[]{:S(2)}) collective-permute-start(f32[64,128]{1,0:T(8,128)S(1)} %get-tuple-element.71), channel_id=1, source_target_pairs={{1,2},{2,1},{3,4},{4,3},{5,6},{6,5},{9,10},{10,9},{11,12},{12,11},... | collective-permute-start | bytes 98312 | tf_op jit(solution)/shard_map/ppermute | solution.py:48
  59.0 1.2 %collective-permute-start.8 = (f32[32,128]{1,0:T(8,128)S(1)}, f32[32,128]{1,0:T(8,128)S(1)}, u32[]{:S(2)}, u32[]{:S(2)}) collective-permute-start(f32[32,128]{1,0:T(8,128)S(1)} %get-tuple-element.63), channel_id=1, source_target_pairs={{0,16},{16,0},{1,17},{17,1},{2,18},{18,2},{3,19},{19,3},{4,20},{20... | collective-permute-start | bytes 49160 | tf_op jit(solution)/shard_map/ppermute | solution.py:845
  60.3 12.7 %copy-start.5 = (f32[1,2,128]{2,1,0:T(2,128)S(1)}, f32[1,2,128]{2,1,0:T(2,128)}, u32[]{:S(2)}) copy-start(f32[1,2,128]{2,1,0:T(2,128)} %param.11) | copy-start | bytes 3076
  65.2 1.2 %collective-permute-start.13 = (f32[32,128]{1,0:T(8,128)S(1)}, f32[32,128]{1,0:T(8,128)S(1)}, u32[]{:S(2)}, u32[]{:S(2)}) collective-permute-start(f32[32,128]{1,0:T(8,128)S(1)} %shard_map.93.floor), channel_id=1, source_target_pairs={{0,16},{16,0},{1,17},{17,1},{2,18},{18,2},{3,19},{19,3},{4,20},{20... | collective-permute-start | bytes 49160 | tf_op jit(solution)/shard_map/ppermute | solution.py:845
  67.4 12.1 %collective-permute-start.14 = (f32[256,128]{1,0:T(8,128)S(1)}, f32[256,128]{1,0:T(8,128)S(1)}, u32[]{:S(2)}, u32[]{:S(2)}) collective-permute-start(f32[256,128]{1,0:T(8,128)S(1)} %get-tuple-element.75), channel_id=1, source_target_pairs={{0,8},{8,0},{1,9},{9,1},{2,10},{10,2},{3,11},{11,3},{4,12},{12,4},... | collective-permute-start | bytes 393224 | tf_op jit(solution)/shard_map/ppermute | solution.py:48
  68.1 11.4 %collective-permute-start.15 = (f32[64,128]{1,0:T(8,128)S(1)}, f32[64,128]{1,0:T(8,128)S(1)}, u32[]{:S(2)}, u32[]{:S(2)}) collective-permute-start(f32[64,128]{1,0:T(8,128)S(1)} %get-tuple-element.76), channel_id=1, source_target_pairs={{0,1},{1,0},{2,3},{3,2},{4,5},{5,4},{6,7},{7,6},{8,9},{9,8},{10,11... | collective-permute-start | bytes 98312 | tf_op jit(solution)/shard_map/ppermute | solution.py:48
  70.1 9.4 %collective-permute-start.16 = (f32[64,128]{1,0:T(8,128)S(1)}, f32[64,128]{1,0:T(8,128)S(1)}, u32[]{:S(2)}, u32[]{:S(2)}) collective-permute-start(f32[64,128]{1,0:T(8,128)S(1)} %get-tuple-element.76), channel_id=1, source_target_pairs={{1,2},{2,1},{3,4},{4,3},{5,6},{6,5},{9,10},{10,9},{11,12},{12,11},... | collective-permute-start | bytes 98312 | tf_op jit(solution)/shard_map/ppermute | solution.py:48

commit v6 on v5

--- a/solution.py
+++ b/solution.py
@@ -307,81 +307,71 @@
     return total
 
 
+def load_kernel(rows, state, winds, state_rows, wind_rows, sems):
+    state_in = Rows(state, state_rows, sems.at[0], rows, True, 0)
+    wind_in = Rows(winds, wind_rows, sems.at[1], rows, True, 0)
+    start_rows(rows, state_in, wind_in)
+    for i in range(rows):
+        state_in.wait(i)
+        wind_in.wait(i)
+
+
 def forward_kernel(rows, levels, coupling, other, field, winds, *rest):
-    *halos, out, s_even, s_odd, packed, low0, low1, wind_ends, wind_dense, dense_g = rest[:-5]
-    cells, wind_cells, out_cells, sides, sems = rest[-5:]
-    leaving = Out(out_cells, out, sems.at[2], rows, False)
-    incoming = Rows(field, cells, sems.at[0], rows, True, 1)
-    wind_in = Rows(winds, wind_cells, sems.at[1], rows, True, 0)
-    start_rows(rows, incoming, wind_in)
+    *halos, out, s_even, s_odd, packed, low0, low1, wind_ends, wind_dense, dense_g, cells, sides = rest
     packed[...] = jnp.zeros_like(packed)
     wind_dense[...] = jnp.zeros_like(wind_dense)
     merge_columns(halos[1], halos[2], sides)
     before, after = read_sides(halos)
     cells[0] = before(slice(None))
+    cells[1] = field[0]
     cells[rows + 1] = after(slice(None))
+    out[0] = jnp.zeros_like(out[0])
+    out[rows + 1] = jnp.zeros_like(out[0])
     groups = levels // GROUP
-    incoming.wait(0)
 
     def row(i, _):
         @pl.when(i < rows - 1)
         def _():
-            incoming.wait(i + 1)
-
-        wind_in.wait(i)
+            cells[i + 2] = field[i + 1]
+
         for m in range(2 * groups // PARTS):
             f, start = m * PARTS // groups, m * PARTS % groups
             values = []
             for group in range(start, start + PARTS):
-                value = forward_point(cells, wind_cells, sides, i, f, group, levels)
+                value = forward_point(cells, winds, sides, i, f, group, levels)
                 if group == 0:
                     value = coupled(couple_forward, value, other, coupling, i, f, rows)
                     put_low((low0, low1), value, i, f, rows)
                 values.append(value)
             base = m * PARTS * GROUP
             for part, value in enumerate(values):
-                out_cells[i, pl.ds(base + part * GROUP, GROUP), :] = value
+                out[i + 1, pl.ds(base + part * GROUP, GROUP), :] = value
             pack_block(packed, values, i, m)
             if f == 0:
-                w = [wind_cells[i, pl.ds(levels + base + part * GROUP, GROUP), :] for part in range(PARTS)]
+                w = [winds[i, pl.ds(levels + base + part * GROUP, GROUP), :] for part in range(PARTS)]
                 pack_block(wind_dense, w, i, m)
-        leaving.start(i)
         return 0
 
     lax.fori_loop(0, rows, row, 0)
-    put_strip(s_even, s_odd, slice(None), out_cells[0], out_cells[rows - 1])
-    wind_ends[0] = wind_cells[0, pl.ds(0, levels), :]
-    wind_ends[1] = wind_cells[rows - 1, pl.ds(0, levels), :]
+    put_strip(s_even, s_odd, slice(None), out[1], out[rows])
+    wind_ends[0] = winds[0, pl.ds(0, levels), :]
+    wind_ends[1] = winds[rows - 1, pl.ds(0, levels), :]
     dense_g[...] = jnp.broadcast_to(dense_row(coupling, 0, rows), dense_g.shape)
-    leaving.finish()
-
-
-def forward_again_kernel(rows, levels, field, winds, cols, cells, wind_cells, sems, col_cells, col_sems):
-    incoming = Rows(field, cells, sems.at[0], rows, False, 1)
-    wind_in = Rows(winds, wind_cells, sems.at[1], rows, True, 0)
-    start_rows(rows, incoming, wind_in)
-    cells[0] = jnp.zeros_like(cells[0])
-    cells[rows + 1] = jnp.zeros_like(cells[0])
+
+
+def forward_again_kernel(rows, levels, cells, winds, cols, col_cells, col_sems):
     groups = levels // GROUP
     width = 2 * levels
-    incoming.wait(0)
 
     def col_copy(i):
         lanes = pl.ds(pl.multiple_of(i * LANES, LANES), LANES)
         return pltpu.make_async_copy(col_cells.at[:, lanes], cols.at[:, lanes], col_sems.at[i])
 
     def row(i, _):
-        @pl.when(i < rows - 1)
-        def _():
-            incoming.wait(i + 1)
-
-        wind_in.wait(i)
         lanes = pl.ds(pl.multiple_of(i * LANES, LANES), LANES)
         for m in range(2 * groups // PARTS):
             f, start = m * PARTS // groups, m * PARTS % groups
-            values = [
-                forward_point(cells, wind_cells, None, i, f, group, levels) for group in range(start, start + PARTS)
-            ]
+            values = [forward_point(cells, winds, None, i, f, group, levels) for group in range(start, start + PARTS)]
             high, low = split(jnp.concatenate(values, axis=0), 2)
             col_cells[pl.ds(m * PARTS * GROUP, PARTS * GROUP), lanes] = high
             col_cells[pl.ds(width + m * PARTS * GROUP, PARTS * GROUP), lanes] = low
@@ -477,11 +467,19 @@
     return low + jnp.where((lane == 0) | (lane == LANES - 1), edge, 0.0)
 
 
-def floor_kernel(rows, levels, low0, *rest):
-    *halos, floor = rest
+def floor_kernel(rows, levels, coupling, other, low0, winds, *rest):
+    *halos, floor, missing = rest
     for f in range(2):
         here = pl.ds(f * rows, rows)
-        floor[here, :] = outside_floor(halos, low0[here, :], f, rows, levels)
+        _, peer = shares_of(coupling[...])
+        share = peer * other[here, :]
+        x_down, x_up = products(share, winds[0])
+        y_down, y_up = products(share, winds[1])
+        right, left = shifted(y_up, y_down, 0.0, rows)
+        spread = (row_after(x_up, 0.0, rows) + row_before(x_down, 0.0, rows)) + (right + left)
+        spread = spread + (CENTRE + VERT_MIX) * share
+        floor[here, :] = outside_floor(halos, low0[here, :] + spread, f, rows, levels)
+        missing[here, :] = VERT_MIX * share
 
 
 def swap_pairs(value):
@@ -497,7 +495,13 @@
     return jnp.where((lane == 0) | (lane == LANES - 1), moved, 0.0)
 
 
-def border_again_kernel(rows, levels, coupling, floor, other, ends, columns, wind_ends, wind_dense, dense_g, *rest):
+def with_level(value, level, new):
+    return jnp.where(lax.broadcasted_iota(jnp.int32, value.shape, 0) == level, new, value)
+
+
+def border_again_kernel(
+    rows, levels, coupling, floor, other, missing, ends, columns, wind_ends, wind_dense, dense_g, *rest
+):
     *halos, s_even, s_odd, packed, sides = rest
     before, after = read_sides(halos)
     sides[...] = swap_pairs(merged(halos[1], halos[2], slice(None)))
@@ -511,8 +515,9 @@
         parts = []
         for f in range(2):
             part = value[f * levels : (f + 1) * levels]
-            at = f * rows + i
-            parts.append(with_first(part, couple_adjoint(part[0:1], other[at : at + 1, :], coupling[i : i + 1, :])))
+            at = slice(f * rows + i, f * rows + i + 1)
+            part = part + with_level(jnp.zeros_like(part), 1, missing[at, :])
+            parts.append(with_first(part, couple_adjoint(floor[at, :], other[at, :], coupling[i : i + 1, :])))
         full.append(jnp.concatenate(parts, axis=0))
     end_rows(full, s_even, s_odd, wind_ends, levels)
     dense = columns[...] + sides[...]
@@ -526,18 +531,18 @@
         corners.append(total)
     dense = dense + jnp.concatenate(corners, axis=0)
     for f in range(2):
+        sub = lax.broadcasted_iota(jnp.int32, dense.shape, 0)
+        dense = dense + jnp.where(sub == f * half + 1, dense_row(missing, f * rows, rows), 0.0)
         mine = dense_row(floor, f * rows, rows)
         mixed = couple_adjoint(mine, dense_row(other, f * rows, rows), dense_g[0:1, :])
         dense = level0_row(dense, mixed, f)
     dense_products(packed, dense, wind_dense)
 
 
-def adjoint_rows(rows, levels, cells, wind_cells, take, each):
+def adjoint_rows(rows, levels, cells, winds, take, each):
     groups = levels // GROUP
     cells[0] = jnp.zeros_like(cells[0])
     cells[rows + 1] = jnp.zeros_like(cells[0])
-    wind_cells[0] = jnp.zeros_like(wind_cells[0])
-    wind_cells[rows + 1] = jnp.zeros_like(wind_cells[0])
     take(0)
 
     def row(i, _):
@@ -548,26 +553,25 @@
         for m in range(2 * groups // PARTS):
             f, start = m * PARTS // groups, m * PARTS % groups
             each(i, m, f, start, [
-                adjoint_point(cells, wind_cells, i, f, group, levels) for group in range(start, start + PARTS)
+                adjoint_point(cells, winds, i, f, group, levels) for group in range(start, start + PARTS)
             ])
         return 0
 
     lax.fori_loop(0, rows, row, 0)
 
 
-def first_adjoint_kernel(
-    rows, levels, coupling, other, field, winds, out, ends, columns, low0, cells, wind_cells, sems
-):
-    wind_in = Rows(winds, wind_cells, sems, rows, True, 1)
-    start_rows(rows, wind_in)
+def first_adjoint_kernel(rows, levels, coupling, field, winds, state, out, ends, columns, low0, state_rows, cells, sems):
+    state_in = Rows(state, state_rows, sems, rows, True, 0)
+    start_rows(rows, state_in)
     columns[...] = jnp.zeros_like(columns)
 
     def take(i):
-        wind_in.wait(i)
         cells[i + 1] = field[i]
         for f in range(2):
             at = pl.ds(f * levels, GROUP)
-            cells[i + 1, at, :] = coupled(couple_adjoint, field[i, at, :], other, coupling, i, f, rows)
+            own, _ = shares_of(coupling[pl.ds(i, 1), :])
+            value = field[i, at, :]
+            cells[i + 1, at, :] = jnp.where(sub_iota() == 0, value - own * value, value)
 
     def each(i, m, f, start, values):
         for part, value in enumerate(values):
@@ -576,29 +580,29 @@
             low0[pl.ds(f * rows + i, 1), :] = values[0][0:1]
         pack_block(columns, values, i, m)
 
-    adjoint_rows(rows, levels, cells, wind_cells, take, each)
+    adjoint_rows(rows, levels, cells, winds, take, each)
     ends[0] = out[0]
     ends[1] = out[rows - 1]
-
-
-def second_adjoint_kernel(rows, levels, coupling, other, field, winds, scale, state, *rest):
-    *halos, out, cells, wind_cells, state_cells, sides, sems = rest
-    wind_in = Rows(winds, wind_cells, sems.at[0], rows, True, 1)
-    state_in = Rows(state, state_cells, sems.at[1], rows, True, 0)
-    start_rows(rows, wind_in, state_in)
+    for i in range(rows):
+        state_in.wait(i)
+
+
+def second_adjoint_kernel(rows, levels, coupling, floor, other, missing, field, winds, scale, state, *rest):
+    *halos, out, cells, sides = rest
     sides[...] = swap_pairs(merged(halos[1], halos[2], slice(None)))
     before, after = read_sides(halos)
     groups = levels // GROUP
 
     def take(i):
-        wind_in.wait(i)
         for group in range(2 * groups):
             at = pl.ds(group * GROUP, GROUP)
             value = field[i, at, :] + edge_lanes(sides, i, group)
             if group % groups == 0:
-                f = group // groups
                 value = value + jnp.where(i == 0, before(at), 0.0) + jnp.where(i == rows - 1, after(at), 0.0)
-                value = coupled(couple_adjoint, value, other, coupling, i, f, rows)
+                here = pl.ds(group // groups * rows + i, 1)
+                value = value + jnp.where(sub_iota() == 1, missing[here, :], 0.0)
+                bottom = couple_adjoint(floor[here, :], other[here, :], coupling[pl.ds(i, 1), :])
+                value = jnp.where(sub_iota() == 0, bottom, value)
             cells[i + 1, at, :] = value
 
     def add_outer(i, side):
@@ -618,13 +622,11 @@
             add_outer(rows - 1, after)
 
     def each(i, m, f, start, values):
-        if m == 0:
-            state_in.wait(i)
         for part, value in enumerate(values):
             at = pl.ds((m * PARTS + part) * GROUP, GROUP)
-            out[i, at, :] = value + scale[at, :] * state_cells[i, at, :]
-
-    adjoint_rows(rows, levels, cells, wind_cells, take_all, each)
+            out[i, at, :] = value + scale[at, :] * state[i, at, :]
+
+    adjoint_rows(rows, levels, cells, winds, take_all, each)
 
 
 def final_kernel(rows, levels, field, *rest):
@@ -698,8 +700,8 @@
                 ]
 
 
-def innovate_kernel(rows, width, tiles, cap, records, cols, extra, bottom, spread, sel, ends, columns, floor, *scratch):
-    col_cells, border_sel, precs, both, sems = scratch
+def innovate_kernel(rows, width, tiles, cap, records, cols, extra, bottom, *rest):
+    spread, sel, ends, columns, floor, col_cells, border_sel, precs, both, sems = rest
     chunks = 8
     copies = []
     for part in range(chunks):
@@ -797,13 +799,19 @@
         floor[4 + f : 5 + f, :] = columns[f * half : f * half + 1, :]
 
 
-def scatter_kernel(rows, width, spread, sel, adjoint, low0):
+def scatter_kernel(rows, width, spread, sel, winds, adjoint, low0, wind_rows, sems):
+    wind_in = Rows(winds, wind_rows, sems, rows, True, 1)
+    start_rows(rows, wind_in)
+    wind_rows[0] = jnp.zeros_like(wind_rows[0])
+    wind_rows[rows + 1] = jnp.zeros_like(wind_rows[0])
     sums = dot(spread[...], sel[...], (1, 0))
     for i in range(rows):
         lanes = slice(i * LANES, (i + 1) * LANES)
         adjoint[i] = sums[:width, lanes] + sums[width:, lanes]
         for f in range(2):
             low0[f * rows + i : f * rows + i + 1, :] = adjoint[i, f * (width // 2) : f * (width // 2) + 1, :]
+    for i in range(rows):
+        wind_in.wait(i)
 
 
 def local(state_incr, winds, coupling, background, obs_dest, obs_col, obs_op, obs_prec):
@@ -825,6 +833,7 @@
     sides = pltpu.VMEM(packed_shape.shape, jnp.float32)
     strip_shapes = [f32(width, LANES), f32(width, LANES), packed_shape]
     field_shape = f32(rows, width, LANES)
+    framed_shape = f32(rows + 2, width, LANES)
     low_shape = f32(fields * rows, LANES)
     cols_shape = ((2 * width, rows * LANES), jnp.bfloat16)
 
@@ -862,28 +871,34 @@
     send = call(functools.partial(route_kernel, tiles, cap), f32(tiles, halves * cap + GROUP, LANES))(
         obs_dest.reshape(1, count), obs_col.reshape(1, count), obs_prec.reshape(1, count), obs_op
     )
-    send, halos[0], halos[2] = lax.optimization_barrier((send, halos[0], halos[2]))
+    send, halos[0], halos[2], state_far, wind_far = lax.optimization_barrier((send, halos[0], halos[2], state, wind))
     records = lax.all_to_all(send, ("gx", "gy"), split_axis=0, concat_axis=0, tiled=True)
 
+    state_rows, wind_rows = run(
+        functools.partial(load_kernel, rows),
+        [field_shape, field_shape],
+        [sems(2, rows)],
+        (state_far, wind_far),
+        far=(0, 1),
+        traffic=10 * MIB,
+    )
+    halos[1], state_rows, wind_rows = lax.optimization_barrier((halos[1], state_rows, wind_rows))
     (floor,) = run(on_rows(forward_floor_kernel), [low_shape], [], (low0, low1, floor_winds, *halos))
     field, s_even, s_odd, packed, low0, low1, wind_ends, wind_dense, dense_g = run(
         on_rows(forward_kernel),
-        [field_shape]
+        [framed_shape]
         + strip_shapes
         + [low_shape] * 2
         + [f32(2, levels, LANES), f32(groups // PARTS * GROUP // 2, LANES), thin_shape],
-        [framed, own, own, sides, sems(3, rows)],
-        (coupling, swap_floor(floor), state, wind, *halos),
-        far=(2, 3),
-        out_far=(0,),
+        [framed, sides],
+        (coupling, swap_floor(floor), state_rows, wind_rows, *halos),
     )
     halos = exchange((s_even, s_odd), packed)
     (cols,) = run(
         on_rows(forward_again_kernel),
         [jax.ShapeDtypeStruct(*cols_shape)],
-        [framed, own, sems(2, rows), pltpu.VMEM(*cols_shape), sems(rows)],
-        (field, wind),
-        far=(0, 1),
+        [pltpu.VMEM(*cols_shape), sems(rows)],
+        (field, wind_rows),
         out_far=(0,),
         traffic=20 * MIB,
     )
@@ -900,7 +915,13 @@
     sel_shape = ((slots, rows * LANES), jnp.bfloat16)
     spread, sel, ends, columns, border_floor = run(
         functools.partial(innovate_kernel, rows, width, tiles, cap),
-        [jax.ShapeDtypeStruct(*spread_shape), jax.ShapeDtypeStruct(*sel_shape), f32(2, width, LANES), packed_shape, thin_shape],
+        [
+            jax.ShapeDtypeStruct(*spread_shape),
+            jax.ShapeDtypeStruct(*sel_shape),
+            f32(2, width, LANES),
+            packed_shape,
+            thin_shape,
+        ],
         [
             pltpu.VMEM(*cols_shape),
             pltpu.VMEM((slots, LANES), jnp.bfloat16),
@@ -919,31 +940,42 @@
         (coupling, swap_floor(border_floor), ends, columns, wind_ends, wind_dense, dense_g),
     )
     halos = exchange(strips[:2], strips[2])
-    adjoint, low0 = run(
-        functools.partial(scatter_kernel, rows, width), [field_shape, low_shape], [], (spread, sel), limit=OBSERVE_VMEM
-    )
-    adjoint, ends, columns, low0 = run(
+    adjoint, low0, wind_rows = run(
+        functools.partial(scatter_kernel, rows, width),
+        [field_shape, low_shape, framed_shape],
+        [sems(rows)],
+        (spread, sel, wind),
+        far=(2,),
+        limit=OBSERVE_VMEM,
+        traffic=8 * MIB,
+    )
+    partner = swap_floor(low0)
+    adjoint, ends, columns, low0, state_rows = run(
         on_rows(first_adjoint_kernel),
-        [field_shape, f32(2, width, LANES), packed_shape, low_shape],
-        [framed, framed, sems(rows)],
-        (coupling, swap_floor(low0), adjoint, wind),
+        [field_shape, f32(2, width, LANES), packed_shape, low_shape, field_shape],
+        [framed, sems(rows)],
+        (coupling, adjoint, wind_rows, state),
         far=(3,),
-    )
-    (floor,) = run(on_rows(floor_kernel), [low_shape], [], (low0, *halos))
+        traffic=16 * MIB,
+    )
+    low0, partner, halos = lax.optimization_barrier((low0, partner, halos))
+    floor, missing = run(
+        on_rows(floor_kernel), [low_shape, low_shape], [], (coupling, partner, low0, floor_winds, *halos)
+    )
     other = swap_floor(floor)
     strips = run(
         on_rows(border_again_kernel),
         strip_shapes,
         [sides],
-        (coupling, floor, other, ends, columns, wind_ends, wind_dense, dense_g, *halos),
+        (coupling, floor, other, missing, ends, columns, wind_ends, wind_dense, dense_g, *halos),
     )
     last_halos = exchange(strips[:2], strips[2])
     (adjoint,) = run(
         on_rows(second_adjoint_kernel),
         [field_shape],
-        [framed, framed, own, sides, sems(2, rows)],
-        (coupling, other, adjoint, wind, scale, state, *halos),
-        far=(3, 5),
+        [framed, sides],
+        (coupling, floor, other, missing, adjoint, wind_rows, scale, state_rows, *halos),
+        traffic=20 * MIB,
     )
     (result,) = run(
         on_rows(final_kernel),

time: 83 us -> 79.3 us (0.955)
  Pallas kernels: 41.5 us -> 38.9 us
  waiting for transfers between devices: 9.89 us -> 7.4 us
  starting transfers between devices: 29.4 us -> 31.2 us
    ppermute x12, waiting for transfers between devices: 4.36 us -> 1.43 us  [pair_swap(): return lax.ppermute(block, axis, route)]
    pallas_call x14 -> x15, Pallas kernels: 39.5 us -> 36.9 us  [run(): call(body, out_shape, scratch, in_specs=specs, out_specs=outs, **kw)(*args)]
    all_to_all x1, waiting for transfers between devices: 0.01 us -> 1.64 us  [local(): lax.all_to_all(send, ('gx', 'gy'), split_axis=0, concat_axis=0, tiled=True)]
    ppermute x12, starting transfers between devices: 23.4 us -> 25 us  [pair_swap(): return lax.ppermute(block, axis, route)]
    ppermute x5, waiting for transfers between devices: 5.53 us -> 4.34 us  [swap_floor(): return lax.ppermute(floor, 'comp', [(0, 1), (1, 0)])]
  transfers between devices with their start and end apart: 18 -> 18, of which waited for: 7 -> 6; matrix products, arithmetic and copies ran while one was open for 1% -> 1% of each run, Pallas kernels for 34% -> 32%
where the time goes in v6:
time: 79.3 us; the launch traced here: 78.6 us
  Pallas kernels  38.9 us (49%)
  starting transfers between devices  31.2 us (39%)
  waiting for transfers between devices  7.4 us (9%)
  local copies, waits for them, and re-layouts  0.83 us (1%)
    pallas_call x15, Pallas kernels, run(): call(body, out_shape, scratch, in_specs=specs, out_specs=outs, **kw)(*args)  36.9 us
    ppermute x12, starting transfers between devices, pair_swap(): return lax.ppermute(block, axis, route)  25 us
    all_to_all x1, starting transfers between devices, local(): lax.all_to_all(send, ('gx', 'gy'), split_axis=0, concat_axis=0, tiled=True)  5.34 us
    ppermute x5, waiting for transfers between devices, swap_floor(): return lax.ppermute(floor, 'comp', [(0, 1), (1, 0)])  4.34 us
    pallas_call x1, Pallas kernels, local(): call(functools.partial(route_kernel, tiles, cap), f32(tiles, halves * cap...  1.98 us
    all_to_all x1, waiting for transfers between devices, local(): lax.all_to_all(send, ('gx', 'gy'), split_axis=0, concat_axis=0, tiled=True)  1.64 us
  transfers between devices with their start and end apart: 18, of which 6 were waited for; matrix products, arithmetic and copies ran while one was open for 1% of the time, Pallas kernels for 32%

profile of v6, /device:TPU:8, one launch (start us, length us, event | category | flops | bytes accessed | tf_op | source)
XLA Modules:
  0.0 78.6 jit_solution(11764285252976525434)
XLA Ops:
  0.0 2.9 %shard_map.83 = (f32[256,128]{1,0:T(8,128)S(1)}, f32[256,128]{1,0:T(8,128)}, f32[64,128]{1,0:T(8,128)S(1)}, f32[32,128]{1,0:T(8,128)S(1)}, f32[32,128]{1,0:T(8,128)S(1)}) custom-call(f32[4096,128]{1,0:T(8,128)} %bitcast.15), custom_call_target="tpu_custom_call" | custom-call | tf_op jit(solution)/shard_map/pallas_call | solution.py:848
  2.9 1.6 %collective-permute-start = (f32[256,128]{1,0:T(8,128)S(1)}, f32[256,128]{1,0:T(8,128)S(1)}, u32[]{:S(2)}, u32[]{:S(2)}) collective-permute-start(f32[256,128]{1,0:T(8,128)S(1)} %get-tuple-element.57), channel_id=1, source_target_pairs={{0,8},{8,0},{1,9},{9,1},{2,10},{10,2},{3,11},{11,3},{4,12},{12,4},... | collective-permute-start | bytes 393224 | tf_op jit(solution)/shard_map/ppermute | solution.py:48
  4.5 3.3 %collective-permute-start.1 = (f32[64,128]{1,0:T(8,128)S(1)}, f32[64,128]{1,0:T(8,128)S(1)}, u32[]{:S(2)}, u32[]{:S(2)}) collective-permute-start(f32[64,128]{1,0:T(8,128)S(1)} %get-tuple-element.58), channel_id=1, source_target_pairs={{1,2},{2,1},{3,4},{4,3},{5,6},{6,5},{9,10},{10,9},{11,12},{12,11},... | collective-permute-start | bytes 98312 | tf_op jit(solution)/shard_map/ppermute | solution.py:48
  7.8 2.0 %shard_map.82 = f32[16,136,128]{2,1,0:T(8,128)} custom-call(s32[1,512]{1,0:T(1,128)S(1)} %bitcast.12, s32[1,512]{1,0:T(1,128)S(1)} %bitcast.13, f32[1,512]{1,0:T(1,128)S(1)} %bitcast.14, f32[512,256]{1,0:T(8,128)S(1)} %copy-done), custom_call_target="tpu_custom_call" | custom-call | tf_op jit(solution)/shard_map/pallas_call | solution.py:871
  9.8 1.4 %collective-permute-done.1.rest_2_ = f32[64,128]{1,0:T(8,128)S(1)} collective-permute-done((f32[64,128]{1,0:T(8,128)S(1)}, f32[64,128]{1,0:T(8,128)S(1)}, u32[]{:S(2)}, u32[]{:S(2)}) %collective-permute-start.1) | collective-permute-done | bytes 32800 | tf_op jit(solution)/shard_map/ppermute | solution.py:48
  11.2 5.3 %all-to-all-start = ((f32[16,136,128]{2,1,0:T(8,128)}), f32[16,136,128]{2,1,0:T(8,128)S(1)}, u32[]{:S(2)}, u32[]{:S(2)}) async-start(f32[16,136,128]{2,1,0:T(8,128)} %shard_map.82), calls=%async_computation | async-start | bytes 2228224 | tf_op jit(solution)/shard_map/all_to_all | solution.py:875
  16.5 1.5 %collective-permute-start.2 = (f32[64,128]{1,0:T(8,128)S(1)}, f32[64,128]{1,0:T(8,128)S(1)}, u32[]{:S(2)}, u32[]{:S(2)}) collective-permute-start(f32[64,128]{1,0:T(8,128)S(1)} %get-tuple-element.58), channel_id=1, source_target_pairs={{0,1},{1,0},{2,3},{3,2},{4,5},{5,4},{6,7},{7,6},{8,9},{9,8},{10,11... | collective-permute-start | bytes 98312 | tf_op jit(solution)/shard_map/ppermute | solution.py:48
  18.0 0.7 slice_bitcast_fusion.winds
  18.7 3.0 %shard_map.84 = (f32[16,256,128]{2,1,0:T(8,128)S(1)}, f32[16,256,128]{2,1,0:T(8,128)S(1)}) custom-call(f32[256,16,128]{2,1,0:T(8,128)} %bitcast.16, f32[256,16,128]{2,1,0:T(8,128)} %bitcast.18), custom_call_target="tpu_custom_call" | custom-call | bytes 10485760 | tf_op jit(solution)/shard_map/pallas_call | solution.py:848
  22.0 1.2 %collective-permute-done.3.other = f32[32,128]{1,0:T(8,128)S(1)} collective-permute-done((f32[32,128]{1,0:T(8,128)S(1)}, f32[32,128]{1,0:T(8,128)S(1)}, u32[]{:S(2)}, u32[]{:S(2)}) %collective-permute-start.3) | collective-permute-done | bytes 16416 | tf_op jit(solution)/shard_map/ppermute | solution.py:854
  23.2 5.5 %shard_map.86 = (f32[18,256,128]{2,1,0:T(8,128)S(1)}, f32[256,128]{1,0:T(8,128)S(1)}, f32[256,128]{1,0:T(8,128)}, f32[64,128]{1,0:T(8,128)S(1)}, f32[32,128]{1,0...) custom-call(f32[16,128]{1,0:T(8,128)S(1)} %copy-done.1, ...), custom_call_target="tpu_custom_call" | custom-call | tf_op jit(solution)/shard_map/pallas_call | solution.py:848
  28.7 1.5 %collective-permute-start.4 = (f32[256,128]{1,0:T(8,128)S(1)}, f32[256,128]{1,0:T(8,128)S(1)}, u32[]{:S(2)}, u32[]{:S(2)}) collective-permute-start(f32[256,128]{1,0:T(8,128)S(1)} %get-tuple-element.72), channel_id=1, source_target_pairs={{0,8},{8,0},{1,9},{9,1},{2,10},{10,2},{3,11},{11,3},{4,12},{12,4},... | collective-permute-start | bytes 393224 | tf_op jit(solution)/shard_map/ppermute | solution.py:48
  30.2 0.6 collective-permute-start.5
  30.7 4.7 %collective-permute-start.6 = (f32[64,128]{1,0:T(8,128)S(1)}, f32[64,128]{1,0:T(8,128)S(1)}, u32[]{:S(2)}, u32[]{:S(2)}) collective-permute-start(f32[64,128]{1,0:T(8,128)S(1)} %get-tuple-element.73), channel_id=1, source_target_pairs={{1,2},{2,1},{3,4},{4,3},{5,6},{6,5},{9,10},{10,9},{11,12},{12,11},... | collective-permute-start | bytes 98312 | tf_op jit(solution)/shard_map/ppermute | solution.py:48
  35.5 3.2 %shard_map.87.cols = bf16[512,2048]{1,0:T(8,128)(2,1)} custom-call(f32[18,256,128]{2,1,0:T(8,128)S(1)} %get-tuple-element.71.cells, f32[16,256,128]{2,1,0:T(8,128)S(1)} %get-tuple-element.70.winds), custom_call_target="tpu_custom_call" | custom-call | bytes 20971520 | tf_op jit(solution)/shard_map/pallas_call | solution.py:848
  39.0 1.2 %collective-permute-done.7.other = f32[32,128]{1,0:T(8,128)S(1)} collective-permute-done((f32[32,128]{1,0:T(8,128)S(1)}, f32[32,128]{1,0:T(8,128)S(1)}, u32[]{:S(2)}, u32[]{:S(2)}) %collective-permute-start.7) | collective-permute-done | bytes 16416 | tf_op jit(solution)/shard_map/ppermute | solution.py:854
  40.4 1.6 %all-to-all-done.records = f32[16,136,128]{2,1,0:T(8,128)S(1)} async-done(((f32[16,136,128]{2,1,0:T(8,128)}), f32[16,136,128]{2,1,0:T(8,128)S(1)}, u32[]{:S(2)}, u32[]{:S(2)}) %all-to-all-start) | async-done | bytes 1114144 | tf_op jit(solution)/shard_map/all_to_all | solution.py:875
  42.0 6.3 %shard_map.90 = (bf16[512,1024]{1,0:T(8,128)(2,1)S(1)}, bf16[1024,2048]{1,0:T(8,128)(2,1)S(1)}, f32[2,256,128]{2,1,0:T(8,128)S(1)}, f32[64,128]{1,0:T(8,128)S(1)}, f32[8,128]{1,0:T(8,128)S(1)}) custom-call(f32[16,136,128]{2,1,0:T(8,128)S(1)} %all-to-all-done.records, bf16[512,2048]{1,0:T(8,128)(2,1)} %shard_map.87.cols, ...), custom_call_target="tpu_custom_call" | custom-call | tf_op jit(solution)/shard_map/pallas_call | solution.py:848
  48.4 1.2 %collective-permute-done.9.other = f32[8,128]{1,0:T(8,128)S(1)} collective-permute-done((f32[8,128]{1,0:T(8,128)S(1)}, f32[8,128]{1,0:T(8,128)S(1)}, u32[]{:S(2)}, u32[]{:S(2)}) %collective-permute-start.9) | collective-permute-done | bytes 4128 | tf_op jit(solution)/shard_map/ppermute | solution.py:854
  49.6 0.7 shard_map.93
  50.3 1.5 %collective-permute-start.10 = (f32[256,128]{1,0:T(8,128)S(1)}, f32[256,128]{1,0:T(8,128)S(1)}, u32[]{:S(2)}, u32[]{:S(2)}) collective-permute-start(f32[256,128]{1,0:T(8,128)S(1)} %get-tuple-element.94), channel_id=1, source_target_pairs={{0,8},{8,0},{1,9},{9,1},{2,10},{10,2},{3,11},{11,3},{4,12},{12,4},... | collective-permute-start | bytes 393224 | tf_op jit(solution)/shard_map/ppermute | solution.py:48
  51.8 3.0 %collective-permute-start.11 = (f32[64,128]{1,0:T(8,128)S(1)}, f32[64,128]{1,0:T(8,128)S(1)}, u32[]{:S(2)}, u32[]{:S(2)}) collective-permute-start(f32[64,128]{1,0:T(8,128)S(1)} %get-tuple-element.95), channel_id=1, source_target_pairs={{0,1},{1,0},{2,3},{3,2},{4,5},{5,4},{6,7},{7,6},{8,9},{9,8},{10,11... | collective-permute-start | bytes 98312 | tf_op jit(solution)/shard_map/ppermute | solution.py:48
  54.8 1.9 %collective-permute-start.12 = (f32[64,128]{1,0:T(8,128)S(1)}, f32[64,128]{1,0:T(8,128)S(1)}, u32[]{:S(2)}, u32[]{:S(2)}) collective-permute-start(f32[64,128]{1,0:T(8,128)S(1)} %get-tuple-element.95), channel_id=1, source_target_pairs={{1,2},{2,1},{3,4},{4,3},{5,6},{6,5},{9,10},{10,9},{11,12},{12,11},... | collective-permute-start | bytes 98312 | tf_op jit(solution)/shard_map/ppermute | solution.py:48
  56.7 3.3 %shard_map.91 = (f32[16,256,128]{2,1,0:T(8,128)S(1)}, f32[32,128]{1,0:T(8,128)S(1)}, f32[18,256,128]{2,1,0:T(8,128)S(1)}) custom-call(bf16[512,1024]{1,0:T(8,128)(2,1)S(1)} %get-tuple-element.84.spread, bf16[1024,2048]{1,0:T(8,128)(2,1)S(1)} %get-tuple-element.85.sel, f32[256,16,128]{2,1,0:T(8,128)} %bitcast.19), custom_call_target="tpu_custom_call" | custom-call | bytes 8388608 | tf_op jit(solution)/shard_map/pallas_call | solution.py:848
  60.1 3.7 %shard_map.92 = (f32[16,256,128]{2,1,0:T(8,128)S(1)}, f32[2,256,128]{2,1,0:T(8,128)S(1)}, f32[64,128]{1,0:T(8,128)S(1)}, f32[32,128]{1,0:T(8,128)S(1)}, f32[16,256,128]{2,1,0:T(8,128)S(1)}) custom-call(f32[16,128]{1,0:T(8,128)S(1)} %copy-done.1, f32[16,256,128]{2,1,0:T(8,128)S(1)} %get-tuple-element.86.field, f32[18,256,128]{2,1,0:T(8,128)S(1)} %get-tuple-element.87.winds, ...), custom_call_target="tpu_custom_call" | custom-call | bytes 16777216 | tf_op jit(solution)/shard_map/pallas_call | solution.py:848
  64.6 0.8 %collective-permute-done.13.other = f32[32,128]{1,0:T(8,128)S(1)} collective-permute-done((f32[32,128]{1,0:T(8,128)S(1)}, f32[32,128]{1,0:T(8,128)S(1)}, u32[]{:S(2)}, u32[]{:S(2)}) %collective-permute-start.13) | collective-permute-done | bytes 16416 | tf_op jit(solution)/shard_map/ppermute | solution.py:854
  65.4 1.0 %shard_map.96 = (f32[256,128]{1,0:T(8,128)S(1)}, f32[256,128]{1,0:T(8,128)}, f32[64,128]{1,0:T(8,128)S(1)}) custom-call(f32[16,128]{1,0:T(8,128)S(1)} %copy-done.1, f32[32,128]{1,0:T(8,128)S(1)} %get-tuple-element.101.floor, f32[32,128]{1,0:T(8,128)S(1)} %collective-permute-done.13.other, f32[32,128]{1,0:T(8,128)S(1)} %get-tuple-element.102.missing, ...), custom_call_target="tpu_custom_call" | custom-call | tf_op jit(solution)/shard_map/pallas_call | solution.py:848
  66.4 0.7 collective-permute-start.14
  67.1 0.9 %collective-permute-start.15 = (f32[64,128]{1,0:T(8,128)S(1)}, f32[64,128]{1,0:T(8,128)S(1)}, u32[]{:S(2)}, u32[]{:S(2)}) collective-permute-start(f32[64,128]{1,0:T(8,128)S(1)} %get-tuple-element.108), channel_id=1, source_target_pairs={{0,1},{1,0},{2,3},{3,2},{4,5},{5,4},{6,7},{7,6},{8,9},{9,8},{10,11... | collective-permute-start | bytes 98312 | tf_op jit(solution)/shard_map/ppermute | solution.py:48
  68.0 3.9 %collective-permute-start.16 = (f32[64,128]{1,0:T(8,128)S(1)}, f32[64,128]{1,0:T(8,128)S(1)}, u32[]{:S(2)}, u32[]{:S(2)}) collective-permute-start(f32[64,128]{1,0:T(8,128)S(1)} %get-tuple-element.108), channel_id=1, source_target_pairs={{1,2},{2,1},{3,4},{4,3},{5,6},{6,5},{9,10},{10,9},{11,12},{12,11},... | collective-permute-start | bytes 98312 | tf_op jit(solution)/shard_map/ppermute | solution.py:48
  72.0 4.1 %shard_map.95.field = f32[16,256,128]{2,1,0:T(8,128)S(1)} custom-call(f32[16,128]{1,0:T(8,128)S(1)} %copy-done.1, f32[32,128]{1,0:T(8,128)S(1)} %get-tuple-element.101.floor, f32[32,128]{1,0:T(8,128)S(1)} %collective-permute-done.13.other, f32[32,128]{1,0:T(8,128)S(1)} %get-tuple-element.102.missing, f32[16,256,128]{2,1,0:T(8,128)S(1)} %get-tuple-element.103.field, ...), custom_call_target="tpu_custom_call" | custom-call | bytes 20971520 | tf_op jit(solution)/shard_map/pallas_call | solution.py:848
  76.1 2.5 %shard_map.97 = f32[256,16,128]{2,1,0:T(8,128)} custom-call(f32[16,256,128]{2,1,0:T(8,128)S(1)} %shard_map.95.field, f32[256,128]{1,0:T(8,128)S(1)} %collective-permute-done.14.rest_0_, f32[64,128]{1,0:T(8,128)S(1)} %collective-permute-done.15.rest_1_, f32[64,128]{1,0:T(8,128)S(1)} %collective-permute-done.16.rest_2_), custom_call_target="tpu_custom_call" | custom-call | tf_op jit(solution)/shard_map/pallas_call | solution.py:848
  (34 shorter events, 1.7 us)
Async XLA Ops:
  0.0 7.8 %copy-start.2 = (s32[512,1]{0,1:T(1,128)S(1)}, s32[512,1]{0,1:T(1,128)}, u32[]{:S(2)}) copy-start(s32[512,1]{0,1:T(1,128)} %param.12) | copy-start | bytes 6148
  0.0 7.8 %copy-start.3 = (s32[512]{0:T(512)S(1)}, s32[512]{0:T(512)}, u32[]{:S(2)}) copy-start(s32[512]{0:T(512)} %param.13) | copy-start | bytes 6148
  0.0 7.8 %copy-start.4 = (f32[512]{0:T(512)S(1)}, f32[512]{0:T(512)}, u32[]{:S(2)}) copy-start(f32[512]{0:T(512)} %param.15) | copy-start | bytes 6148
  0.0 7.8 %copy-start = (f32[512,256]{1,0:T(8,128)S(1)}, f32[512,256]{1,0:T(8,128)}, u32[]{:S(2)}) copy-start(f32[512,256]{1,0:T(8,128)} %op.1) | copy-start | bytes 1572868
  2.9 8.3 %collective-permute-start = (f32[256,128]{1,0:T(8,128)S(1)}, f32[256,128]{1,0:T(8,128)S(1)}, u32[]{:S(2)}, u32[]{:S(2)}) collective-permute-start(f32[256,128]{1,0:T(8,128)S(1)} %get-tuple-element.57), channel_id=1, source_target_pairs={{0,8},{8,0},{1,9},{9,1},{2,10},{10,2},{3,11},{11,3},{4,12},{12,4},... | collective-permute-start | bytes 393224 | tf_op jit(solution)/shard_map/ppermute | solution.py:48
  4.5 6.7 %collective-permute-start.1 = (f32[64,128]{1,0:T(8,128)S(1)}, f32[64,128]{1,0:T(8,128)S(1)}, u32[]{:S(2)}, u32[]{:S(2)}) collective-permute-start(f32[64,128]{1,0:T(8,128)S(1)} %get-tuple-element.58), channel_id=1, source_target_pairs={{1,2},{2,1},{3,4},{4,3},{5,6},{6,5},{9,10},{10,9},{11,12},{12,11},... | collective-permute-start | bytes 98312 | tf_op jit(solution)/shard_map/ppermute | solution.py:48
  11.2 30.8 %all-to-all-start = ((f32[16,136,128]{2,1,0:T(8,128)}), f32[16,136,128]{2,1,0:T(8,128)S(1)}, u32[]{:S(2)}, u32[]{:S(2)}) async-start(f32[16,136,128]{2,1,0:T(8,128)} %shard_map.82), calls=%async_computation | async-start | bytes 2228224 | tf_op jit(solution)/shard_map/all_to_all | solution.py:875
  16.5 5.2 %collective-permute-start.2 = (f32[64,128]{1,0:T(8,128)S(1)}, f32[64,128]{1,0:T(8,128)S(1)}, u32[]{:S(2)}, u32[]{:S(2)}) collective-permute-start(f32[64,128]{1,0:T(8,128)S(1)} %get-tuple-element.58), channel_id=1, source_target_pairs={{0,1},{1,0},{2,3},{3,2},{4,5},{5,4},{6,7},{7,6},{8,9},{9,8},{10,11... | collective-permute-start | bytes 98312 | tf_op jit(solution)/shard_map/ppermute | solution.py:48
  18.7 4.5 %copy-start.1 = (f32[16,128]{1,0:T(8,128)S(1)}, f32[16,128]{1,0:T(8,128)}, u32[]{:S(2)}) copy-start(f32[16,128]{1,0:T(8,128)} %coupling.13) | copy-start | bytes 24580
  21.9 1.2 %collective-permute-start.3 = (f32[32,128]{1,0:T(8,128)S(1)}, f32[32,128]{1,0:T(8,128)S(1)}, u32[]{:S(2)}, u32[]{:S(2)}) collective-permute-start(f32[32,128]{1,0:T(8,128)S(1)} %shard_map.85), channel_id=1, source_target_pairs={{0,16},{16,0},{1,17},{17,1},{2,18},{18,2},{3,19},{19,3},{4,20},{20... | collective-permute-start | bytes 49160 | tf_op jit(solution)/shard_map/ppermute | solution.py:854
  28.7 10.0 %collective-permute-start.4 = (f32[256,128]{1,0:T(8,128)S(1)}, f32[256,128]{1,0:T(8,128)S(1)}, u32[]{:S(2)}, u32[]{:S(2)}) collective-permute-start(f32[256,128]{1,0:T(8,128)S(1)} %get-tuple-element.72), channel_id=1, source_target_pairs={{0,8},{8,0},{1,9},{9,1},{2,10},{10,2},{3,11},{11,3},{4,12},{12,4},... | collective-permute-start | bytes 393224 | tf_op jit(solution)/shard_map/ppermute | solution.py:48
  30.2 8.5 %collective-permute-start.5 = (f32[64,128]{1,0:T(8,128)S(1)}, f32[64,128]{1,0:T(8,128)S(1)}, u32[]{:S(2)}, u32[]{:S(2)}) collective-permute-start(f32[64,128]{1,0:T(8,128)S(1)} %get-tuple-element.73), channel_id=1, source_target_pairs={{0,1},{1,0},{2,3},{3,2},{4,5},{5,4},{6,7},{7,6},{8,9},{9,8},{10,11... | collective-permute-start | bytes 98312 | tf_op jit(solution)/shard_map/ppermute | solution.py:48
  30.7 8.0 %collective-permute-start.6 = (f32[64,128]{1,0:T(8,128)S(1)}, f32[64,128]{1,0:T(8,128)S(1)}, u32[]{:S(2)}, u32[]{:S(2)}) collective-permute-start(f32[64,128]{1,0:T(8,128)S(1)} %get-tuple-element.73), channel_id=1, source_target_pairs={{1,2},{2,1},{3,4},{4,3},{5,6},{6,5},{9,10},{10,9},{11,12},{12,11},... | collective-permute-start | bytes 98312 | tf_op jit(solution)/shard_map/ppermute | solution.py:48
  38.9 1.2 %collective-permute-start.7 = (f32[32,128]{1,0:T(8,128)S(1)}, f32[32,128]{1,0:T(8,128)S(1)}, u32[]{:S(2)}, u32[]{:S(2)}) collective-permute-start(f32[32,128]{1,0:T(8,128)S(1)} %shard_map.88.floor), channel_id=1, source_target_pairs={{0,16},{16,0},{1,17},{17,1},{2,18},{18,2},{3,19},{19,3},{4,20},{20... | collective-permute-start | bytes 49160 | tf_op jit(solution)/shard_map/ppermute | solution.py:854
  48.3 1.2 %collective-permute-start.9 = (f32[8,128]{1,0:T(8,128)S(1)}, f32[8,128]{1,0:T(8,128)S(1)}, u32[]{:S(2)}, u32[]{:S(2)}) collective-permute-start(f32[8,128]{1,0:T(8,128)S(1)} %get-tuple-element.90), channel_id=1, source_target_pairs={{0,16},{16,0},{1,17},{17,1},{2,18},{18,2},{3,19},{19,3},{4,20},{20... | collective-permute-start | bytes 12296 | tf_op jit(solution)/shard_map/ppermute | solution.py:854
  50.3 13.6 %collective-permute-start.10 = (f32[256,128]{1,0:T(8,128)S(1)}, f32[256,128]{1,0:T(8,128)S(1)}, u32[]{:S(2)}, u32[]{:S(2)}) collective-permute-start(f32[256,128]{1,0:T(8,128)S(1)} %get-tuple-element.94), channel_id=1, source_target_pairs={{0,8},{8,0},{1,9},{9,1},{2,10},{10,2},{3,11},{11,3},{4,12},{12,4},... | collective-permute-start | bytes 393224 | tf_op jit(solution)/shard_map/ppermute | solution.py:48
  51.8 12.1 %collective-permute-start.11 = (f32[64,128]{1,0:T(8,128)S(1)}, f32[64,128]{1,0:T(8,128)S(1)}, u32[]{:S(2)}, u32[]{:S(2)}) collective-permute-start(f32[64,128]{1,0:T(8,128)S(1)} %get-tuple-element.95), channel_id=1, source_target_pairs={{0,1},{1,0},{2,3},{3,2},{4,5},{5,4},{6,7},{7,6},{8,9},{9,8},{10,11... | collective-permute-start | bytes 98312 | tf_op jit(solution)/shard_map/ppermute | solution.py:48
  54.8 9.1 %collective-permute-start.12 = (f32[64,128]{1,0:T(8,128)S(1)}, f32[64,128]{1,0:T(8,128)S(1)}, u32[]{:S(2)}, u32[]{:S(2)}) collective-permute-start(f32[64,128]{1,0:T(8,128)S(1)} %get-tuple-element.95), channel_id=1, source_target_pairs={{1,2},{2,1},{3,4},{4,3},{5,6},{6,5},{9,10},{10,9},{11,12},{12,11},... | collective-permute-start | bytes 98312 | tf_op jit(solution)/shard_map/ppermute | solution.py:48
  60.0 3.8 %collective-permute-start.8 = (f32[32,128]{1,0:T(8,128)S(1)}, f32[32,128]{1,0:T(8,128)S(1)}, u32[]{:S(2)}, u32[]{:S(2)}) collective-permute-start(f32[32,128]{1,0:T(8,128)S(1)} %get-tuple-element.89), channel_id=1, source_target_pairs={{0,16},{16,0},{1,17},{17,1},{2,18},{18,2},{3,19},{19,3},{4,20},{20... | collective-permute-start | bytes 49160 | tf_op jit(solution)/shard_map/ppermute | solution.py:854
  60.1 11.8 %copy-start.5 = (f32[1,2,128]{2,1,0:T(2,128)S(1)}, f32[1,2,128]{2,1,0:T(2,128)}, u32[]{:S(2)}) copy-start(f32[1,2,128]{2,1,0:T(2,128)} %param.11) | copy-start | bytes 3076
  64.0 1.4 %collective-permute-start.13 = (f32[32,128]{1,0:T(8,128)S(1)}, f32[32,128]{1,0:T(8,128)S(1)}, u32[]{:S(2)}, u32[]{:S(2)}) collective-permute-start(f32[32,128]{1,0:T(8,128)S(1)} %get-tuple-element.101.floor), channel_id=1, source_target_pairs={{0,16},{16,0},{1,17},{17,1},{2,18},{18,2},{3,19},{19,3},{4,20},{20... | collective-permute-start | bytes 49160 | tf_op jit(solution)/shard_map/ppermute | solution.py:854
  66.4 9.7 %collective-permute-start.14 = (f32[256,128]{1,0:T(8,128)S(1)}, f32[256,128]{1,0:T(8,128)S(1)}, u32[]{:S(2)}, u32[]{:S(2)}) collective-permute-start(f32[256,128]{1,0:T(8,128)S(1)} %get-tuple-element.107), channel_id=1, source_target_pairs={{0,8},{8,0},{1,9},{9,1},{2,10},{10,2},{3,11},{11,3},{4,12},{12,4},... | collective-permute-start | bytes 393224 | tf_op jit(solution)/shard_map/ppermute | solution.py:48
  67.1 9.0 %collective-permute-start.15 = (f32[64,128]{1,0:T(8,128)S(1)}, f32[64,128]{1,0:T(8,128)S(1)}, u32[]{:S(2)}, u32[]{:S(2)}) collective-permute-start(f32[64,128]{1,0:T(8,128)S(1)} %get-tuple-element.108), channel_id=1, source_target_pairs={{0,1},{1,0},{2,3},{3,2},{4,5},{5,4},{6,7},{7,6},{8,9},{9,8},{10,11... | collective-permute-start | bytes 98312 | tf_op jit(solution)/shard_map/ppermute | solution.py:48
  68.0 8.1 %collective-permute-start.16 = (f32[64,128]{1,0:T(8,128)S(1)}, f32[64,128]{1,0:T(8,128)S(1)}, u32[]{:S(2)}, u32[]{:S(2)}) collective-permute-start(f32[64,128]{1,0:T(8,128)S(1)} %get-tuple-element.108), channel_id=1, source_target_pairs={{1,2},{2,1},{3,4},{4,3},{5,6},{6,5},{9,10},{10,9},{11,12},{12,11},... | collective-permute-start | bytes 98312 | tf_op jit(solution)/shard_map/ppermute | solution.py:48

commit v7 on v6

--- a/solution.py
+++ b/solution.py
@@ -48,13 +48,15 @@
     return lax.ppermute(block, axis, route)
 
 
+def pair_sets():
+    return 2 if lax.axis_size("gx") > 2 else 1
+
+
 def exchange(strips, packed):
     y_even = pair_swap(packed, "gy", 0)
     y_odd = pair_swap(packed, "gy", 1)
-    halos = [pair_swap(strips[0], "gx", 0), y_even, y_odd]
-    if lax.axis_size("gx") > 2:
-        halos.append(pair_swap(strips[1], "gx", 1))
-    return halos
+    even, *odd = [pair_swap(strips[start], "gx", start) for start in range(pair_sets())]
+    return [even, y_even, y_odd, *odd]
 
 
 def is_odd(axis):
@@ -83,7 +85,7 @@
 
 
 def merge_columns(y_even, y_odd, sides):
-    sides[...] = merged(y_even, y_odd, slice(None))
+    sides[...] = merged(y_even, y_odd, slice(0, sides.shape[0]))
 
 
 def slot_of(i, part, rows):
@@ -192,10 +194,11 @@
     return jnp.where(sub_iota() == 0, mixed, value)
 
 
-def put_strip(strip_even, strip_odd, at, first, last):
+def put_strip(strips, at, first, last):
     at_odd = is_odd("gx")
-    strip_even[at, :] = jnp.where(at_odd, first, last)
-    strip_odd[at, :] = jnp.where(at_odd, last, first)
+    strips[0, at, :] = jnp.where(at_odd, first, last)
+    if strips.shape[0] > 1:
+        strips[1, at, :] = jnp.where(at_odd, last, first)
 
 
 def put_low(low, value, i, f, rows):
@@ -222,7 +225,7 @@
             group.copy(i).start()
 
 
-def edges_kernel(rows, levels, state, s_even, s_odd, packed, low0, low1, cells, sems):
+def edges_kernel(rows, levels, state, strips, packed, low0, low1, cells, sems):
     part_levels = PARTS * GROUP
     blocks = 2 * levels // part_levels
 
@@ -247,7 +250,7 @@
         start = m * part_levels * rows
         first = cells[pl.ds(start, part_levels, stride=rows), :]
         last = cells[pl.ds(start + rows - 1, part_levels, stride=rows), :]
-        put_strip(s_even, s_odd, pl.ds(pl.multiple_of(m * part_levels, part_levels), part_levels), first, last)
+        put_strip(strips, pl.ds(pl.multiple_of(m * part_levels, part_levels), part_levels), first, last)
         return 0
 
     lax.fori_loop(0, blocks, block, 0)
@@ -256,9 +259,9 @@
             low[f * rows : (f + 1) * rows, :] = cells[pl.ds((f * levels + level) * rows, rows), :]
 
 
-def floor_edge(halos, f, rows, levels):
+def floor_edge(halos, f, rows, levels, more=0.0):
     m = f * (levels // GROUP) // PARTS
-    sides = jnp.broadcast_to(merged(halos[1], halos[2], pl.ds(m * GROUP, 1)), (rows, LANES))
+    sides = jnp.broadcast_to(merged(halos[1], halos[2], pl.ds(m * GROUP, 1)) + more, (rows, LANES))
     return pltpu.roll(sides, 2 * PARTS - 1, 1, stride=2 * PARTS, stride_axis=0)
 
 
@@ -317,14 +320,14 @@
 
 
 def forward_kernel(rows, levels, coupling, other, field, winds, *rest):
-    *halos, out, s_even, s_odd, packed, low0, low1, wind_ends, wind_dense, dense_g, cells, sides = rest
+    *halos, out, strips, packed, low0, low1, wind_ends, wind_dense, dense_g, cells, sides = rest
     packed[...] = jnp.zeros_like(packed)
     wind_dense[...] = jnp.zeros_like(wind_dense)
     merge_columns(halos[1], halos[2], sides)
     before, after = read_sides(halos)
-    cells[0] = before(slice(None))
+    cells[0] = before(pl.ds(0, 2 * levels))
     cells[1] = field[0]
-    cells[rows + 1] = after(slice(None))
+    cells[rows + 1] = after(pl.ds(0, 2 * levels))
     out[0] = jnp.zeros_like(out[0])
     out[rows + 1] = jnp.zeros_like(out[0])
     groups = levels // GROUP
@@ -353,10 +356,17 @@
         return 0
 
     lax.fori_loop(0, rows, row, 0)
-    put_strip(s_even, s_odd, slice(None), out[1], out[rows])
+    put_strip(strips, pl.ds(0, 2 * levels), out[1], out[rows])
     wind_ends[0] = winds[0, pl.ds(0, levels), :]
     wind_ends[1] = winds[rows - 1, pl.ds(0, levels), :]
     dense_g[...] = jnp.broadcast_to(dense_row(coupling, 0, rows), dense_g.shape)
+    _, peer = shares_of(coupling[...])
+    first = products(peer[0:1], winds[0, 0:1, :])[1]
+    last = products(peer[rows - 1 : rows], winds[rows - 1, 0:1, :])[0]
+    whole = (GROUP, LANES)
+    put_strip(strips, slice(2 * levels, 2 * levels + GROUP), jnp.broadcast_to(first, whole), jnp.broadcast_to(last, whole))
+    _, peer = shares_of(dense_g[...])
+    packed[packed.shape[0] - GROUP :, :] = first_and_last(peer, wind_dense[0:1, :])
 
 
 def forward_again_kernel(rows, levels, cells, winds, cols, col_cells, col_sems):
@@ -389,7 +399,7 @@
     for f in range(2):
         here = pl.ds(f * rows, rows)
         bottom[here, :] = couple_forward(floor[here, :], other[here, :], coupling[...])
-    dense_products(dense, swap_pairs(merged(halos[1], halos[2], slice(None))), wind_dense)
+    dense_products(dense, swap_pairs(merged(halos[1], halos[2], slice(0, dense.shape[0]))), wind_dense)
     before, after = read_sides(halos)
     sub = lax.broadcasted_iota(jnp.int32, (levels, LANES), 0)
 
@@ -411,13 +421,17 @@
         put(jnp.concatenate(thin, axis=0), f, slice(2 * LANES, 3 * LANES))
 
 
+def first_and_last(value, wind):
+    down, up = products(value, wind)
+    lane = lax.broadcasted_iota(jnp.int32, down.shape, 1)
+    return jnp.where(lane % 2 == 1, up, down)
+
+
 def dense_products(packed, value, wind_dense):
     half = wind_dense.shape[0]
     for f in range(2):
         at = slice(f * half, (f + 1) * half)
-        down, up = products(value[at], wind_dense[...])
-        lane = lax.broadcasted_iota(jnp.int32, down.shape, 1)
-        packed[at, :] = jnp.where(lane % 2 == 1, up, down)
+        packed[at, :] = first_and_last(value[at], wind_dense[...])
 
 
 def level0_row(value, new, f):
@@ -427,11 +441,11 @@
     return jnp.where((sub == f * half) & (lane % (2 * PARTS) < 2), new, value)
 
 
-def end_rows(ends, s_even, s_odd, wind_ends, levels):
+def end_rows(ends, strips, wind_ends, levels):
     for f in range(2):
         at = slice(f * levels, (f + 1) * levels)
         put_strip(
-            s_even, s_odd, at, products(ends[0][at], wind_ends[0])[1], products(ends[1][at], wind_ends[1])[0]
+            strips, at, products(ends[0][at], wind_ends[0])[1], products(ends[1][at], wind_ends[1])[0]
         )
 
 
@@ -439,36 +453,58 @@
     return jnp.where(lax.broadcasted_iota(jnp.int32, value.shape, 0) == 0, new, value)
 
 
-def border_kernel(rows, levels, coupling, other, ends, columns, wind_ends, wind_dense, dense_g, s_even, s_odd, packed):
-    half = columns.shape[0] // 2
-    dense = columns[...]
-    full = [ends[0], ends[1]]
+def border_strips(rows, levels, coupling, ends, dense, wind_ends, wind_dense, dense_g, strips, packed):
+    half = dense.shape[0] // 2
+    width = 2 * levels
+    own, _ = shares_of(dense_g[0:1, :])
+    new = dense
     for f in range(2):
-        mixed = couple_adjoint(columns[f * half : f * half + 1, :], other[4 + f : 5 + f, :], dense_g[0:1, :])
-        dense = level0_row(dense, mixed, f)
+        bottom = dense[f * half : f * half + 1]
+        new = level0_row(new, bottom - own * bottom, f)
+        packed[2 * half + f : 2 * half + f + 1, :] = bottom
+    dense_products(packed, new, wind_dense)
+    full = []
     for k, i in enumerate((0, rows - 1)):
+        own, _ = shares_of(coupling[i : i + 1, :])
         parts = []
         for f in range(2):
-            value = ends[k, f * levels : (f + 1) * levels, :]
-            at = 2 * k + f
-            parts.append(with_first(value, couple_adjoint(value[0:1], other[at : at + 1, :], coupling[i : i + 1, :])))
-        full[k] = jnp.concatenate(parts, axis=0)
-    dense_products(packed, dense, wind_dense)
-    end_rows(full, s_even, s_odd, wind_ends, levels)
-
-
-def outside_floor(halos, low, f, rows, levels):
+            value = ends[k][f * levels : (f + 1) * levels]
+            parts.append(with_first(value, value[0:1] - own * value[0:1]))
+        full.append(jnp.concatenate(parts, axis=0))
+    end_rows(full, strips, wind_ends, levels)
+    for f in range(2):
+        at = f * levels
+        put_strip(strips, slice(width + f, width + f + 1), ends[0][at : at + 1], ends[1][at : at + 1])
+
+
+def beside_kernel(rows, levels, *rest):
+    *halos, raw = rest
     before, after = read_sides(halos)
-    at = pl.ds(f * levels, 1)
+    at = pl.ds(2 * levels, 2)
+    half = halos[1].shape[0] - GROUP
+    raw[...] = jnp.zeros_like(raw)
+    raw[0:2, :] = before(at)
+    raw[2:4, :] = after(at)
+    raw[4:6, :] = merged(halos[1], halos[2], pl.ds(half, 2))
+
+
+def outside_floor(halos, factors, raw, low, f, rows, levels):
+    before, after = read_sides(halos)
+    factor_before, factor_after = read_sides(factors)
+    at, tail = pl.ds(f * levels, 1), pl.ds(2 * levels, 1)
     sub, lane = sub_iota(rows), lane_iota(rows)
-    low = low + jnp.where(sub == 0, before(at), 0.0) + jnp.where(sub == rows - 1, after(at), 0.0)
-    edge = floor_edge(halos, f, rows, levels)
+    from_before = before(at) + factor_before(tail) * raw[f : f + 1, :]
+    from_after = after(at) + factor_after(tail) * raw[2 + f : 3 + f, :]
+    low = low + jnp.where(sub == 0, from_before, 0.0) + jnp.where(sub == rows - 1, from_after, 0.0)
+    factor = merged(factors[1], factors[2], pl.ds(factors[1].shape[0] - GROUP, 1))
+    edge = floor_edge(halos, f, rows, levels, factor * raw[4 + f : 5 + f, :])
     edge = jnp.where(lane == 0, pltpu.roll(edge, 1, 1), pltpu.roll(edge, LANES - 1, 1))
     return low + jnp.where((lane == 0) | (lane == LANES - 1), edge, 0.0)
 
 
-def floor_kernel(rows, levels, coupling, other, low0, winds, *rest):
-    *halos, floor, missing = rest
+def floor_kernel(rows, levels, coupling, other, low0, raw, winds, *rest):
+    *both, floor, missing = rest
+    halos, factors = both[: len(both) // 2], both[len(both) // 2 :]
     for f in range(2):
         here = pl.ds(f * rows, rows)
         _, peer = shares_of(coupling[...])
@@ -478,7 +514,7 @@
         right, left = shifted(y_up, y_down, 0.0, rows)
         spread = (row_after(x_up, 0.0, rows) + row_before(x_down, 0.0, rows)) + (right + left)
         spread = spread + (CENTRE + VERT_MIX) * share
-        floor[here, :] = outside_floor(halos, low0[here, :] + spread, f, rows, levels)
+        floor[here, :] = outside_floor(halos, factors, raw, low0[here, :] + spread, f, rows, levels)
         missing[here, :] = VERT_MIX * share
 
 
@@ -502,12 +538,12 @@
 def border_again_kernel(
     rows, levels, coupling, floor, other, missing, ends, columns, wind_ends, wind_dense, dense_g, *rest
 ):
-    *halos, s_even, s_odd, packed, sides = rest
+    *halos, strips, packed, sides = rest
     before, after = read_sides(halos)
-    sides[...] = swap_pairs(merged(halos[1], halos[2], slice(None)))
+    sides[...] = swap_pairs(merged(halos[1], halos[2], slice(0, sides.shape[0])))
     half = columns.shape[0] // 2
     groups = levels // GROUP
-    outer = [before(slice(None)), after(slice(None))]
+    outer = [before(pl.ds(0, 2 * levels)), after(pl.ds(0, 2 * levels))]
     full = []
     for k, i in enumerate((0, rows - 1)):
         edges = jnp.concatenate([edge_lanes(sides, i, group) for group in range(2 * groups)], axis=0)
@@ -519,7 +555,7 @@
             part = part + with_level(jnp.zeros_like(part), 1, missing[at, :])
             parts.append(with_first(part, couple_adjoint(floor[at, :], other[at, :], coupling[i : i + 1, :])))
         full.append(jnp.concatenate(parts, axis=0))
-    end_rows(full, s_even, s_odd, wind_ends, levels)
+    end_rows(full, strips, wind_ends, levels)
     dense = columns[...] + sides[...]
     corners = []
     for m in range(2 * groups // PARTS):
@@ -589,7 +625,7 @@
 
 def second_adjoint_kernel(rows, levels, coupling, floor, other, missing, field, winds, scale, state, *rest):
     *halos, out, cells, sides = rest
-    sides[...] = swap_pairs(merged(halos[1], halos[2], slice(None)))
+    sides[...] = swap_pairs(merged(halos[1], halos[2], slice(0, sides.shape[0])))
     before, after = read_sides(halos)
     groups = levels // GROUP
 
@@ -632,7 +668,7 @@
 def final_kernel(rows, levels, field, *rest):
     *halos, out, cells, sides, sems = rest
     leaving = Out(cells, out, sems, rows, True)
-    sides[...] = swap_pairs(merged(halos[1], halos[2], slice(None)))
+    sides[...] = swap_pairs(merged(halos[1], halos[2], slice(0, sides.shape[0])))
     before, after = read_sides(halos)
     groups = levels // GROUP
 
@@ -644,7 +680,7 @@
         leaving.start(i)
         return 0
 
-    lax.fori_loop(1, rows - 1, lambda i, _: add(i, None), 0)
+    lax.fori_loop(1, rows - 1, lambda i, _: add(i, None), 0, unroll=2)
     add(0, before)
     add(rows - 1, after)
     leaving.finish()
@@ -701,7 +737,8 @@
 
 
 def innovate_kernel(rows, width, tiles, cap, records, cols, extra, bottom, *rest):
-    spread, sel, ends, columns, floor, col_cells, border_sel, precs, both, sems = rest
+    coupling, wind_ends, wind_dense, dense_g, spread, sel, strips, packed = rest[:8]
+    col_cells, border_sel, precs, both, sems = rest[8:]
     chunks = 8
     copies = []
     for part in range(chunks):
@@ -782,21 +819,20 @@
 
     terms = dot(spread[...], border_cells, (1, 0))
     border_sums = terms[:width] + terms[width:]
-    ends[0] = border_sums[:, 0:LANES]
-    ends[1] = border_sums[:, LANES : 2 * LANES]
     thin = border_sums[:, 2 * LANES :]
+    dense = []
     for m in range(width // (GROUP * PARTS)):
         total = thin[m * PARTS * GROUP : (m * PARTS + 1) * GROUP]
         for part in range(1, PARTS):
             at = (m * PARTS + part) * GROUP
             total = total + pltpu.roll(thin[at : at + GROUP], 2 * part, 1)
-        columns[m * GROUP : (m + 1) * GROUP, :] = total
-    half = columns.shape[0] // 2
-    floor[...] = jnp.zeros_like(floor)
-    for f in range(2):
-        for k in range(2):
-            floor[2 * k + f : 2 * k + f + 1, :] = ends[k, f * (width // 2) : f * (width // 2) + 1, :]
-        floor[4 + f : 5 + f, :] = columns[f * half : f * half + 1, :]
+        dense.append(total)
+    ends = (border_sums[:, 0:LANES], border_sums[:, LANES : 2 * LANES])
+    packed[packed.shape[0] - GROUP :, :] = jnp.zeros((GROUP, LANES), jnp.float32)
+    put_strip(strips, slice(width, width + GROUP), *[jnp.zeros((GROUP, LANES), jnp.float32)] * 2)
+    border_strips(
+        rows, width // 2, coupling, ends, jnp.concatenate(dense, axis=0), wind_ends, wind_dense, dense_g, strips, packed
+    )
 
 
 def scatter_kernel(rows, width, spread, sel, winds, adjoint, low0, wind_rows, sems):
@@ -831,7 +867,8 @@
     framed = pltpu.VMEM((rows + 2, width, LANES), jnp.float32)
     packed_shape = f32(groups // PARTS * GROUP, LANES)
     sides = pltpu.VMEM(packed_shape.shape, jnp.float32)
-    strip_shapes = [f32(width, LANES), f32(width, LANES), packed_shape]
+    strip_shapes = [f32(pair_sets(), width, LANES), packed_shape]
+    long_shapes = [f32(pair_sets(), width + GROUP, LANES), f32(packed_shape.shape[0] + GROUP, LANES)]
     field_shape = f32(rows, width, LANES)
     framed_shape = f32(rows + 2, width, LANES)
     low_shape = f32(fields * rows, LANES)
@@ -859,14 +896,14 @@
     slots = tiles * cap
     thin_shape = f32(GROUP, LANES)
 
-    s_even, s_odd, packed, low0, low1 = run(
+    strips, packed, low0, low1 = run(
         on_rows(edges_kernel),
         strip_shapes + [low_shape] * 2,
         [pltpu.VMEM((width * rows, LANES), jnp.float32), sems(groups // PARTS)],
         (state_incr.reshape(width * rows, lanes),),
         far=(0,),
     )
-    halos = exchange((s_even, s_odd), packed)
+    halos = exchange(strips, packed)
 
     send = call(functools.partial(route_kernel, tiles, cap), f32(tiles, halves * cap + GROUP, LANES))(
         obs_dest.reshape(1, count), obs_col.reshape(1, count), obs_prec.reshape(1, count), obs_op
@@ -884,16 +921,16 @@
     )
     halos[1], state_rows, wind_rows = lax.optimization_barrier((halos[1], state_rows, wind_rows))
     (floor,) = run(on_rows(forward_floor_kernel), [low_shape], [], (low0, low1, floor_winds, *halos))
-    field, s_even, s_odd, packed, low0, low1, wind_ends, wind_dense, dense_g = run(
+    field, strips, packed, low0, low1, wind_ends, wind_dense, dense_g = run(
         on_rows(forward_kernel),
         [framed_shape]
-        + strip_shapes
+        + long_shapes
         + [low_shape] * 2
         + [f32(2, levels, LANES), f32(groups // PARTS * GROUP // 2, LANES), thin_shape],
         [framed, sides],
         (coupling, swap_floor(floor), state_rows, wind_rows, *halos),
     )
-    halos = exchange((s_even, s_odd), packed)
+    halos = exchange(strips, packed)
     (cols,) = run(
         on_rows(forward_again_kernel),
         [jax.ShapeDtypeStruct(*cols_shape)],
@@ -913,15 +950,9 @@
 
     spread_shape = ((2 * width, slots), jnp.bfloat16)
     sel_shape = ((slots, rows * LANES), jnp.bfloat16)
-    spread, sel, ends, columns, border_floor = run(
+    spread, sel, strips, packed = run(
         functools.partial(innovate_kernel, rows, width, tiles, cap),
-        [
-            jax.ShapeDtypeStruct(*spread_shape),
-            jax.ShapeDtypeStruct(*sel_shape),
-            f32(2, width, LANES),
-            packed_shape,
-            thin_shape,
-        ],
+        [jax.ShapeDtypeStruct(*spread_shape), jax.ShapeDtypeStruct(*sel_shape)] + long_shapes,
         [
             pltpu.VMEM(*cols_shape),
             pltpu.VMEM((slots, LANES), jnp.bfloat16),
@@ -929,17 +960,12 @@
             pltpu.VMEM((slots, 2 * width), jnp.float32),
             sems(8),
         ],
-        (records, cols, extra, bottom),
+        (records, cols, extra, bottom, coupling, wind_ends, wind_dense, dense_g),
         far=(1,),
         limit=OBSERVE_VMEM,
     )
-    strips = run(
-        on_rows(border_kernel),
-        strip_shapes,
-        [],
-        (coupling, swap_floor(border_floor), ends, columns, wind_ends, wind_dense, dense_g),
-    )
-    halos = exchange(strips[:2], strips[2])
+    factors = halos
+    halos = exchange(strips, packed)
     adjoint, low0, wind_rows = run(
         functools.partial(scatter_kernel, rows, width),
         [field_shape, low_shape, framed_shape],
@@ -949,7 +975,9 @@
         limit=OBSERVE_VMEM,
         traffic=8 * MIB,
     )
-    partner = swap_floor(low0)
+    low0, halos = lax.optimization_barrier((low0, halos))
+    (raw,) = run(on_rows(beside_kernel), [thin_shape], [], halos)
+    partner, raw = swap_floor(low0), swap_floor(raw)
     adjoint, ends, columns, low0, state_rows = run(
         on_rows(first_adjoint_kernel),
         [field_shape, f32(2, width, LANES), packed_shape, low_shape, field_shape],
@@ -958,18 +986,21 @@
         far=(3,),
         traffic=16 * MIB,
     )
-    low0, partner, halos = lax.optimization_barrier((low0, partner, halos))
+    low0, partner, raw = lax.optimization_barrier((low0, partner, raw))
     floor, missing = run(
-        on_rows(floor_kernel), [low_shape, low_shape], [], (coupling, partner, low0, floor_winds, *halos)
+        on_rows(floor_kernel),
+        [low_shape, low_shape],
+        [],
+        (coupling, partner, low0, raw, floor_winds, *halos, *factors),
     )
     other = swap_floor(floor)
-    strips = run(
+    strips, packed = run(
         on_rows(border_again_kernel),
         strip_shapes,
         [sides],
         (coupling, floor, other, missing, ends, columns, wind_ends, wind_dense, dense_g, *halos),
     )
-    last_halos = exchange(strips[:2], strips[2])
+    last_halos = exchange(strips, packed)
     (adjoint,) = run(
         on_rows(second_adjoint_kernel),
         [field_shape],

time: 79.3 us -> 76.8 us (0.968)
  the two profiles are of different devices: /device:TPU:8 before, /device:TPU:10 now
where the time goes in v7:
time: 76.8 us; the launch traced here: 76.4 us
  Pallas kernels  36.4 us (47%)
  starting transfers between devices  28.3 us (37%)
  waiting for transfers between devices  10.7 us (14%)
  local copies, waits for them, and re-layouts  0.83 us (1%)
    pallas_call x15, Pallas kernels, run(): call(body, out_shape, scratch, in_specs=specs, out_specs=outs, **kw)(*args)  34.4 us
    ppermute x12, starting transfers between devices, pair_swap(): return lax.ppermute(block, axis, route)  22.2 us
    ppermute x12, waiting for transfers between devices, pair_swap(): return lax.ppermute(block, axis, route)  7.2 us
    all_to_all x1, starting transfers between devices, local(): lax.all_to_all(send, ('gx', 'gy'), split_axis=0, concat_axis=0, tiled=True)  5.31 us
    ppermute x5, waiting for transfers between devices, swap_floor(): return lax.ppermute(floor, 'comp', [(0, 1), (1, 0)])  3.45 us
    pallas_call x1, Pallas kernels, local(): call(functools.partial(route_kernel, tiles, cap), f32(tiles, halves * cap...  1.98 us
  transfers between devices with their start and end apart: 18, of which 7 were waited for; matrix products, arithmetic and copies ran while one was open for 1% of the time, Pallas kernels for 33%

profile of v7, /device:TPU:10, one launch (start us, length us, event | category | flops | bytes accessed | tf_op | source)
XLA Modules:
  0.0 76.4 jit_solution(4332155715445512657)
XLA Ops:
  0.0 2.3 %shard_map.83 = (f32[1,256,128]{2,1,0:T(8,128)S(1)}, f32[64,128]{1,0:T(8,128)S(1)}, f32[32,128]{1,0:T(8,128)S(1)}, f32[32,128]{1,0:T(8,128)S(1)}) custom-call(f32[4096,128]{1,0:T(8,128)} %bitcast.23), custom_call_target="tpu_custom_call" | custom-call | tf_op jit(solution)/shard_map/pallas_call | solution.py:885
  2.3 1.6 %collective-permute-start = (f32[256,128]{1,0:T(8,128)S(1)}, f32[256,128]{1,0:T(8,128)S(1)}, u32[]{:S(2)}, u32[]{:S(2)}) collective-permute-start(f32[256,128]{1,0:T(8,128)S(1)} %bitcast.22), channel_id=1, source_target_pairs={{0,8},{8,0},{1,9},{9,1},{2,10},{10,2},{3,11},{11,3},{4,12},{12,4},... | collective-permute-start | bytes 393224 | tf_op jit(solution)/shard_map/ppermute | solution.py:48
  3.9 3.4 %collective-permute-start.1 = (f32[64,128]{1,0:T(8,128)S(1)}, f32[64,128]{1,0:T(8,128)S(1)}, u32[]{:S(2)}, u32[]{:S(2)}) collective-permute-start(f32[64,128]{1,0:T(8,128)S(1)} %get-tuple-element.57), channel_id=1, source_target_pairs={{1,2},{2,1},{3,4},{4,3},{5,6},{6,5},{9,10},{10,9},{11,12},{12,11},... | collective-permute-start | bytes 98312 | tf_op jit(solution)/shard_map/ppermute | solution.py:48
  7.4 2.0 %shard_map.82 = f32[16,136,128]{2,1,0:T(8,128)} custom-call(s32[1,512]{1,0:T(1,128)S(1)} %bitcast.16, s32[1,512]{1,0:T(1,128)S(1)} %bitcast.17, f32[1,512]{1,0:T(1,128)S(1)} %bitcast.18, f32[512,256]{1,0:T(8,128)S(1)} %copy-done), custom_call_target="tpu_custom_call" | custom-call | tf_op jit(solution)/shard_map/pallas_call | solution.py:908
  9.4 1.2 %collective-permute-done.1.rest_2_ = f32[64,128]{1,0:T(8,128)S(1)} collective-permute-done((f32[64,128]{1,0:T(8,128)S(1)}, f32[64,128]{1,0:T(8,128)S(1)}, u32[]{:S(2)}, u32[]{:S(2)}) %collective-permute-start.1) | collective-permute-done | bytes 32800 | tf_op jit(solution)/shard_map/ppermute | solution.py:48
  10.6 5.3 %all-to-all-start = ((f32[16,136,128]{2,1,0:T(8,128)}), f32[16,136,128]{2,1,0:T(8,128)S(1)}, u32[]{:S(2)}, u32[]{:S(2)}) async-start(f32[16,136,128]{2,1,0:T(8,128)} %shard_map.82), calls=%async_computation | async-start | bytes 2228224 | tf_op jit(solution)/shard_map/all_to_all | solution.py:912
  15.9 0.6 collective-permute-start.2
  16.5 0.7 slice_bitcast_fusion.winds
  17.2 3.0 %shard_map.84 = (f32[16,256,128]{2,1,0:T(8,128)S(1)}, f32[16,256,128]{2,1,0:T(8,128)S(1)}) custom-call(f32[256,16,128]{2,1,0:T(8,128)} %bitcast.24, f32[256,16,128]{2,1,0:T(8,128)} %bitcast.26), custom_call_target="tpu_custom_call" | custom-call | bytes 10485760 | tf_op jit(solution)/shard_map/pallas_call | solution.py:885
  20.5 1.2 %collective-permute-done.3.other = f32[32,128]{1,0:T(8,128)S(1)} collective-permute-done((f32[32,128]{1,0:T(8,128)S(1)}, f32[32,128]{1,0:T(8,128)S(1)}, u32[]{:S(2)}, u32[]{:S(2)}) %collective-permute-start.3) | collective-permute-done | bytes 16416 | tf_op jit(solution)/shard_map/ppermute | solution.py:891
  21.7 4.9 %shard_map.86 = (f32[18,256,128]{2,1,0:T(8,128)S(1)}, f32[1,264,128]{2,1,0:T(8,128)S(1)}, f32[72,128]{1,0:T(8,128)S(1)}, f32[32,128]{1,0:T(8,128)S(1)}, f32[32,1...) custom-call(f32[16,128]{1,0:T(8,128)S(1)} %copy-done.1, ...), custom_call_target="tpu_custom_call" | custom-call | tf_op jit(solution)/shard_map/pallas_call | solution.py:885
  26.6 1.5 %collective-permute-start.4 = (f32[264,128]{1,0:T(8,128)S(1)}, f32[264,128]{1,0:T(8,128)S(1)}, u32[]{:S(2)}, u32[]{:S(2)}) collective-permute-start(f32[264,128]{1,0:T(8,128)S(1)} %bitcast.19), channel_id=1, source_target_pairs={{0,8},{8,0},{1,9},{9,1},{2,10},{10,2},{3,11},{11,3},{4,12},{12,4},... | collective-permute-start | bytes 405512 | tf_op jit(solution)/shard_map/ppermute | solution.py:48
  28.1 1.5 %collective-permute-start.5 = (f32[72,128]{1,0:T(8,128)S(1)}, f32[72,128]{1,0:T(8,128)S(1)}, u32[]{:S(2)}, u32[]{:S(2)}) collective-permute-start(f32[72,128]{1,0:T(8,128)S(1)} %get-tuple-element.72), channel_id=1, source_target_pairs={{0,1},{1,0},{2,3},{3,2},{4,5},{5,4},{6,7},{7,6},{8,9},{9,8},{10,11... | collective-permute-start | bytes 110600 | tf_op jit(solution)/shard_map/ppermute | solution.py:48
  29.6 3.4 %collective-permute-start.6 = (f32[72,128]{1,0:T(8,128)S(1)}, f32[72,128]{1,0:T(8,128)S(1)}, u32[]{:S(2)}, u32[]{:S(2)}) collective-permute-start(f32[72,128]{1,0:T(8,128)S(1)} %get-tuple-element.72), channel_id=1, source_target_pairs={{1,2},{2,1},{3,4},{4,3},{5,6},{6,5},{9,10},{10,9},{11,12},{12,11},... | collective-permute-start | bytes 110600 | tf_op jit(solution)/shard_map/ppermute | solution.py:48
  32.9 3.4 %shard_map.87.cols = bf16[512,2048]{1,0:T(8,128)(2,1)} custom-call(f32[18,256,128]{2,1,0:T(8,128)S(1)} %get-tuple-element.70.cells, f32[16,256,128]{2,1,0:T(8,128)S(1)} %get-tuple-element.69.winds), custom_call_target="tpu_custom_call" | custom-call | bytes 20971520 | tf_op jit(solution)/shard_map/pallas_call | solution.py:885
  36.3 5.2 %collective-permute-done.6.rest_2_.rest_5_ = f32[72,128]{1,0:T(8,128)S(1)} collective-permute-done((f32[72,128]{1,0:T(8,128)S(1)}, f32[72,128]{1,0:T(8,128)S(1)}, u32[]{:S(2)}, u32[]{:S(2)}) %collective-permute-start.6) | collective-permute-done | bytes 36896 | tf_op jit(solution)/shard_map/ppermute | solution.py:48
  41.8 1.2 %collective-permute-done.7.other = f32[32,128]{1,0:T(8,128)S(1)} collective-permute-done((f32[32,128]{1,0:T(8,128)S(1)}, f32[32,128]{1,0:T(8,128)S(1)}, u32[]{:S(2)}, u32[]{:S(2)}) %collective-permute-start.7) | collective-permute-done | bytes 16416 | tf_op jit(solution)/shard_map/ppermute | solution.py:891
  43.2 6.4 %shard_map.90 = (bf16[512,1024]{1,0:T(8,128)(2,1)S(1)}, bf16[1024,2048]{1,0:T(8,128)(2,1)S(1)}, f32[1,264,128]{2,1,0:T(8,128)S(1)}, f32[72,128]{1,0:T(8,128)S(1)}) custom-call(f32[16,136,128]{2,1,0:T(8,128)S(1)} %all-to-all-done.records, bf16[512,2048]{1,0:T(8,128)(2,1)} %shard_map.87.cols, bf16[512,384]{1,0:T(8,128)(2,1)S(1)} %get-tuple-element.81.extra, ...), custom_call_target="tpu_custom_call" | custom-call | tf_op jit(solution)/shard_map/pallas_call | solution.py:885
  49.6 1.4 %collective-permute-start.8 = (f32[264,128]{1,0:T(8,128)S(1)}, f32[264,128]{1,0:T(8,128)S(1)}, u32[]{:S(2)}, u32[]{:S(2)}) collective-permute-start(f32[264,128]{1,0:T(8,128)S(1)} %bitcast.20), channel_id=1, source_target_pairs={{0,8},{8,0},{1,9},{9,1},{2,10},{10,2},{3,11},{11,3},{4,12},{12,4},... | collective-permute-start | bytes 405512 | tf_op jit(solution)/shard_map/ppermute | solution.py:48
  50.9 3.0 %collective-permute-start.10 = (f32[72,128]{1,0:T(8,128)S(1)}, f32[72,128]{1,0:T(8,128)S(1)}, u32[]{:S(2)}, u32[]{:S(2)}) collective-permute-start(f32[72,128]{1,0:T(8,128)S(1)} %get-tuple-element.91), channel_id=1, source_target_pairs={{1,2},{2,1},{3,4},{4,3},{5,6},{6,5},{9,10},{10,9},{11,12},{12,11},... | collective-permute-start | bytes 110600 | tf_op jit(solution)/shard_map/ppermute | solution.py:48
  54.0 3.3 %shard_map.91 = (f32[16,256,128]{2,1,0:T(8,128)S(1)}, f32[32,128]{1,0:T(8,128)S(1)}, f32[18,256,128]{2,1,0:T(8,128)S(1)}) custom-call(bf16[512,1024]{1,0:T(8,128)(2,1)S(1)} %get-tuple-element.84.spread, bf16[1024,2048]{1,0:T(8,128)(2,1)S(1)} %get-tuple-element.85.sel, f32[256,16,128]{2,1,0:T(8,128)} %bitcast.27), custom_call_target="tpu_custom_call" | custom-call | bytes 8388608 | tf_op jit(solution)/shard_map/pallas_call | solution.py:885
  57.3 0.4 collective-permute-done.10.rest_2_
  57.7 0.4 collective-permute-done.9.rest_1_
  58.1 0.5 collective-permute-start.12
  58.6 3.8 %shard_map.92 = (f32[16,256,128]{2,1,0:T(8,128)S(1)}, f32[2,256,128]{2,1,0:T(8,128)S(1)}, f32[64,128]{1,0:T(8,128)S(1)}, f32[32,128]{1,0:T(8,128)S(1)}, f32[16,256,128]{2,1,0:T(8,128)S(1)}) custom-call(f32[16,128]{1,0:T(8,128)S(1)} %copy-done.1, f32[16,256,128]{2,1,0:T(8,128)S(1)} %get-tuple-element.86.field, f32[18,256,128]{2,1,0:T(8,128)S(1)} %get-tuple-element.87.winds, ...), custom_call_target="tpu_custom_call" | custom-call | bytes 16777216 | tf_op jit(solution)/shard_map/pallas_call | solution.py:885
  62.7 1.1 %collective-permute-done.13.other = f32[32,128]{1,0:T(8,128)S(1)} collective-permute-done((f32[32,128]{1,0:T(8,128)S(1)}, f32[32,128]{1,0:T(8,128)S(1)}, u32[]{:S(2)}, u32[]{:S(2)}) %collective-permute-start.13) | collective-permute-done | bytes 16416 | tf_op jit(solution)/shard_map/ppermute | solution.py:891
  63.8 0.4 shard_map.96
  64.2 0.8 %collective-permute-start.14 = (f32[256,128]{1,0:T(8,128)S(1)}, f32[256,128]{1,0:T(8,128)S(1)}, u32[]{:S(2)}, u32[]{:S(2)}) collective-permute-start(f32[256,128]{1,0:T(8,128)S(1)} %bitcast.21), channel_id=1, source_target_pairs={{0,8},{8,0},{1,9},{9,1},{2,10},{10,2},{3,11},{11,3},{4,12},{12,4},... | collective-permute-start | bytes 393224 | tf_op jit(solution)/shard_map/ppermute | solution.py:48
  65.0 1.2 %collective-permute-start.15 = (f32[64,128]{1,0:T(8,128)S(1)}, f32[64,128]{1,0:T(8,128)S(1)}, u32[]{:S(2)}, u32[]{:S(2)}) collective-permute-start(f32[64,128]{1,0:T(8,128)S(1)} %get-tuple-element.106), channel_id=1, source_target_pairs={{0,1},{1,0},{2,3},{3,2},{4,5},{5,4},{6,7},{7,6},{8,9},{9,8},{10,11... | collective-permute-start | bytes 98312 | tf_op jit(solution)/shard_map/ppermute | solution.py:48
  66.2 3.9 %collective-permute-start.16 = (f32[64,128]{1,0:T(8,128)S(1)}, f32[64,128]{1,0:T(8,128)S(1)}, u32[]{:S(2)}, u32[]{:S(2)}) collective-permute-start(f32[64,128]{1,0:T(8,128)S(1)} %get-tuple-element.106), channel_id=1, source_target_pairs={{1,2},{2,1},{3,4},{4,3},{5,6},{6,5},{9,10},{10,9},{11,12},{12,11},... | collective-permute-start | bytes 98312 | tf_op jit(solution)/shard_map/ppermute | solution.py:48
  70.2 4.2 %shard_map.95.field = f32[16,256,128]{2,1,0:T(8,128)S(1)} custom-call(f32[16,128]{1,0:T(8,128)S(1)} %copy-done.1, f32[32,128]{1,0:T(8,128)S(1)} %get-tuple-element.99.floor, f32[32,128]{1,0:T(8,128)S(1)} %collective-permute-done.13.other, f32[32,128]{1,0:T(8,128)S(1)} %get-tuple-element.100.missing, f32[16,256,128]{2,1,0:T(8,128)S(1)} %get-tuple-element.101.field, ...), custom_call_target="tpu_custom_call" | custom-call | bytes 20971520 | tf_op jit(solution)/shard_map/pallas_call | solution.py:885
  74.5 2.0 %shard_map.97 = f32[256,16,128]{2,1,0:T(8,128)} custom-call(f32[16,256,128]{2,1,0:T(8,128)S(1)} %shard_map.95.field, f32[256,128]{1,0:T(8,128)S(1)} %collective-permute-done.14.rest_0_, f32[64,128]{1,0:T(8,128)S(1)} %collective-permute-done.15.rest_1_, f32[64,128]{1,0:T(8,128)S(1)} %collective-permute-done.16.rest_2_), custom_call_target="tpu_custom_call" | custom-call | tf_op jit(solution)/shard_map/pallas_call | solution.py:885
  (34 shorter events, 1.2 us)
Async XLA Ops:
  0.0 7.4 %copy-start.2 = (s32[512,1]{0,1:T(1,128)S(1)}, s32[512,1]{0,1:T(1,128)}, u32[]{:S(2)}) copy-start(s32[512,1]{0,1:T(1,128)} %param.12) | copy-start | bytes 6148
  0.0 7.4 %copy-start.3 = (s32[512]{0:T(512)S(1)}, s32[512]{0:T(512)}, u32[]{:S(2)}) copy-start(s32[512]{0:T(512)} %param.13) | copy-start | bytes 6148
  0.0 7.4 %copy-start.4 = (f32[512]{0:T(512)S(1)}, f32[512]{0:T(512)}, u32[]{:S(2)}) copy-start(f32[512]{0:T(512)} %param.15) | copy-start | bytes 6148
  0.0 7.4 %copy-start = (f32[512,256]{1,0:T(8,128)S(1)}, f32[512,256]{1,0:T(8,128)}, u32[]{:S(2)}) copy-start(f32[512,256]{1,0:T(8,128)} %op.1) | copy-start | bytes 1572868
  2.3 8.3 %collective-permute-start = (f32[256,128]{1,0:T(8,128)S(1)}, f32[256,128]{1,0:T(8,128)S(1)}, u32[]{:S(2)}, u32[]{:S(2)}) collective-permute-start(f32[256,128]{1,0:T(8,128)S(1)} %bitcast.22), channel_id=1, source_target_pairs={{0,8},{8,0},{1,9},{9,1},{2,10},{10,2},{3,11},{11,3},{4,12},{12,4},... | collective-permute-start | bytes 393224 | tf_op jit(solution)/shard_map/ppermute | solution.py:48
  3.9 6.7 %collective-permute-start.1 = (f32[64,128]{1,0:T(8,128)S(1)}, f32[64,128]{1,0:T(8,128)S(1)}, u32[]{:S(2)}, u32[]{:S(2)}) collective-permute-start(f32[64,128]{1,0:T(8,128)S(1)} %get-tuple-element.57), channel_id=1, source_target_pairs={{1,2},{2,1},{3,4},{4,3},{5,6},{6,5},{9,10},{10,9},{11,12},{12,11},... | collective-permute-start | bytes 98312 | tf_op jit(solution)/shard_map/ppermute | solution.py:48
  10.6 32.6 %all-to-all-start = ((f32[16,136,128]{2,1,0:T(8,128)}), f32[16,136,128]{2,1,0:T(8,128)S(1)}, u32[]{:S(2)}, u32[]{:S(2)}) async-start(f32[16,136,128]{2,1,0:T(8,128)} %shard_map.82), calls=%async_computation | async-start | bytes 2228224 | tf_op jit(solution)/shard_map/all_to_all | solution.py:912
  15.9 4.3 %collective-permute-start.2 = (f32[64,128]{1,0:T(8,128)S(1)}, f32[64,128]{1,0:T(8,128)S(1)}, u32[]{:S(2)}, u32[]{:S(2)}) collective-permute-start(f32[64,128]{1,0:T(8,128)S(1)} %get-tuple-element.57), channel_id=1, source_target_pairs={{0,1},{1,0},{2,3},{3,2},{4,5},{5,4},{6,7},{7,6},{8,9},{9,8},{10,11... | collective-permute-start | bytes 98312 | tf_op jit(solution)/shard_map/ppermute | solution.py:48
  17.2 4.5 %copy-start.1 = (f32[16,128]{1,0:T(8,128)S(1)}, f32[16,128]{1,0:T(8,128)}, u32[]{:S(2)}) copy-start(f32[16,128]{1,0:T(8,128)} %coupling.11) | copy-start | bytes 24580
  20.4 1.2 %collective-permute-start.3 = (f32[32,128]{1,0:T(8,128)S(1)}, f32[32,128]{1,0:T(8,128)S(1)}, u32[]{:S(2)}, u32[]{:S(2)}) collective-permute-start(f32[32,128]{1,0:T(8,128)S(1)} %shard_map.85), channel_id=1, source_target_pairs={{0,16},{16,0},{1,17},{17,1},{2,18},{18,2},{3,19},{19,3},{4,20},{20... | collective-permute-start | bytes 49160 | tf_op jit(solution)/shard_map/ppermute | solution.py:891
  26.6 14.9 %collective-permute-start.4 = (f32[264,128]{1,0:T(8,128)S(1)}, f32[264,128]{1,0:T(8,128)S(1)}, u32[]{:S(2)}, u32[]{:S(2)}) collective-permute-start(f32[264,128]{1,0:T(8,128)S(1)} %bitcast.19), channel_id=1, source_target_pairs={{0,8},{8,0},{1,9},{9,1},{2,10},{10,2},{3,11},{11,3},{4,12},{12,4},... | collective-permute-start | bytes 405512 | tf_op jit(solution)/shard_map/ppermute | solution.py:48
  28.1 8.2 %collective-permute-start.5 = (f32[72,128]{1,0:T(8,128)S(1)}, f32[72,128]{1,0:T(8,128)S(1)}, u32[]{:S(2)}, u32[]{:S(2)}) collective-permute-start(f32[72,128]{1,0:T(8,128)S(1)} %get-tuple-element.72), channel_id=1, source_target_pairs={{0,1},{1,0},{2,3},{3,2},{4,5},{5,4},{6,7},{7,6},{8,9},{9,8},{10,11... | collective-permute-start | bytes 110600 | tf_op jit(solution)/shard_map/ppermute | solution.py:48
  29.6 11.9 %collective-permute-start.6 = (f32[72,128]{1,0:T(8,128)S(1)}, f32[72,128]{1,0:T(8,128)S(1)}, u32[]{:S(2)}, u32[]{:S(2)}) collective-permute-start(f32[72,128]{1,0:T(8,128)S(1)} %get-tuple-element.72), channel_id=1, source_target_pairs={{1,2},{2,1},{3,4},{4,3},{5,6},{6,5},{9,10},{10,9},{11,12},{12,11},... | collective-permute-start | bytes 110600 | tf_op jit(solution)/shard_map/ppermute | solution.py:48
  41.7 1.2 %collective-permute-start.7 = (f32[32,128]{1,0:T(8,128)S(1)}, f32[32,128]{1,0:T(8,128)S(1)}, u32[]{:S(2)}, u32[]{:S(2)}) collective-permute-start(f32[32,128]{1,0:T(8,128)S(1)} %shard_map.88.floor), channel_id=1, source_target_pairs={{0,16},{16,0},{1,17},{17,1},{2,18},{18,2},{3,19},{19,3},{4,20},{20... | collective-permute-start | bytes 49160 | tf_op jit(solution)/shard_map/ppermute | solution.py:891
  49.6 8.5 %collective-permute-start.8 = (f32[264,128]{1,0:T(8,128)S(1)}, f32[264,128]{1,0:T(8,128)S(1)}, u32[]{:S(2)}, u32[]{:S(2)}) collective-permute-start(f32[264,128]{1,0:T(8,128)S(1)} %bitcast.20), channel_id=1, source_target_pairs={{0,8},{8,0},{1,9},{9,1},{2,10},{10,2},{3,11},{11,3},{4,12},{12,4},... | collective-permute-start | bytes 405512 | tf_op jit(solution)/shard_map/ppermute | solution.py:48
  50.9 6.8 %collective-permute-start.10 = (f32[72,128]{1,0:T(8,128)S(1)}, f32[72,128]{1,0:T(8,128)S(1)}, u32[]{:S(2)}, u32[]{:S(2)}) collective-permute-start(f32[72,128]{1,0:T(8,128)S(1)} %get-tuple-element.91), channel_id=1, source_target_pairs={{1,2},{2,1},{3,4},{4,3},{5,6},{6,5},{9,10},{10,9},{11,12},{12,11},... | collective-permute-start | bytes 110600 | tf_op jit(solution)/shard_map/ppermute | solution.py:48
  53.9 4.1 %collective-permute-start.9 = (f32[72,128]{1,0:T(8,128)S(1)}, f32[72,128]{1,0:T(8,128)S(1)}, u32[]{:S(2)}, u32[]{:S(2)}) collective-permute-start(f32[72,128]{1,0:T(8,128)S(1)} %get-tuple-element.91), channel_id=1, source_target_pairs={{0,1},{1,0},{2,3},{3,2},{4,5},{5,4},{6,7},{7,6},{8,9},{9,8},{10,11... | collective-permute-start | bytes 110600 | tf_op jit(solution)/shard_map/ppermute | solution.py:48
  58.1 4.4 %collective-permute-start.11 = (f32[32,128]{1,0:T(8,128)S(1)}, f32[32,128]{1,0:T(8,128)S(1)}, u32[]{:S(2)}, u32[]{:S(2)}) collective-permute-start(f32[32,128]{1,0:T(8,128)S(1)} %get-tuple-element.92), channel_id=1, source_target_pairs={{0,16},{16,0},{1,17},{17,1},{2,18},{18,2},{3,19},{19,3},{4,20},{20... | collective-permute-start | bytes 49160 | tf_op jit(solution)/shard_map/ppermute | solution.py:891
  58.1 4.3 %collective-permute-start.12 = (f32[8,128]{1,0:T(8,128)S(1)}, f32[8,128]{1,0:T(8,128)S(1)}, u32[]{:S(2)}, u32[]{:S(2)}) collective-permute-start(f32[8,128]{1,0:T(8,128)S(1)} %shard_map.93), channel_id=1, source_target_pairs={{0,16},{16,0},{1,17},{17,1},{2,18},{18,2},{3,19},{19,3},{4,20},{20... | collective-permute-start | bytes 12296 | tf_op jit(solution)/shard_map/ppermute | solution.py:891
  58.6 11.5 %copy-start.5 = (f32[1,2,128]{2,1,0:T(2,128)S(1)}, f32[1,2,128]{2,1,0:T(2,128)}, u32[]{:S(2)}) copy-start(f32[1,2,128]{2,1,0:T(2,128)} %param.11) | copy-start | bytes 3076
  62.6 1.2 %collective-permute-start.13 = (f32[32,128]{1,0:T(8,128)S(1)}, f32[32,128]{1,0:T(8,128)S(1)}, u32[]{:S(2)}, u32[]{:S(2)}) collective-permute-start(f32[32,128]{1,0:T(8,128)S(1)} %get-tuple-element.99.floor), channel_id=1, source_target_pairs={{0,16},{16,0},{1,17},{17,1},{2,18},{18,2},{3,19},{19,3},{4,20},{20... | collective-permute-start | bytes 49160 | tf_op jit(solution)/shard_map/ppermute | solution.py:891
  64.2 10.2 %collective-permute-start.14 = (f32[256,128]{1,0:T(8,128)S(1)}, f32[256,128]{1,0:T(8,128)S(1)}, u32[]{:S(2)}, u32[]{:S(2)}) collective-permute-start(f32[256,128]{1,0:T(8,128)S(1)} %bitcast.21), channel_id=1, source_target_pairs={{0,8},{8,0},{1,9},{9,1},{2,10},{10,2},{3,11},{11,3},{4,12},{12,4},... | collective-permute-start | bytes 393224 | tf_op jit(solution)/shard_map/ppermute | solution.py:48
  65.0 9.4 %collective-permute-start.15 = (f32[64,128]{1,0:T(8,128)S(1)}, f32[64,128]{1,0:T(8,128)S(1)}, u32[]{:S(2)}, u32[]{:S(2)}) collective-permute-start(f32[64,128]{1,0:T(8,128)S(1)} %get-tuple-element.106), channel_id=1, source_target_pairs={{0,1},{1,0},{2,3},{3,2},{4,5},{5,4},{6,7},{7,6},{8,9},{9,8},{10,11... | collective-permute-start | bytes 98312 | tf_op jit(solution)/shard_map/ppermute | solution.py:48
  66.2 8.2 %collective-permute-start.16 = (f32[64,128]{1,0:T(8,128)S(1)}, f32[64,128]{1,0:T(8,128)S(1)}, u32[]{:S(2)}, u32[]{:S(2)}) collective-permute-start(f32[64,128]{1,0:T(8,128)S(1)} %get-tuple-element.106), channel_id=1, source_target_pairs={{1,2},{2,1},{3,4},{4,3},{5,6},{6,5},{9,10},{10,9},{11,12},{12,11},... | collective-permute-start | bytes 98312 | tf_op jit(solution)/shard_map/ppermute | solution.py:48

commit v8 on v7

--- a/solution.py
+++ b/solution.py
@@ -259,9 +259,9 @@
             low[f * rows : (f + 1) * rows, :] = cells[pl.ds((f * levels + level) * rows, rows), :]
 
 
-def floor_edge(halos, f, rows, levels, more=0.0):
+def floor_edge(halos, f, rows, levels):
     m = f * (levels // GROUP) // PARTS
-    sides = jnp.broadcast_to(merged(halos[1], halos[2], pl.ds(m * GROUP, 1)) + more, (rows, LANES))
+    sides = jnp.broadcast_to(merged(halos[1], halos[2], pl.ds(m * GROUP, 1)), (rows, LANES))
     return pltpu.roll(sides, 2 * PARTS - 1, 1, stride=2 * PARTS, stride_axis=0)
 
 
@@ -310,13 +310,19 @@
     return total
 
 
-def load_kernel(rows, state, winds, state_rows, wind_rows, sems):
+def load_kernel(rows, state, winds, state_rows, wind_rows, state_later, wind_later, sems):
     state_in = Rows(state, state_rows, sems.at[0], rows, True, 0)
     wind_in = Rows(winds, wind_rows, sems.at[1], rows, True, 0)
+    state_out = Out(state_rows, state_later, sems.at[2], rows, False)
+    wind_out = Out(wind_rows, wind_later, sems.at[3], rows, False)
     start_rows(rows, state_in, wind_in)
     for i in range(rows):
         state_in.wait(i)
         wind_in.wait(i)
+        state_out.start(i)
+        wind_out.start(i)
+    state_out.finish()
+    wind_out.finish()
 
 
 def forward_kernel(rows, levels, coupling, other, field, winds, *rest):
@@ -394,8 +400,13 @@
 
 
 def outside_kernel(rows, levels, coupling, floor, other, wind_ends, wind_dense, *rest):
-    *halos, extra, bottom, dense = rest
+    *halos, extra, bottom, factors, dense = rest
     width = 2 * levels
+    tail = pl.ds(width, 1)
+    factors[...] = jnp.zeros_like(factors)
+    for k, side in enumerate(read_sides(halos)):
+        factors[k : k + 1, :] = side(tail)
+    factors[2:3, :] = merged(halos[1], halos[2], pl.ds(dense.shape[0], 1))
     for f in range(2):
         here = pl.ds(f * rows, rows)
         bottom[here, :] = couple_forward(floor[here, :], other[here, :], coupling[...])
@@ -477,34 +488,18 @@
         put_strip(strips, slice(width + f, width + f + 1), ends[0][at : at + 1], ends[1][at : at + 1])
 
 
-def beside_kernel(rows, levels, *rest):
-    *halos, raw = rest
-    before, after = read_sides(halos)
-    at = pl.ds(2 * levels, 2)
-    half = halos[1].shape[0] - GROUP
-    raw[...] = jnp.zeros_like(raw)
-    raw[0:2, :] = before(at)
-    raw[2:4, :] = after(at)
-    raw[4:6, :] = merged(halos[1], halos[2], pl.ds(half, 2))
-
-
-def outside_floor(halos, factors, raw, low, f, rows, levels):
-    before, after = read_sides(halos)
-    factor_before, factor_after = read_sides(factors)
-    at, tail = pl.ds(f * levels, 1), pl.ds(2 * levels, 1)
+def to_border(low, before, after, sides, rows):
     sub, lane = sub_iota(rows), lane_iota(rows)
-    from_before = before(at) + factor_before(tail) * raw[f : f + 1, :]
-    from_after = after(at) + factor_after(tail) * raw[2 + f : 3 + f, :]
-    low = low + jnp.where(sub == 0, from_before, 0.0) + jnp.where(sub == rows - 1, from_after, 0.0)
-    factor = merged(factors[1], factors[2], pl.ds(factors[1].shape[0] - GROUP, 1))
-    edge = floor_edge(halos, f, rows, levels, factor * raw[4 + f : 5 + f, :])
+    low = low + jnp.where(sub == 0, before, 0.0) + jnp.where(sub == rows - 1, after, 0.0)
+    edge = pltpu.roll(jnp.broadcast_to(sides, (rows, LANES)), 2 * PARTS - 1, 1, stride=2 * PARTS, stride_axis=0)
     edge = jnp.where(lane == 0, pltpu.roll(edge, 1, 1), pltpu.roll(edge, LANES - 1, 1))
     return low + jnp.where((lane == 0) | (lane == LANES - 1), edge, 0.0)
 
 
-def floor_kernel(rows, levels, coupling, other, low0, raw, winds, *rest):
-    *both, floor, missing = rest
-    halos, factors = both[: len(both) // 2], both[len(both) // 2 :]
+def floor_kernel(rows, levels, coupling, other, low0, winds, *rest):
+    *halos, floor, missing = rest
+    before, after = read_sides(halos)
+    half = halos[1].shape[0] - GROUP
     for f in range(2):
         here = pl.ds(f * rows, rows)
         _, peer = shares_of(coupling[...])
@@ -514,8 +509,24 @@
         right, left = shifted(y_up, y_down, 0.0, rows)
         spread = (row_after(x_up, 0.0, rows) + row_before(x_down, 0.0, rows)) + (right + left)
         spread = spread + (CENTRE + VERT_MIX) * share
-        floor[here, :] = outside_floor(halos, factors, raw, low0[here, :] + spread, f, rows, levels)
+        at = pl.ds(f * levels, 1)
+        sides = merged(halos[1], halos[2], pl.ds(f * half // 2, 1))
+        floor[here, :] = to_border(low0[here, :] + spread, before(at), after(at), sides, rows)
         missing[here, :] = VERT_MIX * share
+    raw = 2 * rows
+    floor[raw : raw + 2, :] = before(pl.ds(2 * levels, 2))
+    floor[raw + 2 : raw + 4, :] = after(pl.ds(2 * levels, 2))
+    floor[raw + 4 : raw + 6, :] = merged(halos[1], halos[2], pl.ds(half, 2))
+    floor[raw + 6 : raw + GROUP, :] = jnp.zeros((2, LANES), jnp.float32)
+
+
+def level0_kernel(rows, levels, floor, other, factors, partner, floor_out, other_out):
+    raw = 2 * rows
+    for mine, theirs, factor, at, out in ((floor, other, factors, 0, floor_out), (other, floor, partner, raw, other_out)):
+        for f in range(2):
+            here = pl.ds(f * rows, rows)
+            parts = [factor[at + k : at + k + 1, :] * theirs[raw + 2 * k + f : raw + 2 * k + f + 1, :] for k in range(3)]
+            out[here, :] = to_border(mine[here, :], *parts, rows)
 
 
 def swap_pairs(value):
@@ -597,8 +608,8 @@
 
 
 def first_adjoint_kernel(rows, levels, coupling, field, winds, state, out, ends, columns, low0, state_rows, cells, sems):
-    state_in = Rows(state, state_rows, sems, rows, True, 0)
-    start_rows(rows, state_in)
+    state_in = pltpu.make_async_copy(state, state_rows, sems.at[0])
+    state_in.start()
     columns[...] = jnp.zeros_like(columns)
 
     def take(i):
@@ -619,8 +630,7 @@
     adjoint_rows(rows, levels, cells, winds, take, each)
     ends[0] = out[0]
     ends[1] = out[rows - 1]
-    for i in range(rows):
-        state_in.wait(i)
+    state_in.wait()
 
 
 def second_adjoint_kernel(rows, levels, coupling, floor, other, missing, field, winds, scale, state, *rest):
@@ -738,12 +748,13 @@
 
 def innovate_kernel(rows, width, tiles, cap, records, cols, extra, bottom, *rest):
     coupling, wind_ends, wind_dense, dense_g, spread, sel, strips, packed = rest[:8]
-    col_cells, border_sel, precs, both, sems = rest[8:]
+    col_cells, precs, both, sems = rest[8:]
+    inside = rows * LANES
     chunks = 8
     copies = []
     for part in range(chunks):
         at = pl.ds(part * (2 * width // chunks), 2 * width // chunks)
-        copies.append(pltpu.make_async_copy(cols.at[at], col_cells.at[at], sems.at[part]))
+        copies.append(pltpu.make_async_copy(cols.at[at], col_cells.at[at, pl.ds(0, inside)], sems.at[part]))
         copies[-1].start()
     halves = width // LANES
     count = tiles * cap
@@ -774,7 +785,7 @@
             sel[at, i * LANES : (i + 1) * LANES] = jnp.where(column == float(i * LANES), 1.0, 0.0).astype(
                 jnp.bfloat16
             )
-        border_sel[at, :] = jnp.where(place == border, 1.0, 0.0).astype(jnp.bfloat16)
+        sel[at, inside:] = jnp.where(place == border, 1.0, 0.0).astype(jnp.bfloat16)
         return 0
 
     lax.fori_loop(0, count // step, select, 0)
@@ -790,9 +801,15 @@
                 old = col_cells[at, lanes].astype(jnp.float32)
                 new = jnp.where(first, value.astype(jnp.float32), old)
                 col_cells[at, lanes] = new.astype(jnp.bfloat16)
+    for k, i in enumerate((0, rows - 1)):
+        lanes = slice(i * LANES, (i + 1) * LANES)
+        old = col_cells[:width, lanes].astype(jnp.float32) + col_cells[width:, lanes].astype(jnp.float32)
+        more = extra[:, k * LANES : (k + 1) * LANES].astype(jnp.float32)
+        high, low = split(old + (more[:width] + more[width:]), 2)
+        col_cells[:width, lanes] = high
+        col_cells[width:, lanes] = low
+    col_cells[:, inside:] = extra[:, 2 * LANES :]
     both[...] = dot(sel[...], col_cells[...], (1, 1))
-    border_cells = jnp.concatenate([sel[:, 0:LANES], sel[:, (rows - 1) * LANES : rows * LANES], border_sel[...]], axis=1)
-    both[...] += dot(border_cells, extra[...], (1, 1))
 
     def weigh(block, _):
         at = pl.ds(pl.multiple_of(block * LANES, LANES), LANES)
@@ -817,6 +834,7 @@
 
     lax.fori_loop(0, count // LANES, weigh, 0, unroll=4)
 
+    border_cells = jnp.concatenate([sel[:, 0:LANES], sel[:, (rows - 1) * LANES :]], axis=1)
     terms = dot(spread[...], border_cells, (1, 0))
     border_sums = terms[:width] + terms[width:]
     thin = border_sums[:, 2 * LANES :]
@@ -835,19 +853,19 @@
     )
 
 
-def scatter_kernel(rows, width, spread, sel, winds, adjoint, low0, wind_rows, sems):
-    wind_in = Rows(winds, wind_rows, sems, rows, True, 1)
-    start_rows(rows, wind_in)
+def scatter_kernel(rows, width, spread, sel, winds, factors, adjoint, low0, wind_rows, sems):
+    low0[2 * rows :, :] = factors[...]
+    wind_in = pltpu.make_async_copy(winds, wind_rows.at[pl.ds(1, rows)], sems.at[0])
+    wind_in.start()
     wind_rows[0] = jnp.zeros_like(wind_rows[0])
     wind_rows[rows + 1] = jnp.zeros_like(wind_rows[0])
-    sums = dot(spread[...], sel[...], (1, 0))
+    sums = dot(spread[...], sel[:, : rows * LANES], (1, 0))
     for i in range(rows):
         lanes = slice(i * LANES, (i + 1) * LANES)
         adjoint[i] = sums[:width, lanes] + sums[width:, lanes]
         for f in range(2):
             low0[f * rows + i : f * rows + i + 1, :] = adjoint[i, f * (width // 2) : f * (width // 2) + 1, :]
-    for i in range(rows):
-        wind_in.wait(i)
+    wind_in.wait()
 
 
 def local(state_incr, winds, coupling, background, obs_dest, obs_col, obs_op, obs_prec):
@@ -911,12 +929,13 @@
     send, halos[0], halos[2], state_far, wind_far = lax.optimization_barrier((send, halos[0], halos[2], state, wind))
     records = lax.all_to_all(send, ("gx", "gy"), split_axis=0, concat_axis=0, tiled=True)
 
-    state_rows, wind_rows = run(
+    state_rows, wind_rows, state_later, wind_later = run(
         functools.partial(load_kernel, rows),
-        [field_shape, field_shape],
-        [sems(2, rows)],
+        [field_shape] * 4,
+        [sems(4, rows)],
         (state_far, wind_far),
         far=(0, 1),
+        out_far=(2, 3),
         traffic=10 * MIB,
     )
     halos[1], state_rows, wind_rows = lax.optimization_barrier((halos[1], state_rows, wind_rows))
@@ -941,21 +960,20 @@
     )
     cols, halos = lax.optimization_barrier((cols, halos))
     (floor,) = run(on_rows(forward_floor_kernel), [low_shape], [], (low0, low1, floor_winds, *halos))
-    extra, bottom = run(
+    extra, bottom, factors = run(
         on_rows(outside_kernel),
-        [jax.ShapeDtypeStruct((2 * width, 3 * LANES), jnp.bfloat16), low_shape],
+        [jax.ShapeDtypeStruct((2 * width, 3 * LANES), jnp.bfloat16), low_shape, thin_shape],
         [sides],
         (coupling, floor, swap_floor(floor), wind_ends, wind_dense, *halos),
     )
 
     spread_shape = ((2 * width, slots), jnp.bfloat16)
-    sel_shape = ((slots, rows * LANES), jnp.bfloat16)
+    sel_shape = ((slots, (rows + 1) * LANES), jnp.bfloat16)
     spread, sel, strips, packed = run(
         functools.partial(innovate_kernel, rows, width, tiles, cap),
         [jax.ShapeDtypeStruct(*spread_shape), jax.ShapeDtypeStruct(*sel_shape)] + long_shapes,
         [
-            pltpu.VMEM(*cols_shape),
-            pltpu.VMEM((slots, LANES), jnp.bfloat16),
+            pltpu.VMEM((2 * width, (rows + 1) * LANES), jnp.bfloat16),
             pltpu.VMEM((slots, LANES), jnp.float32),
             pltpu.VMEM((slots, 2 * width), jnp.float32),
             sems(8),
@@ -964,36 +982,38 @@
         far=(1,),
         limit=OBSERVE_VMEM,
     )
-    factors = halos
     halos = exchange(strips, packed)
     adjoint, low0, wind_rows = run(
         functools.partial(scatter_kernel, rows, width),
-        [field_shape, low_shape, framed_shape],
-        [sems(rows)],
-        (spread, sel, wind),
+        [field_shape, f32(fields * rows + GROUP, LANES), framed_shape],
+        [sems(1)],
+        (spread, sel, wind_later, factors),
         far=(2,),
         limit=OBSERVE_VMEM,
         traffic=8 * MIB,
     )
-    low0, halos = lax.optimization_barrier((low0, halos))
-    (raw,) = run(on_rows(beside_kernel), [thin_shape], [], halos)
-    partner, raw = swap_floor(low0), swap_floor(raw)
+    partner = swap_floor(low0)
     adjoint, ends, columns, low0, state_rows = run(
         on_rows(first_adjoint_kernel),
         [field_shape, f32(2, width, LANES), packed_shape, low_shape, field_shape],
-        [framed, sems(rows)],
-        (coupling, adjoint, wind_rows, state),
+        [framed, sems(1)],
+        (coupling, adjoint, wind_rows, state_later),
         far=(3,),
         traffic=16 * MIB,
     )
-    low0, partner, raw = lax.optimization_barrier((low0, partner, raw))
+    low0, partner, halos = lax.optimization_barrier((low0, partner, halos))
     floor, missing = run(
         on_rows(floor_kernel),
+        [f32(fields * rows + GROUP, LANES), low_shape],
+        [],
+        (coupling, partner, low0, floor_winds, *halos),
+    )
+    floor, other = run(
+        on_rows(level0_kernel),
         [low_shape, low_shape],
         [],
-        (coupling, partner, low0, raw, floor_winds, *halos, *factors),
-    )
-    other = swap_floor(floor)
+        (floor, swap_floor(floor), factors, partner),
+    )
     strips, packed = run(
         on_rows(border_again_kernel),
         strip_shapes,

time: 76.8 us -> 75 us (0.977)
  the two profiles are of different devices: /device:TPU:10 before, /device:TPU:8 now
where the time goes in v8:
time: 75 us; the launch traced here: 74.3 us
  Pallas kernels  37.1 us (49%)
  starting transfers between devices  30 us (40%)
  waiting for transfers between devices  6.11 us (8%)
  local copies, waits for them, and re-layouts  0.83 us (1%)
    pallas_call x15, Pallas kernels, run(): call(body, out_shape, scratch, in_specs=specs, out_specs=outs, **kw)(*args)  35.1 us
    ppermute x12, starting transfers between devices, pair_swap(): return lax.ppermute(block, axis, route)  23.9 us
    all_to_all x1, starting transfers between devices, local(): lax.all_to_all(send, ('gx', 'gy'), split_axis=0, concat_axis=0, tiled=True)  5.34 us
    ppermute x4, waiting for transfers between devices, swap_floor(): return lax.ppermute(floor, 'comp', [(0, 1), (1, 0)])  3.19 us
    pallas_call x1, Pallas kernels, local(): call(functools.partial(route_kernel, tiles, cap), f32(tiles, halves * cap...  2.04 us
    all_to_all x1, waiting for transfers between devices, local(): lax.all_to_all(send, ('gx', 'gy'), split_axis=0, concat_axis=0, tiled=True)  1.52 us
  transfers between devices with their start and end apart: 17, of which 5 were waited for; matrix products, arithmetic and copies ran while one was open for 1% of the time, Pallas kernels for 35%

profile of v8, /device:TPU:8, one launch (start us, length us, event | category | flops | bytes accessed | tf_op | source)
XLA Modules:
  0.0 74.3 jit_solution(16490193320834176909)
XLA Ops:
  0.0 2.3 %shard_map.83 = (f32[1,256,128]{2,1,0:T(8,128)S(1)}, f32[64,128]{1,0:T(8,128)S(1)}, f32[32,128]{1,0:T(8,128)S(1)}, f32[32,128]{1,0:T(8,128)S(1)}) custom-call(f32[4096,128]{1,0:T(8,128)} %bitcast.23), custom_call_target="tpu_custom_call" | custom-call | tf_op jit(solution)/shard_map/pallas_call | solution.py:903
  2.3 1.6 %collective-permute-start = (f32[256,128]{1,0:T(8,128)S(1)}, f32[256,128]{1,0:T(8,128)S(1)}, u32[]{:S(2)}, u32[]{:S(2)}) collective-permute-start(f32[256,128]{1,0:T(8,128)S(1)} %bitcast.22), channel_id=1, source_target_pairs={{0,8},{8,0},{1,9},{9,1},{2,10},{10,2},{3,11},{11,3},{4,12},{12,4},... | collective-permute-start | bytes 393224 | tf_op jit(solution)/shard_map/ppermute | solution.py:48
  3.9 3.3 %collective-permute-start.1 = (f32[64,128]{1,0:T(8,128)S(1)}, f32[64,128]{1,0:T(8,128)S(1)}, u32[]{:S(2)}, u32[]{:S(2)}) collective-permute-start(f32[64,128]{1,0:T(8,128)S(1)} %get-tuple-element.60), channel_id=1, source_target_pairs={{1,2},{2,1},{3,4},{4,3},{5,6},{6,5},{9,10},{10,9},{11,12},{12,11},... | collective-permute-start | bytes 98312 | tf_op jit(solution)/shard_map/ppermute | solution.py:48
  7.2 2.0 %shard_map.82 = f32[16,136,128]{2,1,0:T(8,128)} custom-call(s32[1,512]{1,0:T(1,128)S(1)} %bitcast.16, s32[1,512]{1,0:T(1,128)S(1)} %bitcast.17, f32[1,512]{1,0:T(1,128)S(1)} %bitcast.18, f32[512,256]{1,0:T(8,128)S(1)} %copy-done), custom_call_target="tpu_custom_call" | custom-call | tf_op jit(solution)/shard_map/pallas_call | solution.py:926
  9.3 1.3 %collective-permute-done.1.rest_2_ = f32[64,128]{1,0:T(8,128)S(1)} collective-permute-done((f32[64,128]{1,0:T(8,128)S(1)}, f32[64,128]{1,0:T(8,128)S(1)}, u32[]{:S(2)}, u32[]{:S(2)}) %collective-permute-start.1) | collective-permute-done | bytes 32800 | tf_op jit(solution)/shard_map/ppermute | solution.py:48
  10.6 5.3 %all-to-all-start = ((f32[16,136,128]{2,1,0:T(8,128)}), f32[16,136,128]{2,1,0:T(8,128)S(1)}, u32[]{:S(2)}, u32[]{:S(2)}) async-start(f32[16,136,128]{2,1,0:T(8,128)} %shard_map.82), calls=%async_computation | async-start | bytes 2228224 | tf_op jit(solution)/shard_map/all_to_all | solution.py:930
  15.9 1.5 %collective-permute-start.2 = (f32[64,128]{1,0:T(8,128)S(1)}, f32[64,128]{1,0:T(8,128)S(1)}, u32[]{:S(2)}, u32[]{:S(2)}) collective-permute-start(f32[64,128]{1,0:T(8,128)S(1)} %get-tuple-element.60), channel_id=1, source_target_pairs={{0,1},{1,0},{2,3},{3,2},{4,5},{5,4},{6,7},{7,6},{8,9},{9,8},{10,11... | collective-permute-start | bytes 98312 | tf_op jit(solution)/shard_map/ppermute | solution.py:48
  17.4 0.7 slice_bitcast_fusion.winds
  18.1 5.0 %shard_map.84 = (f32[16,256,128]{2,1,0:T(8,128)S(1)}, f32[16,256,128]{2,1,0:T(8,128)S(1)}, f32[16,256,128]{2,1,0:T(8,128)}, f32[16,256,128]{2,1,0:T(8,128)}) custom-call(f32[256,16,128]{2,1,0:T(8,128)} %bitcast.24, f32[256,16,128]{2,1,0:T(8,128)} %bitcast.25), custom_call_target="tpu_custom_call" | custom-call | bytes 10485760 | tf_op jit(solution)/shard_map/pallas_call | solution.py:903
  23.4 1.2 %collective-permute-done.3.other = f32[32,128]{1,0:T(8,128)S(1)} collective-permute-done((f32[32,128]{1,0:T(8,128)S(1)}, f32[32,128]{1,0:T(8,128)S(1)}, u32[]{:S(2)}, u32[]{:S(2)}) %collective-permute-start.3) | collective-permute-done | bytes 16416 | tf_op jit(solution)/shard_map/ppermute | solution.py:909
  24.5 4.9 %shard_map.86 = (f32[18,256,128]{2,1,0:T(8,128)S(1)}, f32[1,264,128]{2,1,0:T(8,128)S(1)}, f32[72,128]{1,0:T(8,128)S(1)}, f32[32,128]{1,0:T(8,128)S(1)}, f32[32,1...) custom-call(f32[16,128]{1,0:T(8,128)S(1)} %copy-done.1, ...), custom_call_target="tpu_custom_call" | custom-call | tf_op jit(solution)/shard_map/pallas_call | solution.py:903
  29.4 1.5 %collective-permute-start.4 = (f32[264,128]{1,0:T(8,128)S(1)}, f32[264,128]{1,0:T(8,128)S(1)}, u32[]{:S(2)}, u32[]{:S(2)}) collective-permute-start(f32[264,128]{1,0:T(8,128)S(1)} %bitcast.20), channel_id=1, source_target_pairs={{0,8},{8,0},{1,9},{9,1},{2,10},{10,2},{3,11},{11,3},{4,12},{12,4},... | collective-permute-start | bytes 405512 | tf_op jit(solution)/shard_map/ppermute | solution.py:48
  31.0 0.6 collective-permute-start.5
  31.5 3.4 %collective-permute-start.6 = (f32[72,128]{1,0:T(8,128)S(1)}, f32[72,128]{1,0:T(8,128)S(1)}, u32[]{:S(2)}, u32[]{:S(2)}) collective-permute-start(f32[72,128]{1,0:T(8,128)S(1)} %get-tuple-element.75), channel_id=1, source_target_pairs={{1,2},{2,1},{3,4},{4,3},{5,6},{6,5},{9,10},{10,9},{11,12},{12,11},... | collective-permute-start | bytes 110600 | tf_op jit(solution)/shard_map/ppermute | solution.py:48
  34.9 3.3 %shard_map.87.cols = bf16[512,2048]{1,0:T(8,128)(2,1)} custom-call(f32[18,256,128]{2,1,0:T(8,128)S(1)} %get-tuple-element.73.cells, f32[16,256,128]{2,1,0:T(8,128)S(1)} %get-tuple-element.72.winds), custom_call_target="tpu_custom_call" | custom-call | bytes 20971520 | tf_op jit(solution)/shard_map/pallas_call | solution.py:903
  38.5 1.2 %collective-permute-done.7.other = f32[32,128]{1,0:T(8,128)S(1)} collective-permute-done((f32[32,128]{1,0:T(8,128)S(1)}, f32[32,128]{1,0:T(8,128)S(1)}, u32[]{:S(2)}, u32[]{:S(2)}) %collective-permute-start.7) | collective-permute-done | bytes 16416 | tf_op jit(solution)/shard_map/ppermute | solution.py:909
  39.7 0.2 shard_map.89
  39.9 1.5 %all-to-all-done.records = f32[16,136,128]{2,1,0:T(8,128)S(1)} async-done(((f32[16,136,128]{2,1,0:T(8,128)}), f32[16,136,128]{2,1,0:T(8,128)S(1)}, u32[]{:S(2)}, u32[]{:S(2)}) %all-to-all-start) | async-done | bytes 1114144 | tf_op jit(solution)/shard_map/all_to_all | solution.py:930
  41.4 6.1 %shard_map.90 = (bf16[512,1024]{1,0:T(8,128)(2,1)S(1)}, bf16[1024,2176]{1,0:T(8,128)(2,1)S(1)}, f32[1,264,128]{2,1,0:T(8,128)S(1)}, f32[72,128]{1,0:T(8,128)S(1)}) custom-call(f32[16,136,128]{2,1,0:T(8,128)S(1)} %all-to-all-done.records, bf16[512,2048]{1,0:T(8,128)(2,1)} %shard_map.87.cols, bf16[512,384]{1,0:T(8,128)(2,1)S(1)} %get-tuple-element.84.extra, ...), custom_call_target="tpu_custom_call" | custom-call | tf_op jit(solution)/shard_map/pallas_call | solution.py:903
  47.6 1.5 %collective-permute-start.9 = (f32[264,128]{1,0:T(8,128)S(1)}, f32[264,128]{1,0:T(8,128)S(1)}, u32[]{:S(2)}, u32[]{:S(2)}) collective-permute-start(f32[264,128]{1,0:T(8,128)S(1)} %bitcast.19), channel_id=1, source_target_pairs={{0,8},{8,0},{1,9},{9,1},{2,10},{10,2},{3,11},{11,3},{4,12},{12,4},... | collective-permute-start | bytes 405512 | tf_op jit(solution)/shard_map/ppermute | solution.py:48
  49.1 3.1 %collective-permute-start.10 = (f32[72,128]{1,0:T(8,128)S(1)}, f32[72,128]{1,0:T(8,128)S(1)}, u32[]{:S(2)}, u32[]{:S(2)}) collective-permute-start(f32[72,128]{1,0:T(8,128)S(1)} %get-tuple-element.97), channel_id=1, source_target_pairs={{0,1},{1,0},{2,3},{3,2},{4,5},{5,4},{6,7},{7,6},{8,9},{9,8},{10,11... | collective-permute-start | bytes 110600 | tf_op jit(solution)/shard_map/ppermute | solution.py:48
  52.2 1.9 %collective-permute-start.11 = (f32[72,128]{1,0:T(8,128)S(1)}, f32[72,128]{1,0:T(8,128)S(1)}, u32[]{:S(2)}, u32[]{:S(2)}) collective-permute-start(f32[72,128]{1,0:T(8,128)S(1)} %get-tuple-element.97), channel_id=1, source_target_pairs={{1,2},{2,1},{3,4},{4,3},{5,6},{6,5},{9,10},{10,9},{11,12},{12,11},... | collective-permute-start | bytes 110600 | tf_op jit(solution)/shard_map/ppermute | solution.py:48
  54.1 2.4 %shard_map.91 = (f32[16,256,128]{2,1,0:T(8,128)S(1)}, f32[40,128]{1,0:T(8,128)S(1)}, f32[18,256,128]{2,1,0:T(8,128)S(1)}) custom-call(bf16[512,1024]{1,0:T(8,128)(2,1)S(1)} %get-tuple-element.87.spread, bf16[1024,2176]{1,0:T(8,128)(2,1)S(1)} %get-tuple-element.88.sel, f32[16,256,128]{2,1,0:T(8,128)} %get-tuple-element.89.winds, ...), custom_call_target="tpu_custom_call" | custom-call | bytes 8388608 | tf_op jit(solution)/shard_map/pallas_call | solution.py:903
  56.6 3.7 %shard_map.92 = (f32[16,256,128]{2,1,0:T(8,128)S(1)}, f32[2,256,128]{2,1,0:T(8,128)S(1)}, f32[64,128]{1,0:T(8,128)S(1)}, f32[32,128]{1,0:T(8,128)S(1)}, f32[16,256,128]{2,1,0:T(8,128)S(1)}) custom-call(f32[16,128]{1,0:T(8,128)S(1)} %copy-done.1, f32[16,256,128]{2,1,0:T(8,128)S(1)} %get-tuple-element.91.field, f32[18,256,128]{2,1,0:T(8,128)S(1)} %get-tuple-element.92.winds, ...), custom_call_target="tpu_custom_call" | custom-call | bytes 16777216 | tf_op jit(solution)/shard_map/pallas_call | solution.py:903
  60.5 0.5 collective-permute-start.12
  61.0 0.8 %collective-permute-done.12.other = f32[40,128]{1,0:T(8,128)S(1)} collective-permute-done((f32[40,128]{1,0:T(8,128)S(1)}, f32[40,128]{1,0:T(8,128)S(1)}, u32[]{:S(2)}, u32[]{:S(2)}) %collective-permute-start.12) | collective-permute-done | bytes 20512 | tf_op jit(solution)/shard_map/ppermute | solution.py:909
  62.0 0.4 shard_map.96
  62.4 0.7 collective-permute-start.13
  63.2 0.9 %collective-permute-start.14 = (f32[64,128]{1,0:T(8,128)S(1)}, f32[64,128]{1,0:T(8,128)S(1)}, u32[]{:S(2)}, u32[]{:S(2)}) collective-permute-start(f32[64,128]{1,0:T(8,128)S(1)} %get-tuple-element.112), channel_id=1, source_target_pairs={{0,1},{1,0},{2,3},{3,2},{4,5},{5,4},{6,7},{7,6},{8,9},{9,8},{10,11... | collective-permute-start | bytes 98312 | tf_op jit(solution)/shard_map/ppermute | solution.py:48
  64.1 3.9 %collective-permute-start.15 = (f32[64,128]{1,0:T(8,128)S(1)}, f32[64,128]{1,0:T(8,128)S(1)}, u32[]{:S(2)}, u32[]{:S(2)}) collective-permute-start(f32[64,128]{1,0:T(8,128)S(1)} %get-tuple-element.112), channel_id=1, source_target_pairs={{1,2},{2,1},{3,4},{4,3},{5,6},{6,5},{9,10},{10,9},{11,12},{12,11},... | collective-permute-start | bytes 98312 | tf_op jit(solution)/shard_map/ppermute | solution.py:48
  68.1 4.2 %shard_map.95.field = f32[16,256,128]{2,1,0:T(8,128)S(1)} custom-call(f32[16,128]{1,0:T(8,128)S(1)} %copy-done.1, f32[32,128]{1,0:T(8,128)S(1)} %get-tuple-element.104.floor, f32[32,128]{1,0:T(8,128)S(1)} %get-tuple-element.105.other, f32[32,128]{1,0:T(8,128)S(1)} %get-tuple-element.106.missing, f32[16,256,128]{2,1,0:T(8,128)S(1)} %get-tuple-element.107.field, ...), custom_call_target="tpu_custom_call" | custom-call | bytes 20971520 | tf_op jit(solution)/shard_map/pallas_call | solution.py:903
  72.4 2.0 %shard_map.97 = f32[256,16,128]{2,1,0:T(8,128)} custom-call(f32[16,256,128]{2,1,0:T(8,128)S(1)} %shard_map.95.field, f32[256,128]{1,0:T(8,128)S(1)} %collective-permute-done.13.rest_0_, f32[64,128]{1,0:T(8,128)S(1)} %collective-permute-done.14.rest_1_, f32[64,128]{1,0:T(8,128)S(1)} %collective-permute-done.15.rest_2_), custom_call_target="tpu_custom_call" | custom-call | tf_op jit(solution)/shard_map/pallas_call | solution.py:903
  (32 shorter events, 1.0 us)
Async XLA Ops:
  0.0 7.2 %copy-start.2 = (s32[512,1]{0,1:T(1,128)S(1)}, s32[512,1]{0,1:T(1,128)}, u32[]{:S(2)}) copy-start(s32[512,1]{0,1:T(1,128)} %param.12) | copy-start | bytes 6148
  0.0 7.2 %copy-start.3 = (s32[512]{0:T(512)S(1)}, s32[512]{0:T(512)}, u32[]{:S(2)}) copy-start(s32[512]{0:T(512)} %param.13) | copy-start | bytes 6148
  0.0 7.2 %copy-start.4 = (f32[512]{0:T(512)S(1)}, f32[512]{0:T(512)}, u32[]{:S(2)}) copy-start(f32[512]{0:T(512)} %param.15) | copy-start | bytes 6148
  0.0 7.2 %copy-start = (f32[512,256]{1,0:T(8,128)S(1)}, f32[512,256]{1,0:T(8,128)}, u32[]{:S(2)}) copy-start(f32[512,256]{1,0:T(8,128)} %op.1) | copy-start | bytes 1572868
  2.3 8.3 %collective-permute-start = (f32[256,128]{1,0:T(8,128)S(1)}, f32[256,128]{1,0:T(8,128)S(1)}, u32[]{:S(2)}, u32[]{:S(2)}) collective-permute-start(f32[256,128]{1,0:T(8,128)S(1)} %bitcast.22), channel_id=1, source_target_pairs={{0,8},{8,0},{1,9},{9,1},{2,10},{10,2},{3,11},{11,3},{4,12},{12,4},... | collective-permute-start | bytes 393224 | tf_op jit(solution)/shard_map/ppermute | solution.py:48
  3.9 6.7 %collective-permute-start.1 = (f32[64,128]{1,0:T(8,128)S(1)}, f32[64,128]{1,0:T(8,128)S(1)}, u32[]{:S(2)}, u32[]{:S(2)}) collective-permute-start(f32[64,128]{1,0:T(8,128)S(1)} %get-tuple-element.60), channel_id=1, source_target_pairs={{1,2},{2,1},{3,4},{4,3},{5,6},{6,5},{9,10},{10,9},{11,12},{12,11},... | collective-permute-start | bytes 98312 | tf_op jit(solution)/shard_map/ppermute | solution.py:48
  10.6 30.8 %all-to-all-start = ((f32[16,136,128]{2,1,0:T(8,128)}), f32[16,136,128]{2,1,0:T(8,128)S(1)}, u32[]{:S(2)}, u32[]{:S(2)}) async-start(f32[16,136,128]{2,1,0:T(8,128)} %shard_map.82), calls=%async_computation | async-start | bytes 2228224 | tf_op jit(solution)/shard_map/all_to_all | solution.py:930
  15.9 7.2 %collective-permute-start.2 = (f32[64,128]{1,0:T(8,128)S(1)}, f32[64,128]{1,0:T(8,128)S(1)}, u32[]{:S(2)}, u32[]{:S(2)}) collective-permute-start(f32[64,128]{1,0:T(8,128)S(1)} %get-tuple-element.60), channel_id=1, source_target_pairs={{0,1},{1,0},{2,3},{3,2},{4,5},{5,4},{6,7},{7,6},{8,9},{9,8},{10,11... | collective-permute-start | bytes 98312 | tf_op jit(solution)/shard_map/ppermute | solution.py:48
  18.1 6.4 %copy-start.1 = (f32[16,128]{1,0:T(8,128)S(1)}, f32[16,128]{1,0:T(8,128)}, u32[]{:S(2)}) copy-start(f32[16,128]{1,0:T(8,128)} %coupling.11) | copy-start | bytes 24580
  23.3 1.2 %collective-permute-start.3 = (f32[32,128]{1,0:T(8,128)S(1)}, f32[32,128]{1,0:T(8,128)S(1)}, u32[]{:S(2)}, u32[]{:S(2)}) collective-permute-start(f32[32,128]{1,0:T(8,128)S(1)} %shard_map.85), channel_id=1, source_target_pairs={{0,16},{16,0},{1,17},{17,1},{2,18},{18,2},{3,19},{19,3},{4,20},{20... | collective-permute-start | bytes 49160 | tf_op jit(solution)/shard_map/ppermute | solution.py:909
  29.4 8.8 %collective-permute-start.4 = (f32[264,128]{1,0:T(8,128)S(1)}, f32[264,128]{1,0:T(8,128)S(1)}, u32[]{:S(2)}, u32[]{:S(2)}) collective-permute-start(f32[264,128]{1,0:T(8,128)S(1)} %bitcast.20), channel_id=1, source_target_pairs={{0,8},{8,0},{1,9},{9,1},{2,10},{10,2},{3,11},{11,3},{4,12},{12,4},... | collective-permute-start | bytes 405512 | tf_op jit(solution)/shard_map/ppermute | solution.py:48
  31.0 7.3 %collective-permute-start.5 = (f32[72,128]{1,0:T(8,128)S(1)}, f32[72,128]{1,0:T(8,128)S(1)}, u32[]{:S(2)}, u32[]{:S(2)}) collective-permute-start(f32[72,128]{1,0:T(8,128)S(1)} %get-tuple-element.75), channel_id=1, source_target_pairs={{0,1},{1,0},{2,3},{3,2},{4,5},{5,4},{6,7},{7,6},{8,9},{9,8},{10,11... | collective-permute-start | bytes 110600 | tf_op jit(solution)/shard_map/ppermute | solution.py:48
  31.5 6.7 %collective-permute-start.6 = (f32[72,128]{1,0:T(8,128)S(1)}, f32[72,128]{1,0:T(8,128)S(1)}, u32[]{:S(2)}, u32[]{:S(2)}) collective-permute-start(f32[72,128]{1,0:T(8,128)S(1)} %get-tuple-element.75), channel_id=1, source_target_pairs={{1,2},{2,1},{3,4},{4,3},{5,6},{6,5},{9,10},{10,9},{11,12},{12,11},... | collective-permute-start | bytes 110600 | tf_op jit(solution)/shard_map/ppermute | solution.py:48
  38.4 1.2 %collective-permute-start.7 = (f32[32,128]{1,0:T(8,128)S(1)}, f32[32,128]{1,0:T(8,128)S(1)}, u32[]{:S(2)}, u32[]{:S(2)}) collective-permute-start(f32[32,128]{1,0:T(8,128)S(1)} %shard_map.88.floor), channel_id=1, source_target_pairs={{0,16},{16,0},{1,17},{17,1},{2,18},{18,2},{3,19},{19,3},{4,20},{20... | collective-permute-start | bytes 49160 | tf_op jit(solution)/shard_map/ppermute | solution.py:909
  47.6 12.7 %collective-permute-start.9 = (f32[264,128]{1,0:T(8,128)S(1)}, f32[264,128]{1,0:T(8,128)S(1)}, u32[]{:S(2)}, u32[]{:S(2)}) collective-permute-start(f32[264,128]{1,0:T(8,128)S(1)} %bitcast.19), channel_id=1, source_target_pairs={{0,8},{8,0},{1,9},{9,1},{2,10},{10,2},{3,11},{11,3},{4,12},{12,4},... | collective-permute-start | bytes 405512 | tf_op jit(solution)/shard_map/ppermute | solution.py:48
  49.1 11.2 %collective-permute-start.10 = (f32[72,128]{1,0:T(8,128)S(1)}, f32[72,128]{1,0:T(8,128)S(1)}, u32[]{:S(2)}, u32[]{:S(2)}) collective-permute-start(f32[72,128]{1,0:T(8,128)S(1)} %get-tuple-element.97), channel_id=1, source_target_pairs={{0,1},{1,0},{2,3},{3,2},{4,5},{5,4},{6,7},{7,6},{8,9},{9,8},{10,11... | collective-permute-start | bytes 110600 | tf_op jit(solution)/shard_map/ppermute | solution.py:48
  52.2 8.1 %collective-permute-start.11 = (f32[72,128]{1,0:T(8,128)S(1)}, f32[72,128]{1,0:T(8,128)S(1)}, u32[]{:S(2)}, u32[]{:S(2)}) collective-permute-start(f32[72,128]{1,0:T(8,128)S(1)} %get-tuple-element.97), channel_id=1, source_target_pairs={{1,2},{2,1},{3,4},{4,3},{5,6},{6,5},{9,10},{10,9},{11,12},{12,11},... | collective-permute-start | bytes 110600 | tf_op jit(solution)/shard_map/ppermute | solution.py:48
  56.5 3.8 %collective-permute-start.8 = (f32[40,128]{1,0:T(8,128)S(1)}, f32[40,128]{1,0:T(8,128)S(1)}, u32[]{:S(2)}, u32[]{:S(2)}) collective-permute-start(f32[40,128]{1,0:T(8,128)S(1)} %get-tuple-element.95), channel_id=1, source_target_pairs={{0,16},{16,0},{1,17},{17,1},{2,18},{18,2},{3,19},{19,3},{4,20},{20... | collective-permute-start | bytes 61448 | tf_op jit(solution)/shard_map/ppermute | solution.py:909
  56.6 11.4 %copy-start.5 = (f32[1,2,128]{2,1,0:T(2,128)S(1)}, f32[1,2,128]{2,1,0:T(2,128)}, u32[]{:S(2)}) copy-start(f32[1,2,128]{2,1,0:T(2,128)} %param.11) | copy-start | bytes 3076
  60.5 1.4 %collective-permute-start.12 = (f32[40,128]{1,0:T(8,128)S(1)}, f32[40,128]{1,0:T(8,128)S(1)}, u32[]{:S(2)}, u32[]{:S(2)}) collective-permute-start(f32[40,128]{1,0:T(8,128)S(1)} %get-tuple-element.103.floor), channel_id=1, source_target_pairs={{0,16},{16,0},{1,17},{17,1},{2,18},{18,2},{3,19},{19,3},{4,20},{20... | collective-permute-start | bytes 61448 | tf_op jit(solution)/shard_map/ppermute | solution.py:909
  62.4 9.9 %collective-permute-start.13 = (f32[256,128]{1,0:T(8,128)S(1)}, f32[256,128]{1,0:T(8,128)S(1)}, u32[]{:S(2)}, u32[]{:S(2)}) collective-permute-start(f32[256,128]{1,0:T(8,128)S(1)} %bitcast.21), channel_id=1, source_target_pairs={{0,8},{8,0},{1,9},{9,1},{2,10},{10,2},{3,11},{11,3},{4,12},{12,4},... | collective-permute-start | bytes 393224 | tf_op jit(solution)/shard_map/ppermute | solution.py:48
  63.2 9.1 %collective-permute-start.14 = (f32[64,128]{1,0:T(8,128)S(1)}, f32[64,128]{1,0:T(8,128)S(1)}, u32[]{:S(2)}, u32[]{:S(2)}) collective-permute-start(f32[64,128]{1,0:T(8,128)S(1)} %get-tuple-element.112), channel_id=1, source_target_pairs={{0,1},{1,0},{2,3},{3,2},{4,5},{5,4},{6,7},{7,6},{8,9},{9,8},{10,11... | collective-permute-start | bytes 98312 | tf_op jit(solution)/shard_map/ppermute | solution.py:48
  64.1 8.2 %collective-permute-start.15 = (f32[64,128]{1,0:T(8,128)S(1)}, f32[64,128]{1,0:T(8,128)S(1)}, u32[]{:S(2)}, u32[]{:S(2)}) collective-permute-start(f32[64,128]{1,0:T(8,128)S(1)} %get-tuple-element.112), channel_id=1, source_target_pairs={{1,2},{2,1},{3,4},{4,3},{5,6},{6,5},{9,10},{10,9},{11,12},{12,11},... | collective-permute-start | bytes 98312 | tf_op jit(solution)/shard_map/ppermute | solution.py:48

commit v9 on v8

--- a/solution.py
+++ b/solution.py
@@ -586,25 +586,27 @@
     dense_products(packed, dense, wind_dense)
 
 
-def adjoint_rows(rows, levels, cells, winds, take, each):
+def adjoint_rows(rows, levels, cells, winds, take, each, behind=None):
     groups = levels // GROUP
     cells[0] = jnp.zeros_like(cells[0])
     cells[rows + 1] = jnp.zeros_like(cells[0])
     take(0)
+    take(1)
 
     def row(i, _):
-        @pl.when(i < rows - 1)
-        def _():
-            take(i + 1)
-
+        if behind is not None:
+            behind(jnp.maximum(i - 1, 0))
         for m in range(2 * groups // PARTS):
             f, start = m * PARTS // groups, m * PARTS % groups
             each(i, m, f, start, [
                 adjoint_point(cells, winds, i, f, group, levels) for group in range(start, start + PARTS)
             ])
+        take(jnp.minimum(i + 2, rows - 2))
         return 0
 
     lax.fori_loop(0, rows, row, 0)
+    if behind is not None:
+        behind(rows - 1)
 
 
 def first_adjoint_kernel(rows, levels, coupling, field, winds, state, out, ends, columns, low0, state_rows, cells, sems):
@@ -625,9 +627,15 @@
             out[i, pl.ds((m * PARTS + part) * GROUP, GROUP), :] = value
         if start == 0:
             low0[pl.ds(f * rows + i, 1), :] = values[0][0:1]
-        pack_block(columns, values, i, m)
-
-    adjoint_rows(rows, levels, cells, winds, take, each)
+
+    def pack(i):
+        for m in range(columns.shape[0] // GROUP):
+            values = [out[i, pl.ds((m * PARTS + part) * GROUP, GROUP), :] for part in range(PARTS)]
+            pack_block(columns, values, i, m)
+
+    out[0] = jnp.zeros_like(out[0])
+    take(rows - 1)
+    adjoint_rows(rows, levels, cells, winds, take, each, pack)
     ends[0] = out[0]
     ends[1] = out[rows - 1]
     state_in.wait()
@@ -639,40 +647,29 @@
     before, after = read_sides(halos)
     groups = levels // GROUP
 
-    def take(i):
+    def take(i, outer=None):
         for group in range(2 * groups):
             at = pl.ds(group * GROUP, GROUP)
             value = field[i, at, :] + edge_lanes(sides, i, group)
+            if outer is not None:
+                value = value + outer(at)
             if group % groups == 0:
-                value = value + jnp.where(i == 0, before(at), 0.0) + jnp.where(i == rows - 1, after(at), 0.0)
                 here = pl.ds(group // groups * rows + i, 1)
                 value = value + jnp.where(sub_iota() == 1, missing[here, :], 0.0)
                 bottom = couple_adjoint(floor[here, :], other[here, :], coupling[pl.ds(i, 1), :])
                 value = jnp.where(sub_iota() == 0, bottom, value)
             cells[i + 1, at, :] = value
 
-    def add_outer(i, side):
-        for f in range(2):
-            at = pl.ds(f * levels + GROUP, levels - GROUP)
-            cells[i + 1, at, :] = cells[i + 1, at, :] + side(at)
-
-    def take_all(i):
-        take(i)
-
-        @pl.when(i == 0)
-        def _():
-            add_outer(0, before)
-
-        @pl.when(i == rows - 1)
-        def _():
-            add_outer(rows - 1, after)
+    def take_inner(i):
+        take(i, before if isinstance(i, int) and i == 0 else None)
 
     def each(i, m, f, start, values):
         for part, value in enumerate(values):
             at = pl.ds((m * PARTS + part) * GROUP, GROUP)
             out[i, at, :] = value + scale[at, :] * state[i, at, :]
 
-    adjoint_rows(rows, levels, cells, winds, take_all, each)
+    take(rows - 1, after)
+    adjoint_rows(rows, levels, cells, winds, take_inner, each)
 
 
 def final_kernel(rows, levels, field, *rest):
@@ -690,7 +687,7 @@
         leaving.start(i)
         return 0
 
-    lax.fori_loop(1, rows - 1, lambda i, _: add(i, None), 0, unroll=2)
+    lax.fori_loop(1, rows - 1, lambda i, _: add(i, None), 0, unroll=7)
     add(0, before)
     add(rows - 1, after)
     leaving.finish()

time: 75 us -> 73.6 us (0.981)
  Pallas kernels: 37.1 us -> 35.7 us
    pallas_call x15, Pallas kernels: 35.1 us -> 33.7 us  [run(): call(body, out_shape, scratch, in_specs=specs, out_specs=outs, **kw)(*args)]
  transfers between devices with their start and end apart: 17 -> 17, of which waited for: 5 -> 5; matrix products, arithmetic and copies ran while one was open for 1% -> 1% of each run, Pallas kernels for 35% -> 34%
where the time goes in v9:
time: 73.6 us; the launch traced here: 72.9 us
  Pallas kernels  35.7 us (49%)
  starting transfers between devices  30 us (41%)
  waiting for transfers between devices  6.11 us (8%)
  local copies, waits for them, and re-layouts  0.83 us (1%)
    pallas_call x15, Pallas kernels, run(): call(body, out_shape, scratch, in_specs=specs, out_specs=outs, **kw)(*args)  33.7 us
    ppermute x12, starting transfers between devices, pair_swap(): return lax.ppermute(block, axis, route)  23.9 us
    all_to_all x1, starting transfers between devices, local(): lax.all_to_all(send, ('gx', 'gy'), split_axis=0, concat_axis=0, tiled=True)  5.34 us
    ppermute x4, waiting for transfers between devices, swap_floor(): return lax.ppermute(floor, 'comp', [(0, 1), (1, 0)])  3.19 us
    pallas_call x1, Pallas kernels, local(): call(functools.partial(route_kernel, tiles, cap), f32(tiles, halves * cap...  2.04 us
    all_to_all x1, waiting for transfers between devices, local(): lax.all_to_all(send, ('gx', 'gy'), split_axis=0, concat_axis=0, tiled=True)  1.52 us
  transfers between devices with their start and end apart: 17, of which 5 were waited for; matrix products, arithmetic and copies ran while one was open for 1% of the time, Pallas kernels for 34%

profile of v9, /device:TPU:8, one launch (start us, length us, event | category | flops | bytes accessed | tf_op | source)
XLA Modules:
  0.0 72.9 jit_solution(11887586219196051551)
XLA Ops:
  0.0 2.3 %shard_map.83 = (f32[1,256,128]{2,1,0:T(8,128)S(1)}, f32[64,128]{1,0:T(8,128)S(1)}, f32[32,128]{1,0:T(8,128)S(1)}, f32[32,128]{1,0:T(8,128)S(1)}) custom-call(f32[4096,128]{1,0:T(8,128)} %bitcast.23), custom_call_target="tpu_custom_call" | custom-call | tf_op jit(solution)/shard_map/pallas_call | solution.py:900
  2.3 1.6 %collective-permute-start = (f32[256,128]{1,0:T(8,128)S(1)}, f32[256,128]{1,0:T(8,128)S(1)}, u32[]{:S(2)}, u32[]{:S(2)}) collective-permute-start(f32[256,128]{1,0:T(8,128)S(1)} %bitcast.22), channel_id=1, source_target_pairs={{0,8},{8,0},{1,9},{9,1},{2,10},{10,2},{3,11},{11,3},{4,12},{12,4},... | collective-permute-start | bytes 393224 | tf_op jit(solution)/shard_map/ppermute | solution.py:48
  3.9 3.3 %collective-permute-start.1 = (f32[64,128]{1,0:T(8,128)S(1)}, f32[64,128]{1,0:T(8,128)S(1)}, u32[]{:S(2)}, u32[]{:S(2)}) collective-permute-start(f32[64,128]{1,0:T(8,128)S(1)} %get-tuple-element.60), channel_id=1, source_target_pairs={{1,2},{2,1},{3,4},{4,3},{5,6},{6,5},{9,10},{10,9},{11,12},{12,11},... | collective-permute-start | bytes 98312 | tf_op jit(solution)/shard_map/ppermute | solution.py:48
  7.2 2.0 %shard_map.82 = f32[16,136,128]{2,1,0:T(8,128)} custom-call(s32[1,512]{1,0:T(1,128)S(1)} %bitcast.16, s32[1,512]{1,0:T(1,128)S(1)} %bitcast.17, f32[1,512]{1,0:T(1,128)S(1)} %bitcast.18, f32[512,256]{1,0:T(8,128)S(1)} %copy-done), custom_call_target="tpu_custom_call" | custom-call | tf_op jit(solution)/shard_map/pallas_call | solution.py:923
  9.3 1.3 %collective-permute-done.1.rest_2_ = f32[64,128]{1,0:T(8,128)S(1)} collective-permute-done((f32[64,128]{1,0:T(8,128)S(1)}, f32[64,128]{1,0:T(8,128)S(1)}, u32[]{:S(2)}, u32[]{:S(2)}) %collective-permute-start.1) | collective-permute-done | bytes 32800 | tf_op jit(solution)/shard_map/ppermute | solution.py:48
  10.6 5.3 %all-to-all-start = ((f32[16,136,128]{2,1,0:T(8,128)}), f32[16,136,128]{2,1,0:T(8,128)S(1)}, u32[]{:S(2)}, u32[]{:S(2)}) async-start(f32[16,136,128]{2,1,0:T(8,128)} %shard_map.82), calls=%async_computation | async-start | bytes 2228224 | tf_op jit(solution)/shard_map/all_to_all | solution.py:927
  15.9 1.5 %collective-permute-start.2 = (f32[64,128]{1,0:T(8,128)S(1)}, f32[64,128]{1,0:T(8,128)S(1)}, u32[]{:S(2)}, u32[]{:S(2)}) collective-permute-start(f32[64,128]{1,0:T(8,128)S(1)} %get-tuple-element.60), channel_id=1, source_target_pairs={{0,1},{1,0},{2,3},{3,2},{4,5},{5,4},{6,7},{7,6},{8,9},{9,8},{10,11... | collective-permute-start | bytes 98312 | tf_op jit(solution)/shard_map/ppermute | solution.py:48
  17.4 0.7 slice_bitcast_fusion.winds
  18.1 5.0 %shard_map.84 = (f32[16,256,128]{2,1,0:T(8,128)S(1)}, f32[16,256,128]{2,1,0:T(8,128)S(1)}, f32[16,256,128]{2,1,0:T(8,128)}, f32[16,256,128]{2,1,0:T(8,128)}) custom-call(f32[256,16,128]{2,1,0:T(8,128)} %bitcast.24, f32[256,16,128]{2,1,0:T(8,128)} %bitcast.25), custom_call_target="tpu_custom_call" | custom-call | bytes 10485760 | tf_op jit(solution)/shard_map/pallas_call | solution.py:900
  23.4 1.2 %collective-permute-done.3.other = f32[32,128]{1,0:T(8,128)S(1)} collective-permute-done((f32[32,128]{1,0:T(8,128)S(1)}, f32[32,128]{1,0:T(8,128)S(1)}, u32[]{:S(2)}, u32[]{:S(2)}) %collective-permute-start.3) | collective-permute-done | bytes 16416 | tf_op jit(solution)/shard_map/ppermute | solution.py:906
  24.5 4.9 %shard_map.86 = (f32[18,256,128]{2,1,0:T(8,128)S(1)}, f32[1,264,128]{2,1,0:T(8,128)S(1)}, f32[72,128]{1,0:T(8,128)S(1)}, f32[32,128]{1,0:T(8,128)S(1)}, f32[32,1...) custom-call(f32[16,128]{1,0:T(8,128)S(1)} %copy-done.1, ...), custom_call_target="tpu_custom_call" | custom-call | tf_op jit(solution)/shard_map/pallas_call | solution.py:900
  29.4 1.5 %collective-permute-start.4 = (f32[264,128]{1,0:T(8,128)S(1)}, f32[264,128]{1,0:T(8,128)S(1)}, u32[]{:S(2)}, u32[]{:S(2)}) collective-permute-start(f32[264,128]{1,0:T(8,128)S(1)} %bitcast.20), channel_id=1, source_target_pairs={{0,8},{8,0},{1,9},{9,1},{2,10},{10,2},{3,11},{11,3},{4,12},{12,4},... | collective-permute-start | bytes 405512 | tf_op jit(solution)/shard_map/ppermute | solution.py:48
  31.0 0.6 collective-permute-start.5
  31.5 3.4 %collective-permute-start.6 = (f32[72,128]{1,0:T(8,128)S(1)}, f32[72,128]{1,0:T(8,128)S(1)}, u32[]{:S(2)}, u32[]{:S(2)}) collective-permute-start(f32[72,128]{1,0:T(8,128)S(1)} %get-tuple-element.75), channel_id=1, source_target_pairs={{1,2},{2,1},{3,4},{4,3},{5,6},{6,5},{9,10},{10,9},{11,12},{12,11},... | collective-permute-start | bytes 110600 | tf_op jit(solution)/shard_map/ppermute | solution.py:48
  34.9 3.3 %shard_map.87.cols = bf16[512,2048]{1,0:T(8,128)(2,1)} custom-call(f32[18,256,128]{2,1,0:T(8,128)S(1)} %get-tuple-element.73.cells, f32[16,256,128]{2,1,0:T(8,128)S(1)} %get-tuple-element.72.winds), custom_call_target="tpu_custom_call" | custom-call | bytes 20971520 | tf_op jit(solution)/shard_map/pallas_call | solution.py:900
  38.5 1.2 %collective-permute-done.7.other = f32[32,128]{1,0:T(8,128)S(1)} collective-permute-done((f32[32,128]{1,0:T(8,128)S(1)}, f32[32,128]{1,0:T(8,128)S(1)}, u32[]{:S(2)}, u32[]{:S(2)}) %collective-permute-start.7) | collective-permute-done | bytes 16416 | tf_op jit(solution)/shard_map/ppermute | solution.py:906
  39.7 0.2 shard_map.89
  39.9 1.5 %all-to-all-done.records = f32[16,136,128]{2,1,0:T(8,128)S(1)} async-done(((f32[16,136,128]{2,1,0:T(8,128)}), f32[16,136,128]{2,1,0:T(8,128)S(1)}, u32[]{:S(2)}, u32[]{:S(2)}) %all-to-all-start) | async-done | bytes 1114144 | tf_op jit(solution)/shard_map/all_to_all | solution.py:927
  41.4 6.1 %shard_map.90 = (bf16[512,1024]{1,0:T(8,128)(2,1)S(1)}, bf16[1024,2176]{1,0:T(8,128)(2,1)S(1)}, f32[1,264,128]{2,1,0:T(8,128)S(1)}, f32[72,128]{1,0:T(8,128)S(1)}) custom-call(f32[16,136,128]{2,1,0:T(8,128)S(1)} %all-to-all-done.records, bf16[512,2048]{1,0:T(8,128)(2,1)} %shard_map.87.cols, bf16[512,384]{1,0:T(8,128)(2,1)S(1)} %get-tuple-element.84.extra, ...), custom_call_target="tpu_custom_call" | custom-call | tf_op jit(solution)/shard_map/pallas_call | solution.py:900
  47.6 1.5 %collective-permute-start.9 = (f32[264,128]{1,0:T(8,128)S(1)}, f32[264,128]{1,0:T(8,128)S(1)}, u32[]{:S(2)}, u32[]{:S(2)}) collective-permute-start(f32[264,128]{1,0:T(8,128)S(1)} %bitcast.19), channel_id=1, source_target_pairs={{0,8},{8,0},{1,9},{9,1},{2,10},{10,2},{3,11},{11,3},{4,12},{12,4},... | collective-permute-start | bytes 405512 | tf_op jit(solution)/shard_map/ppermute | solution.py:48
  49.1 3.1 %collective-permute-start.10 = (f32[72,128]{1,0:T(8,128)S(1)}, f32[72,128]{1,0:T(8,128)S(1)}, u32[]{:S(2)}, u32[]{:S(2)}) collective-permute-start(f32[72,128]{1,0:T(8,128)S(1)} %get-tuple-element.97), channel_id=1, source_target_pairs={{0,1},{1,0},{2,3},{3,2},{4,5},{5,4},{6,7},{7,6},{8,9},{9,8},{10,11... | collective-permute-start | bytes 110600 | tf_op jit(solution)/shard_map/ppermute | solution.py:48
  52.2 1.9 %collective-permute-start.11 = (f32[72,128]{1,0:T(8,128)S(1)}, f32[72,128]{1,0:T(8,128)S(1)}, u32[]{:S(2)}, u32[]{:S(2)}) collective-permute-start(f32[72,128]{1,0:T(8,128)S(1)} %get-tuple-element.97), channel_id=1, source_target_pairs={{1,2},{2,1},{3,4},{4,3},{5,6},{6,5},{9,10},{10,9},{11,12},{12,11},... | collective-permute-start | bytes 110600 | tf_op jit(solution)/shard_map/ppermute | solution.py:48
  54.1 2.4 %shard_map.91 = (f32[16,256,128]{2,1,0:T(8,128)S(1)}, f32[40,128]{1,0:T(8,128)S(1)}, f32[18,256,128]{2,1,0:T(8,128)S(1)}) custom-call(bf16[512,1024]{1,0:T(8,128)(2,1)S(1)} %get-tuple-element.87.spread, bf16[1024,2176]{1,0:T(8,128)(2,1)S(1)} %get-tuple-element.88.sel, f32[16,256,128]{2,1,0:T(8,128)} %get-tuple-element.89.winds, ...), custom_call_target="tpu_custom_call" | custom-call | bytes 8388608 | tf_op jit(solution)/shard_map/pallas_call | solution.py:900
  56.6 3.6 %shard_map.92 = (f32[16,256,128]{2,1,0:T(8,128)S(1)}, f32[2,256,128]{2,1,0:T(8,128)S(1)}, f32[64,128]{1,0:T(8,128)S(1)}, f32[32,128]{1,0:T(8,128)S(1)}, f32[16,256,128]{2,1,0:T(8,128)S(1)}) custom-call(f32[16,128]{1,0:T(8,128)S(1)} %copy-done.1, f32[16,256,128]{2,1,0:T(8,128)S(1)} %get-tuple-element.91.field, f32[18,256,128]{2,1,0:T(8,128)S(1)} %get-tuple-element.92.winds, ...), custom_call_target="tpu_custom_call" | custom-call | bytes 16777216 | tf_op jit(solution)/shard_map/pallas_call | solution.py:900
  60.4 0.5 collective-permute-start.12
  61.0 0.8 %collective-permute-done.12.other = f32[40,128]{1,0:T(8,128)S(1)} collective-permute-done((f32[40,128]{1,0:T(8,128)S(1)}, f32[40,128]{1,0:T(8,128)S(1)}, u32[]{:S(2)}, u32[]{:S(2)}) %collective-permute-start.12) | collective-permute-done | bytes 20512 | tf_op jit(solution)/shard_map/ppermute | solution.py:906
  62.0 0.4 shard_map.96
  62.4 0.7 %collective-permute-start.13 = (f32[256,128]{1,0:T(8,128)S(1)}, f32[256,128]{1,0:T(8,128)S(1)}, u32[]{:S(2)}, u32[]{:S(2)}) collective-permute-start(f32[256,128]{1,0:T(8,128)S(1)} %bitcast.21), channel_id=1, source_target_pairs={{0,8},{8,0},{1,9},{9,1},{2,10},{10,2},{3,11},{11,3},{4,12},{12,4},... | collective-permute-start | bytes 393224 | tf_op jit(solution)/shard_map/ppermute | solution.py:48
  63.1 0.9 %collective-permute-start.14 = (f32[64,128]{1,0:T(8,128)S(1)}, f32[64,128]{1,0:T(8,128)S(1)}, u32[]{:S(2)}, u32[]{:S(2)}) collective-permute-start(f32[64,128]{1,0:T(8,128)S(1)} %get-tuple-element.112), channel_id=1, source_target_pairs={{0,1},{1,0},{2,3},{3,2},{4,5},{5,4},{6,7},{7,6},{8,9},{9,8},{10,11... | collective-permute-start | bytes 98312 | tf_op jit(solution)/shard_map/ppermute | solution.py:48
  64.0 3.9 %collective-permute-start.15 = (f32[64,128]{1,0:T(8,128)S(1)}, f32[64,128]{1,0:T(8,128)S(1)}, u32[]{:S(2)}, u32[]{:S(2)}) collective-permute-start(f32[64,128]{1,0:T(8,128)S(1)} %get-tuple-element.112), channel_id=1, source_target_pairs={{1,2},{2,1},{3,4},{4,3},{5,6},{6,5},{9,10},{10,9},{11,12},{12,11},... | collective-permute-start | bytes 98312 | tf_op jit(solution)/shard_map/ppermute | solution.py:48
  68.0 3.2 %shard_map.95.field = f32[16,256,128]{2,1,0:T(8,128)S(1)} custom-call(f32[16,128]{1,0:T(8,128)S(1)} %copy-done.1, f32[32,128]{1,0:T(8,128)S(1)} %get-tuple-element.104.floor, f32[32,128]{1,0:T(8,128)S(1)} %get-tuple-element.105.other, f32[32,128]{1,0:T(8,128)S(1)} %get-tuple-element.106.missing, f32[16,256,128]{2,1,0:T(8,128)S(1)} %get-tuple-element.107.field, ...), custom_call_target="tpu_custom_call" | custom-call | bytes 20971520 | tf_op jit(solution)/shard_map/pallas_call | solution.py:900
  71.3 1.7 %shard_map.97 = f32[256,16,128]{2,1,0:T(8,128)} custom-call(f32[16,256,128]{2,1,0:T(8,128)S(1)} %shard_map.95.field, f32[256,128]{1,0:T(8,128)S(1)} %collective-permute-done.13.rest_0_, f32[64,128]{1,0:T(8,128)S(1)} %collective-permute-done.14.rest_1_, f32[64,128]{1,0:T(8,128)S(1)} %collective-permute-done.15.rest_2_), custom_call_target="tpu_custom_call" | custom-call | tf_op jit(solution)/shard_map/pallas_call | solution.py:900
  (32 shorter events, 1.0 us)
Async XLA Ops:
  0.0 7.2 %copy-start.2 = (s32[512,1]{0,1:T(1,128)S(1)}, s32[512,1]{0,1:T(1,128)}, u32[]{:S(2)}) copy-start(s32[512,1]{0,1:T(1,128)} %param.12) | copy-start | bytes 6148
  0.0 7.2 %copy-start.3 = (s32[512]{0:T(512)S(1)}, s32[512]{0:T(512)}, u32[]{:S(2)}) copy-start(s32[512]{0:T(512)} %param.13) | copy-start | bytes 6148
  0.0 7.2 %copy-start.4 = (f32[512]{0:T(512)S(1)}, f32[512]{0:T(512)}, u32[]{:S(2)}) copy-start(f32[512]{0:T(512)} %param.15) | copy-start | bytes 6148
  0.0 7.2 %copy-start = (f32[512,256]{1,0:T(8,128)S(1)}, f32[512,256]{1,0:T(8,128)}, u32[]{:S(2)}) copy-start(f32[512,256]{1,0:T(8,128)} %op.1) | copy-start | bytes 1572868
  2.3 8.3 %collective-permute-start = (f32[256,128]{1,0:T(8,128)S(1)}, f32[256,128]{1,0:T(8,128)S(1)}, u32[]{:S(2)}, u32[]{:S(2)}) collective-permute-start(f32[256,128]{1,0:T(8,128)S(1)} %bitcast.22), channel_id=1, source_target_pairs={{0,8},{8,0},{1,9},{9,1},{2,10},{10,2},{3,11},{11,3},{4,12},{12,4},... | collective-permute-start | bytes 393224 | tf_op jit(solution)/shard_map/ppermute | solution.py:48
  3.9 6.7 %collective-permute-start.1 = (f32[64,128]{1,0:T(8,128)S(1)}, f32[64,128]{1,0:T(8,128)S(1)}, u32[]{:S(2)}, u32[]{:S(2)}) collective-permute-start(f32[64,128]{1,0:T(8,128)S(1)} %get-tuple-element.60), channel_id=1, source_target_pairs={{1,2},{2,1},{3,4},{4,3},{5,6},{6,5},{9,10},{10,9},{11,12},{12,11},... | collective-permute-start | bytes 98312 | tf_op jit(solution)/shard_map/ppermute | solution.py:48
  10.6 30.8 %all-to-all-start = ((f32[16,136,128]{2,1,0:T(8,128)}), f32[16,136,128]{2,1,0:T(8,128)S(1)}, u32[]{:S(2)}, u32[]{:S(2)}) async-start(f32[16,136,128]{2,1,0:T(8,128)} %shard_map.82), calls=%async_computation | async-start | bytes 2228224 | tf_op jit(solution)/shard_map/all_to_all | solution.py:927
  15.9 7.2 %collective-permute-start.2 = (f32[64,128]{1,0:T(8,128)S(1)}, f32[64,128]{1,0:T(8,128)S(1)}, u32[]{:S(2)}, u32[]{:S(2)}) collective-permute-start(f32[64,128]{1,0:T(8,128)S(1)} %get-tuple-element.60), channel_id=1, source_target_pairs={{0,1},{1,0},{2,3},{3,2},{4,5},{5,4},{6,7},{7,6},{8,9},{9,8},{10,11... | collective-permute-start | bytes 98312 | tf_op jit(solution)/shard_map/ppermute | solution.py:48
  18.1 6.4 %copy-start.1 = (f32[16,128]{1,0:T(8,128)S(1)}, f32[16,128]{1,0:T(8,128)}, u32[]{:S(2)}) copy-start(f32[16,128]{1,0:T(8,128)} %coupling.11) | copy-start | bytes 24580
  23.3 1.2 %collective-permute-start.3 = (f32[32,128]{1,0:T(8,128)S(1)}, f32[32,128]{1,0:T(8,128)S(1)}, u32[]{:S(2)}, u32[]{:S(2)}) collective-permute-start(f32[32,128]{1,0:T(8,128)S(1)} %shard_map.85), channel_id=1, source_target_pairs={{0,16},{16,0},{1,17},{17,1},{2,18},{18,2},{3,19},{19,3},{4,20},{20... | collective-permute-start | bytes 49160 | tf_op jit(solution)/shard_map/ppermute | solution.py:906
  29.4 8.8 %collective-permute-start.4 = (f32[264,128]{1,0:T(8,128)S(1)}, f32[264,128]{1,0:T(8,128)S(1)}, u32[]{:S(2)}, u32[]{:S(2)}) collective-permute-start(f32[264,128]{1,0:T(8,128)S(1)} %bitcast.20), channel_id=1, source_target_pairs={{0,8},{8,0},{1,9},{9,1},{2,10},{10,2},{3,11},{11,3},{4,12},{12,4},... | collective-permute-start | bytes 405512 | tf_op jit(solution)/shard_map/ppermute | solution.py:48
  31.0 7.3 %collective-permute-start.5 = (f32[72,128]{1,0:T(8,128)S(1)}, f32[72,128]{1,0:T(8,128)S(1)}, u32[]{:S(2)}, u32[]{:S(2)}) collective-permute-start(f32[72,128]{1,0:T(8,128)S(1)} %get-tuple-element.75), channel_id=1, source_target_pairs={{0,1},{1,0},{2,3},{3,2},{4,5},{5,4},{6,7},{7,6},{8,9},{9,8},{10,11... | collective-permute-start | bytes 110600 | tf_op jit(solution)/shard_map/ppermute | solution.py:48
  31.5 6.7 %collective-permute-start.6 = (f32[72,128]{1,0:T(8,128)S(1)}, f32[72,128]{1,0:T(8,128)S(1)}, u32[]{:S(2)}, u32[]{:S(2)}) collective-permute-start(f32[72,128]{1,0:T(8,128)S(1)} %get-tuple-element.75), channel_id=1, source_target_pairs={{1,2},{2,1},{3,4},{4,3},{5,6},{6,5},{9,10},{10,9},{11,12},{12,11},... | collective-permute-start | bytes 110600 | tf_op jit(solution)/shard_map/ppermute | solution.py:48
  38.4 1.2 %collective-permute-start.7 = (f32[32,128]{1,0:T(8,128)S(1)}, f32[32,128]{1,0:T(8,128)S(1)}, u32[]{:S(2)}, u32[]{:S(2)}) collective-permute-start(f32[32,128]{1,0:T(8,128)S(1)} %shard_map.88.floor), channel_id=1, source_target_pairs={{0,16},{16,0},{1,17},{17,1},{2,18},{18,2},{3,19},{19,3},{4,20},{20... | collective-permute-start | bytes 49160 | tf_op jit(solution)/shard_map/ppermute | solution.py:906
  47.6 12.7 %collective-permute-start.9 = (f32[264,128]{1,0:T(8,128)S(1)}, f32[264,128]{1,0:T(8,128)S(1)}, u32[]{:S(2)}, u32[]{:S(2)}) collective-permute-start(f32[264,128]{1,0:T(8,128)S(1)} %bitcast.19), channel_id=1, source_target_pairs={{0,8},{8,0},{1,9},{9,1},{2,10},{10,2},{3,11},{11,3},{4,12},{12,4},... | collective-permute-start | bytes 405512 | tf_op jit(solution)/shard_map/ppermute | solution.py:48
  49.1 11.1 %collective-permute-start.10 = (f32[72,128]{1,0:T(8,128)S(1)}, f32[72,128]{1,0:T(8,128)S(1)}, u32[]{:S(2)}, u32[]{:S(2)}) collective-permute-start(f32[72,128]{1,0:T(8,128)S(1)} %get-tuple-element.97), channel_id=1, source_target_pairs={{0,1},{1,0},{2,3},{3,2},{4,5},{5,4},{6,7},{7,6},{8,9},{9,8},{10,11... | collective-permute-start | bytes 110600 | tf_op jit(solution)/shard_map/ppermute | solution.py:48
  52.2 8.0 %collective-permute-start.11 = (f32[72,128]{1,0:T(8,128)S(1)}, f32[72,128]{1,0:T(8,128)S(1)}, u32[]{:S(2)}, u32[]{:S(2)}) collective-permute-start(f32[72,128]{1,0:T(8,128)S(1)} %get-tuple-element.97), channel_id=1, source_target_pairs={{1,2},{2,1},{3,4},{4,3},{5,6},{6,5},{9,10},{10,9},{11,12},{12,11},... | collective-permute-start | bytes 110600 | tf_op jit(solution)/shard_map/ppermute | solution.py:48
  56.5 3.7 %collective-permute-start.8 = (f32[40,128]{1,0:T(8,128)S(1)}, f32[40,128]{1,0:T(8,128)S(1)}, u32[]{:S(2)}, u32[]{:S(2)}) collective-permute-start(f32[40,128]{1,0:T(8,128)S(1)} %get-tuple-element.95), channel_id=1, source_target_pairs={{0,16},{16,0},{1,17},{17,1},{2,18},{18,2},{3,19},{19,3},{4,20},{20... | collective-permute-start | bytes 61448 | tf_op jit(solution)/shard_map/ppermute | solution.py:906
  56.6 11.3 %copy-start.5 = (f32[1,2,128]{2,1,0:T(2,128)S(1)}, f32[1,2,128]{2,1,0:T(2,128)}, u32[]{:S(2)}) copy-start(f32[1,2,128]{2,1,0:T(2,128)} %param.11) | copy-start | bytes 3076
  60.4 1.4 %collective-permute-start.12 = (f32[40,128]{1,0:T(8,128)S(1)}, f32[40,128]{1,0:T(8,128)S(1)}, u32[]{:S(2)}, u32[]{:S(2)}) collective-permute-start(f32[40,128]{1,0:T(8,128)S(1)} %get-tuple-element.103.floor), channel_id=1, source_target_pairs={{0,16},{16,0},{1,17},{17,1},{2,18},{18,2},{3,19},{19,3},{4,20},{20... | collective-permute-start | bytes 61448 | tf_op jit(solution)/shard_map/ppermute | solution.py:906
  62.4 8.9 %collective-permute-start.13 = (f32[256,128]{1,0:T(8,128)S(1)}, f32[256,128]{1,0:T(8,128)S(1)}, u32[]{:S(2)}, u32[]{:S(2)}) collective-permute-start(f32[256,128]{1,0:T(8,128)S(1)} %bitcast.21), channel_id=1, source_target_pairs={{0,8},{8,0},{1,9},{9,1},{2,10},{10,2},{3,11},{11,3},{4,12},{12,4},... | collective-permute-start | bytes 393224 | tf_op jit(solution)/shard_map/ppermute | solution.py:48
  63.1 8.1 %collective-permute-start.14 = (f32[64,128]{1,0:T(8,128)S(1)}, f32[64,128]{1,0:T(8,128)S(1)}, u32[]{:S(2)}, u32[]{:S(2)}) collective-permute-start(f32[64,128]{1,0:T(8,128)S(1)} %get-tuple-element.112), channel_id=1, source_target_pairs={{0,1},{1,0},{2,3},{3,2},{4,5},{5,4},{6,7},{7,6},{8,9},{9,8},{10,11... | collective-permute-start | bytes 98312 | tf_op jit(solution)/shard_map/ppermute | solution.py:48
  64.0 7.2 %collective-permute-start.15 = (f32[64,128]{1,0:T(8,128)S(1)}, f32[64,128]{1,0:T(8,128)S(1)}, u32[]{:S(2)}, u32[]{:S(2)}) collective-permute-start(f32[64,128]{1,0:T(8,128)S(1)} %get-tuple-element.112), channel_id=1, source_target_pairs={{1,2},{2,1},{3,4},{4,3},{5,6},{6,5},{9,10},{10,9},{11,12},{12,11},... | collective-permute-start | bytes 98312 | tf_op jit(solution)/shard_map/ppermute | solution.py:48

commit v10 on v9

--- a/solution.py
+++ b/solution.py
@@ -604,7 +604,7 @@
         take(jnp.minimum(i + 2, rows - 2))
         return 0
 
-    lax.fori_loop(0, rows, row, 0)
+    lax.fori_loop(0, rows, row, 0, unroll=1 if behind is None else 2)
     if behind is not None:
         behind(rows - 1)
 
@@ -758,7 +758,7 @@
     aux = halves * cap
     own = lax.broadcasted_iota(jnp.int32, (cap, LANES), 1) == lax.broadcasted_iota(jnp.int32, (cap, LANES), 0)
     ones = jnp.ones((LANES, LANES), jnp.bfloat16)
-    step = 256
+    step = 512
     lane = lax.broadcasted_iota(jnp.int32, (step, LANES), 1)
     border = (rows - 1 - lane // (2 * PARTS)) * LANES + jnp.where(lane % 2 == 1, 0, LANES - 1)
     border = jnp.where(lane % (2 * PARTS) < 2, border, -1).astype(jnp.float32)

time: 73.6 us -> 73.1 us (level)
  no operation moved by 1% of the time
where the time goes in v10:
time: 73.1 us; the launch traced here: 72.4 us
  Pallas kernels  35.2 us (48%)
  starting transfers between devices  30 us (41%)
  waiting for transfers between devices  6.11 us (8%)
  local copies, waits for them, and re-layouts  0.83 us (1%)
    pallas_call x15, Pallas kernels, run(): call(body, out_shape, scratch, in_specs=specs, out_specs=outs, **kw)(*args)  33.1 us
    ppermute x12, starting transfers between devices, pair_swap(): return lax.ppermute(block, axis, route)  23.9 us
    all_to_all x1, starting transfers between devices, local(): lax.all_to_all(send, ('gx', 'gy'), split_axis=0, concat_axis=0, tiled=True)  5.34 us
    ppermute x4, waiting for transfers between devices, swap_floor(): return lax.ppermute(floor, 'comp', [(0, 1), (1, 0)])  3.19 us
    pallas_call x1, Pallas kernels, local(): call(functools.partial(route_kernel, tiles, cap), f32(tiles, halves * cap...  2.04 us
    all_to_all x1, waiting for transfers between devices, local(): lax.all_to_all(send, ('gx', 'gy'), split_axis=0, concat_axis=0, tiled=True)  1.52 us
  transfers between devices with their start and end apart: 17, of which 5 were waited for; matrix products, arithmetic and copies ran while one was open for 1% of the time, Pallas kernels for 34%

profile of v10, /device:TPU:8, one launch (start us, length us, event | category | flops | bytes accessed | tf_op | source)
XLA Modules:
  0.0 72.4 jit_solution(7931824192242013771)
XLA Ops:
  0.0 2.3 %shard_map.83 = (f32[1,256,128]{2,1,0:T(8,128)S(1)}, f32[64,128]{1,0:T(8,128)S(1)}, f32[32,128]{1,0:T(8,128)S(1)}, f32[32,128]{1,0:T(8,128)S(1)}) custom-call(f32[4096,128]{1,0:T(8,128)} %bitcast.23), custom_call_target="tpu_custom_call" | custom-call | tf_op jit(solution)/shard_map/pallas_call | solution.py:900
  2.3 1.6 %collective-permute-start = (f32[256,128]{1,0:T(8,128)S(1)}, f32[256,128]{1,0:T(8,128)S(1)}, u32[]{:S(2)}, u32[]{:S(2)}) collective-permute-start(f32[256,128]{1,0:T(8,128)S(1)} %bitcast.22), channel_id=1, source_target_pairs={{0,8},{8,0},{1,9},{9,1},{2,10},{10,2},{3,11},{11,3},{4,12},{12,4},... | collective-permute-start | bytes 393224 | tf_op jit(solution)/shard_map/ppermute | solution.py:48
  3.9 3.3 %collective-permute-start.1 = (f32[64,128]{1,0:T(8,128)S(1)}, f32[64,128]{1,0:T(8,128)S(1)}, u32[]{:S(2)}, u32[]{:S(2)}) collective-permute-start(f32[64,128]{1,0:T(8,128)S(1)} %get-tuple-element.60), channel_id=1, source_target_pairs={{1,2},{2,1},{3,4},{4,3},{5,6},{6,5},{9,10},{10,9},{11,12},{12,11},... | collective-permute-start | bytes 98312 | tf_op jit(solution)/shard_map/ppermute | solution.py:48
  7.2 2.0 %shard_map.82 = f32[16,136,128]{2,1,0:T(8,128)} custom-call(s32[1,512]{1,0:T(1,128)S(1)} %bitcast.16, s32[1,512]{1,0:T(1,128)S(1)} %bitcast.17, f32[1,512]{1,0:T(1,128)S(1)} %bitcast.18, f32[512,256]{1,0:T(8,128)S(1)} %copy-done), custom_call_target="tpu_custom_call" | custom-call | tf_op jit(solution)/shard_map/pallas_call | solution.py:923
  9.3 1.3 %collective-permute-done.1.rest_2_ = f32[64,128]{1,0:T(8,128)S(1)} collective-permute-done((f32[64,128]{1,0:T(8,128)S(1)}, f32[64,128]{1,0:T(8,128)S(1)}, u32[]{:S(2)}, u32[]{:S(2)}) %collective-permute-start.1) | collective-permute-done | bytes 32800 | tf_op jit(solution)/shard_map/ppermute | solution.py:48
  10.6 5.3 %all-to-all-start = ((f32[16,136,128]{2,1,0:T(8,128)}), f32[16,136,128]{2,1,0:T(8,128)S(1)}, u32[]{:S(2)}, u32[]{:S(2)}) async-start(f32[16,136,128]{2,1,0:T(8,128)} %shard_map.82), calls=%async_computation | async-start | bytes 2228224 | tf_op jit(solution)/shard_map/all_to_all | solution.py:927
  15.9 1.5 %collective-permute-start.2 = (f32[64,128]{1,0:T(8,128)S(1)}, f32[64,128]{1,0:T(8,128)S(1)}, u32[]{:S(2)}, u32[]{:S(2)}) collective-permute-start(f32[64,128]{1,0:T(8,128)S(1)} %get-tuple-element.60), channel_id=1, source_target_pairs={{0,1},{1,0},{2,3},{3,2},{4,5},{5,4},{6,7},{7,6},{8,9},{9,8},{10,11... | collective-permute-start | bytes 98312 | tf_op jit(solution)/shard_map/ppermute | solution.py:48
  17.4 0.7 slice_bitcast_fusion.winds
  18.1 5.0 %shard_map.84 = (f32[16,256,128]{2,1,0:T(8,128)S(1)}, f32[16,256,128]{2,1,0:T(8,128)S(1)}, f32[16,256,128]{2,1,0:T(8,128)}, f32[16,256,128]{2,1,0:T(8,128)}) custom-call(f32[256,16,128]{2,1,0:T(8,128)} %bitcast.24, f32[256,16,128]{2,1,0:T(8,128)} %bitcast.25), custom_call_target="tpu_custom_call" | custom-call | bytes 10485760 | tf_op jit(solution)/shard_map/pallas_call | solution.py:900
  23.4 1.2 %collective-permute-done.3.other = f32[32,128]{1,0:T(8,128)S(1)} collective-permute-done((f32[32,128]{1,0:T(8,128)S(1)}, f32[32,128]{1,0:T(8,128)S(1)}, u32[]{:S(2)}, u32[]{:S(2)}) %collective-permute-start.3) | collective-permute-done | bytes 16416 | tf_op jit(solution)/shard_map/ppermute | solution.py:906
  24.5 4.9 %shard_map.86 = (f32[18,256,128]{2,1,0:T(8,128)S(1)}, f32[1,264,128]{2,1,0:T(8,128)S(1)}, f32[72,128]{1,0:T(8,128)S(1)}, f32[32,128]{1,0:T(8,128)S(1)}, f32[32,1...) custom-call(f32[16,128]{1,0:T(8,128)S(1)} %copy-done.1, ...), custom_call_target="tpu_custom_call" | custom-call | tf_op jit(solution)/shard_map/pallas_call | solution.py:900
  29.4 1.5 %collective-permute-start.4 = (f32[264,128]{1,0:T(8,128)S(1)}, f32[264,128]{1,0:T(8,128)S(1)}, u32[]{:S(2)}, u32[]{:S(2)}) collective-permute-start(f32[264,128]{1,0:T(8,128)S(1)} %bitcast.20), channel_id=1, source_target_pairs={{0,8},{8,0},{1,9},{9,1},{2,10},{10,2},{3,11},{11,3},{4,12},{12,4},... | collective-permute-start | bytes 405512 | tf_op jit(solution)/shard_map/ppermute | solution.py:48
  31.0 0.6 collective-permute-start.5
  31.5 3.4 %collective-permute-start.6 = (f32[72,128]{1,0:T(8,128)S(1)}, f32[72,128]{1,0:T(8,128)S(1)}, u32[]{:S(2)}, u32[]{:S(2)}) collective-permute-start(f32[72,128]{1,0:T(8,128)S(1)} %get-tuple-element.75), channel_id=1, source_target_pairs={{1,2},{2,1},{3,4},{4,3},{5,6},{6,5},{9,10},{10,9},{11,12},{12,11},... | collective-permute-start | bytes 110600 | tf_op jit(solution)/shard_map/ppermute | solution.py:48
  34.9 3.3 %shard_map.87.cols = bf16[512,2048]{1,0:T(8,128)(2,1)} custom-call(f32[18,256,128]{2,1,0:T(8,128)S(1)} %get-tuple-element.73.cells, f32[16,256,128]{2,1,0:T(8,128)S(1)} %get-tuple-element.72.winds), custom_call_target="tpu_custom_call" | custom-call | bytes 20971520 | tf_op jit(solution)/shard_map/pallas_call | solution.py:900
  38.5 1.2 %collective-permute-done.7.other = f32[32,128]{1,0:T(8,128)S(1)} collective-permute-done((f32[32,128]{1,0:T(8,128)S(1)}, f32[32,128]{1,0:T(8,128)S(1)}, u32[]{:S(2)}, u32[]{:S(2)}) %collective-permute-start.7) | collective-permute-done | bytes 16416 | tf_op jit(solution)/shard_map/ppermute | solution.py:906
  39.7 0.2 shard_map.89
  39.9 1.5 %all-to-all-done.records = f32[16,136,128]{2,1,0:T(8,128)S(1)} async-done(((f32[16,136,128]{2,1,0:T(8,128)}), f32[16,136,128]{2,1,0:T(8,128)S(1)}, u32[]{:S(2)}, u32[]{:S(2)}) %all-to-all-start) | async-done | bytes 1114144 | tf_op jit(solution)/shard_map/all_to_all | solution.py:927
  41.4 5.9 %shard_map.90 = (bf16[512,1024]{1,0:T(8,128)(2,1)S(1)}, bf16[1024,2176]{1,0:T(8,128)(2,1)S(1)}, f32[1,264,128]{2,1,0:T(8,128)S(1)}, f32[72,128]{1,0:T(8,128)S(1)}) custom-call(f32[16,136,128]{2,1,0:T(8,128)S(1)} %all-to-all-done.records, bf16[512,2048]{1,0:T(8,128)(2,1)} %shard_map.87.cols, bf16[512,384]{1,0:T(8,128)(2,1)S(1)} %get-tuple-element.84.extra, ...), custom_call_target="tpu_custom_call" | custom-call | tf_op jit(solution)/shard_map/pallas_call | solution.py:900
  47.3 1.5 %collective-permute-start.9 = (f32[264,128]{1,0:T(8,128)S(1)}, f32[264,128]{1,0:T(8,128)S(1)}, u32[]{:S(2)}, u32[]{:S(2)}) collective-permute-start(f32[264,128]{1,0:T(8,128)S(1)} %bitcast.19), channel_id=1, source_target_pairs={{0,8},{8,0},{1,9},{9,1},{2,10},{10,2},{3,11},{11,3},{4,12},{12,4},... | collective-permute-start | bytes 405512 | tf_op jit(solution)/shard_map/ppermute | solution.py:48
  48.8 3.1 %collective-permute-start.10 = (f32[72,128]{1,0:T(8,128)S(1)}, f32[72,128]{1,0:T(8,128)S(1)}, u32[]{:S(2)}, u32[]{:S(2)}) collective-permute-start(f32[72,128]{1,0:T(8,128)S(1)} %get-tuple-element.97), channel_id=1, source_target_pairs={{0,1},{1,0},{2,3},{3,2},{4,5},{5,4},{6,7},{7,6},{8,9},{9,8},{10,11... | collective-permute-start | bytes 110600 | tf_op jit(solution)/shard_map/ppermute | solution.py:48
  52.0 1.9 %collective-permute-start.11 = (f32[72,128]{1,0:T(8,128)S(1)}, f32[72,128]{1,0:T(8,128)S(1)}, u32[]{:S(2)}, u32[]{:S(2)}) collective-permute-start(f32[72,128]{1,0:T(8,128)S(1)} %get-tuple-element.97), channel_id=1, source_target_pairs={{1,2},{2,1},{3,4},{4,3},{5,6},{6,5},{9,10},{10,9},{11,12},{12,11},... | collective-permute-start | bytes 110600 | tf_op jit(solution)/shard_map/ppermute | solution.py:48
  53.9 2.4 %shard_map.91 = (f32[16,256,128]{2,1,0:T(8,128)S(1)}, f32[40,128]{1,0:T(8,128)S(1)}, f32[18,256,128]{2,1,0:T(8,128)S(1)}) custom-call(bf16[512,1024]{1,0:T(8,128)(2,1)S(1)} %get-tuple-element.87.spread, bf16[1024,2176]{1,0:T(8,128)(2,1)S(1)} %get-tuple-element.88.sel, f32[16,256,128]{2,1,0:T(8,128)} %get-tuple-element.89.winds, ...), custom_call_target="tpu_custom_call" | custom-call | bytes 8388608 | tf_op jit(solution)/shard_map/pallas_call | solution.py:900
  56.4 3.3 %shard_map.92 = (f32[16,256,128]{2,1,0:T(8,128)S(1)}, f32[2,256,128]{2,1,0:T(8,128)S(1)}, f32[64,128]{1,0:T(8,128)S(1)}, f32[32,128]{1,0:T(8,128)S(1)}, f32[16,256,128]{2,1,0:T(8,128)S(1)}) custom-call(f32[16,128]{1,0:T(8,128)S(1)} %copy-done.1, f32[16,256,128]{2,1,0:T(8,128)S(1)} %get-tuple-element.91.field, f32[18,256,128]{2,1,0:T(8,128)S(1)} %get-tuple-element.92.winds, ...), custom_call_target="tpu_custom_call" | custom-call | bytes 16777216 | tf_op jit(solution)/shard_map/pallas_call | solution.py:900
  59.9 0.5 collective-permute-start.12
  60.4 0.8 %collective-permute-done.12.other = f32[40,128]{1,0:T(8,128)S(1)} collective-permute-done((f32[40,128]{1,0:T(8,128)S(1)}, f32[40,128]{1,0:T(8,128)S(1)}, u32[]{:S(2)}, u32[]{:S(2)}) %collective-permute-start.12) | collective-permute-done | bytes 20512 | tf_op jit(solution)/shard_map/ppermute | solution.py:906
  61.4 0.4 shard_map.96
  61.9 0.7 %collective-permute-start.13 = (f32[256,128]{1,0:T(8,128)S(1)}, f32[256,128]{1,0:T(8,128)S(1)}, u32[]{:S(2)}, u32[]{:S(2)}) collective-permute-start(f32[256,128]{1,0:T(8,128)S(1)} %bitcast.21), channel_id=1, source_target_pairs={{0,8},{8,0},{1,9},{9,1},{2,10},{10,2},{3,11},{11,3},{4,12},{12,4},... | collective-permute-start | bytes 393224 | tf_op jit(solution)/shard_map/ppermute | solution.py:48
  62.6 0.9 %collective-permute-start.14 = (f32[64,128]{1,0:T(8,128)S(1)}, f32[64,128]{1,0:T(8,128)S(1)}, u32[]{:S(2)}, u32[]{:S(2)}) collective-permute-start(f32[64,128]{1,0:T(8,128)S(1)} %get-tuple-element.112), channel_id=1, source_target_pairs={{0,1},{1,0},{2,3},{3,2},{4,5},{5,4},{6,7},{7,6},{8,9},{9,8},{10,11... | collective-permute-start | bytes 98312 | tf_op jit(solution)/shard_map/ppermute | solution.py:48
  63.5 3.9 %collective-permute-start.15 = (f32[64,128]{1,0:T(8,128)S(1)}, f32[64,128]{1,0:T(8,128)S(1)}, u32[]{:S(2)}, u32[]{:S(2)}) collective-permute-start(f32[64,128]{1,0:T(8,128)S(1)} %get-tuple-element.112), channel_id=1, source_target_pairs={{1,2},{2,1},{3,4},{4,3},{5,6},{6,5},{9,10},{10,9},{11,12},{12,11},... | collective-permute-start | bytes 98312 | tf_op jit(solution)/shard_map/ppermute | solution.py:48
  67.5 3.2 %shard_map.95.field = f32[16,256,128]{2,1,0:T(8,128)S(1)} custom-call(f32[16,128]{1,0:T(8,128)S(1)} %copy-done.1, f32[32,128]{1,0:T(8,128)S(1)} %get-tuple-element.104.floor, f32[32,128]{1,0:T(8,128)S(1)} %get-tuple-element.105.other, f32[32,128]{1,0:T(8,128)S(1)} %get-tuple-element.106.missing, f32[16,256,128]{2,1,0:T(8,128)S(1)} %get-tuple-element.107.field, ...), custom_call_target="tpu_custom_call" | custom-call | bytes 20971520 | tf_op jit(solution)/shard_map/pallas_call | solution.py:900
  70.8 1.7 %shard_map.97 = f32[256,16,128]{2,1,0:T(8,128)} custom-call(f32[16,256,128]{2,1,0:T(8,128)S(1)} %shard_map.95.field, f32[256,128]{1,0:T(8,128)S(1)} %collective-permute-done.13.rest_0_, f32[64,128]{1,0:T(8,128)S(1)} %collective-permute-done.14.rest_1_, f32[64,128]{1,0:T(8,128)S(1)} %collective-permute-done.15.rest_2_), custom_call_target="tpu_custom_call" | custom-call | tf_op jit(solution)/shard_map/pallas_call | solution.py:900
  (32 shorter events, 1.0 us)
Async XLA Ops:
  0.0 7.2 %copy-start.2 = (s32[512,1]{0,1:T(1,128)S(1)}, s32[512,1]{0,1:T(1,128)}, u32[]{:S(2)}) copy-start(s32[512,1]{0,1:T(1,128)} %param.12) | copy-start | bytes 6148
  0.0 7.2 %copy-start.3 = (s32[512]{0:T(512)S(1)}, s32[512]{0:T(512)}, u32[]{:S(2)}) copy-start(s32[512]{0:T(512)} %param.13) | copy-start | bytes 6148
  0.0 7.2 %copy-start.4 = (f32[512]{0:T(512)S(1)}, f32[512]{0:T(512)}, u32[]{:S(2)}) copy-start(f32[512]{0:T(512)} %param.15) | copy-start | bytes 6148
  0.0 7.2 %copy-start = (f32[512,256]{1,0:T(8,128)S(1)}, f32[512,256]{1,0:T(8,128)}, u32[]{:S(2)}) copy-start(f32[512,256]{1,0:T(8,128)} %op.1) | copy-start | bytes 1572868
  2.3 8.3 %collective-permute-start = (f32[256,128]{1,0:T(8,128)S(1)}, f32[256,128]{1,0:T(8,128)S(1)}, u32[]{:S(2)}, u32[]{:S(2)}) collective-permute-start(f32[256,128]{1,0:T(8,128)S(1)} %bitcast.22), channel_id=1, source_target_pairs={{0,8},{8,0},{1,9},{9,1},{2,10},{10,2},{3,11},{11,3},{4,12},{12,4},... | collective-permute-start | bytes 393224 | tf_op jit(solution)/shard_map/ppermute | solution.py:48
  3.9 6.7 %collective-permute-start.1 = (f32[64,128]{1,0:T(8,128)S(1)}, f32[64,128]{1,0:T(8,128)S(1)}, u32[]{:S(2)}, u32[]{:S(2)}) collective-permute-start(f32[64,128]{1,0:T(8,128)S(1)} %get-tuple-element.60), channel_id=1, source_target_pairs={{1,2},{2,1},{3,4},{4,3},{5,6},{6,5},{9,10},{10,9},{11,12},{12,11},... | collective-permute-start | bytes 98312 | tf_op jit(solution)/shard_map/ppermute | solution.py:48
  10.6 30.8 %all-to-all-start = ((f32[16,136,128]{2,1,0:T(8,128)}), f32[16,136,128]{2,1,0:T(8,128)S(1)}, u32[]{:S(2)}, u32[]{:S(2)}) async-start(f32[16,136,128]{2,1,0:T(8,128)} %shard_map.82), calls=%async_computation | async-start | bytes 2228224 | tf_op jit(solution)/shard_map/all_to_all | solution.py:927
  15.9 7.2 %collective-permute-start.2 = (f32[64,128]{1,0:T(8,128)S(1)}, f32[64,128]{1,0:T(8,128)S(1)}, u32[]{:S(2)}, u32[]{:S(2)}) collective-permute-start(f32[64,128]{1,0:T(8,128)S(1)} %get-tuple-element.60), channel_id=1, source_target_pairs={{0,1},{1,0},{2,3},{3,2},{4,5},{5,4},{6,7},{7,6},{8,9},{9,8},{10,11... | collective-permute-start | bytes 98312 | tf_op jit(solution)/shard_map/ppermute | solution.py:48
  18.1 6.4 %copy-start.1 = (f32[16,128]{1,0:T(8,128)S(1)}, f32[16,128]{1,0:T(8,128)}, u32[]{:S(2)}) copy-start(f32[16,128]{1,0:T(8,128)} %coupling.11) | copy-start | bytes 24580
  23.3 1.2 %collective-permute-start.3 = (f32[32,128]{1,0:T(8,128)S(1)}, f32[32,128]{1,0:T(8,128)S(1)}, u32[]{:S(2)}, u32[]{:S(2)}) collective-permute-start(f32[32,128]{1,0:T(8,128)S(1)} %shard_map.85), channel_id=1, source_target_pairs={{0,16},{16,0},{1,17},{17,1},{2,18},{18,2},{3,19},{19,3},{4,20},{20... | collective-permute-start | bytes 49160 | tf_op jit(solution)/shard_map/ppermute | solution.py:906
  29.4 8.8 %collective-permute-start.4 = (f32[264,128]{1,0:T(8,128)S(1)}, f32[264,128]{1,0:T(8,128)S(1)}, u32[]{:S(2)}, u32[]{:S(2)}) collective-permute-start(f32[264,128]{1,0:T(8,128)S(1)} %bitcast.20), channel_id=1, source_target_pairs={{0,8},{8,0},{1,9},{9,1},{2,10},{10,2},{3,11},{11,3},{4,12},{12,4},... | collective-permute-start | bytes 405512 | tf_op jit(solution)/shard_map/ppermute | solution.py:48
  31.0 7.3 %collective-permute-start.5 = (f32[72,128]{1,0:T(8,128)S(1)}, f32[72,128]{1,0:T(8,128)S(1)}, u32[]{:S(2)}, u32[]{:S(2)}) collective-permute-start(f32[72,128]{1,0:T(8,128)S(1)} %get-tuple-element.75), channel_id=1, source_target_pairs={{0,1},{1,0},{2,3},{3,2},{4,5},{5,4},{6,7},{7,6},{8,9},{9,8},{10,11... | collective-permute-start | bytes 110600 | tf_op jit(solution)/shard_map/ppermute | solution.py:48
  31.5 6.7 %collective-permute-start.6 = (f32[72,128]{1,0:T(8,128)S(1)}, f32[72,128]{1,0:T(8,128)S(1)}, u32[]{:S(2)}, u32[]{:S(2)}) collective-permute-start(f32[72,128]{1,0:T(8,128)S(1)} %get-tuple-element.75), channel_id=1, source_target_pairs={{1,2},{2,1},{3,4},{4,3},{5,6},{6,5},{9,10},{10,9},{11,12},{12,11},... | collective-permute-start | bytes 110600 | tf_op jit(solution)/shard_map/ppermute | solution.py:48
  38.4 1.2 %collective-permute-start.7 = (f32[32,128]{1,0:T(8,128)S(1)}, f32[32,128]{1,0:T(8,128)S(1)}, u32[]{:S(2)}, u32[]{:S(2)}) collective-permute-start(f32[32,128]{1,0:T(8,128)S(1)} %shard_map.88.floor), channel_id=1, source_target_pairs={{0,16},{16,0},{1,17},{17,1},{2,18},{18,2},{3,19},{19,3},{4,20},{20... | collective-permute-start | bytes 49160 | tf_op jit(solution)/shard_map/ppermute | solution.py:906
  47.3 12.4 %collective-permute-start.9 = (f32[264,128]{1,0:T(8,128)S(1)}, f32[264,128]{1,0:T(8,128)S(1)}, u32[]{:S(2)}, u32[]{:S(2)}) collective-permute-start(f32[264,128]{1,0:T(8,128)S(1)} %bitcast.19), channel_id=1, source_target_pairs={{0,8},{8,0},{1,9},{9,1},{2,10},{10,2},{3,11},{11,3},{4,12},{12,4},... | collective-permute-start | bytes 405512 | tf_op jit(solution)/shard_map/ppermute | solution.py:48
  48.8 10.9 %collective-permute-start.10 = (f32[72,128]{1,0:T(8,128)S(1)}, f32[72,128]{1,0:T(8,128)S(1)}, u32[]{:S(2)}, u32[]{:S(2)}) collective-permute-start(f32[72,128]{1,0:T(8,128)S(1)} %get-tuple-element.97), channel_id=1, source_target_pairs={{0,1},{1,0},{2,3},{3,2},{4,5},{5,4},{6,7},{7,6},{8,9},{9,8},{10,11... | collective-permute-start | bytes 110600 | tf_op jit(solution)/shard_map/ppermute | solution.py:48
  52.0 7.7 %collective-permute-start.11 = (f32[72,128]{1,0:T(8,128)S(1)}, f32[72,128]{1,0:T(8,128)S(1)}, u32[]{:S(2)}, u32[]{:S(2)}) collective-permute-start(f32[72,128]{1,0:T(8,128)S(1)} %get-tuple-element.97), channel_id=1, source_target_pairs={{1,2},{2,1},{3,4},{4,3},{5,6},{6,5},{9,10},{10,9},{11,12},{12,11},... | collective-permute-start | bytes 110600 | tf_op jit(solution)/shard_map/ppermute | solution.py:48
  56.3 3.4 %collective-permute-start.8 = (f32[40,128]{1,0:T(8,128)S(1)}, f32[40,128]{1,0:T(8,128)S(1)}, u32[]{:S(2)}, u32[]{:S(2)}) collective-permute-start(f32[40,128]{1,0:T(8,128)S(1)} %get-tuple-element.95), channel_id=1, source_target_pairs={{0,16},{16,0},{1,17},{17,1},{2,18},{18,2},{3,19},{19,3},{4,20},{20... | collective-permute-start | bytes 61448 | tf_op jit(solution)/shard_map/ppermute | solution.py:906
  56.3 11.1 %copy-start.5 = (f32[1,2,128]{2,1,0:T(2,128)S(1)}, f32[1,2,128]{2,1,0:T(2,128)}, u32[]{:S(2)}) copy-start(f32[1,2,128]{2,1,0:T(2,128)} %param.11) | copy-start | bytes 3076
  59.9 1.4 %collective-permute-start.12 = (f32[40,128]{1,0:T(8,128)S(1)}, f32[40,128]{1,0:T(8,128)S(1)}, u32[]{:S(2)}, u32[]{:S(2)}) collective-permute-start(f32[40,128]{1,0:T(8,128)S(1)} %get-tuple-element.103.floor), channel_id=1, source_target_pairs={{0,16},{16,0},{1,17},{17,1},{2,18},{18,2},{3,19},{19,3},{4,20},{20... | collective-permute-start | bytes 61448 | tf_op jit(solution)/shard_map/ppermute | solution.py:906
  61.9 8.9 %collective-permute-start.13 = (f32[256,128]{1,0:T(8,128)S(1)}, f32[256,128]{1,0:T(8,128)S(1)}, u32[]{:S(2)}, u32[]{:S(2)}) collective-permute-start(f32[256,128]{1,0:T(8,128)S(1)} %bitcast.21), channel_id=1, source_target_pairs={{0,8},{8,0},{1,9},{9,1},{2,10},{10,2},{3,11},{11,3},{4,12},{12,4},... | collective-permute-start | bytes 393224 | tf_op jit(solution)/shard_map/ppermute | solution.py:48
  62.6 8.1 %collective-permute-start.14 = (f32[64,128]{1,0:T(8,128)S(1)}, f32[64,128]{1,0:T(8,128)S(1)}, u32[]{:S(2)}, u32[]{:S(2)}) collective-permute-start(f32[64,128]{1,0:T(8,128)S(1)} %get-tuple-element.112), channel_id=1, source_target_pairs={{0,1},{1,0},{2,3},{3,2},{4,5},{5,4},{6,7},{7,6},{8,9},{9,8},{10,11... | collective-permute-start | bytes 98312 | tf_op jit(solution)/shard_map/ppermute | solution.py:48
  63.5 7.2 %collective-permute-start.15 = (f32[64,128]{1,0:T(8,128)S(1)}, f32[64,128]{1,0:T(8,128)S(1)}, u32[]{:S(2)}, u32[]{:S(2)}) collective-permute-start(f32[64,128]{1,0:T(8,128)S(1)} %get-tuple-element.112), channel_id=1, source_target_pairs={{1,2},{2,1},{3,4},{4,3},{5,6},{6,5},{9,10},{10,9},{11,12},{12,11},... | collective-permute-start | bytes 98312 | tf_op jit(solution)/shard_map/ppermute | solution.py:48

commit v11 on v10

--- a/solution.py
+++ b/solution.py
@@ -333,16 +333,13 @@
     before, after = read_sides(halos)
     cells[0] = before(pl.ds(0, 2 * levels))
     cells[1] = field[0]
+    cells[2] = field[1]
     cells[rows + 1] = after(pl.ds(0, 2 * levels))
     out[0] = jnp.zeros_like(out[0])
     out[rows + 1] = jnp.zeros_like(out[0])
     groups = levels // GROUP
 
     def row(i, _):
-        @pl.when(i < rows - 1)
-        def _():
-            cells[i + 2] = field[i + 1]
-
         for m in range(2 * groups // PARTS):
             f, start = m * PARTS // groups, m * PARTS % groups
             values = []
@@ -359,6 +356,8 @@
             if f == 0:
                 w = [winds[i, pl.ds(levels + base + part * GROUP, GROUP), :] for part in range(PARTS)]
                 pack_block(wind_dense, w, i, m)
+        ahead = jnp.minimum(i + 2, rows - 1)
+        cells[ahead + 1] = field[ahead]
         return 0
 
     lax.fori_loop(0, rows, row, 0)

time: 73.1 us -> 73.1 us (level)
  no operation moved by 1% of the time
where the time goes in v11:
time: 73.1 us; the launch traced here: 72.4 us
  Pallas kernels  35.3 us (48%)
  starting transfers between devices  30 us (41%)
  waiting for transfers between devices  5.97 us (8%)
  local copies, waits for them, and re-layouts  0.83 us (1%)
    pallas_call x15, Pallas kernels, run(): call(body, out_shape, scratch, in_specs=specs, out_specs=outs, **kw)(*args)  33.3 us
    ppermute x12, starting transfers between devices, pair_swap(): return lax.ppermute(block, axis, route)  23.9 us
    all_to_all x1, starting transfers between devices, local(): lax.all_to_all(send, ('gx', 'gy'), split_axis=0, concat_axis=0, tiled=True)  5.34 us
    ppermute x4, waiting for transfers between devices, swap_floor(): return lax.ppermute(floor, 'comp', [(0, 1), (1, 0)])  3.19 us
    pallas_call x1, Pallas kernels, local(): call(functools.partial(route_kernel, tiles, cap), f32(tiles, halves * cap...  2.04 us
  transfers between devices with their start and end apart: 17, of which 5 were waited for; matrix products, arithmetic and copies ran while one was open for 1% of the time, Pallas kernels for 34%

profile of v11, /device:TPU:8, one launch (start us, length us, event | category | flops | bytes accessed | tf_op | source)
XLA Modules:
  0.0 72.4 jit_solution(2899268554108833324)
XLA Ops:
  0.0 2.3 %shard_map.83 = (f32[1,256,128]{2,1,0:T(8,128)S(1)}, f32[64,128]{1,0:T(8,128)S(1)}, f32[32,128]{1,0:T(8,128)S(1)}, f32[32,128]{1,0:T(8,128)S(1)}) custom-call(f32[4096,128]{1,0:T(8,128)} %bitcast.23), custom_call_target="tpu_custom_call" | custom-call | tf_op jit(solution)/shard_map/pallas_call | solution.py:899
  2.3 1.6 %collective-permute-start = (f32[256,128]{1,0:T(8,128)S(1)}, f32[256,128]{1,0:T(8,128)S(1)}, u32[]{:S(2)}, u32[]{:S(2)}) collective-permute-start(f32[256,128]{1,0:T(8,128)S(1)} %bitcast.22), channel_id=1, source_target_pairs={{0,8},{8,0},{1,9},{9,1},{2,10},{10,2},{3,11},{11,3},{4,12},{12,4},... | collective-permute-start | bytes 393224 | tf_op jit(solution)/shard_map/ppermute | solution.py:48
  3.9 3.3 %collective-permute-start.1 = (f32[64,128]{1,0:T(8,128)S(1)}, f32[64,128]{1,0:T(8,128)S(1)}, u32[]{:S(2)}, u32[]{:S(2)}) collective-permute-start(f32[64,128]{1,0:T(8,128)S(1)} %get-tuple-element.60), channel_id=1, source_target_pairs={{1,2},{2,1},{3,4},{4,3},{5,6},{6,5},{9,10},{10,9},{11,12},{12,11},... | collective-permute-start | bytes 98312 | tf_op jit(solution)/shard_map/ppermute | solution.py:48
  7.2 2.0 %shard_map.82 = f32[16,136,128]{2,1,0:T(8,128)} custom-call(s32[1,512]{1,0:T(1,128)S(1)} %bitcast.16, s32[1,512]{1,0:T(1,128)S(1)} %bitcast.17, f32[1,512]{1,0:T(1,128)S(1)} %bitcast.18, f32[512,256]{1,0:T(8,128)S(1)} %copy-done), custom_call_target="tpu_custom_call" | custom-call | tf_op jit(solution)/shard_map/pallas_call | solution.py:922
  9.3 1.3 %collective-permute-done.1.rest_2_ = f32[64,128]{1,0:T(8,128)S(1)} collective-permute-done((f32[64,128]{1,0:T(8,128)S(1)}, f32[64,128]{1,0:T(8,128)S(1)}, u32[]{:S(2)}, u32[]{:S(2)}) %collective-permute-start.1) | collective-permute-done | bytes 32800 | tf_op jit(solution)/shard_map/ppermute | solution.py:48
  10.6 5.3 %all-to-all-start = ((f32[16,136,128]{2,1,0:T(8,128)}), f32[16,136,128]{2,1,0:T(8,128)S(1)}, u32[]{:S(2)}, u32[]{:S(2)}) async-start(f32[16,136,128]{2,1,0:T(8,128)} %shard_map.82), calls=%async_computation | async-start | bytes 2228224 | tf_op jit(solution)/shard_map/all_to_all | solution.py:926
  15.9 1.5 %collective-permute-start.2 = (f32[64,128]{1,0:T(8,128)S(1)}, f32[64,128]{1,0:T(8,128)S(1)}, u32[]{:S(2)}, u32[]{:S(2)}) collective-permute-start(f32[64,128]{1,0:T(8,128)S(1)} %get-tuple-element.60), channel_id=1, source_target_pairs={{0,1},{1,0},{2,3},{3,2},{4,5},{5,4},{6,7},{7,6},{8,9},{9,8},{10,11... | collective-permute-start | bytes 98312 | tf_op jit(solution)/shard_map/ppermute | solution.py:48
  17.4 0.7 slice_bitcast_fusion.winds
  18.1 5.0 %shard_map.84 = (f32[16,256,128]{2,1,0:T(8,128)S(1)}, f32[16,256,128]{2,1,0:T(8,128)S(1)}, f32[16,256,128]{2,1,0:T(8,128)}, f32[16,256,128]{2,1,0:T(8,128)}) custom-call(f32[256,16,128]{2,1,0:T(8,128)} %bitcast.24, f32[256,16,128]{2,1,0:T(8,128)} %bitcast.25), custom_call_target="tpu_custom_call" | custom-call | bytes 10485760 | tf_op jit(solution)/shard_map/pallas_call | solution.py:899
  23.4 1.2 %collective-permute-done.3.other = f32[32,128]{1,0:T(8,128)S(1)} collective-permute-done((f32[32,128]{1,0:T(8,128)S(1)}, f32[32,128]{1,0:T(8,128)S(1)}, u32[]{:S(2)}, u32[]{:S(2)}) %collective-permute-start.3) | collective-permute-done | bytes 16416 | tf_op jit(solution)/shard_map/ppermute | solution.py:905
  24.5 5.0 %shard_map.86 = (f32[18,256,128]{2,1,0:T(8,128)S(1)}, f32[1,264,128]{2,1,0:T(8,128)S(1)}, f32[72,128]{1,0:T(8,128)S(1)}, f32[32,128]{1,0:T(8,128)S(1)}, f32[32,1...) custom-call(f32[16,128]{1,0:T(8,128)S(1)} %copy-done.1, ...), custom_call_target="tpu_custom_call" | custom-call | tf_op jit(solution)/shard_map/pallas_call | solution.py:899
  29.6 1.5 %collective-permute-start.4 = (f32[264,128]{1,0:T(8,128)S(1)}, f32[264,128]{1,0:T(8,128)S(1)}, u32[]{:S(2)}, u32[]{:S(2)}) collective-permute-start(f32[264,128]{1,0:T(8,128)S(1)} %bitcast.20), channel_id=1, source_target_pairs={{0,8},{8,0},{1,9},{9,1},{2,10},{10,2},{3,11},{11,3},{4,12},{12,4},... | collective-permute-start | bytes 405512 | tf_op jit(solution)/shard_map/ppermute | solution.py:48
  31.1 0.6 collective-permute-start.5
  31.7 3.4 %collective-permute-start.6 = (f32[72,128]{1,0:T(8,128)S(1)}, f32[72,128]{1,0:T(8,128)S(1)}, u32[]{:S(2)}, u32[]{:S(2)}) collective-permute-start(f32[72,128]{1,0:T(8,128)S(1)} %get-tuple-element.75), channel_id=1, source_target_pairs={{1,2},{2,1},{3,4},{4,3},{5,6},{6,5},{9,10},{10,9},{11,12},{12,11},... | collective-permute-start | bytes 110600 | tf_op jit(solution)/shard_map/ppermute | solution.py:48
  35.0 3.3 %shard_map.87.cols = bf16[512,2048]{1,0:T(8,128)(2,1)} custom-call(f32[18,256,128]{2,1,0:T(8,128)S(1)} %get-tuple-element.73.cells, f32[16,256,128]{2,1,0:T(8,128)S(1)} %get-tuple-element.72.winds), custom_call_target="tpu_custom_call" | custom-call | bytes 20971520 | tf_op jit(solution)/shard_map/pallas_call | solution.py:899
  38.7 1.2 %collective-permute-done.7.other = f32[32,128]{1,0:T(8,128)S(1)} collective-permute-done((f32[32,128]{1,0:T(8,128)S(1)}, f32[32,128]{1,0:T(8,128)S(1)}, u32[]{:S(2)}, u32[]{:S(2)}) %collective-permute-start.7) | collective-permute-done | bytes 16416 | tf_op jit(solution)/shard_map/ppermute | solution.py:905
  39.8 0.2 shard_map.89
  40.0 1.4 %all-to-all-done.records = f32[16,136,128]{2,1,0:T(8,128)S(1)} async-done(((f32[16,136,128]{2,1,0:T(8,128)}), f32[16,136,128]{2,1,0:T(8,128)S(1)}, u32[]{:S(2)}, u32[]{:S(2)}) %all-to-all-start) | async-done | bytes 1114144 | tf_op jit(solution)/shard_map/all_to_all | solution.py:926
  41.4 5.9 %shard_map.90 = (bf16[512,1024]{1,0:T(8,128)(2,1)S(1)}, bf16[1024,2176]{1,0:T(8,128)(2,1)S(1)}, f32[1,264,128]{2,1,0:T(8,128)S(1)}, f32[72,128]{1,0:T(8,128)S(1)}) custom-call(f32[16,136,128]{2,1,0:T(8,128)S(1)} %all-to-all-done.records, bf16[512,2048]{1,0:T(8,128)(2,1)} %shard_map.87.cols, bf16[512,384]{1,0:T(8,128)(2,1)S(1)} %get-tuple-element.84.extra, ...), custom_call_target="tpu_custom_call" | custom-call | tf_op jit(solution)/shard_map/pallas_call | solution.py:899
  47.3 1.5 %collective-permute-start.9 = (f32[264,128]{1,0:T(8,128)S(1)}, f32[264,128]{1,0:T(8,128)S(1)}, u32[]{:S(2)}, u32[]{:S(2)}) collective-permute-start(f32[264,128]{1,0:T(8,128)S(1)} %bitcast.19), channel_id=1, source_target_pairs={{0,8},{8,0},{1,9},{9,1},{2,10},{10,2},{3,11},{11,3},{4,12},{12,4},... | collective-permute-start | bytes 405512 | tf_op jit(solution)/shard_map/ppermute | solution.py:48
  48.8 3.1 %collective-permute-start.10 = (f32[72,128]{1,0:T(8,128)S(1)}, f32[72,128]{1,0:T(8,128)S(1)}, u32[]{:S(2)}, u32[]{:S(2)}) collective-permute-start(f32[72,128]{1,0:T(8,128)S(1)} %get-tuple-element.97), channel_id=1, source_target_pairs={{0,1},{1,0},{2,3},{3,2},{4,5},{5,4},{6,7},{7,6},{8,9},{9,8},{10,11... | collective-permute-start | bytes 110600 | tf_op jit(solution)/shard_map/ppermute | solution.py:48
  51.9 1.9 %collective-permute-start.11 = (f32[72,128]{1,0:T(8,128)S(1)}, f32[72,128]{1,0:T(8,128)S(1)}, u32[]{:S(2)}, u32[]{:S(2)}) collective-permute-start(f32[72,128]{1,0:T(8,128)S(1)} %get-tuple-element.97), channel_id=1, source_target_pairs={{1,2},{2,1},{3,4},{4,3},{5,6},{6,5},{9,10},{10,9},{11,12},{12,11},... | collective-permute-start | bytes 110600 | tf_op jit(solution)/shard_map/ppermute | solution.py:48
  53.8 2.4 %shard_map.91 = (f32[16,256,128]{2,1,0:T(8,128)S(1)}, f32[40,128]{1,0:T(8,128)S(1)}, f32[18,256,128]{2,1,0:T(8,128)S(1)}) custom-call(bf16[512,1024]{1,0:T(8,128)(2,1)S(1)} %get-tuple-element.87.spread, bf16[1024,2176]{1,0:T(8,128)(2,1)S(1)} %get-tuple-element.88.sel, f32[16,256,128]{2,1,0:T(8,128)} %get-tuple-element.89.winds, ...), custom_call_target="tpu_custom_call" | custom-call | bytes 8388608 | tf_op jit(solution)/shard_map/pallas_call | solution.py:899
  56.3 3.3 %shard_map.92 = (f32[16,256,128]{2,1,0:T(8,128)S(1)}, f32[2,256,128]{2,1,0:T(8,128)S(1)}, f32[64,128]{1,0:T(8,128)S(1)}, f32[32,128]{1,0:T(8,128)S(1)}, f32[16,256,128]{2,1,0:T(8,128)S(1)}) custom-call(f32[16,128]{1,0:T(8,128)S(1)} %copy-done.1, f32[16,256,128]{2,1,0:T(8,128)S(1)} %get-tuple-element.91.field, f32[18,256,128]{2,1,0:T(8,128)S(1)} %get-tuple-element.92.winds, ...), custom_call_target="tpu_custom_call" | custom-call | bytes 16777216 | tf_op jit(solution)/shard_map/pallas_call | solution.py:899
  59.8 0.5 collective-permute-start.12
  60.4 0.8 %collective-permute-done.12.other = f32[40,128]{1,0:T(8,128)S(1)} collective-permute-done((f32[40,128]{1,0:T(8,128)S(1)}, f32[40,128]{1,0:T(8,128)S(1)}, u32[]{:S(2)}, u32[]{:S(2)}) %collective-permute-start.12) | collective-permute-done | bytes 20512 | tf_op jit(solution)/shard_map/ppermute | solution.py:905
  61.4 0.4 shard_map.96
  61.8 0.8 %collective-permute-start.13 = (f32[256,128]{1,0:T(8,128)S(1)}, f32[256,128]{1,0:T(8,128)S(1)}, u32[]{:S(2)}, u32[]{:S(2)}) collective-permute-start(f32[256,128]{1,0:T(8,128)S(1)} %bitcast.21), channel_id=1, source_target_pairs={{0,8},{8,0},{1,9},{9,1},{2,10},{10,2},{3,11},{11,3},{4,12},{12,4},... | collective-permute-start | bytes 393224 | tf_op jit(solution)/shard_map/ppermute | solution.py:48
  62.6 0.9 %collective-permute-start.14 = (f32[64,128]{1,0:T(8,128)S(1)}, f32[64,128]{1,0:T(8,128)S(1)}, u32[]{:S(2)}, u32[]{:S(2)}) collective-permute-start(f32[64,128]{1,0:T(8,128)S(1)} %get-tuple-element.112), channel_id=1, source_target_pairs={{0,1},{1,0},{2,3},{3,2},{4,5},{5,4},{6,7},{7,6},{8,9},{9,8},{10,11... | collective-permute-start | bytes 98312 | tf_op jit(solution)/shard_map/ppermute | solution.py:48
  63.5 3.9 %collective-permute-start.15 = (f32[64,128]{1,0:T(8,128)S(1)}, f32[64,128]{1,0:T(8,128)S(1)}, u32[]{:S(2)}, u32[]{:S(2)}) collective-permute-start(f32[64,128]{1,0:T(8,128)S(1)} %get-tuple-element.112), channel_id=1, source_target_pairs={{1,2},{2,1},{3,4},{4,3},{5,6},{6,5},{9,10},{10,9},{11,12},{12,11},... | collective-permute-start | bytes 98312 | tf_op jit(solution)/shard_map/ppermute | solution.py:48
  67.5 3.2 %shard_map.95.field = f32[16,256,128]{2,1,0:T(8,128)S(1)} custom-call(f32[16,128]{1,0:T(8,128)S(1)} %copy-done.1, f32[32,128]{1,0:T(8,128)S(1)} %get-tuple-element.104.floor, f32[32,128]{1,0:T(8,128)S(1)} %get-tuple-element.105.other, f32[32,128]{1,0:T(8,128)S(1)} %get-tuple-element.106.missing, f32[16,256,128]{2,1,0:T(8,128)S(1)} %get-tuple-element.107.field, ...), custom_call_target="tpu_custom_call" | custom-call | bytes 20971520 | tf_op jit(solution)/shard_map/pallas_call | solution.py:899
  70.8 1.7 %shard_map.97 = f32[256,16,128]{2,1,0:T(8,128)} custom-call(f32[16,256,128]{2,1,0:T(8,128)S(1)} %shard_map.95.field, f32[256,128]{1,0:T(8,128)S(1)} %collective-permute-done.13.rest_0_, f32[64,128]{1,0:T(8,128)S(1)} %collective-permute-done.14.rest_1_, f32[64,128]{1,0:T(8,128)S(1)} %collective-permute-done.15.rest_2_), custom_call_target="tpu_custom_call" | custom-call | tf_op jit(solution)/shard_map/pallas_call | solution.py:899
  (32 shorter events, 1.0 us)
Async XLA Ops:
  0.0 7.2 %copy-start.2 = (s32[512,1]{0,1:T(1,128)S(1)}, s32[512,1]{0,1:T(1,128)}, u32[]{:S(2)}) copy-start(s32[512,1]{0,1:T(1,128)} %param.12) | copy-start | bytes 6148
  0.0 7.2 %copy-start.3 = (s32[512]{0:T(512)S(1)}, s32[512]{0:T(512)}, u32[]{:S(2)}) copy-start(s32[512]{0:T(512)} %param.13) | copy-start | bytes 6148
  0.0 7.2 %copy-start.4 = (f32[512]{0:T(512)S(1)}, f32[512]{0:T(512)}, u32[]{:S(2)}) copy-start(f32[512]{0:T(512)} %param.15) | copy-start | bytes 6148
  0.0 7.2 %copy-start = (f32[512,256]{1,0:T(8,128)S(1)}, f32[512,256]{1,0:T(8,128)}, u32[]{:S(2)}) copy-start(f32[512,256]{1,0:T(8,128)} %op.1) | copy-start | bytes 1572868
  2.3 8.3 %collective-permute-start = (f32[256,128]{1,0:T(8,128)S(1)}, f32[256,128]{1,0:T(8,128)S(1)}, u32[]{:S(2)}, u32[]{:S(2)}) collective-permute-start(f32[256,128]{1,0:T(8,128)S(1)} %bitcast.22), channel_id=1, source_target_pairs={{0,8},{8,0},{1,9},{9,1},{2,10},{10,2},{3,11},{11,3},{4,12},{12,4},... | collective-permute-start | bytes 393224 | tf_op jit(solution)/shard_map/ppermute | solution.py:48
  3.9 6.7 %collective-permute-start.1 = (f32[64,128]{1,0:T(8,128)S(1)}, f32[64,128]{1,0:T(8,128)S(1)}, u32[]{:S(2)}, u32[]{:S(2)}) collective-permute-start(f32[64,128]{1,0:T(8,128)S(1)} %get-tuple-element.60), channel_id=1, source_target_pairs={{1,2},{2,1},{3,4},{4,3},{5,6},{6,5},{9,10},{10,9},{11,12},{12,11},... | collective-permute-start | bytes 98312 | tf_op jit(solution)/shard_map/ppermute | solution.py:48
  10.6 30.8 %all-to-all-start = ((f32[16,136,128]{2,1,0:T(8,128)}), f32[16,136,128]{2,1,0:T(8,128)S(1)}, u32[]{:S(2)}, u32[]{:S(2)}) async-start(f32[16,136,128]{2,1,0:T(8,128)} %shard_map.82), calls=%async_computation | async-start | bytes 2228224 | tf_op jit(solution)/shard_map/all_to_all | solution.py:926
  15.9 7.2 %collective-permute-start.2 = (f32[64,128]{1,0:T(8,128)S(1)}, f32[64,128]{1,0:T(8,128)S(1)}, u32[]{:S(2)}, u32[]{:S(2)}) collective-permute-start(f32[64,128]{1,0:T(8,128)S(1)} %get-tuple-element.60), channel_id=1, source_target_pairs={{0,1},{1,0},{2,3},{3,2},{4,5},{5,4},{6,7},{7,6},{8,9},{9,8},{10,11... | collective-permute-start | bytes 98312 | tf_op jit(solution)/shard_map/ppermute | solution.py:48
  18.1 6.4 %copy-start.1 = (f32[16,128]{1,0:T(8,128)S(1)}, f32[16,128]{1,0:T(8,128)}, u32[]{:S(2)}) copy-start(f32[16,128]{1,0:T(8,128)} %coupling.11) | copy-start | bytes 24580
  23.3 1.2 %collective-permute-start.3 = (f32[32,128]{1,0:T(8,128)S(1)}, f32[32,128]{1,0:T(8,128)S(1)}, u32[]{:S(2)}, u32[]{:S(2)}) collective-permute-start(f32[32,128]{1,0:T(8,128)S(1)} %shard_map.85), channel_id=1, source_target_pairs={{0,16},{16,0},{1,17},{17,1},{2,18},{18,2},{3,19},{19,3},{4,20},{20... | collective-permute-start | bytes 49160 | tf_op jit(solution)/shard_map/ppermute | solution.py:905
  29.6 8.8 %collective-permute-start.4 = (f32[264,128]{1,0:T(8,128)S(1)}, f32[264,128]{1,0:T(8,128)S(1)}, u32[]{:S(2)}, u32[]{:S(2)}) collective-permute-start(f32[264,128]{1,0:T(8,128)S(1)} %bitcast.20), channel_id=1, source_target_pairs={{0,8},{8,0},{1,9},{9,1},{2,10},{10,2},{3,11},{11,3},{4,12},{12,4},... | collective-permute-start | bytes 405512 | tf_op jit(solution)/shard_map/ppermute | solution.py:48
  31.1 7.3 %collective-permute-start.5 = (f32[72,128]{1,0:T(8,128)S(1)}, f32[72,128]{1,0:T(8,128)S(1)}, u32[]{:S(2)}, u32[]{:S(2)}) collective-permute-start(f32[72,128]{1,0:T(8,128)S(1)} %get-tuple-element.75), channel_id=1, source_target_pairs={{0,1},{1,0},{2,3},{3,2},{4,5},{5,4},{6,7},{7,6},{8,9},{9,8},{10,11... | collective-permute-start | bytes 110600 | tf_op jit(solution)/shard_map/ppermute | solution.py:48
  31.7 6.7 %collective-permute-start.6 = (f32[72,128]{1,0:T(8,128)S(1)}, f32[72,128]{1,0:T(8,128)S(1)}, u32[]{:S(2)}, u32[]{:S(2)}) collective-permute-start(f32[72,128]{1,0:T(8,128)S(1)} %get-tuple-element.75), channel_id=1, source_target_pairs={{1,2},{2,1},{3,4},{4,3},{5,6},{6,5},{9,10},{10,9},{11,12},{12,11},... | collective-permute-start | bytes 110600 | tf_op jit(solution)/shard_map/ppermute | solution.py:48
  38.6 1.2 %collective-permute-start.7 = (f32[32,128]{1,0:T(8,128)S(1)}, f32[32,128]{1,0:T(8,128)S(1)}, u32[]{:S(2)}, u32[]{:S(2)}) collective-permute-start(f32[32,128]{1,0:T(8,128)S(1)} %shard_map.88.floor), channel_id=1, source_target_pairs={{0,16},{16,0},{1,17},{17,1},{2,18},{18,2},{3,19},{19,3},{4,20},{20... | collective-permute-start | bytes 49160 | tf_op jit(solution)/shard_map/ppermute | solution.py:905
  47.3 12.4 %collective-permute-start.9 = (f32[264,128]{1,0:T(8,128)S(1)}, f32[264,128]{1,0:T(8,128)S(1)}, u32[]{:S(2)}, u32[]{:S(2)}) collective-permute-start(f32[264,128]{1,0:T(8,128)S(1)} %bitcast.19), channel_id=1, source_target_pairs={{0,8},{8,0},{1,9},{9,1},{2,10},{10,2},{3,11},{11,3},{4,12},{12,4},... | collective-permute-start | bytes 405512 | tf_op jit(solution)/shard_map/ppermute | solution.py:48
  48.8 10.8 %collective-permute-start.10 = (f32[72,128]{1,0:T(8,128)S(1)}, f32[72,128]{1,0:T(8,128)S(1)}, u32[]{:S(2)}, u32[]{:S(2)}) collective-permute-start(f32[72,128]{1,0:T(8,128)S(1)} %get-tuple-element.97), channel_id=1, source_target_pairs={{0,1},{1,0},{2,3},{3,2},{4,5},{5,4},{6,7},{7,6},{8,9},{9,8},{10,11... | collective-permute-start | bytes 110600 | tf_op jit(solution)/shard_map/ppermute | solution.py:48
  51.9 7.7 %collective-permute-start.11 = (f32[72,128]{1,0:T(8,128)S(1)}, f32[72,128]{1,0:T(8,128)S(1)}, u32[]{:S(2)}, u32[]{:S(2)}) collective-permute-start(f32[72,128]{1,0:T(8,128)S(1)} %get-tuple-element.97), channel_id=1, source_target_pairs={{1,2},{2,1},{3,4},{4,3},{5,6},{6,5},{9,10},{10,9},{11,12},{12,11},... | collective-permute-start | bytes 110600 | tf_op jit(solution)/shard_map/ppermute | solution.py:48
  56.2 3.4 %collective-permute-start.8 = (f32[40,128]{1,0:T(8,128)S(1)}, f32[40,128]{1,0:T(8,128)S(1)}, u32[]{:S(2)}, u32[]{:S(2)}) collective-permute-start(f32[40,128]{1,0:T(8,128)S(1)} %get-tuple-element.95), channel_id=1, source_target_pairs={{0,16},{16,0},{1,17},{17,1},{2,18},{18,2},{3,19},{19,3},{4,20},{20... | collective-permute-start | bytes 61448 | tf_op jit(solution)/shard_map/ppermute | solution.py:905
  56.3 11.1 %copy-start.5 = (f32[1,2,128]{2,1,0:T(2,128)S(1)}, f32[1,2,128]{2,1,0:T(2,128)}, u32[]{:S(2)}) copy-start(f32[1,2,128]{2,1,0:T(2,128)} %param.11) | copy-start | bytes 3076
  59.8 1.4 %collective-permute-start.12 = (f32[40,128]{1,0:T(8,128)S(1)}, f32[40,128]{1,0:T(8,128)S(1)}, u32[]{:S(2)}, u32[]{:S(2)}) collective-permute-start(f32[40,128]{1,0:T(8,128)S(1)} %get-tuple-element.103.floor), channel_id=1, source_target_pairs={{0,16},{16,0},{1,17},{17,1},{2,18},{18,2},{3,19},{19,3},{4,20},{20... | collective-permute-start | bytes 61448 | tf_op jit(solution)/shard_map/ppermute | solution.py:905
  61.8 8.9 %collective-permute-start.13 = (f32[256,128]{1,0:T(8,128)S(1)}, f32[256,128]{1,0:T(8,128)S(1)}, u32[]{:S(2)}, u32[]{:S(2)}) collective-permute-start(f32[256,128]{1,0:T(8,128)S(1)} %bitcast.21), channel_id=1, source_target_pairs={{0,8},{8,0},{1,9},{9,1},{2,10},{10,2},{3,11},{11,3},{4,12},{12,4},... | collective-permute-start | bytes 393224 | tf_op jit(solution)/shard_map/ppermute | solution.py:48
  62.6 8.1 %collective-permute-start.14 = (f32[64,128]{1,0:T(8,128)S(1)}, f32[64,128]{1,0:T(8,128)S(1)}, u32[]{:S(2)}, u32[]{:S(2)}) collective-permute-start(f32[64,128]{1,0:T(8,128)S(1)} %get-tuple-element.112), channel_id=1, source_target_pairs={{0,1},{1,0},{2,3},{3,2},{4,5},{5,4},{6,7},{7,6},{8,9},{9,8},{10,11... | collective-permute-start | bytes 98312 | tf_op jit(solution)/shard_map/ppermute | solution.py:48
  63.5 7.2 %collective-permute-start.15 = (f32[64,128]{1,0:T(8,128)S(1)}, f32[64,128]{1,0:T(8,128)S(1)}, u32[]{:S(2)}, u32[]{:S(2)}) collective-permute-start(f32[64,128]{1,0:T(8,128)S(1)} %get-tuple-element.112), channel_id=1, source_target_pairs={{1,2},{2,1},{3,4},{4,3},{5,6},{6,5},{9,10},{10,9},{11,12},{12,11},... | collective-permute-start | bytes 98312 | tf_op jit(solution)/shard_map/ppermute | solution.py:48

commit v12 on v10

--- a/solution.py
+++ b/solution.py
@@ -747,7 +747,7 @@
     coupling, wind_ends, wind_dense, dense_g, spread, sel, strips, packed = rest[:8]
     col_cells, precs, both, sems = rest[8:]
     inside = rows * LANES
-    chunks = 8
+    chunks = 4
     copies = []
     for part in range(chunks):
         at = pl.ds(part * (2 * width // chunks), 2 * width // chunks)
@@ -973,7 +973,7 @@
             pltpu.VMEM((2 * width, (rows + 1) * LANES), jnp.bfloat16),
             pltpu.VMEM((slots, LANES), jnp.float32),
             pltpu.VMEM((slots, 2 * width), jnp.float32),
-            sems(8),
+            sems(4),
         ],
         (records, cols, extra, bottom, coupling, wind_ends, wind_dense, dense_g),
         far=(1,),

time: 73.1 us -> 73.1 us (level)
  no operation moved by 1% of the time
where the time goes in v12:
time: 73.1 us; the launch traced here: 72.4 us
  Pallas kernels  35.2 us (48%)
  starting transfers between devices  30 us (41%)
  waiting for transfers between devices  6.11 us (8%)
  local copies, waits for them, and re-layouts  0.83 us (1%)
    pallas_call x15, Pallas kernels, run(): call(body, out_shape, scratch, in_specs=specs, out_specs=outs, **kw)(*args)  33.1 us
    ppermute x12, starting transfers between devices, pair_swap(): return lax.ppermute(block, axis, route)  23.9 us
    all_to_all x1, starting transfers between devices, local(): lax.all_to_all(send, ('gx', 'gy'), split_axis=0, concat_axis=0, tiled=True)  5.34 us
    ppermute x4, waiting for transfers between devices, swap_floor(): return lax.ppermute(floor, 'comp', [(0, 1), (1, 0)])  3.19 us
    pallas_call x1, Pallas kernels, local(): call(functools.partial(route_kernel, tiles, cap), f32(tiles, halves * cap...  2.04 us
    all_to_all x1, waiting for transfers between devices, local(): lax.all_to_all(send, ('gx', 'gy'), split_axis=0, concat_axis=0, tiled=True)  1.52 us
  transfers between devices with their start and end apart: 17, of which 5 were waited for; matrix products, arithmetic and copies ran while one was open for 1% of the time, Pallas kernels for 34%

profile of v12, /device:TPU:8, one launch (start us, length us, event | category | flops | bytes accessed | tf_op | source)
XLA Modules:
  0.0 72.4 jit_solution(9847025396053684150)
XLA Ops:
  0.0 2.3 %shard_map.83 = (f32[1,256,128]{2,1,0:T(8,128)S(1)}, f32[64,128]{1,0:T(8,128)S(1)}, f32[32,128]{1,0:T(8,128)S(1)}, f32[32,128]{1,0:T(8,128)S(1)}) custom-call(f32[4096,128]{1,0:T(8,128)} %bitcast.23), custom_call_target="tpu_custom_call" | custom-call | tf_op jit(solution)/shard_map/pallas_call | solution.py:900
  2.3 1.6 %collective-permute-start = (f32[256,128]{1,0:T(8,128)S(1)}, f32[256,128]{1,0:T(8,128)S(1)}, u32[]{:S(2)}, u32[]{:S(2)}) collective-permute-start(f32[256,128]{1,0:T(8,128)S(1)} %bitcast.22), channel_id=1, source_target_pairs={{0,8},{8,0},{1,9},{9,1},{2,10},{10,2},{3,11},{11,3},{4,12},{12,4},... | collective-permute-start | bytes 393224 | tf_op jit(solution)/shard_map/ppermute | solution.py:48
  3.9 3.3 %collective-permute-start.1 = (f32[64,128]{1,0:T(8,128)S(1)}, f32[64,128]{1,0:T(8,128)S(1)}, u32[]{:S(2)}, u32[]{:S(2)}) collective-permute-start(f32[64,128]{1,0:T(8,128)S(1)} %get-tuple-element.60), channel_id=1, source_target_pairs={{1,2},{2,1},{3,4},{4,3},{5,6},{6,5},{9,10},{10,9},{11,12},{12,11},... | collective-permute-start | bytes 98312 | tf_op jit(solution)/shard_map/ppermute | solution.py:48
  7.2 2.0 %shard_map.82 = f32[16,136,128]{2,1,0:T(8,128)} custom-call(s32[1,512]{1,0:T(1,128)S(1)} %bitcast.16, s32[1,512]{1,0:T(1,128)S(1)} %bitcast.17, f32[1,512]{1,0:T(1,128)S(1)} %bitcast.18, f32[512,256]{1,0:T(8,128)S(1)} %copy-done), custom_call_target="tpu_custom_call" | custom-call | tf_op jit(solution)/shard_map/pallas_call | solution.py:923
  9.3 1.3 %collective-permute-done.1.rest_2_ = f32[64,128]{1,0:T(8,128)S(1)} collective-permute-done((f32[64,128]{1,0:T(8,128)S(1)}, f32[64,128]{1,0:T(8,128)S(1)}, u32[]{:S(2)}, u32[]{:S(2)}) %collective-permute-start.1) | collective-permute-done | bytes 32800 | tf_op jit(solution)/shard_map/ppermute | solution.py:48
  10.6 5.3 %all-to-all-start = ((f32[16,136,128]{2,1,0:T(8,128)}), f32[16,136,128]{2,1,0:T(8,128)S(1)}, u32[]{:S(2)}, u32[]{:S(2)}) async-start(f32[16,136,128]{2,1,0:T(8,128)} %shard_map.82), calls=%async_computation | async-start | bytes 2228224 | tf_op jit(solution)/shard_map/all_to_all | solution.py:927
  15.9 1.5 %collective-permute-start.2 = (f32[64,128]{1,0:T(8,128)S(1)}, f32[64,128]{1,0:T(8,128)S(1)}, u32[]{:S(2)}, u32[]{:S(2)}) collective-permute-start(f32[64,128]{1,0:T(8,128)S(1)} %get-tuple-element.60), channel_id=1, source_target_pairs={{0,1},{1,0},{2,3},{3,2},{4,5},{5,4},{6,7},{7,6},{8,9},{9,8},{10,11... | collective-permute-start | bytes 98312 | tf_op jit(solution)/shard_map/ppermute | solution.py:48
  17.4 0.7 slice_bitcast_fusion.winds
  18.1 5.0 %shard_map.84 = (f32[16,256,128]{2,1,0:T(8,128)S(1)}, f32[16,256,128]{2,1,0:T(8,128)S(1)}, f32[16,256,128]{2,1,0:T(8,128)}, f32[16,256,128]{2,1,0:T(8,128)}) custom-call(f32[256,16,128]{2,1,0:T(8,128)} %bitcast.24, f32[256,16,128]{2,1,0:T(8,128)} %bitcast.25), custom_call_target="tpu_custom_call" | custom-call | bytes 10485760 | tf_op jit(solution)/shard_map/pallas_call | solution.py:900
  23.4 1.2 %collective-permute-done.3.other = f32[32,128]{1,0:T(8,128)S(1)} collective-permute-done((f32[32,128]{1,0:T(8,128)S(1)}, f32[32,128]{1,0:T(8,128)S(1)}, u32[]{:S(2)}, u32[]{:S(2)}) %collective-permute-start.3) | collective-permute-done | bytes 16416 | tf_op jit(solution)/shard_map/ppermute | solution.py:906
  24.5 4.9 %shard_map.86 = (f32[18,256,128]{2,1,0:T(8,128)S(1)}, f32[1,264,128]{2,1,0:T(8,128)S(1)}, f32[72,128]{1,0:T(8,128)S(1)}, f32[32,128]{1,0:T(8,128)S(1)}, f32[32,1...) custom-call(f32[16,128]{1,0:T(8,128)S(1)} %copy-done.1, ...), custom_call_target="tpu_custom_call" | custom-call | tf_op jit(solution)/shard_map/pallas_call | solution.py:900
  29.4 1.5 %collective-permute-start.4 = (f32[264,128]{1,0:T(8,128)S(1)}, f32[264,128]{1,0:T(8,128)S(1)}, u32[]{:S(2)}, u32[]{:S(2)}) collective-permute-start(f32[264,128]{1,0:T(8,128)S(1)} %bitcast.20), channel_id=1, source_target_pairs={{0,8},{8,0},{1,9},{9,1},{2,10},{10,2},{3,11},{11,3},{4,12},{12,4},... | collective-permute-start | bytes 405512 | tf_op jit(solution)/shard_map/ppermute | solution.py:48
  31.0 0.6 collective-permute-start.5
  31.5 3.4 %collective-permute-start.6 = (f32[72,128]{1,0:T(8,128)S(1)}, f32[72,128]{1,0:T(8,128)S(1)}, u32[]{:S(2)}, u32[]{:S(2)}) collective-permute-start(f32[72,128]{1,0:T(8,128)S(1)} %get-tuple-element.75), channel_id=1, source_target_pairs={{1,2},{2,1},{3,4},{4,3},{5,6},{6,5},{9,10},{10,9},{11,12},{12,11},... | collective-permute-start | bytes 110600 | tf_op jit(solution)/shard_map/ppermute | solution.py:48
  34.9 3.3 %shard_map.87.cols = bf16[512,2048]{1,0:T(8,128)(2,1)} custom-call(f32[18,256,128]{2,1,0:T(8,128)S(1)} %get-tuple-element.73.cells, f32[16,256,128]{2,1,0:T(8,128)S(1)} %get-tuple-element.72.winds), custom_call_target="tpu_custom_call" | custom-call | bytes 20971520 | tf_op jit(solution)/shard_map/pallas_call | solution.py:900
  38.5 1.2 %collective-permute-done.7.other = f32[32,128]{1,0:T(8,128)S(1)} collective-permute-done((f32[32,128]{1,0:T(8,128)S(1)}, f32[32,128]{1,0:T(8,128)S(1)}, u32[]{:S(2)}, u32[]{:S(2)}) %collective-permute-start.7) | collective-permute-done | bytes 16416 | tf_op jit(solution)/shard_map/ppermute | solution.py:906
  39.7 0.2 shard_map.89
  39.9 1.5 %all-to-all-done.records = f32[16,136,128]{2,1,0:T(8,128)S(1)} async-done(((f32[16,136,128]{2,1,0:T(8,128)}), f32[16,136,128]{2,1,0:T(8,128)S(1)}, u32[]{:S(2)}, u32[]{:S(2)}) %all-to-all-start) | async-done | bytes 1114144 | tf_op jit(solution)/shard_map/all_to_all | solution.py:927
  41.4 5.9 %shard_map.90 = (bf16[512,1024]{1,0:T(8,128)(2,1)S(1)}, bf16[1024,2176]{1,0:T(8,128)(2,1)S(1)}, f32[1,264,128]{2,1,0:T(8,128)S(1)}, f32[72,128]{1,0:T(8,128)S(1)}) custom-call(f32[16,136,128]{2,1,0:T(8,128)S(1)} %all-to-all-done.records, bf16[512,2048]{1,0:T(8,128)(2,1)} %shard_map.87.cols, bf16[512,384]{1,0:T(8,128)(2,1)S(1)} %get-tuple-element.84.extra, ...), custom_call_target="tpu_custom_call" | custom-call | tf_op jit(solution)/shard_map/pallas_call | solution.py:900
  47.3 1.5 %collective-permute-start.9 = (f32[264,128]{1,0:T(8,128)S(1)}, f32[264,128]{1,0:T(8,128)S(1)}, u32[]{:S(2)}, u32[]{:S(2)}) collective-permute-start(f32[264,128]{1,0:T(8,128)S(1)} %bitcast.19), channel_id=1, source_target_pairs={{0,8},{8,0},{1,9},{9,1},{2,10},{10,2},{3,11},{11,3},{4,12},{12,4},... | collective-permute-start | bytes 405512 | tf_op jit(solution)/shard_map/ppermute | solution.py:48
  48.8 3.1 %collective-permute-start.10 = (f32[72,128]{1,0:T(8,128)S(1)}, f32[72,128]{1,0:T(8,128)S(1)}, u32[]{:S(2)}, u32[]{:S(2)}) collective-permute-start(f32[72,128]{1,0:T(8,128)S(1)} %get-tuple-element.97), channel_id=1, source_target_pairs={{0,1},{1,0},{2,3},{3,2},{4,5},{5,4},{6,7},{7,6},{8,9},{9,8},{10,11... | collective-permute-start | bytes 110600 | tf_op jit(solution)/shard_map/ppermute | solution.py:48
  51.9 1.9 %collective-permute-start.11 = (f32[72,128]{1,0:T(8,128)S(1)}, f32[72,128]{1,0:T(8,128)S(1)}, u32[]{:S(2)}, u32[]{:S(2)}) collective-permute-start(f32[72,128]{1,0:T(8,128)S(1)} %get-tuple-element.97), channel_id=1, source_target_pairs={{1,2},{2,1},{3,4},{4,3},{5,6},{6,5},{9,10},{10,9},{11,12},{12,11},... | collective-permute-start | bytes 110600 | tf_op jit(solution)/shard_map/ppermute | solution.py:48
  53.9 2.4 %shard_map.91 = (f32[16,256,128]{2,1,0:T(8,128)S(1)}, f32[40,128]{1,0:T(8,128)S(1)}, f32[18,256,128]{2,1,0:T(8,128)S(1)}) custom-call(bf16[512,1024]{1,0:T(8,128)(2,1)S(1)} %get-tuple-element.87.spread, bf16[1024,2176]{1,0:T(8,128)(2,1)S(1)} %get-tuple-element.88.sel, f32[16,256,128]{2,1,0:T(8,128)} %get-tuple-element.89.winds, ...), custom_call_target="tpu_custom_call" | custom-call | bytes 8388608 | tf_op jit(solution)/shard_map/pallas_call | solution.py:900
  56.3 3.3 %shard_map.92 = (f32[16,256,128]{2,1,0:T(8,128)S(1)}, f32[2,256,128]{2,1,0:T(8,128)S(1)}, f32[64,128]{1,0:T(8,128)S(1)}, f32[32,128]{1,0:T(8,128)S(1)}, f32[16,256,128]{2,1,0:T(8,128)S(1)}) custom-call(f32[16,128]{1,0:T(8,128)S(1)} %copy-done.1, f32[16,256,128]{2,1,0:T(8,128)S(1)} %get-tuple-element.91.field, f32[18,256,128]{2,1,0:T(8,128)S(1)} %get-tuple-element.92.winds, ...), custom_call_target="tpu_custom_call" | custom-call | bytes 16777216 | tf_op jit(solution)/shard_map/pallas_call | solution.py:900
  59.9 0.5 collective-permute-start.12
  60.4 0.8 %collective-permute-done.12.other = f32[40,128]{1,0:T(8,128)S(1)} collective-permute-done((f32[40,128]{1,0:T(8,128)S(1)}, f32[40,128]{1,0:T(8,128)S(1)}, u32[]{:S(2)}, u32[]{:S(2)}) %collective-permute-start.12) | collective-permute-done | bytes 20512 | tf_op jit(solution)/shard_map/ppermute | solution.py:906
  61.4 0.4 shard_map.96
  61.8 0.7 %collective-permute-start.13 = (f32[256,128]{1,0:T(8,128)S(1)}, f32[256,128]{1,0:T(8,128)S(1)}, u32[]{:S(2)}, u32[]{:S(2)}) collective-permute-start(f32[256,128]{1,0:T(8,128)S(1)} %bitcast.21), channel_id=1, source_target_pairs={{0,8},{8,0},{1,9},{9,1},{2,10},{10,2},{3,11},{11,3},{4,12},{12,4},... | collective-permute-start | bytes 393224 | tf_op jit(solution)/shard_map/ppermute | solution.py:48
  62.6 0.9 %collective-permute-start.14 = (f32[64,128]{1,0:T(8,128)S(1)}, f32[64,128]{1,0:T(8,128)S(1)}, u32[]{:S(2)}, u32[]{:S(2)}) collective-permute-start(f32[64,128]{1,0:T(8,128)S(1)} %get-tuple-element.112), channel_id=1, source_target_pairs={{0,1},{1,0},{2,3},{3,2},{4,5},{5,4},{6,7},{7,6},{8,9},{9,8},{10,11... | collective-permute-start | bytes 98312 | tf_op jit(solution)/shard_map/ppermute | solution.py:48
  63.5 3.9 %collective-permute-start.15 = (f32[64,128]{1,0:T(8,128)S(1)}, f32[64,128]{1,0:T(8,128)S(1)}, u32[]{:S(2)}, u32[]{:S(2)}) collective-permute-start(f32[64,128]{1,0:T(8,128)S(1)} %get-tuple-element.112), channel_id=1, source_target_pairs={{1,2},{2,1},{3,4},{4,3},{5,6},{6,5},{9,10},{10,9},{11,12},{12,11},... | collective-permute-start | bytes 98312 | tf_op jit(solution)/shard_map/ppermute | solution.py:48
  67.5 3.2 %shard_map.95.field = f32[16,256,128]{2,1,0:T(8,128)S(1)} custom-call(f32[16,128]{1,0:T(8,128)S(1)} %copy-done.1, f32[32,128]{1,0:T(8,128)S(1)} %get-tuple-element.104.floor, f32[32,128]{1,0:T(8,128)S(1)} %get-tuple-element.105.other, f32[32,128]{1,0:T(8,128)S(1)} %get-tuple-element.106.missing, f32[16,256,128]{2,1,0:T(8,128)S(1)} %get-tuple-element.107.field, ...), custom_call_target="tpu_custom_call" | custom-call | bytes 20971520 | tf_op jit(solution)/shard_map/pallas_call | solution.py:900
  70.7 1.7 %shard_map.97 = f32[256,16,128]{2,1,0:T(8,128)} custom-call(f32[16,256,128]{2,1,0:T(8,128)S(1)} %shard_map.95.field, f32[256,128]{1,0:T(8,128)S(1)} %collective-permute-done.13.rest_0_, f32[64,128]{1,0:T(8,128)S(1)} %collective-permute-done.14.rest_1_, f32[64,128]{1,0:T(8,128)S(1)} %collective-permute-done.15.rest_2_), custom_call_target="tpu_custom_call" | custom-call | tf_op jit(solution)/shard_map/pallas_call | solution.py:900
  (32 shorter events, 1.0 us)
Async XLA Ops:
  0.0 7.2 %copy-start.2 = (s32[512,1]{0,1:T(1,128)S(1)}, s32[512,1]{0,1:T(1,128)}, u32[]{:S(2)}) copy-start(s32[512,1]{0,1:T(1,128)} %param.12) | copy-start | bytes 6148
  0.0 7.2 %copy-start.3 = (s32[512]{0:T(512)S(1)}, s32[512]{0:T(512)}, u32[]{:S(2)}) copy-start(s32[512]{0:T(512)} %param.13) | copy-start | bytes 6148
  0.0 7.2 %copy-start.4 = (f32[512]{0:T(512)S(1)}, f32[512]{0:T(512)}, u32[]{:S(2)}) copy-start(f32[512]{0:T(512)} %param.15) | copy-start | bytes 6148
  0.0 7.2 %copy-start = (f32[512,256]{1,0:T(8,128)S(1)}, f32[512,256]{1,0:T(8,128)}, u32[]{:S(2)}) copy-start(f32[512,256]{1,0:T(8,128)} %op.1) | copy-start | bytes 1572868
  2.3 8.3 %collective-permute-start = (f32[256,128]{1,0:T(8,128)S(1)}, f32[256,128]{1,0:T(8,128)S(1)}, u32[]{:S(2)}, u32[]{:S(2)}) collective-permute-start(f32[256,128]{1,0:T(8,128)S(1)} %bitcast.22), channel_id=1, source_target_pairs={{0,8},{8,0},{1,9},{9,1},{2,10},{10,2},{3,11},{11,3},{4,12},{12,4},... | collective-permute-start | bytes 393224 | tf_op jit(solution)/shard_map/ppermute | solution.py:48
  3.9 6.7 %collective-permute-start.1 = (f32[64,128]{1,0:T(8,128)S(1)}, f32[64,128]{1,0:T(8,128)S(1)}, u32[]{:S(2)}, u32[]{:S(2)}) collective-permute-start(f32[64,128]{1,0:T(8,128)S(1)} %get-tuple-element.60), channel_id=1, source_target_pairs={{1,2},{2,1},{3,4},{4,3},{5,6},{6,5},{9,10},{10,9},{11,12},{12,11},... | collective-permute-start | bytes 98312 | tf_op jit(solution)/shard_map/ppermute | solution.py:48
  10.6 30.8 %all-to-all-start = ((f32[16,136,128]{2,1,0:T(8,128)}), f32[16,136,128]{2,1,0:T(8,128)S(1)}, u32[]{:S(2)}, u32[]{:S(2)}) async-start(f32[16,136,128]{2,1,0:T(8,128)} %shard_map.82), calls=%async_computation | async-start | bytes 2228224 | tf_op jit(solution)/shard_map/all_to_all | solution.py:927
  15.9 7.2 %collective-permute-start.2 = (f32[64,128]{1,0:T(8,128)S(1)}, f32[64,128]{1,0:T(8,128)S(1)}, u32[]{:S(2)}, u32[]{:S(2)}) collective-permute-start(f32[64,128]{1,0:T(8,128)S(1)} %get-tuple-element.60), channel_id=1, source_target_pairs={{0,1},{1,0},{2,3},{3,2},{4,5},{5,4},{6,7},{7,6},{8,9},{9,8},{10,11... | collective-permute-start | bytes 98312 | tf_op jit(solution)/shard_map/ppermute | solution.py:48
  18.1 6.4 %copy-start.1 = (f32[16,128]{1,0:T(8,128)S(1)}, f32[16,128]{1,0:T(8,128)}, u32[]{:S(2)}) copy-start(f32[16,128]{1,0:T(8,128)} %coupling.11) | copy-start | bytes 24580
  23.3 1.2 %collective-permute-start.3 = (f32[32,128]{1,0:T(8,128)S(1)}, f32[32,128]{1,0:T(8,128)S(1)}, u32[]{:S(2)}, u32[]{:S(2)}) collective-permute-start(f32[32,128]{1,0:T(8,128)S(1)} %shard_map.85), channel_id=1, source_target_pairs={{0,16},{16,0},{1,17},{17,1},{2,18},{18,2},{3,19},{19,3},{4,20},{20... | collective-permute-start | bytes 49160 | tf_op jit(solution)/shard_map/ppermute | solution.py:906
  29.4 8.8 %collective-permute-start.4 = (f32[264,128]{1,0:T(8,128)S(1)}, f32[264,128]{1,0:T(8,128)S(1)}, u32[]{:S(2)}, u32[]{:S(2)}) collective-permute-start(f32[264,128]{1,0:T(8,128)S(1)} %bitcast.20), channel_id=1, source_target_pairs={{0,8},{8,0},{1,9},{9,1},{2,10},{10,2},{3,11},{11,3},{4,12},{12,4},... | collective-permute-start | bytes 405512 | tf_op jit(solution)/shard_map/ppermute | solution.py:48
  31.0 7.3 %collective-permute-start.5 = (f32[72,128]{1,0:T(8,128)S(1)}, f32[72,128]{1,0:T(8,128)S(1)}, u32[]{:S(2)}, u32[]{:S(2)}) collective-permute-start(f32[72,128]{1,0:T(8,128)S(1)} %get-tuple-element.75), channel_id=1, source_target_pairs={{0,1},{1,0},{2,3},{3,2},{4,5},{5,4},{6,7},{7,6},{8,9},{9,8},{10,11... | collective-permute-start | bytes 110600 | tf_op jit(solution)/shard_map/ppermute | solution.py:48
  31.5 6.7 %collective-permute-start.6 = (f32[72,128]{1,0:T(8,128)S(1)}, f32[72,128]{1,0:T(8,128)S(1)}, u32[]{:S(2)}, u32[]{:S(2)}) collective-permute-start(f32[72,128]{1,0:T(8,128)S(1)} %get-tuple-element.75), channel_id=1, source_target_pairs={{1,2},{2,1},{3,4},{4,3},{5,6},{6,5},{9,10},{10,9},{11,12},{12,11},... | collective-permute-start | bytes 110600 | tf_op jit(solution)/shard_map/ppermute | solution.py:48
  38.4 1.2 %collective-permute-start.7 = (f32[32,128]{1,0:T(8,128)S(1)}, f32[32,128]{1,0:T(8,128)S(1)}, u32[]{:S(2)}, u32[]{:S(2)}) collective-permute-start(f32[32,128]{1,0:T(8,128)S(1)} %shard_map.88.floor), channel_id=1, source_target_pairs={{0,16},{16,0},{1,17},{17,1},{2,18},{18,2},{3,19},{19,3},{4,20},{20... | collective-permute-start | bytes 49160 | tf_op jit(solution)/shard_map/ppermute | solution.py:906
  47.3 12.4 %collective-permute-start.9 = (f32[264,128]{1,0:T(8,128)S(1)}, f32[264,128]{1,0:T(8,128)S(1)}, u32[]{:S(2)}, u32[]{:S(2)}) collective-permute-start(f32[264,128]{1,0:T(8,128)S(1)} %bitcast.19), channel_id=1, source_target_pairs={{0,8},{8,0},{1,9},{9,1},{2,10},{10,2},{3,11},{11,3},{4,12},{12,4},... | collective-permute-start | bytes 405512 | tf_op jit(solution)/shard_map/ppermute | solution.py:48
  48.8 10.9 %collective-permute-start.10 = (f32[72,128]{1,0:T(8,128)S(1)}, f32[72,128]{1,0:T(8,128)S(1)}, u32[]{:S(2)}, u32[]{:S(2)}) collective-permute-start(f32[72,128]{1,0:T(8,128)S(1)} %get-tuple-element.97), channel_id=1, source_target_pairs={{0,1},{1,0},{2,3},{3,2},{4,5},{5,4},{6,7},{7,6},{8,9},{9,8},{10,11... | collective-permute-start | bytes 110600 | tf_op jit(solution)/shard_map/ppermute | solution.py:48
  51.9 7.7 %collective-permute-start.11 = (f32[72,128]{1,0:T(8,128)S(1)}, f32[72,128]{1,0:T(8,128)S(1)}, u32[]{:S(2)}, u32[]{:S(2)}) collective-permute-start(f32[72,128]{1,0:T(8,128)S(1)} %get-tuple-element.97), channel_id=1, source_target_pairs={{1,2},{2,1},{3,4},{4,3},{5,6},{6,5},{9,10},{10,9},{11,12},{12,11},... | collective-permute-start | bytes 110600 | tf_op jit(solution)/shard_map/ppermute | solution.py:48
  56.2 3.4 %collective-permute-start.8 = (f32[40,128]{1,0:T(8,128)S(1)}, f32[40,128]{1,0:T(8,128)S(1)}, u32[]{:S(2)}, u32[]{:S(2)}) collective-permute-start(f32[40,128]{1,0:T(8,128)S(1)} %get-tuple-element.95), channel_id=1, source_target_pairs={{0,16},{16,0},{1,17},{17,1},{2,18},{18,2},{3,19},{19,3},{4,20},{20... | collective-permute-start | bytes 61448 | tf_op jit(solution)/shard_map/ppermute | solution.py:906
  56.3 11.1 %copy-start.5 = (f32[1,2,128]{2,1,0:T(2,128)S(1)}, f32[1,2,128]{2,1,0:T(2,128)}, u32[]{:S(2)}) copy-start(f32[1,2,128]{2,1,0:T(2,128)} %param.11) | copy-start | bytes 3076
  59.9 1.4 %collective-permute-start.12 = (f32[40,128]{1,0:T(8,128)S(1)}, f32[40,128]{1,0:T(8,128)S(1)}, u32[]{:S(2)}, u32[]{:S(2)}) collective-permute-start(f32[40,128]{1,0:T(8,128)S(1)} %get-tuple-element.103.floor), channel_id=1, source_target_pairs={{0,16},{16,0},{1,17},{17,1},{2,18},{18,2},{3,19},{19,3},{4,20},{20... | collective-permute-start | bytes 61448 | tf_op jit(solution)/shard_map/ppermute | solution.py:906
  61.8 8.9 %collective-permute-start.13 = (f32[256,128]{1,0:T(8,128)S(1)}, f32[256,128]{1,0:T(8,128)S(1)}, u32[]{:S(2)}, u32[]{:S(2)}) collective-permute-start(f32[256,128]{1,0:T(8,128)S(1)} %bitcast.21), channel_id=1, source_target_pairs={{0,8},{8,0},{1,9},{9,1},{2,10},{10,2},{3,11},{11,3},{4,12},{12,4},... | collective-permute-start | bytes 393224 | tf_op jit(solution)/shard_map/ppermute | solution.py:48
  62.6 8.1 %collective-permute-start.14 = (f32[64,128]{1,0:T(8,128)S(1)}, f32[64,128]{1,0:T(8,128)S(1)}, u32[]{:S(2)}, u32[]{:S(2)}) collective-permute-start(f32[64,128]{1,0:T(8,128)S(1)} %get-tuple-element.112), channel_id=1, source_target_pairs={{0,1},{1,0},{2,3},{3,2},{4,5},{5,4},{6,7},{7,6},{8,9},{9,8},{10,11... | collective-permute-start | bytes 98312 | tf_op jit(solution)/shard_map/ppermute | solution.py:48
  63.5 7.2 %collective-permute-start.15 = (f32[64,128]{1,0:T(8,128)S(1)}, f32[64,128]{1,0:T(8,128)S(1)}, u32[]{:S(2)}, u32[]{:S(2)}) collective-permute-start(f32[64,128]{1,0:T(8,128)S(1)} %get-tuple-element.112), channel_id=1, source_target_pairs={{1,2},{2,1},{3,4},{4,3},{5,6},{6,5},{9,10},{10,9},{11,12},{12,11},... | collective-permute-start | bytes 98312 | tf_op jit(solution)/shard_map/ppermute | solution.py:48
